TPU v7x, 256 devices: a whole 4x4x8 slice. The times are simulated.
256 devices in a mesh: dp: 32 (over y_lo, z, core), fsdp: 8 (over x, y_hi).
Axes of the slice: x: 4, y: 4 (y_hi: 2, y_lo: 2; y = y_hi * 2 + y_lo), z: 8, core: 2. Of those that a mesh axis runs over, the one named last changes fastest.
Arguments:
- features: bfloat16 [1024, 8, 8, 3072], P(('dp', 'fsdp')), may hold values from -8 to 8
- text_embed: bfloat16 [1024, 1152], P(('dp', 'fsdp')), may hold values from -1 to 1
- img_ids: int32 [1024], P(('dp', 'fsdp')), may hold values from 0 to 63
- txt_ids: int32 [1024], P(('dp', 'fsdp')), may hold values from 0 to 63
- kernel: float32 [7, 7, 3072], replicated, may hold values from -0.875 to 0.875
- norm_gain: float32 [3072], replicated, may hold values from 0.1 to 1.9
- head_gain: float32 [3072], replicated, may hold values from 0.1 to 1.9
- projection: bfloat16 [3072, 1152], P('fsdp'), may hold values from -0.109375 to 0.109375
- logit_scale: float32 [1], replicated, may hold values from 3 to 6
- logit_bias: float32 [1], replicated, may hold values from -4 to -1
Outputs:
- grad_features: bfloat16 [1024, 8, 8, 3072], P(('dp', 'fsdp'))
- grad_text: float32 [1024, 1152], P(('dp', 'fsdp'))
- grad_proj: float32 [3072, 1152], P('fsdp')
All inputs are finite; a program needn't handle non-finite values.
Results may differ from a plain program's by a relative error of at most 0.007.
Values may be sent and summed in bfloat16 or wider, within the bound.
No kernel may reach another device: no remote copies, remote signals or barrier semaphores. Data moves between devices by JAX's collectives and lax.ppermute only.
A program may use at most 128 MiB of HBM per device.

v0:
```python
import jax
import jax.numpy as jnp
from jax import lax
from jax.sharding import PartitionSpec as P

EPSILON = 1e-06


def block_pool(widened, kernel, norm_gain):
    margin = kernel.shape[0] // 2
    filtered = lax.conv_general_dilated(
        widened,
        kernel[:, :, None, :],
        (1, 1),
        ((margin, margin), (margin, margin)),
        dimension_numbers=("NHWC", "HWIO", "NHWC"),
        feature_group_count=widened.shape[3],
        precision=lax.Precision.HIGHEST,
    )
    average = jnp.mean(filtered, axis=-1, keepdims=True)
    centred = filtered - average
    spread = jnp.mean(centred * centred, axis=-1, keepdims=True)
    normed = centred * lax.rsqrt(spread + EPSILON) * norm_gain
    return jnp.mean(widened + normed, axis=(1, 2))


def head_norm(pooled):
    average = jnp.mean(pooled, axis=-1, keepdims=True)
    centred = pooled - average
    spread = jnp.mean(centred * centred, axis=-1, keepdims=True)
    return centred * lax.rsqrt(spread + EPSILON)


def unit_rows(values):
    return values * lax.rsqrt(jnp.sum(values * values, axis=-1, keepdims=True) + EPSILON)


def pair_weights(left_units, left_ids, right_units, right_ids, scale, shift):
    logits = (
        scale * jnp.einsum("ie,je->ij", left_units, right_units, preferred_element_type=jnp.float32)
        + shift
    )
    signs = jnp.where(left_ids[:, None] == right_ids[None, :], 1.0, -1.0).astype(jnp.float32)
    return (-signs * jax.nn.sigmoid(-signs * logits)).astype(jnp.bfloat16)


def local(
    features,
    text_embed,
    img_ids,
    txt_ids,
    kernel,
    norm_gain,
    head_gain,
    projection,
    logit_scale,
    logit_bias,
):
    scale = logit_scale[0]
    shift = logit_bias[0]
    widened = features.astype(jnp.float32)

    def local_pool(field):
        return block_pool(field, kernel, norm_gain)

    pooled, block_back = jax.vjp(local_pool, widened)
    normalized, head_back = jax.vjp(head_norm, pooled)
    head_input = (normalized * head_gain).astype(jnp.bfloat16)
    local_rows = head_input.shape[0]
    width_share = projection.shape[0]
    group_input = lax.all_gather(head_input, "fsdp", axis=0, tiled=True)
    own_columns = lax.dynamic_slice_in_dim(
        group_input, lax.axis_index("fsdp") * width_share, width_share, 1
    )
    embedded = lax.psum_scatter(
        jnp.dot(
            lax.slice_in_dim(own_columns, 0, lax.axis_size("fsdp") * local_rows, axis=0),
            projection,
            preferred_element_type=jnp.float32,
        ),
        "fsdp",
        scatter_dimension=0,
        tiled=True,
    )
    image_unit, image_back = jax.vjp(unit_rows, embedded)
    text_unit, text_back = jax.vjp(unit_rows, text_embed.astype(jnp.float32))
    image_low = image_unit.astype(jnp.bfloat16)
    text_low = text_unit.astype(jnp.bfloat16)
    total_rows = local_rows * lax.axis_size("dp") * lax.axis_size("fsdp")
    embed_width = text_low.shape[1]
    start_state = (
        jnp.zeros((local_rows, embed_width), jnp.float32),
        jnp.zeros((local_rows, total_rows), jnp.bfloat16),
    )
    tiles = lax.all_gather(text_low, ("dp", "fsdp"), axis=0, tiled=True)
    tile_ids = lax.all_gather(txt_ids, ("dp", "fsdp"), axis=0, tiled=True)
    weights = pair_weights(image_low, img_ids, tiles, tile_ids, scale, shift)
    image_acc = start_state[0] + scale * jnp.einsum(
        "ij,je->ie", weights, tiles, preferred_element_type=jnp.float32
    )
    table = lax.dynamic_update_slice_in_dim(start_state[1], weights, jnp.int32(0), 1)
    block_weights = lax.slice_in_dim(table, 0, lax.axis_size(("dp", "fsdp")) * local_rows, axis=1)
    text_grad = lax.psum_scatter(
        scale
        * jnp.einsum("ij,ie->je", block_weights, image_low, preferred_element_type=jnp.float32),
        ("dp", "fsdp"),
        scatter_dimension=0,
        tiled=True,
    )
    embed_low = image_back(image_acc)[0].astype(jnp.bfloat16)
    grad_text = text_back(text_grad)[0]
    group_grad = lax.all_gather(embed_low, "fsdp", axis=0, tiled=True)
    head_part = jnp.einsum("ie,ce->ic", group_grad, projection, preferred_element_type=jnp.float32)
    head_grad = lax.all_to_all(head_part, "fsdp", split_axis=0, concat_axis=1, tiled=True)
    proj_share = jnp.einsum(
        "ic,ie->ce", own_columns, group_grad, preferred_element_type=jnp.float32
    )
    grad_proj = lax.psum(proj_share, "dp")
    pooled_grad = head_back(head_grad * head_gain)[0]
    grad_features = block_back(pooled_grad)[0].astype(jnp.bfloat16)
    return (grad_features, grad_text, grad_proj)


def solution(mesh):
    placed = (
        P(("dp", "fsdp"), None, None, None),
        P(("dp", "fsdp"), None),
        P(("dp", "fsdp")),
        P(("dp", "fsdp")),
        P(),
        P(),
        P(),
        P("fsdp", None),
        P(),
        P(),
    )
    return jax.shard_map(
        local,
        mesh=mesh,
        in_specs=placed,
        out_specs=(P(("dp", "fsdp"), None, None, None), P(("dp", "fsdp"), None), P("fsdp", None)),
        check_vma=False,
    )
```

profile of v0, /device:TPU:1, one launch (start us, length us, event | category | flops | bytes accessed | tf_op | source)
XLA Modules:
  0.0 1286.9 jit_solution(17123776816485163385)
XLA Ops:
  8.0 0.0 copy-start
  8.0 0.0 all-reduce.9.cloned.1.call-start
  8.1 17.1 %fusion.36 = (f32[4,8,8]{0,2,1:T(8,128)S(1)}, f32[4,8,8,3072]{3,0,2,1:T(4,128)S(1)}) fusion(f32[7,7,1,3072]{3,1,0,2:T(8,128)} %bitcast.36, bf16[4,8,8,3072]{3,2,1,0:T(8,128)(2,1)} %param.10), kind=kOutput, calls=%fused_computation.73 | convolution fusion | flops 286260992 | bytes 5321728 | tf_op jit(solution)/shard_map/jvp()/conv_general_dilated | solution.py:11
  25.2 0.0 copy-start.1
  25.2 0.0 copy-start.3
  25.2 0.0 copy-start.5
  25.3 1.0 multiply_reduce_fusion
  26.2 1.5 copy-done.3
  27.8 0.0 copy-done.5
  27.8 2.5 add_reduce_fusion
  30.3 0.0 copy-done.1
  30.3 0.1 broadcast_multiply_fusion
  30.5 0.2 multiply_reduce_fusion.2
  30.7 0.0 copy-done.7
  30.7 0.1 fusion.21
  30.8 29.2 %all-gather = bf16[8,4,3072]{2,1,0:T(4,128)(2,1)S(1)} all-gather(bf16[1,4,3072]{2,1,0:T(4,128)(2,1)S(1)} %fusion.21), channel_id=1, replica_groups=mesh['dp'=32,'fsdp'=8] {'fsdp'}, dimensions={0}, use_global_device_ids=true | all-gather | bytes 221184 | tf_op jit(solution)/shard_map/all_gather | solution.py:71
  60.0 0.0 copy-start.4
  60.1 0.0 copy-done
  60.1 0.9 fusion.24
  61.0 0.0 all-reduce.9.cloned.1.call-update
  61.0 0.0 all-gather.5.cloned.1.call-start
  61.1 0.0 copy-done.6
  61.1 0.1 fusion.27
  61.2 0.7 fusion.30
  61.9 0.0 all-gather.5.cloned.1.call-update
  61.9 0.0 all-reduce.11.cloned.1.call-start
  63.3 0.0 copy-done.11
  63.3 0.6 dynamic-slice
  64.5 0.0 copy-done.10
  64.5 0.2 dynamic-update-slice
  64.8 85.6 %all-reduce = s32[1024]{0:T(1024)S(1)} all-reduce(s32[1024]{0:T(1024)S(1)} %dynamic-update-slice), channel_id=1, replica_groups=mesh['dp'=32,'fsdp'=8] {'dp','fsdp'}, use_global_device_ids=true, to_apply=%add | all-reduce | flops 1024 | bytes 8192
  150.4 2.5 all-reduce.9.cloned.1.call-done
  152.9 0.9 multiply_reduce_fusion.4
  153.8 0.0 copy-done.4
  153.8 617.5 %all-gather.5.cloned.1.call-done = bf16[256,4,1152]{2,1,0:T(4,128)(2,1)} async-done(((bf16[1,4,1152]{2,1,0:T(4,128)(2,1)}), bf16[256,4,1152]{2,1,0:T(4,128)(2,1)}) %all-gather.5.cloned.1.call-update) | async-done | bytes 2359312 | tf_op jit(solution)/shard_map/all_gather | solution.py:95
  771.3 3.9 reshape.123
  775.2 0.0 copy-done.8
  775.2 1.5 fusion.13
  776.7 3.8 convolution_multiply_fusion
  780.5 0.0 all-reduce.11.cloned.1.call-update
  780.5 1.3 multiply_reduce_fusion.3
  781.9 0.9 fusion.31
  782.7 27.9 %all-gather.2 = bf16[8,4,1152]{2,1,0:T(4,128)(2,1)S(1)} all-gather(bf16[1,4,1152]{2,1,0:T(4,128)(2,1)S(1)} %fusion.31), channel_id=1, replica_groups=mesh['dp'=32,'fsdp'=8] {'fsdp'}, dimensions={0}, use_global_device_ids=true | all-gather | bytes 82944 | tf_op jit(solution)/shard_map/all_gather | solution.py:112
  810.7 0.3 fusion.37
  811.0 0.7 all_to_all.14
  811.7 3.3 all-to-all-start
  815.0 0.2 all-reduce.7.cloned.1.call-start
  815.3 2.4 fusion.22
  817.6 0.0 all-reduce.7.cloned.1.call-update
  817.7 3.9 all-to-all-done
  821.6 0.2 multiply_reduce_fusion.1
  821.8 0.2 fusion.19
  822.0 0.1 fusion.18
  822.1 3.2 fusion.1
  825.3 0.0 copy-done.2
  825.3 1.7 fusion.14
  827.1 1.9 fusion.49
  829.0 12.2 fusion
  841.2 1.6 copy.24
  842.9 206.0 %all-reduce.11.cloned.1.call-done = f32[1024,1152]{1,0:T(8,128)} async-done(((f32[1024,1152]{1,0:T(8,128)}), f32[1024,1152]{1,0:T(8,128)}) %all-reduce.11.cloned.1.call-update) | async-done | bytes 4718608
  1048.8 0.9 fusion.29
  1049.8 1.5 add_add_fusion.4
  1051.2 225.3 %all-reduce.7.cloned.1.call-done = f32[384,1152]{1,0:T(8,128)} async-done(((f32[384,1152]{1,0:T(8,128)}), f32[384,1152]{1,0:T(8,128)}) %all-reduce.7.cloned.1.call-update) | async-done | bytes 1769488 | tf_op jit(solution)/shard_map/psum | solution.py:118
  1276.5 2.8 copy.43
  (24 shorter events, 0.2 us)
Async XLA Ops:
  8.0 52.1 %copy-start = (bf16[384,1152]{1,0:T(8,128)(2,1)S(1)}, bf16[384,1152]{1,0:T(8,128)(2,1)}, u32[]{:S(2)}) copy-start(bf16[384,1152]{1,0:T(8,128)(2,1)} %param.17) | copy-start | bytes 2654212
  8.0 144.9 %all-reduce.9.cloned.1.call-start = ((), (), s32[]{:S(2)}) async-start(), calls=%async_computation.3 | async-start | bytes 294912
  25.2 5.1 copy-start.1
  25.2 2.5 copy-start.3
  25.2 2.5 copy-start.5
  26.2 4.5 copy-start.7
  27.8 33.3 %copy-start.6 = (bf16[4,1152]{1,0:T(4,128)(2,1)S(1)}, bf16[4,1152]{1,0:T(4,128)(2,1)}, u32[]{:S(2)}) copy-start(bf16[4,1152]{1,0:T(4,128)(2,1)} %param.11) | copy-start | bytes 27652
  27.8 35.5 %copy-start.11 = (u32[256]{0:T(256)S(1)}, u32[256]{0:T(256)}, u32[]{:S(2)}) copy-start(u32[256]{0:T(256)} %constant.52) | copy-start | bytes 3076
  27.8 36.7 %copy-start.10 = (s32[4]{0:T(128)S(1)}, s32[4]{0:T(128)}, u32[]{:S(2)}) copy-start(s32[4]{0:T(128)} %param.13) | copy-start | bytes 52
  60.0 715.2 %copy-start.8 = (s32[4]{0:T(128)S(1)}, s32[4]{0:T(128)}, u32[]{:S(2)}) copy-start(s32[4]{0:T(128)} %param.12) | copy-start | bytes 52
  60.0 93.8 %copy-start.4 = (bf16[32,3072]{1,0:T(8,128)(2,1)}, bf16[32,3072]{1,0:T(8,128)(2,1)S(1)}, u32[]{:S(2)}) copy-start(bf16[32,3072]{1,0:T(8,128)(2,1)S(1)} %reshape.121) | copy-start | bytes 589828
  61.0 710.3 %all-gather.5.cloned.1.call-start = ((), (), s32[]{:S(2)}) async-start(), calls=%async_computation.2 | async-start | bytes 2368512 | tf_op jit(solution)/shard_map/all_gather | solution.py:95
  61.9 986.9 %all-reduce.11.cloned.1.call-start = ((), (), s32[]{:S(2)}) async-start(), calls=%async_computation.4 | async-start | bytes 9437184
  811.7 9.9 all-to-all-start
  815.0 461.5 %all-reduce.7.cloned.1.call-start = ((), (), s32[]{:S(2)}) async-start(), calls=%async_computation.1 | async-start | bytes 3538944 | tf_op jit(solution)/shard_map/psum | solution.py:118
  821.6 3.8 copy-start.2
  827.1 2.0 copy-start.9
Sparse Core Ops, SparseCore 0:
  61.1 91.7 all-reduce.8
Sparse Core Ops, SparseCore 1:
  64.1 707.2 all-gather.4
  780.6 268.2 all-reduce.10
  1051.9 224.5 all-reduce.6
where the time goes:
time: 1290 us
  waiting for transfers between devices  1060 us (82%)
  blocking collectives  143 us (11%)
  matrix products  39.6 us (3%)
  between operations  17.9 us (1%)
  other arithmetic  16.3 us (1%)
    all_gather x1, waiting for transfers between devices, local(): tiles = lax.all_gather(text_low, ('dp', 'fsdp'), axis=0, tiled=True)  618 us
    psum x1, waiting for transfers between devices, local(): grad_proj = lax.psum(proj_share, 'dp')  225 us
    unnamed x6, waiting for transfers between devices  209 us
    unnamed x1, blocking collectives  85.6 us
    conv_general_dilated x2, matrix products, block_pool(): lax.conv_general_dilated(widened, kernel[:, :, None, :], (1, 1), ((margin...  29.3 us
    all_gather x1, blocking collectives, local(): group_input = lax.all_gather(head_input, 'fsdp', axis=0, tiled=True)  29.2 us
    all_gather x1, blocking collectives, local(): group_grad = lax.all_gather(embed_low, 'fsdp', axis=0, tiled=True)  27.9 us
  transfers between devices with their start and end apart: 5, of which 5 were waited for; matrix products, arithmetic and copies ran while one was open for 2% of the time, Pallas kernels for 0%

commit v1 on v0

v1 whole, which is shorter than its diff:
```python
import jax
import jax.numpy as jnp
from jax import lax
from jax.sharding import Mesh, PartitionSpec as P

EPSILON = 1e-06
AXES = ("y_lo", "z", "core", "x", "y_hi")
SIZES = (2, 8, 2, 4, 2)
ALL = AXES
GROUP = ("x", "y_hi")
LINE = ("y_lo", "z")
IDS = 128
HALF = 640


def block_pool(widened, kernel, norm_gain):
    margin = kernel.shape[0] // 2
    filtered = lax.conv_general_dilated(
        widened,
        kernel[:, :, None, :],
        (1, 1),
        ((margin, margin), (margin, margin)),
        dimension_numbers=("NHWC", "HWIO", "NHWC"),
        feature_group_count=widened.shape[3],
        precision=lax.Precision.HIGHEST,
    )
    average = jnp.mean(filtered, axis=-1, keepdims=True)
    centred = filtered - average
    spread = jnp.mean(centred * centred, axis=-1, keepdims=True)
    normed = centred * lax.rsqrt(spread + EPSILON) * norm_gain
    return jnp.mean(widened + normed, axis=(1, 2))


def head_norm(pooled):
    average = jnp.mean(pooled, axis=-1, keepdims=True)
    centred = pooled - average
    spread = jnp.mean(centred * centred, axis=-1, keepdims=True)
    return centred * lax.rsqrt(spread + EPSILON)


def inverse_length(values):
    return lax.rsqrt(jnp.sum(values * values, axis=-1, keepdims=True) + EPSILON)


def length_back(unit, inverse, cotangent):
    return inverse * (cotangent - unit * jnp.sum(unit * cotangent, axis=-1, keepdims=True))


def exchange(blocks, axes):
    return lax.all_to_all(blocks, axes, 0, 0, tiled=True)


def spread_out(block, axes, count):
    return exchange(jnp.broadcast_to(block[None], (count,) + block.shape), axes)


def swap_core(block):
    return lax.ppermute(block, "core", ((0, 1), (1, 0)))


def one_hot(ids):
    return (ids[:, None] == lax.broadcasted_iota(jnp.int32, (1, IDS), 1)).astype(jnp.bfloat16)


def dot(left, right, left_dim, right_dim):
    return lax.dot_general(
        left, right, (((left_dim,), (right_dim,)), ((), ())), preferred_element_type=jnp.float32
    )


def pair_weights(image_low, image_hot, text_low, text_hot, scale, shift):
    logits = scale * dot(image_low, text_low, 1, 1) + shift
    signs = 2.0 * dot(image_hot, text_hot, 1, 1) - 1.0
    return (-signs * jax.nn.sigmoid(-signs * logits)).astype(jnp.bfloat16)


def local(
    features,
    text_embed,
    img_ids,
    txt_ids,
    kernel,
    norm_gain,
    head_gain,
    projection,
    logit_scale,
    logit_bias,
):
    scale = logit_scale[0]
    shift = logit_bias[0]
    core = lax.axis_index("core")
    rows = text_embed.shape[0]
    width = text_embed.shape[1]
    share = projection.shape[0]
    group = lax.axis_size(GROUP)
    line = lax.axis_size(LINE)
    mine = lax.axis_index(GROUP)

    text_wide = text_embed.astype(jnp.float32)
    text_inverse = inverse_length(text_wide)
    text_unit = text_wide * text_inverse
    packed = jnp.concatenate([text_unit.astype(jnp.bfloat16), one_hot(txt_ids)], axis=1)
    group_texts = spread_out(packed, GROUP, group).reshape(group * rows, width + IDS)
    near_texts = spread_out(group_texts, LINE, line)
    far_texts = swap_core(near_texts)

    widened = features.astype(jnp.float32)

    def local_pool(field):
        return block_pool(field, kernel, norm_gain)

    pooled, block_back = jax.vjp(local_pool, widened)
    normalized, head_back = jax.vjp(head_norm, pooled)
    head_input = (normalized * head_gain).astype(jnp.bfloat16)

    split_input = head_input.reshape(rows, group, share).transpose(1, 0, 2)
    hot = jnp.broadcast_to(one_hot(img_ids)[None], (group, rows, IDS))
    received = exchange(jnp.concatenate([split_input, hot], axis=2), GROUP)
    received = received.reshape(group * rows, share + IDS)
    own_columns = received[:, :share]
    image_hot = received[:, share:]
    partial = dot(own_columns, projection, 1, 0).astype(jnp.bfloat16)
    embedded = jnp.sum(spread_out(partial, GROUP, group).astype(jnp.float32), axis=0)
    image_inverse = inverse_length(embedded)
    image_unit = embedded * image_inverse
    image_low = image_unit.astype(jnp.bfloat16)

    near_flat = near_texts.reshape(line * group * rows, width + IDS)
    far_flat = far_texts.reshape(line * group * rows, width + IDS)
    near_weights = pair_weights(
        image_low, image_hot, near_flat[:, :width], near_flat[:, width:], scale, shift
    )
    far_weights = pair_weights(
        image_low, image_hot, far_flat[:, :width], far_flat[:, width:], scale, shift
    )
    image_grad = scale * (
        dot(near_weights, near_flat[:, :width], 1, 0) + dot(far_weights, far_flat[:, :width], 1, 0)
    )
    embed_low = length_back(image_unit, image_inverse, image_grad).astype(jnp.bfloat16)

    head_part = dot(embed_low, projection, 1, 1)
    head_blocks = exchange(head_part.reshape(group, rows, share), GROUP)
    head_grad = head_blocks.transpose(1, 0, 2).reshape(rows, group * share)

    keep_at = core * (width - HALF)
    give_at = (1 - core) * (width - HALF)
    give = dot(own_columns, lax.dynamic_slice_in_dim(embed_low, give_at, HALF, 1), 0, 0)
    keep = dot(own_columns, lax.dynamic_slice_in_dim(embed_low, keep_at, HALF, 1), 0, 0)
    pair_sum = keep + swap_core(give.astype(jnp.bfloat16)).astype(jnp.float32)
    strips = exchange(pair_sum.astype(jnp.bfloat16).reshape(line, share // line, HALF), LINE)
    strip = jnp.sum(strips.astype(jnp.float32), axis=0).astype(jnp.bfloat16)
    near_half = spread_out(strip, LINE, line).reshape(share, HALF)
    far_half = swap_core(near_half)
    low_half = jnp.where(core == 0, near_half, far_half)
    high_half = jnp.where(core == 0, far_half, near_half)
    grad_proj = jnp.concatenate([low_half, high_half[:, 2 * HALF - width :]], axis=1).astype(
        jnp.float32
    )

    def own_texts(weights):
        blocks = weights.reshape(group * rows, line, group, rows)
        picked = lax.dynamic_slice_in_dim(blocks, mine, 1, 2)
        return picked.reshape(group * rows, line * rows)

    text_near = dot(own_texts(near_weights), image_low, 0, 0)
    text_far = dot(own_texts(far_weights), image_low, 0, 0)
    text_pair = text_near + swap_core(text_far.astype(jnp.bfloat16)).astype(jnp.float32)
    text_blocks = exchange(text_pair.astype(jnp.bfloat16).reshape(line, rows, width), LINE)
    text_grad = scale * jnp.sum(text_blocks.astype(jnp.float32), axis=0)
    grad_text = length_back(text_unit, text_inverse, text_grad)

    pooled_grad = head_back(head_grad * head_gain)[0]
    grad_features = block_back(pooled_grad)[0].astype(jnp.bfloat16)
    return (grad_features, grad_text, grad_proj)


def solution(mesh):
    fine = Mesh(mesh.devices.reshape(SIZES), AXES)
    placed = (
        P(ALL, None, None, None),
        P(ALL, None),
        P(ALL),
        P(ALL),
        P(),
        P(),
        P(),
        P(GROUP, None),
        P(),
        P(),
    )
    return jax.shard_map(
        local,
        mesh=fine,
        in_specs=placed,
        out_specs=(P(ALL, None, None, None), P(ALL, None), P(GROUP, None)),
        check_vma=False,
    )
```

time: 1290 us -> 186 us (0.14)
  waiting for transfers between devices: 1060 us -> 65.9 us
  blocking collectives: 143 us -> 0 us
  starting transfers between devices: 3.7 us -> 50.9 us
  between operations: 17.9 us -> 2.31 us
    all_gather x1 -> x0, waiting for transfers between devices: 618 us -> none  [local(): tiles = lax.all_gather(text_low, ('dp', 'fsdp'), axis=0, tiled=True)]
    psum x1 -> x0, waiting for transfers between devices: 225 us -> none  [local(): grad_proj = lax.psum(proj_share, 'dp')]
    unnamed x6 -> x0, waiting for transfers between devices: 209 us -> none
    unnamed x1 -> x0, blocking collectives: 85.6 us -> none
    all_to_all x1 -> x8, waiting for transfers between devices: 3.88 us -> 63.7 us  [exchange(): return lax.all_to_all(blocks, axes, 0, 0, tiled=True)]
    all_gather x2 -> x0, blocking collectives: 57.1 us -> none  [the longest x1 29.2 us: local(): group_input = lax.all_gather(head_input, 'fsdp', axis=0, tiled=True)]
    all_to_all x1 -> x8, starting transfers between devices: 3.35 us -> 40.6 us  [exchange(): return lax.all_to_all(blocks, axes, 0, 0, tiled=True)]
  transfers between devices with their start and end apart: 5 -> 12, of which waited for: 5 -> 9; matrix products, arithmetic and copies ran while one was open for 2% -> 17% of each run, Pallas kernels for 0% -> 0%
where the time goes in v1:
time: 186 us; the launch traced here: 185 us
  waiting for transfers between devices  65.9 us (35%)
  starting transfers between devices  50.9 us (27%)
  matrix products  37.8 us (20%)
  other arithmetic  19.5 us (10%)
  local copies, waits for them, and re-layouts  8.39 us (5%)
  between operations  2.31 us (1%)
    all_to_all x8, waiting for transfers between devices, exchange(): return lax.all_to_all(blocks, axes, 0, 0, tiled=True)  63.7 us
    all_to_all x8, starting transfers between devices, exchange(): return lax.all_to_all(blocks, axes, 0, 0, tiled=True)  40.6 us
    conv_general_dilated x2, matrix products, block_pool(): lax.conv_general_dilated(widened, kernel[:, :, None, :], (1, 1), ((margin...  30 us
    ppermute x4, starting transfers between devices, swap_core(): return lax.ppermute(block, 'core', ((0, 1), (1, 0)))  10.3 us
    dot_general x12, matrix products, dot(): lax.dot_general(left, right, (((left_dim,), (right_dim,)), ((), ())), pre...  7.79 us
    conv_general_dilated x1, other arithmetic, block_pool(): lax.conv_general_dilated(widened, kernel[:, :, None, :], (1, 1), ((margin...  4.41 us
  transfers between devices with their start and end apart: 12, of which 9 were waited for; matrix products, arithmetic and copies ran while one was open for 17% of the time, Pallas kernels for 0%

profile of v1, /device:TPU:1, one launch (start us, length us, event | category | flops | bytes accessed | tf_op | source)
XLA Modules:
  0.0 184.9 jit_solution(2140359214708500196)
XLA Ops:
  0.6 0.8 fusion.59
  1.5 17.1 %fusion.65 = (f32[4,8,8]{0,2,1:T(8,128)S(1)}, f32[4,8,8,3072]{3,0,2,1:T(4,128)S(1)}) fusion(f32[7,7,1,3072]{3,1,0,2:T(8,128)} %bitcast.56, bf16[4,8,8,3072]{3,2,1,0:T(8,128)(2,1)} %param.10), kind=kOutput, calls=%fused_computation.113 | convolution fusion | flops 286260992 | bytes 5321728 | tf_op jit(solution)/shard_map/jvp()/conv_general_dilated | solution.py:18
  18.6 1.0 multiply_reduce_fusion
  19.6 1.5 copy-done.2
  21.1 2.5 %add_reduce_fusion = f32[4,3072]{1,0:T(4,128)S(1)} fusion(f32[4,8,8,3072]{3,0,2,1:T(4,128)S(1)} %get-tuple-element.15, f32[3072]{0:T(1024)S(1)} %copy-done.3, f32[4,8,8]{0,2,1:T(8,128)S(1)} %fusion.45, f32[4,8,8]{0,2,1:T(8,128)S(1)} %broadcast_multiply_fusion.1, bf16[4,8,8,3072]{3,2,1,0:T(8,128)(2,1)S(1)} %copy-done.2), kind=kLoop, calls=%fused_computation.7 | loop fusion | flops 4706304 | bytes 4782080 | tf_op jit(solution)/shard_map/jvp()/reduce_sum | solution.py:31
  23.6 0.1 fusion.64
  23.8 0.2 multiply_reduce_fusion.4
  24.1 0.6 pad_maximum_fusion
  24.8 7.5 %all-to-all-start = ((bf16[8,4,512]{2,1,0:T(4,128)(2,1)}), bf16[8,4,512]{2,1,0:T(4,128)(2,1)S(1)}, u32[]{:S(2)}, u32[]{:S(2)}) async-start(bf16[8,4,512]{2,1,0:T(4,128)(2,1)} %pad_maximum_fusion), calls=%async_computation | async-start | bytes 65536 | tf_op jit(solution)/shard_map/all_to_all | solution.py:50
  32.3 0.1 fusion.56
  32.6 6.3 %all-to-all-done = bf16[8,4,512]{2,1,0:T(4,128)(2,1)S(1)} async-done(((bf16[8,4,512]{2,1,0:T(4,128)(2,1)}), bf16[8,4,512]{2,1,0:T(4,128)(2,1)S(1)}, u32[]{:S(2)}, u32[]{:S(2)}) %all-to-all-start) | async-done | bytes 32800 | tf_op jit(solution)/shard_map/all_to_all | solution.py:50
  38.9 0.7 broadcast_in_dim.31
  39.5 3.4 %all-to-all-start.2 = ((bf16[8,4,1280]{2,1,0:T(4,128)(2,1)}), bf16[8,4,1280]{2,1,0:T(4,128)(2,1)S(1)}, u32[]{:S(2)}, u32[]{:S(2)}) async-start(bf16[8,4,1280]{2,1,0:T(4,128)(2,1)} %broadcast_in_dim.31), calls=%async_computation.2 | async-start | bytes 163840 | tf_op jit(solution)/shard_map/all_to_all | solution.py:50
  42.9 0.3 convolution_convert_fusion.1
  43.2 6.3 %all-to-all-done.2 = bf16[8,4,1280]{2,1,0:T(4,128)(2,1)S(1)} async-done(((bf16[8,4,1280]{2,1,0:T(4,128)(2,1)}), bf16[8,4,1280]{2,1,0:T(4,128)(2,1)S(1)}, u32[]{:S(2)}, u32[]{:S(2)}) %all-to-all-start.2) | async-done | bytes 81952 | tf_op jit(solution)/shard_map/all_to_all | solution.py:50
  49.4 0.9 broadcast_in_dim.30
  50.3 3.5 %all-to-all-start.1 = ((bf16[8,32,1152]{2,1,0:T(8,128)(2,1)}), bf16[8,32,1152]{2,1,0:T(8,128)(2,1)S(1)}, u32[]{:S(2)}, u32[]{:S(2)}) async-start(bf16[8,32,1152]{2,1,0:T(8,128)(2,1)} %broadcast_in_dim.30), calls=%async_computation.1 | async-start | bytes 1179648 | tf_op jit(solution)/shard_map/all_to_all | solution.py:50
  53.9 8.9 %all-to-all-done.1 = bf16[8,32,1152]{2,1,0:T(8,128)(2,1)S(1)} async-done(((bf16[8,32,1152]{2,1,0:T(8,128)(2,1)}), bf16[8,32,1152]{2,1,0:T(8,128)(2,1)S(1)}, u32[]{:S(2)}, u32[]{:S(2)}) %all-to-all-start.1) | async-done | bytes 589856 | tf_op jit(solution)/shard_map/all_to_all | solution.py:50
  62.8 1.2 broadcast_in_dim.33
  64.0 8.4 %all-to-all-start.3 = ((bf16[16,32,1280]{2,1,0:T(8,128)(2,1)}), bf16[16,32,1280]{2,1,0:T(8,128)(2,1)S(1)}, u32[]{:S(2)}, u32[]{:S(2)}) async-start(bf16[16,32,1280]{2,1,0:T(8,128)(2,1)} %broadcast_in_dim.33), calls=%async_computation.3 | async-start | bytes 2621440 | tf_op jit(solution)/shard_map/all_to_all | solution.py:50
  73.8 0.1 multiply_reduce_fusion.2
  73.9 25.4 %all-to-all-done.3 = bf16[16,32,1280]{2,1,0:T(8,128)(2,1)S(1)} async-done(((bf16[16,32,1280]{2,1,0:T(8,128)(2,1)}), bf16[16,32,1280]{2,1,0:T(8,128)(2,1)S(1)}, u32[]{:S(2)}, u32[]{:S(2)}) %all-to-all-start.3) | async-done | bytes 1310752 | tf_op jit(solution)/shard_map/all_to_all | solution.py:50
  99.4 6.7 %collective-permute-start = (bf16[16,32,1280]{2,1,0:T(8,128)(2,1)S(1)}, bf16[16,32,1280]{2,1,0:T(8,128)(2,1)}, u32[]{:S(2)}, u32[]{:S(2)}) collective-permute-start(bf16[16,32,1280]{2,1,0:T(8,128)(2,1)S(1)} %all-to-all-done.3), channel_id=1, source_target_pairs={{0,8},{8,0},{1,9},{9,1},{2,10},{10,2},{3,11},{11,3},{4,12},{12,4},... | collective-permute-start | bytes 3932168 | tf_op jit(solution)/shard_map/ppermute | solution.py:58
  106.2 0.2 fusion.10
  106.3 0.5 fusion.26
  106.8 0.1 copy.32
  107.0 0.3 fusion.29
  107.3 1.6 collective-permute-done
  108.9 1.1 fusion.8
  110.0 1.8 fusion.25
  111.7 0.1 copy.33
  111.8 1.7 multiply_reduce_fusion.1
  113.5 0.1 multiply_convert_fusion
  113.7 0.3 fusion.66
  114.0 0.7 reshape.181
  114.7 3.9 %all-to-all-start.4 = ((f32[8,4,384]{2,1,0:T(4,128)}), f32[8,4,384]{2,1,0:T(4,128)S(1)}, u32[]{:S(2)}, u32[]{:S(2)}) async-start(f32[8,4,384]{2,1,0:T(4,128)} %reshape.181), calls=%async_computation.4 | async-start | bytes 98304 | tf_op jit(solution)/shard_map/all_to_all | solution.py:50
  118.6 0.2 convolution_convert_fusion
  118.7 0.7 collective-permute-start.1
  119.5 0.3 convolution_convert_fusion.2
  119.8 0.1 collective-permute-start.2
  119.9 5.2 %all-to-all-done.4 = f32[8,4,384]{2,1,0:T(4,128)S(1)} async-done(((f32[8,4,384]{2,1,0:T(4,128)}), f32[8,4,384]{2,1,0:T(4,128)S(1)}, u32[]{:S(2)}, u32[]{:S(2)}) %all-to-all-start.4) | async-done | bytes 49184 | tf_op jit(solution)/shard_map/all_to_all | solution.py:50
  125.2 0.2 multiply_reduce_fusion.3
  125.4 0.2 fusion.39
  125.6 0.1 fusion.38
  125.7 2.8 %fusion.1 = f32[4,8,8]{0,2,1:T(8,128)S(1)} fusion(f32[4,8,8,3072]{3,0,2,1:T(4,128)} %copy-done.1, f32[4,3072]{1,0:T(4,128)S(1)} %fusion.38, f32[3072]{0:T(1024)S(1)} %copy-done.3, f32[4,8,8]{0,2,1:T(8,128)S(1)} %broadcast_multiply_fusion.1), kind=kLoop, calls=%fused_computation.5 | loop fusion | flops 3145472 | bytes 3209216 | tf_op jit(solution)/shard_map/transpose(jvp())/reduce_sum | solution.py:30
  128.6 1.1 add_convert_fusion
  129.7 3.6 %all-to-all-start.6 = ((bf16[16,24,640]{2,1,0:T(8,128)(2,1)}), bf16[16,24,640]{2,1,0:T(8,128)(2,1)S(1)}, u32[]{:S(2)}, u32[]{:S(2)}) async-start(bf16[16,24,640]{2,1,0:T(8,128)(2,1)} %bitcast.14), calls=%async_computation.6 | async-start | bytes 983040 | tf_op jit(solution)/shard_map/all_to_all | solution.py:50
  133.3 3.1 %fusion.32 = f32[4,8,8]{0,2,1:T(8,128)S(1)} fusion(f32[4,8,8]{0,2,1:T(8,128)S(1)} %multiply_multiply_fusion.2, f32[4,8,8,3072]{3,0,2,1:T(4,128)} %copy-done.1, f32[4,8,8]{0,2,1:T(8,128)S(1)} %broadcast_multiply_fusion.1, f32[4,8,8]{0,2,1:T(8,128)S(1)} %fusion.45, f32[3072]{0:T(1024)S(1)} %copy-done.3, f32[4,3072]{1,0:T(4,128)S(1)} %fusion.38), kind=kLoop, calls=%fused_computation.49 | loop fusion | flops 5504768 | bytes 3211264 | tf_op jit(solution)/shard_map/transpose(jvp())/reduce_sum | solution.py:28
  136.4 0.2 add_convert_fusion.1
  136.6 0.7 reshape.187
  137.3 8.5 %all-to-all-done.6 = bf16[16,24,640]{2,1,0:T(8,128)(2,1)S(1)} async-done(((bf16[16,24,640]{2,1,0:T(8,128)(2,1)}), bf16[16,24,640]{2,1,0:T(8,128)(2,1)S(1)}, u32[]{:S(2)}, u32[]{:S(2)}) %all-to-all-start.6) | async-done | bytes 491552 | tf_op jit(solution)/shard_map/all_to_all | solution.py:50
  145.8 5.9 %all-to-all-start.5 = ((bf16[16,4,1152]{2,1,0:T(4,128)(2,1)}), bf16[16,4,1152]{2,1,0:T(4,128)(2,1)S(1)}, u32[]{:S(2)}, u32[]{:S(2)}) async-start(bf16[16,4,1152]{2,1,0:T(4,128)(2,1)} %reshape.187), calls=%async_computation.5 | async-start | bytes 294912 | tf_op jit(solution)/shard_map/all_to_all | solution.py:50
  151.7 4.4 %fusion.81 = f32[4,8,8,3072]{3,0,2,1:T(4,128)} fusion(f32[4,8,8]{0,2,1:T(8,128)S(1)} %negate_multiply_fusion, f32[4,8,8]{0,2,1:T(8,128)S(1)} %multiply_multiply_fusion.2, f32[4,8,8,3072]{3,0,2,1:T(4,128)} %copy-done.1, f32[4,8,8]{0,2,1:T(8,128)S(1)} %broadcast_multiply_fusion.1, f32[4,8,8]{0,2,1:T(8,128)S(1)} %fusion.45, f32[3072]{0:T(1024)S(1)} %copy-done.3, ...), kind=kLoop, calls=%fused_computation.6.clone.1 | loop fusion | flops 5505024 | bytes 6356992 | tf_op jit(solution)/shard_map/transpose(jvp())/conv_general_dilated | solution.py:18
  156.2 3.0 %all-to-all-done.5 = bf16[16,4,1152]{2,1,0:T(4,128)(2,1)S(1)} async-done(((bf16[16,4,1152]{2,1,0:T(4,128)(2,1)}), bf16[16,4,1152]{2,1,0:T(4,128)(2,1)S(1)}, u32[]{:S(2)}, u32[]{:S(2)}) %all-to-all-start.5) | async-done | bytes 147488 | tf_op jit(solution)/shard_map/all_to_all | solution.py:50
  159.2 0.8 broadcast_in_dim.80
  160.0 4.5 %all-to-all-start.7 = ((bf16[16,24,640]{2,1,0:T(8,128)(2,1)}), bf16[16,24,640]{2,1,0:T(8,128)(2,1)S(1)}, u32[]{:S(2)}, u32[]{:S(2)}) async-start(bf16[16,24,640]{2,1,0:T(8,128)(2,1)} %broadcast_in_dim.80), calls=%async_computation.7 | async-start | bytes 983040 | tf_op jit(solution)/shard_map/all_to_all | solution.py:50
  164.5 13.0 %fusion = bf16[4,8,8,3072]{3,0,2,1:T(4,128)(2,1)S(1)} fusion(f32[4,3072]{1,0:T(4,128)S(1)} %fusion.38, f32[7,7,3072,1]{2,1,0,3:T(8,128)S(1)} %bitcast.57, f32[4,8,8,3072]{3,0,2,1:T(4,128)} %fusion.81), kind=kOutput, calls=%fused_computation.4 | convolution fusion | flops 287047680 | bytes 5369856 | tf_op jit(solution)/shard_map/transpose(jvp())/conv_general_dilated | solution.py:18
  177.5 1.6 copy.34
  179.2 2.7 %collective-permute-start.3 = (bf16[384,640]{1,0:T(8,128)(2,1)S(1)}, bf16[384,640]{1,0:T(8,128)(2,1)S(1)}, u32[]{:S(2)}, u32[]{:S(2)}) collective-permute-start(bf16[384,640]{1,0:T(8,128)(2,1)S(1)} %bitcast.46), channel_id=1, source_target_pairs={{0,8},{8,0},{1,9},{9,1},{2,10},{10,2},{3,11},{11,3},{4,12},{12,4},... | collective-permute-start | bytes 1474568 | tf_op jit(solution)/shard_map/ppermute | solution.py:58
  181.9 0.2 fusion.53
  182.1 0.7 fusion.55
  182.8 0.6 collective-permute-done.3
  183.5 0.1 broadcast_select_fusion
  183.6 1.3 maximum_convert_fusion
  (43 shorter events, 0.8 us)
Async XLA Ops:
  0.6 42.3 %copy-start = (bf16[384,1152]{1,0:T(8,128)(2,1)S(1)}, bf16[384,1152]{1,0:T(8,128)(2,1)}, u32[]{:S(2)}) copy-start(bf16[384,1152]{1,0:T(8,128)(2,1)} %param.17) | copy-start | bytes 2654212
  18.5 5.1 %copy-start.1 = (f32[4,8,8,3072]{3,0,2,1:T(4,128)}, f32[4,8,8,3072]{3,0,2,1:T(4,128)S(1)}, u32[]{:S(2)}) copy-start(f32[4,8,8,3072]{3,0,2,1:T(4,128)S(1)} %get-tuple-element.15) | copy-start | bytes 9437188
  18.5 2.5 %copy-start.2 = (bf16[4,8,8,3072]{3,2,1,0:T(8,128)(2,1)S(1)}, bf16[4,8,8,3072]{3,2,1,0:T(8,128)(2,1)}, u32[]{:S(2)}) copy-start(bf16[4,8,8,3072]{3,2,1,0:T(8,128)(2,1)} %param.10) | copy-start | bytes 4718596
  18.5 2.5 %copy-start.3 = (f32[3072]{0:T(1024)S(1)}, f32[3072]{0:T(1024)}, u32[]{:S(2)}) copy-start(f32[3072]{0:T(1024)} %param.15) | copy-start | bytes 36868
  19.5 4.5 %copy-start.5 = (f32[3072]{0:T(1024)S(1)}, f32[3072]{0:T(1024)}, u32[]{:S(2)}) copy-start(f32[3072]{0:T(1024)} %param.16) | copy-start | bytes 36868
  19.5 12.7 %copy-start.7 = (s32[4]{0:T(128)S(1)}, s32[4]{0:T(128)}, u32[]{:S(2)}) copy-start(s32[4]{0:T(128)} %param.13) | copy-start | bytes 52
  19.5 12.8 %copy-start.4 = (bf16[4,1152]{1,0:T(4,128)(2,1)S(1)}, bf16[4,1152]{1,0:T(4,128)(2,1)}, u32[]{:S(2)}) copy-start(bf16[4,1152]{1,0:T(4,128)(2,1)} %param.11) | copy-start | bytes 27652
  24.8 14.1 %all-to-all-start = ((bf16[8,4,512]{2,1,0:T(4,128)(2,1)}), bf16[8,4,512]{2,1,0:T(4,128)(2,1)S(1)}, u32[]{:S(2)}, u32[]{:S(2)}) async-start(bf16[8,4,512]{2,1,0:T(4,128)(2,1)} %pad_maximum_fusion), calls=%async_computation | async-start | bytes 65536 | tf_op jit(solution)/shard_map/all_to_all | solution.py:50
  39.5 9.9 %all-to-all-start.2 = ((bf16[8,4,1280]{2,1,0:T(4,128)(2,1)}), bf16[8,4,1280]{2,1,0:T(4,128)(2,1)S(1)}, u32[]{:S(2)}, u32[]{:S(2)}) async-start(bf16[8,4,1280]{2,1,0:T(4,128)(2,1)} %broadcast_in_dim.31), calls=%async_computation.2 | async-start | bytes 163840 | tf_op jit(solution)/shard_map/all_to_all | solution.py:50
  50.3 12.5 %all-to-all-start.1 = ((bf16[8,32,1152]{2,1,0:T(8,128)(2,1)}), bf16[8,32,1152]{2,1,0:T(8,128)(2,1)S(1)}, u32[]{:S(2)}, u32[]{:S(2)}) async-start(bf16[8,32,1152]{2,1,0:T(8,128)(2,1)} %broadcast_in_dim.30), calls=%async_computation.1 | async-start | bytes 1179648 | tf_op jit(solution)/shard_map/all_to_all | solution.py:50
  64.0 35.4 %all-to-all-start.3 = ((bf16[16,32,1280]{2,1,0:T(8,128)(2,1)}), bf16[16,32,1280]{2,1,0:T(8,128)(2,1)S(1)}, u32[]{:S(2)}, u32[]{:S(2)}) async-start(bf16[16,32,1280]{2,1,0:T(8,128)(2,1)} %broadcast_in_dim.33), calls=%async_computation.3 | async-start | bytes 2621440 | tf_op jit(solution)/shard_map/all_to_all | solution.py:50
  99.4 9.5 %collective-permute-start = (bf16[16,32,1280]{2,1,0:T(8,128)(2,1)S(1)}, bf16[16,32,1280]{2,1,0:T(8,128)(2,1)}, u32[]{:S(2)}, u32[]{:S(2)}) collective-permute-start(bf16[16,32,1280]{2,1,0:T(8,128)(2,1)S(1)} %all-to-all-done.3), channel_id=1, source_target_pairs={{0,8},{8,0},{1,9},{9,1},{2,10},{10,2},{3,11},{11,3},{4,12},{12,4},... | collective-permute-start | bytes 3932168 | tf_op jit(solution)/shard_map/ppermute | solution.py:58
  114.7 10.5 %all-to-all-start.4 = ((f32[8,4,384]{2,1,0:T(4,128)}), f32[8,4,384]{2,1,0:T(4,128)S(1)}, u32[]{:S(2)}, u32[]{:S(2)}) async-start(f32[8,4,384]{2,1,0:T(4,128)} %reshape.181), calls=%async_computation.4 | async-start | bytes 98304 | tf_op jit(solution)/shard_map/all_to_all | solution.py:50
  118.7 17.7 %collective-permute-start.1 = (bf16[64,1152]{1,0:T(8,128)(2,1)S(1)}, bf16[64,1152]{1,0:T(8,128)(2,1)S(1)}, u32[]{:S(2)}, u32[]{:S(2)}) collective-permute-start(bf16[64,1152]{1,0:T(8,128)(2,1)S(1)} %convolution_convert_fusion), channel_id=1, source_target_pairs={{0,8},{8,0},{1,9},{9,1},{2,10},{10,2},{3,11},{11,3},{4,12},{12,4},... | collective-permute-start | bytes 442376 | tf_op jit(solution)/shard_map/ppermute | solution.py:58
  119.8 8.8 %collective-permute-start.2 = (bf16[384,640]{1,0:T(8,128)(2,1)S(1)}, bf16[384,640]{1,0:T(8,128)(2,1)S(1)}, u32[]{:S(2)}, u32[]{:S(2)}) collective-permute-start(bf16[384,640]{1,0:T(8,128)(2,1)S(1)} %convolution_convert_fusion.2), channel_id=1, source_target_pairs={{0,8},{8,0},{1,9},{9,1},{2,10},{10,2},{3,11},{11,3},{4,12},{12,4},... | collective-permute-start | bytes 1474568 | tf_op jit(solution)/shard_map/ppermute | solution.py:58
  129.7 16.1 %all-to-all-start.6 = ((bf16[16,24,640]{2,1,0:T(8,128)(2,1)}), bf16[16,24,640]{2,1,0:T(8,128)(2,1)S(1)}, u32[]{:S(2)}, u32[]{:S(2)}) async-start(bf16[16,24,640]{2,1,0:T(8,128)(2,1)} %bitcast.14), calls=%async_computation.6 | async-start | bytes 983040 | tf_op jit(solution)/shard_map/all_to_all | solution.py:50
  145.8 13.4 %all-to-all-start.5 = ((bf16[16,4,1152]{2,1,0:T(4,128)(2,1)}), bf16[16,4,1152]{2,1,0:T(4,128)(2,1)S(1)}, u32[]{:S(2)}, u32[]{:S(2)}) async-start(bf16[16,4,1152]{2,1,0:T(4,128)(2,1)} %reshape.187), calls=%async_computation.5 | async-start | bytes 294912 | tf_op jit(solution)/shard_map/all_to_all | solution.py:50
  151.7 12.9 %copy-start.6 = (f32[7,7,3072]{2,1,0:T(8,128)S(1)}, f32[7,7,3072]{2,1,0:T(8,128)}, u32[]{:S(2)}) copy-start(f32[7,7,3072]{2,1,0:T(8,128)} %param.14) | copy-start | bytes 1806340
  160.0 19.2 %all-to-all-start.7 = ((bf16[16,24,640]{2,1,0:T(8,128)(2,1)}), bf16[16,24,640]{2,1,0:T(8,128)(2,1)S(1)}, u32[]{:S(2)}, u32[]{:S(2)}) async-start(bf16[16,24,640]{2,1,0:T(8,128)(2,1)} %broadcast_in_dim.80), calls=%async_computation.7 | async-start | bytes 983040 | tf_op jit(solution)/shard_map/all_to_all | solution.py:50
  179.2 4.2 %collective-permute-start.3 = (bf16[384,640]{1,0:T(8,128)(2,1)S(1)}, bf16[384,640]{1,0:T(8,128)(2,1)S(1)}, u32[]{:S(2)}, u32[]{:S(2)}) collective-permute-start(bf16[384,640]{1,0:T(8,128)(2,1)S(1)} %bitcast.46), channel_id=1, source_target_pairs={{0,8},{8,0},{1,9},{9,1},{2,10},{10,2},{3,11},{11,3},{4,12},{12,4},... | collective-permute-start | bytes 1474568 | tf_op jit(solution)/shard_map/ppermute | solution.py:58

commit v2 on v1

v2 whole, which is shorter than its diff:
```python
import jax
import jax.numpy as jnp
from jax import lax
from jax.experimental import pallas as pl
from jax.experimental.pallas import tpu as pltpu
from jax.sharding import Mesh, PartitionSpec as P

EPSILON = 1e-06
AXES = ("y_lo", "z", "core", "x", "y_hi")
SIZES = (2, 8, 2, 4, 2)
ALL = AXES
GROUP = ("x", "y_hi")
LINE = ("y_lo", "z")
PLANE = ("y_lo", "z", "y_hi")
MIB = 1024 * 1024
BIG = 60
IDS = 128
HALF = 640
LANES = 128
SIDE = 8
CELLS = 64
TAPS = 7
VMEM = pl.BlockSpec(memory_space=pltpu.VMEM)
SMEM = pl.BlockSpec(memory_space=pltpu.SMEM)
HBM = pl.BlockSpec(memory_space=pltpu.HBM)
STEPS = 4
PEERS = tuple((step_x, step_y) for step_x in range(4) for step_y in range(2))
BF16 = jnp.bfloat16
F32 = jnp.float32


def shape_of(dims, dtype):
    return jax.ShapeDtypeStruct(dims, dtype)


def call(body, outs, operands, name, micros, scratch=(), grant=40):
    specs = tuple(spec for _, spec in outs)
    shapes = tuple(shape for shape, _ in outs)
    single = len(outs) == 1
    return pl.pallas_call(
        body,
        out_shape=shapes[0] if single else shapes,
        in_specs=[spec for _, spec in operands],
        out_specs=specs[0] if single else specs,
        scratch_shapes=list(scratch),
        compiler_params=pltpu.CompilerParams(vmem_limit_bytes=grant * MIB),
        cost_estimate=pl.CostEstimate(
            flops=0, bytes_accessed=int(micros * 3e6), transcendentals=0
        ),
        name=name,
    )(*[operand for operand, _ in operands])


def group_peer(x, y_hi, step_x, step_y):
    return lax.rem(x + step_x, 4) * 2 + lax.rem(y_hi + step_y, 2)


def tap_weights(kernel_ref, at, column, flip):
    place = lax.broadcasted_iota(jnp.int32, (SIDE, LANES), 0) + (column - TAPS // 2)
    valid = (place >= 0) & (place < SIDE)
    weights = []
    for row in range(TAPS):
        if flip:
            line = kernel_ref[TAPS - 1 - row, pl.ds(TAPS - 1 - column, 1), at]
        else:
            line = kernel_ref[row, pl.ds(column, 1), at]
        weights.append(jnp.where(valid, jnp.broadcast_to(line, (SIDE, LANES)), 0.0))
    return weights


def filter_rows(fields, sums, kernel_ref, at, flip):
    for column in range(TAPS):
        weights = tap_weights(kernel_ref, at, column, flip)
        shift = (TAPS // 2 - column) % SIDE
        for field, total in zip(fields, sums):
            for source in range(SIDE):
                moved = field[source] if shift == 0 else pltpu.roll(field[source], shift, 0)
                for row in range(TAPS):
                    target = source - row + TAPS // 2
                    if 0 <= target < SIDE:
                        term = moved * weights[row]
                        total[target] = term if total[target] is None else total[target] + term
    return sums


def forward_kernel(
    field_hbm, kernel_hbm, gain_hbm, head_gain_hbm, ids_hbm,
    filtered_hbm, mean_ref, inverse_ref, normal_ref, send_ref,
    field_ref, kernel_ref, gain_ref, head_gain_ref, ids_ref, filtered_ref, pooled_ref, total_ref,
    field_sems, kernel_sems, small_sems, out_sems,
):
    images = field_ref.shape[0] // CELLS
    channels = field_ref.shape[1]
    chunks = channels // LANES
    part = 1.0 / channels
    block = channels // STEPS
    per_block = chunks // STEPS

    def block_at(step):
        return pl.ds(pl.multiple_of(step * block, LANES), block)

    def field_copy(step):
        at = block_at(step)
        return pltpu.make_async_copy(field_hbm.at[:, at], field_ref.at[:, at], field_sems.at[step])

    def kernel_copy(step):
        at = block_at(step)
        return pltpu.make_async_copy(
            kernel_hbm.at[:, :, at], kernel_ref.at[:, :, at], kernel_sems.at[step]
        )

    def filtered_copy(step):
        at = block_at(step)
        return pltpu.make_async_copy(filtered_ref.at[:, at], filtered_hbm.at[:, at], out_sems.at[step])

    small_copies = [
        pltpu.make_async_copy(gain_hbm, gain_ref, small_sems.at[0]),
        pltpu.make_async_copy(head_gain_hbm, head_gain_ref, small_sems.at[1]),
        pltpu.make_async_copy(ids_hbm, ids_ref, small_sems.at[2]),
    ]
    for step in range(STEPS):
        field_copy(step).start()
        kernel_copy(step).start()
    for copy in small_copies:
        copy.start()

    total_ref[...] = jnp.zeros_like(total_ref)

    def filter_chunk(chunk, carry):
        step = chunk // per_block

        @pl.when(chunk == step * per_block)
        def _():
            field_copy(step).wait()
            kernel_copy(step).wait()

        at = pl.ds(pl.multiple_of(chunk * LANES, LANES), LANES)
        for first in range(0, images, 2):
            fields = []
            for image in range(first, first + 2):
                rows = []
                for pair in range(SIDE // 2):
                    both = field_ref[pl.ds(image * CELLS + pair * 2 * SIDE, 2 * SIDE), at]
                    both = both.astype(jnp.float32)
                    rows += [both[:SIDE], both[SIDE:]]
                fields.append(rows)
            sums = [[None] * SIDE for _ in fields]
            filter_rows(fields, sums, kernel_ref, at, False)
            for offset, total in enumerate(sums):
                for row in range(SIDE):
                    cells = pl.ds((first + offset) * CELLS + row * SIDE, SIDE)
                    filtered_ref[cells, at] = total[row]
                    total_ref[cells, :] += total[row]
        return carry

    lax.fori_loop(0, chunks, filter_chunk, 0)
    for step in range(STEPS):
        filtered_copy(step).start()
    for copy in small_copies:
        copy.wait()
    mean_ref[...] = jnp.broadcast_to(
        jnp.sum(total_ref[...], axis=1, keepdims=True) * part, mean_ref.shape
    )

    for image in range(images):
        cells = pl.ds(image * CELLS, CELLS)
        average = mean_ref[cells, :]

        def spread_chunk(chunk, squares):
            at = pl.ds(pl.multiple_of(chunk * LANES, LANES), LANES)
            centred = filtered_ref[cells, at] - average
            return squares + centred * centred

        squares = lax.fori_loop(
            0, chunks, spread_chunk, jnp.zeros((CELLS, LANES), jnp.float32), unroll=4
        )
        spread = jnp.sum(squares, axis=1, keepdims=True) * part
        inverse_ref[cells, :] = jnp.broadcast_to(lax.rsqrt(spread + EPSILON), (CELLS, LANES))

    for image in range(images):
        cells = pl.ds(image * CELLS, CELLS)
        average = mean_ref[cells, :]
        inverse = inverse_ref[cells, :]

        def pool_chunk(chunk, carry):
            at = pl.ds(pl.multiple_of(chunk * LANES, LANES), LANES)
            normal = (filtered_ref[cells, at] - average) * inverse
            mixed = field_ref[cells, at].astype(jnp.float32) + normal * gain_ref[:, at]
            pooled_ref[pl.ds(image, 1), at] = jnp.sum(mixed, axis=0, keepdims=True) * (1.0 / CELLS)
            return carry

        lax.fori_loop(0, chunks, pool_chunk, 0, unroll=2)

    pooled = pooled_ref[...]
    centred = pooled - jnp.sum(pooled, axis=1, keepdims=True) * part
    spread = jnp.sum(centred * centred, axis=1, keepdims=True) * part
    head_inverse = lax.rsqrt(spread + EPSILON)
    normal = centred * head_inverse
    normal_ref[:, :channels] = normal
    normal_ref[:, channels:] = jnp.broadcast_to(head_inverse, (images, LANES))
    head_input = (normal * head_gain_ref[...]).astype(jnp.bfloat16)
    hot = hot_rows(ids_ref, images)
    group = send_ref.shape[0]
    share = channels // group
    for owner in range(group):
        send_ref[owner, :, :share] = head_input[:, owner * share : (owner + 1) * share]
        send_ref[owner, :, share:] = hot
    for step in range(STEPS):
        filtered_copy(step).wait()


def block_forward(features, kernel, norm_gain, head_gain, img_ids, group):
    images, channels = features.shape[0], features.shape[3]
    cells = images * CELLS
    dma = pltpu.SemaphoreType.DMA
    return call(
        forward_kernel,
        (
            (shape_of((cells, channels), F32), HBM),
            (shape_of((cells, LANES), F32), VMEM),
            (shape_of((cells, LANES), F32), VMEM),
            (shape_of((images, channels + LANES), F32), VMEM),
            (shape_of((group, images, channels // group + IDS), BF16), VMEM),
        ),
        (
            (features.reshape(cells, channels), HBM),
            (kernel, HBM),
            (norm_gain.reshape(1, channels), HBM),
            (head_gain.reshape(1, channels), HBM),
            (img_ids, HBM),
        ),
        "block_forward",
        14,
        scratch=(
            pltpu.VMEM((cells, channels), BF16),
            pltpu.VMEM(kernel.shape, F32),
            pltpu.VMEM((1, channels), F32),
            pltpu.VMEM((1, channels), F32),
            pltpu.SMEM(img_ids.shape, jnp.int32),
            pltpu.VMEM((cells, channels), F32),
            pltpu.VMEM((images, channels), F32),
            pltpu.VMEM((cells, LANES), F32),
            dma((STEPS,)),
            dma((STEPS,)),
            dma((3,)),
            dma((STEPS,)),
        ),
        grant=BIG,
    )


def backward_kernel(
    b0, b1, b2, b3, b4, b5, b6, b7, normal_hbm, gain_hbm, head_gain_hbm,
    filtered_hbm, mean_hbm, inverse_hbm, kernel_hbm, after_hbm,
    out_hbm,
    blocks_ref, normal_ref, gain_ref, head_gain_ref, filtered_ref, mean_ref, inverse_ref, kernel_ref,
    out_ref, even_ref, lean_ref, pull_ref, tilt_ref,
    block_sems, small_sems, filtered_sems, out_sems,
):
    del after_hbm
    images, channels = even_ref.shape
    blocks = (b0, b1, b2, b3, b4, b5, b6, b7)
    share = channels // len(blocks)
    wide = channels // STEPS

    def block_at(step):
        return pl.ds(pl.multiple_of(step * wide, LANES), wide)

    def out_copy(step):
        at = block_at(step)
        return pltpu.make_async_copy(out_ref.at[:, at], out_hbm.at[:, at], out_sems.at[step])

    head_copies = [
        pltpu.make_async_copy(block, blocks_ref.at[index], block_sems.at[index])
        for index, block in enumerate(blocks)
    ]
    small_copies = [
        pltpu.make_async_copy(source, target, small_sems.at[index])
        for index, (source, target) in enumerate((
            (head_gain_hbm, head_gain_ref), (gain_hbm, gain_ref), (normal_hbm, normal_ref),
            (mean_hbm, mean_ref), (inverse_hbm, inverse_ref),
        ))
    ]
    filtered_copies = [
        pltpu.make_async_copy(
            filtered_hbm.at[:, block_at(step)], filtered_ref.at[:, block_at(step)],
            filtered_sems.at[step],
        )
        for step in range(STEPS)
    ]
    kernel_copy = pltpu.make_async_copy(kernel_hbm, kernel_ref, small_sems.at[5])
    for copy in (*head_copies, *small_copies, *filtered_copies, kernel_copy):
        copy.start()
    chunks = channels // LANES
    per_block = chunks // STEPS
    part = 1.0 / channels

    for copy in (*head_copies, *small_copies):
        copy.wait()
    x, y_hi = lax.axis_index("x"), lax.axis_index("y_hi")
    for index, (step_x, step_y) in enumerate(PEERS):
        owner = group_peer(x, y_hi, 4 - step_x, step_y)
        at = pl.ds(pl.multiple_of(owner * share, LANES), share)
        tilt_ref[:, at] = blocks_ref[index] * head_gain_ref[:, at]
    cotangent = tilt_ref[...]
    normal = normal_ref[:, :channels]
    level = jnp.sum(cotangent, axis=1, keepdims=True) * part
    lean = jnp.sum(cotangent * normal, axis=1, keepdims=True) * part
    pooled_grad = normal_ref[:, channels : channels + 1] * (cotangent - level - normal * lean)
    even = pooled_grad * (1.0 / CELLS)
    even_ref[...] = even
    pull = even * gain_ref[...]
    pull_ref[...] = pull
    tilt_ref[...] = pull - jnp.sum(pull, axis=1, keepdims=True) * part

    for step in range(STEPS):
        filtered_copies[step].wait()
        for image in range(images):
            cells = pl.ds(image * CELLS, CELLS)
            average = mean_ref[cells, :]

            def lean_chunk(chunk, total):
                at = pl.ds(pl.multiple_of(chunk * LANES, LANES), LANES)
                return total + (filtered_ref[cells, at] - average) * pull_ref[pl.ds(image, 1), at]

            total = jnp.zeros((CELLS, LANES), F32) if step == 0 else lean_ref[cells, :]
            lean_ref[cells, :] = lax.fori_loop(
                step * per_block, (step + 1) * per_block, lean_chunk, total, unroll=True
            )
    inverse = inverse_ref[...]
    mean_lean = jnp.sum(lean_ref[...], axis=1, keepdims=True) * part
    lean_ref[...] = inverse * (inverse * (inverse * mean_lean))
    kernel_copy.wait()

    def filter_chunk(chunk, carry):
        at = pl.ds(pl.multiple_of(chunk * LANES, LANES), LANES)
        for first in range(0, images, 2):
            fields = []
            sums = []
            for image in range(first, first + 2):
                tilt = jnp.broadcast_to(tilt_ref[pl.ds(image, 1), at], (SIDE, LANES))
                even = jnp.broadcast_to(even_ref[pl.ds(image, 1), at], (SIDE, LANES))
                rows = []
                for row in range(SIDE):
                    cells = pl.ds(image * CELLS + row * SIDE, SIDE)
                    rows.append(
                        inverse_ref[cells, :] * tilt
                        - lean_ref[cells, :] * (filtered_ref[cells, at] - mean_ref[cells, :])
                    )
                fields.append(rows)
                sums.append([even] * SIDE)
            filter_rows(fields, sums, kernel_ref, at, True)
            for offset, total in enumerate(sums):
                for pair in range(SIDE // 2):
                    both = jnp.concatenate(total[2 * pair : 2 * pair + 2], axis=0)
                    cells = pl.ds((first + offset) * CELLS + pair * 2 * SIDE, 2 * SIDE)
                    out_ref[cells, at] = both.astype(jnp.bfloat16)
        step = chunk // per_block

        @pl.when(chunk == step * per_block + per_block - 1)
        def _():
            out_copy(step).start()

        return carry

    lax.fori_loop(0, chunks, filter_chunk, 0)
    for step in range(STEPS):
        out_copy(step).wait()


def block_backward(blocks, normal, norm_gain, head_gain, filtered, mean, inverse, kernel, after):
    cells, channels = filtered.shape
    images = cells // CELLS
    dma = pltpu.SemaphoreType.DMA
    out = call(
        backward_kernel,
        ((shape_of((cells, channels), BF16), HBM),),
        tuple(
            (array, HBM)
            for array in (
                *blocks, normal, norm_gain.reshape(1, channels), head_gain.reshape(1, channels),
                filtered, mean, inverse, kernel, after,
            )
        ),
        "block_backward",
        14,
        scratch=(
            pltpu.VMEM((len(blocks),) + blocks[0].shape, F32),
            pltpu.VMEM(normal.shape, F32),
            pltpu.VMEM((1, channels), F32),
            pltpu.VMEM((1, channels), F32),
            pltpu.VMEM((cells, channels), F32),
            pltpu.VMEM((cells, LANES), F32),
            pltpu.VMEM((cells, LANES), F32),
            pltpu.VMEM(kernel.shape, F32),
            pltpu.VMEM((cells, channels), BF16),
            pltpu.VMEM((images, channels), F32),
            pltpu.VMEM((cells, LANES), F32),
            pltpu.VMEM((images, channels), F32),
            pltpu.VMEM((images, channels), F32),
            dma((len(blocks),)),
            dma((6,)),
            dma((STEPS,)),
            dma((STEPS,)),
        ),
        grant=BIG,
    )
    return out.reshape(images, SIDE, SIDE, channels)


def dot(left, right, left_dim, right_dim):
    return lax.dot_general(
        left, right, (((left_dim,), (right_dim,)), ((), ())), preferred_element_type=F32
    )


def inverse_length(values):
    return lax.rsqrt(jnp.sum(values * values, axis=-1, keepdims=True) + EPSILON)


def length_back(unit, inverse, cotangent):
    return inverse * (cotangent - unit * jnp.sum(unit * cotangent, axis=-1, keepdims=True))


def hot_rows(ids_ref, rows):
    row = lax.broadcasted_iota(jnp.int32, (rows, IDS), 0)
    ids = jnp.zeros((rows, IDS), jnp.int32)
    for index in range(rows):
        ids = jnp.where(row == index, ids_ref[index], ids)
    lane = lax.broadcasted_iota(jnp.int32, (rows, IDS), 1)
    return jnp.where(ids == lane, 1.0, 0.0).astype(BF16)


def pack_kernel(text_hbm, ids_hbm, out_ref, text_ref, ids_ref, sems):
    copies = [
        pltpu.make_async_copy(text_hbm, text_ref, sems.at[0]),
        pltpu.make_async_copy(ids_hbm, ids_ref, sems.at[1]),
    ]
    for copy in copies:
        copy.start()
    for copy in copies:
        copy.wait()
    rows, width = text_ref.shape
    text = text_ref[...].astype(F32)
    unit = (text * inverse_length(text)).astype(BF16)
    hot = hot_rows(ids_ref, rows)
    for target in range(out_ref.shape[0]):
        out_ref[target, :, :width] = unit
        out_ref[target, :, width:] = hot


def line_kernel(plane_ref, after_ref, out_ref):
    del after_ref
    plane, rows, _ = plane_ref.shape
    line = plane // 2
    y_hi = lax.axis_index("y_hi")
    for side in range(2):
        part = lax.rem(y_hi + side, 2)
        for first in range(0, line, 4):
            four = [plane_ref[(first + offset) * 2 + part].astype(F32) for offset in range(4)]
            at = (side * line + first) * rows
            out_ref[at : at + 4 * rows, :] = jnp.concatenate(four, axis=0).astype(BF16)


def partial_kernel(received_ref, projection_ref, out_ref, columns_ref, hot_ref):
    group = received_ref.shape[0]
    share = projection_ref.shape[0]
    rows = jnp.concatenate([received_ref[owner].astype(F32) for owner in range(group)], axis=0)
    columns = rows[:, :share].astype(BF16)
    columns_ref[...] = columns
    hot_ref[...] = rows[:, share:].astype(BF16)
    partial = dot(columns, projection_ref[...], 1, 0).astype(BF16)
    for target in range(group):
        out_ref[target] = partial


def pair_kernel(
    partials_ref, columns_ref, hot_ref, projection_ref, t0, t1, t2, t3, t4, t5, t6, t7,
    scale_ref, shift_ref,
    h0, h1, h2, h3, h4, h5, h6, h7, keep_ref, give_ref,
    low_ref, embed_ref, rows_ref, near_ref, far_ref, head_ref,
):
    group, images, width = partials_ref.shape
    blocks = (t0, t1, t2, t3, t4, t5, t6, t7)
    scale, shift, core = scale_ref[0], shift_ref[0], lax.axis_index("core")
    embedded = partials_ref[0].astype(F32)
    for owner in range(1, group):
        embedded += partials_ref[owner].astype(F32)
    inverse = inverse_length(embedded)
    unit = embedded * inverse
    low = unit.astype(BF16)
    low_ref[...] = low
    hot = hot_ref[...]
    weights = []
    for block in blocks:
        logits = scale * dot(low, block[:, :width], 1, 1) + shift
        signs = 2.0 * dot(hot, block[:, width:], 1, 1) - 1.0
        weights.append((-signs * jax.nn.sigmoid(-signs * logits)).astype(BF16))
    image_grad = dot(weights[0], t0[:, :width], 1, 0)
    for weight, block in zip(weights[1:], blocks[1:]):
        image_grad += dot(weight, block[:, :width], 1, 0)
    embed = length_back(unit, inverse, scale * image_grad).astype(BF16)
    embed_ref[...] = embed
    head = dot(embed, projection_ref[...], 1, 1)
    rows = images // group
    for owner in range(group):
        head_ref[owner] = head[owner * rows : (owner + 1) * rows]
    x, y_hi = lax.axis_index("x"), lax.axis_index("y_hi")
    for (step_x, step_y), out_ref in zip(PEERS, (h0, h1, h2, h3, h4, h5, h6, h7)):
        out_ref[...] = head_ref[group_peer(x, y_hi, step_x, step_y)]
    columns = columns_ref[...]
    line = keep_ref.shape[0]
    own = weights[0][:, : line * rows]
    other = weights[4][:, : line * rows]
    strip = columns.shape[1] // line
    for out_ref, side, first, second in (
        (give_ref, 1 - core, other, own),
        (keep_ref, core, own, other),
    ):
        at = pl.ds(pl.multiple_of(side * (width - HALF), LANES), HALF)
        rows_ref[...] = dot(columns, embed_ref[:, at], 0, 0)
        low_half = low_ref[:, at]
        near_ref[...] = dot(first, low_half, 0, 0)
        far_ref[...] = dot(second, low_half, 0, 0)
        for target in range(line):
            texts = slice(target * rows, (target + 1) * rows)
            stacked = jnp.concatenate(
                [rows_ref[target * strip : (target + 1) * strip], near_ref[texts], far_ref[texts]],
                axis=0,
            )
            out_ref[target] = stacked.astype(out_ref.dtype)


def add_kernel(keep_ref, got_ref, out_ref):
    out_ref[...] = (keep_ref[...] + got_ref[...].astype(F32)).astype(BF16)


def strip_kernel(strips_ref, out_ref, mine_ref, theirs_ref):
    line, rows, half = strips_ref.shape
    texts = mine_ref.shape[0]
    strip = rows - 2 * texts
    total = strips_ref[0].astype(F32)
    for source in range(1, line):
        total += strips_ref[source].astype(F32)
    low = total[:strip].astype(BF16)
    for target in range(line):
        out_ref[target] = low
    mine_ref[...] = total[strip : strip + texts]
    theirs_ref[...] = total[strip + texts :]


def text_kernel(text_ref, mine_ref, got_ref, scale_ref, out_ref):
    width = text_ref.shape[1]
    text = text_ref[...].astype(F32)
    inverse = inverse_length(text)
    first = lax.axis_index("core") == 0
    mine, got = mine_ref[...], got_ref[...]
    left = jnp.where(first, mine, got)
    right = jnp.where(first, got, mine)
    grad = jnp.concatenate([left, right[:, 2 * HALF - width :]], axis=1)
    out_ref[...] = length_back(text * inverse, inverse, scale_ref[0] * grad)


def join_kernel(near_ref, far_ref, out_ref):
    core = lax.axis_index("core")
    width = out_ref.shape[1]

    def put(left, right):
        out_ref[:, :HALF] = left[...].astype(F32)
        out_ref[:, HALF:] = right[:, 2 * HALF - width :].astype(F32)

    pl.when(core == 0)(lambda: put(near_ref, far_ref))
    pl.when(core != 0)(lambda: put(far_ref, near_ref))


def exchange(blocks, axes):
    return lax.all_to_all(blocks, axes, 0, 0, tiled=True)


def swap_core(block):
    return lax.ppermute(block, "core", ((0, 1), (1, 0)))


def along_x(block, step):
    return lax.ppermute(block, "x", tuple((i, (i + step) % 4) for i in range(4)))


def local(
    features,
    text_embed,
    img_ids,
    txt_ids,
    kernel,
    norm_gain,
    head_gain,
    projection,
    logit_scale,
    logit_bias,
):
    rows, width = text_embed.shape
    share = projection.shape[0]
    group = lax.axis_size(GROUP)
    line = lax.axis_size(LINE)
    images = group * rows
    texts = line * rows
    strip = share // line
    dma = pltpu.SemaphoreType.DMA

    packed = call(
        pack_kernel,
        ((shape_of((2 * line, rows, width + IDS), BF16), VMEM),),
        ((text_embed, HBM), (txt_ids, HBM)),
        "text_pack", 1,
        scratch=(
            pltpu.VMEM((rows, width), BF16), pltpu.SMEM((rows,), jnp.int32), dma((2,)),
        ),
        grant=BIG,
    )
    gathered = exchange(packed, PLANE)
    filtered, mean, inverse, normal, send = block_forward(
        features, kernel, norm_gain, head_gain, img_ids, group
    )
    gathered, send = lax.optimization_barrier((gathered, send))
    received = exchange(send, GROUP)
    partials, columns, hot = call(
        partial_kernel,
        (
            (shape_of((group, images, width), BF16), VMEM),
            (shape_of((images, share), BF16), VMEM),
            (shape_of((images, IDS), BF16), VMEM),
        ),
        ((received, VMEM), (projection, VMEM)),
        "partial_embed", 2,
    )
    near = [
        call(
            line_kernel,
            ((shape_of((2 * texts, width + IDS), BF16), VMEM),),
            ((gathered, VMEM), (columns, VMEM)),
            "line_rows", 1,
        )
    ]
    near += [along_x(near[0], step) for step in (1, 3, 2)]
    far = [swap_core(block) for block in near]
    partials = exchange(partials, GROUP)
    results = call(
        pair_kernel,
        ((shape_of((rows, share), F32), VMEM),) * group
        + (
            (shape_of((line, strip + 2 * rows, HALF), F32), VMEM),
            (shape_of((line, strip + 2 * rows, HALF), BF16), VMEM),
        ),
        tuple((array, VMEM) for array in (partials, columns, hot, projection, *near, *far))
        + ((logit_scale, SMEM), (logit_bias, SMEM)),
        "pairs", 6,
        scratch=(
            pltpu.VMEM((images, width), BF16),
            pltpu.VMEM((images, width), BF16),
            pltpu.VMEM((share, HALF), F32),
            pltpu.VMEM((texts, HALF), F32),
            pltpu.VMEM((texts, HALF), F32),
            pltpu.VMEM((group, rows, share), F32),
        ),
    )
    head_parts, (keep, give) = results[:group], results[group:]
    strips = call(
        add_kernel, ((shape_of(keep.shape, BF16), VMEM),), ((keep, VMEM), (swap_core(give), VMEM)),
        "strip_add", 1,
        grant=BIG,
    )
    strips = exchange(strips, LINE)
    head_blocks = [head_parts[0]]
    for (step_x, step_y), part in zip(PEERS[1:], head_parts[1:]):
        pairs = tuple(
            (at, (at // 2 + step_x) % 4 * 2 + (at % 2 + step_y) % 2) for at in range(group)
        )
        head_blocks.append(lax.ppermute(part, GROUP, pairs))
    strips, *head_blocks = lax.optimization_barrier((strips, *head_blocks))
    sums, mine, theirs = call(
        strip_kernel,
        (
            (shape_of((line, strip, HALF), BF16), VMEM),
            (shape_of((rows, HALF), F32), VMEM),
            (shape_of((rows, HALF), F32), VMEM),
        ),
        ((strips, VMEM),),
        "strip_sum", 1,
        grant=BIG,
    )
    near_half = exchange(sums, LINE).reshape(share, HALF)
    grad_features = block_backward(
        head_blocks, normal, norm_gain, head_gain, filtered, mean, inverse, kernel, mine
    )
    near_half, theirs, grad_features = lax.optimization_barrier((near_half, theirs, grad_features))
    grad_text = call(
        text_kernel,
        ((shape_of((rows, width), F32), VMEM),),
        ((text_embed, VMEM), (mine, VMEM), (swap_core(theirs), VMEM), (logit_scale, SMEM)),
        "text_grad", 1,
    )
    grad_proj = call(
        join_kernel,
        ((shape_of((share, width), F32), VMEM),),
        ((near_half, VMEM), (swap_core(near_half), VMEM)),
        "proj_join", 2,
    )
    return (grad_features, grad_text, grad_proj)


def solution(mesh):
    fine = Mesh(mesh.devices.reshape(SIZES), AXES)
    placed = (
        P(ALL, None, None, None),
        P(ALL, None),
        P(ALL),
        P(ALL),
        P(),
        P(),
        P(),
        P(GROUP, None),
        P(),
        P(),
    )
    return jax.shard_map(
        local,
        mesh=fine,
        in_specs=placed,
        out_specs=(P(ALL, None, None, None), P(ALL, None), P(GROUP, None)),
        check_vma=False,
    )
```

time: 186 us -> 133 us (0.72)
  waiting for transfers between devices: 65.9 us -> 8.74 us
  Pallas kernels: 0 us -> 41.6 us
  matrix products: 37.8 us -> 0 us
  other arithmetic: 19.5 us -> 0 us
  blocking collectives: 0 us -> 13 us
  starting transfers between devices: 50.9 us -> 63.8 us
  local copies, waits for them, and re-layouts: 8.39 us -> 3.37 us
    all_to_all x8 -> x4, waiting for transfers between devices: 63.7 us -> 1.46 us  [exchange(): return lax.all_to_all(blocks, axes, 0, 0, tiled=True)]
    pallas_call x0 -> x10, Pallas kernels: none -> 41.6 us  [call(): pl.pallas_call(body, out_shape=shapes[0] if single else shapes, in_specs=...]
    conv_general_dilated x2 -> x0, matrix products: 30 us -> none  [block_pool(): lax.conv_general_dilated(widened, kernel[:, :, None, :], (1, 1), ((margin...]
    ppermute x0 -> x10, starting transfers between devices: none -> 15.1 us  [the longest x7 12.3 us: local(): head_blocks.append(lax.ppermute(part, GROUP, pairs))]
    all_to_all x0 -> x1, blocking collectives: none -> 13 us  [exchange(): return lax.all_to_all(blocks, axes, 0, 0, tiled=True)]
    all_to_all x8 -> x4, starting transfers between devices: 40.6 us -> 29.1 us  [exchange(): return lax.all_to_all(blocks, axes, 0, 0, tiled=True)]
    reduce_sum x14 -> x0, other arithmetic: 10.9 us -> none  [the longest x1 3.13 us: block_pool(): centred = filtered - average]
    ppermute x4 -> x7, starting transfers between devices: 10.3 us -> 19.6 us  [swap_core(): return lax.ppermute(block, 'core', ((0, 1), (1, 0)))]
  transfers between devices with their start and end apart: 12 -> 21, of which waited for: 9 -> 7; matrix products, arithmetic and copies ran while one was open for 17% -> 0% of each run, Pallas kernels for 0% -> 22%
where the time goes in v2:
time: 133 us
  starting transfers between devices  63.8 us (48%)
  Pallas kernels  41.6 us (31%)
  blocking collectives  13 us (10%)
  waiting for transfers between devices  8.74 us (7%)
  local copies, waits for them, and re-layouts  3.37 us (3%)
  between operations  2.15 us (2%)
    pallas_call x10, Pallas kernels, call(): pl.pallas_call(body, out_shape=shapes[0] if single else shapes, in_specs=...  41.6 us
    all_to_all x4, starting transfers between devices, exchange(): return lax.all_to_all(blocks, axes, 0, 0, tiled=True)  29.1 us
    ppermute x7, starting transfers between devices, swap_core(): return lax.ppermute(block, 'core', ((0, 1), (1, 0)))  19.6 us
    all_to_all x1, blocking collectives, exchange(): return lax.all_to_all(blocks, axes, 0, 0, tiled=True)  13 us
    ppermute x7, starting transfers between devices, local(): head_blocks.append(lax.ppermute(part, GROUP, pairs))  12.3 us
    ppermute x7, waiting for transfers between devices, local(): head_blocks.append(lax.ppermute(part, GROUP, pairs))  3.85 us
    unnamed x30, local copies, waits for them, and re-layouts  3.37 us
    ppermute x7, waiting for transfers between devices, swap_core(): return lax.ppermute(block, 'core', ((0, 1), (1, 0)))  3.13 us
  transfers between devices with their start and end apart: 21, of which 7 were waited for; matrix products, arithmetic and copies ran while one was open for 0% of the time, Pallas kernels for 22%

profile of v2, /device:TPU:1, one launch (start us, length us, event | category | flops | bytes accessed | tf_op | source)
XLA Modules:
  0.0 132.7 jit_solution(16834348562152751857)
XLA Ops:
  0.6 1.7 %text_pack.1 = bf16[32,4,1280]{2,1,0:T(4,128)(2,1)} custom-call(bf16[4,1152]{1,0:T(4,128)(2,1)} %text_ref.1, s32[4]{0:T(128)} %ids_hbm.2), custom_call_target="tpu_custom_call" | custom-call | bytes 3000000 | tf_op jit(solution)/shard_map/text_pack/pallas_call | solution.py:40
  2.3 0.0 copy-start
  2.3 12.2 %all-to-all-start = ((bf16[32,4,1280]{2,1,0:T(4,128)(2,1)}), bf16[32,4,1280]{2,1,0:T(4,128)(2,1)S(1)}, u32[]{:S(2)}, u32[]{:S(2)}) async-start(bf16[32,4,1280]{2,1,0:T(4,128)(2,1)} %text_pack.1), calls=%async_computation | async-start | bytes 655360 | tf_op jit(solution)/shard_map/all_to_all | solution.py:577
  14.5 14.9 %block_forward.1 = (f32[256,3072]{1,0:T(8,128)}, f32[256,128]{1,0:T(8,128)}, f32[256,128]{1,0:T(8,128)}, f32[4,3200]{1,0:T(4,128)}, bf16[8,4,512]{2,1,0:T(4,128)(2,1)}) custom-call(bf16[256,3072]{1,0:T(8,128)(2,1)} %bitcast.7, f32[7,7,3072]{2,1,0:T(8,128)} %kernel_hbm.3, f32[1,3072]{1,0:T(1,128)} %bitcast.9, f32[1,3072]{1,0:T(1,128)} %bitcast.11, s32[4]{0:T(128)} %ids_hbm.3), custom_call_target="tpu_custom_call" | custom-call | bytes 42000000 | tf_op jit(solution)/shard_map/block_forward/pallas_call | solution.py:40
  29.4 0.0 all-to-all-done.plane_ref
  29.4 13.0 %all_to_all.25.received_ref = bf16[8,4,512]{2,1,0:T(4,128)(2,1)S(1)} all-to-all(bf16[8,4,512]{2,1,0:T(4,128)(2,1)} %get-tuple-element.39), channel_id=1, replica_groups=mesh['y_lo'=2,'z'=8,'core'=2,'x'=4,'y_hi'=2] {'x','y_hi'}, dimensions={0} | all-to-all | bytes 65536 | tf_op jit(solution)/shard_map/all_to_all | solution.py:577
  42.5 1.1 partial_embed.1
  43.6 0.1 line_rows.1.t0
  43.7 1.1 collective-permute-start.2
  44.7 1.7 %collective-permute-start.1 = (bf16[128,1280]{1,0:T(8,128)(2,1)S(1)}, bf16[128,1280]{1,0:T(8,128)(2,1)S(1)}, u32[]{:S(2)}, u32[]{:S(2)}) collective-permute-start(bf16[128,1280]{1,0:T(8,128)(2,1)S(1)} %line_rows.1.t0), channel_id=1, source_target_pairs={{0,6},{2,0},{4,2},{6,4},{1,7},{3,1},{5,3},{7,5},{8,14},{10,8},{12,... | collective-permute-start | bytes 983048 | tf_op jit(solution)/shard_map/ppermute | solution.py:585
  46.4 0.0 collective-permute-start
  46.4 4.2 %all-to-all-start.2 = ((bf16[8,32,1152]{2,1,0:T(8,128)(2,1)}), bf16[8,32,1152]{2,1,0:T(8,128)(2,1)S(1)}, u32[]{:S(2)}, u32[]{:S(2)}) async-start(bf16[8,32,1152]{2,1,0:T(8,128)(2,1)} %get-tuple-element.40), calls=%async_computation.2 | async-start | bytes 1179648 | tf_op jit(solution)/shard_map/all_to_all | solution.py:577
  50.6 3.7 %collective-permute-start.3 = (bf16[128,1280]{1,0:T(8,128)(2,1)S(1)}, bf16[128,1280]{1,0:T(8,128)(2,1)S(1)}, u32[]{:S(2)}, u32[]{:S(2)}) collective-permute-start(bf16[128,1280]{1,0:T(8,128)(2,1)S(1)} %line_rows.1.t0), channel_id=1, source_target_pairs={{0,8},{8,0},{1,9},{9,1},{2,10},{10,2},{3,11},{11,3},{4,12},{12,4},... | collective-permute-start | bytes 983048 | tf_op jit(solution)/shard_map/ppermute | solution.py:581
  54.3 0.0 collective-permute-done.2.t3
  54.3 4.3 %collective-permute-start.6 = (bf16[128,1280]{1,0:T(8,128)(2,1)S(1)}, bf16[128,1280]{1,0:T(8,128)(2,1)S(1)}, u32[]{:S(2)}, u32[]{:S(2)}) collective-permute-start(bf16[128,1280]{1,0:T(8,128)(2,1)S(1)} %collective-permute-done.2.t3), channel_id=1, source_target_pairs={{0,8},{8,0},{1,9},{9,1},{2,10},{10,2},{3,11},{11,3},{4,12},{12,4},... | collective-permute-start | bytes 983048 | tf_op jit(solution)/shard_map/ppermute | solution.py:581
  58.6 0.3 collective-permute-done.1.t2
  58.9 5.2 %collective-permute-start.5 = (bf16[128,1280]{1,0:T(8,128)(2,1)S(1)}, bf16[128,1280]{1,0:T(8,128)(2,1)}, u32[]{:S(2)}, u32[]{:S(2)}) collective-permute-start(bf16[128,1280]{1,0:T(8,128)(2,1)S(1)} %collective-permute-done.1.t2), channel_id=1, source_target_pairs={{0,8},{8,0},{1,9},{9,1},{2,10},{10,2},{3,11},{11,3},{4,12},{12,4},... | collective-permute-start | bytes 983048 | tf_op jit(solution)/shard_map/ppermute | solution.py:581
  64.1 0.0 collective-permute-done.t1
  64.1 0.7 collective-permute-start.4
  66.1 0.0 collective-permute-done.3.t4
  66.1 0.6 all-to-all-done.2.partials_ref
  66.8 0.0 collective-permute-done.6.t7
  66.8 0.0 collective-permute-done.5.t6
  66.8 0.0 collective-permute-done.4.t5
  66.8 3.5 %pairs.1 = (f32[4,384]{1,0:T(4,128)S(1)}, f32[4,384]{1,0:T(4,128)S(1)}, f32[4,384]{1,0:T(4,128)S(1)}, f32[4,384]{1,0:T(4,128)S(1)}, f32[4,384]{1,0:T(4,128)S(1)}...) custom-call(bf16[8,32,1152]{2,1,0:T(8,128)(2,1)S(1)} %all-to-all-don, ...), custom_call_target="tpu_custom_call" | custom-call | bytes 18000000 | tf_op jit(solution)/shard_map/pairs/pallas_call | solution.py:40
  70.3 0.0 copy-start.1
  70.3 1.0 copy-done.1
  71.3 0.6 copy-done.4
  71.9 2.0 %collective-permute-start.7 = (bf16[16,32,640]{2,1,0:T(8,128)(2,1)S(1)}, bf16[16,32,640]{2,1,0:T(8,128)(2,1)S(1)}, u32[]{:S(2)}, u32[]{:S(2)}) collective-permute-start(bf16[16,32,640]{2,1,0:T(8,128)(2,1)S(1)} %get-tuple-element.45), channel_id=1, source_target_pairs={{0,8},{8,0},{1,9},{9,1},{2,10},{10,2},{3,11},{11,3},{4,12},{12,4},... | collective-permute-start | bytes 1966088 | tf_op jit(solution)/shard_map/ppermute | solution.py:581
  73.9 1.7 %collective-permute-done.7.got_ref = bf16[16,32,640]{2,1,0:T(8,128)(2,1)S(1)} collective-permute-done((bf16[16,32,640]{2,1,0:T(8,128)(2,1)S(1)}, bf16[16,32,640]{2,1,0:T(8,128)(2,1)S(1)}, u32[]{:S(2)}, u32[]{:S(2)}) %collective-permute-start.7) | collective-permute-done | bytes 655392 | tf_op jit(solution)/shard_map/ppermute | solution.py:581
  75.6 0.8 copy-done.6
  76.4 2.4 %strip_add.1 = bf16[16,32,640]{2,1,0:T(8,128)(2,1)} custom-call(f32[16,32,640]{2,1,0:T(8,128)} %copy-done.1, bf16[16,32,640]{2,1,0:T(8,128)(2,1)} %copy-done.6), custom_call_target="tpu_custom_call" | custom-call | bytes 3000000 | tf_op jit(solution)/shard_map/strip_add/pallas_call | solution.py:40
  78.9 6.5 %all-to-all-start.3 = ((bf16[16,32,640]{2,1,0:T(8,128)(2,1)}), bf16[16,32,640]{2,1,0:T(8,128)(2,1)S(1)}, u32[]{:S(2)}, u32[]{:S(2)}) async-start(bf16[16,32,640]{2,1,0:T(8,128)(2,1)} %strip_add.1), calls=%async_computation.3 | async-start | bytes 1310720 | tf_op jit(solution)/shard_map/all_to_all | solution.py:577
  85.4 2.6 %collective-permute-start.8 = (f32[4,384]{1,0:T(4,128)S(1)}, f32[4,384]{1,0:T(4,128)S(1)}, u32[]{:S(2)}, u32[]{:S(2)}) collective-permute-start(f32[4,384]{1,0:T(4,128)S(1)} %get-tuple-element.47), channel_id=1, source_target_pairs={{0,1},{1,0},{2,3},{3,2},{4,5},{5,4},{6,7},{7,6},{8,9},{9,8},{10,11... | collective-permute-start | bytes 18440 | tf_op jit(solution)/shard_map/ppermute | solution.py:677
  88.0 0.3 collective-permute-start.9
  88.3 0.8 collective-permute-start.10
  89.1 3.0 %collective-permute-start.11 = (f32[4,384]{1,0:T(4,128)S(1)}, f32[4,384]{1,0:T(4,128)S(1)}, u32[]{:S(2)}, u32[]{:S(2)}) collective-permute-start(f32[4,384]{1,0:T(4,128)S(1)} %get-tuple-element.50), channel_id=1, source_target_pairs={{0,4},{1,5},{2,6},{3,7},{4,0},{5,1},{6,2},{7,3},{8,12},{9,13},{10,... | collective-permute-start | bytes 18440 | tf_op jit(solution)/shard_map/ppermute | solution.py:677
  92.0 2.2 %collective-permute-start.12 = (f32[4,384]{1,0:T(4,128)S(1)}, f32[4,384]{1,0:T(4,128)S(1)}, u32[]{:S(2)}, u32[]{:S(2)}) collective-permute-start(f32[4,384]{1,0:T(4,128)S(1)} %get-tuple-element.51), channel_id=1, source_target_pairs={{0,5},{1,4},{2,7},{3,6},{4,1},{5,0},{6,3},{7,2},{8,13},{9,12},{10,... | collective-permute-start | bytes 18440 | tf_op jit(solution)/shard_map/ppermute | solution.py:677
  94.3 0.0 collective-permute-done.8.b1
  94.3 2.1 %collective-permute-start.13 = (f32[4,384]{1,0:T(4,128)S(1)}, f32[4,384]{1,0:T(4,128)S(1)}, u32[]{:S(2)}, u32[]{:S(2)}) collective-permute-start(f32[4,384]{1,0:T(4,128)S(1)} %get-tuple-element.52), channel_id=1, source_target_pairs={{0,6},{1,7},{2,0},{3,1},{4,2},{5,3},{6,4},{7,5},{8,14},{9,15},{10,... | collective-permute-start | bytes 18440 | tf_op jit(solution)/shard_map/ppermute | solution.py:677
  96.4 0.0 collective-permute-done.9.b2
  96.4 1.3 collective-permute-start.14
  97.7 0.0 collective-permute-done.10.b3
  97.7 0.0 collective-permute-done.11.b4
  97.7 0.7 collective-permute-done.12.b5
  98.5 0.0 collective-permute-done.13.b6
  98.5 3.1 %collective-permute-done.14.b7 = f32[4,384]{1,0:T(4,128)S(1)} collective-permute-done((f32[4,384]{1,0:T(4,128)S(1)}, f32[4,384]{1,0:T(4,128)S(1)}, u32[]{:S(2)}, u32[]{:S(2)}) %collective-permute-start.14) | collective-permute-done | bytes 6176 | tf_op jit(solution)/shard_map/ppermute | solution.py:677
  101.6 0.8 all-to-all-done.3.strips_ref
  102.4 0.8 copy-done.5
  103.2 2.0 %strip_sum.1 = (bf16[16,24,640]{2,1,0:T(8,128)(2,1)}, f32[4,640]{1,0:T(4,128)}, f32[4,640]{1,0:T(4,128)}) custom-call(bf16[16,32,640]{2,1,0:T(8,128)(2,1)} %copy-done.5), custom_call_target="tpu_custom_call" | custom-call | bytes 3000000 | tf_op jit(solution)/shard_map/strip_sum/pallas_call | solution.py:40
  105.2 6.2 %all-to-all-start.4 = ((bf16[16,24,640]{2,1,0:T(8,128)(2,1)}), bf16[16,24,640]{2,1,0:T(8,128)(2,1)S(1)}, u32[]{:S(2)}, u32[]{:S(2)}) async-start(bf16[16,24,640]{2,1,0:T(8,128)(2,1)} %get-tuple-element.55), calls=%async_computation.4 | async-start | bytes 983040 | tf_op jit(solution)/shard_map/all_to_all | solution.py:577
  111.4 0.0 copy-done.7
  111.4 0.0 copy-done.8
  111.5 0.0 copy-done.9
  111.5 0.0 copy-start.2
  111.5 0.0 copy-start.3
  111.5 13.9 %block_backward.1 = bf16[256,3072]{1,0:T(8,128)(2,1)} custom-call(f32[4,384]{1,0:T(4,128)} %copy-done.4, f32[4,384]{1,0:T(4,128)} %copy-done.7, f32[4,384]{1,0:T(4,128)} %copy-done.8, f32[4,384]{1,0:T(4,128)} %copy-done.9, f32[4,384]{1,0:T(4,128)} %copy-done.10, f32[4,384]{1,0:T(4,128)} %copy-done.11, f32[4,384]{1,0:T(4,128)} %copy-done.12, ...), custom_call_target="tpu_custom_call" | custom-call | bytes 42000000 | tf_op jit(solution)/shard_map/block_backward/pallas_call | solution.py:40
  125.4 0.0 all-to-all-done.4
  125.4 3.7 %collective-permute-start.16 = (bf16[384,640]{1,0:T(8,128)(2,1)S(1)}, bf16[384,640]{1,0:T(8,128)(2,1)S(1)}, u32[]{:S(2)}, u32[]{:S(2)}) collective-permute-start(bf16[384,640]{1,0:T(8,128)(2,1)S(1)} %bitcast.5), channel_id=1, source_target_pairs={{0,8},{8,0},{1,9},{9,1},{2,10},{10,2},{3,11},{11,3},{4,12},{12,4},... | collective-permute-start | bytes 1474568 | tf_op jit(solution)/shard_map/ppermute | solution.py:581
  129.1 0.1 collective-permute-start.15
  129.2 1.4 %collective-permute-done.15.got_ref = f32[4,640]{1,0:T(4,128)S(1)} collective-permute-done((f32[4,640]{1,0:T(4,128)S(1)}, f32[4,640]{1,0:T(4,128)S(1)}, u32[]{:S(2)}, u32[]{:S(2)}) %collective-permute-start.15) | collective-permute-done | bytes 10272 | tf_op jit(solution)/shard_map/ppermute | solution.py:581
  130.6 0.8 text_grad.1
  131.4 0.0 collective-permute-done.16.far_ref
  131.4 1.3 proj_join.1
  (19 shorter events, 0.0 us)
Async XLA Ops:
  2.3 40.2 %copy-start = (bf16[384,1152]{1,0:T(8,128)(2,1)S(1)}, bf16[384,1152]{1,0:T(8,128)(2,1)}, u32[]{:S(2)}) copy-start(bf16[384,1152]{1,0:T(8,128)(2,1)} %projection_ref.3) | copy-start | bytes 2654212
  2.3 27.1 %all-to-all-start = ((bf16[32,4,1280]{2,1,0:T(4,128)(2,1)}), bf16[32,4,1280]{2,1,0:T(4,128)(2,1)S(1)}, u32[]{:S(2)}, u32[]{:S(2)}) async-start(bf16[32,4,1280]{2,1,0:T(4,128)(2,1)} %text_pack.1), calls=%async_computation | async-start | bytes 655360 | tf_op jit(solution)/shard_map/all_to_all | solution.py:577
  43.7 10.6 %collective-permute-start.2 = (bf16[128,1280]{1,0:T(8,128)(2,1)S(1)}, bf16[128,1280]{1,0:T(8,128)(2,1)S(1)}, u32[]{:S(2)}, u32[]{:S(2)}) collective-permute-start(bf16[128,1280]{1,0:T(8,128)(2,1)S(1)} %line_rows.1.t0), channel_id=1, source_target_pairs={{0,4},{2,6},{4,0},{6,2},{1,5},{3,7},{5,1},{7,3},{8,12},{10,14},{12... | collective-permute-start | bytes 983048 | tf_op jit(solution)/shard_map/ppermute | solution.py:585
  44.7 14.1 %collective-permute-start.1 = (bf16[128,1280]{1,0:T(8,128)(2,1)S(1)}, bf16[128,1280]{1,0:T(8,128)(2,1)S(1)}, u32[]{:S(2)}, u32[]{:S(2)}) collective-permute-start(bf16[128,1280]{1,0:T(8,128)(2,1)S(1)} %line_rows.1.t0), channel_id=1, source_target_pairs={{0,6},{2,0},{4,2},{6,4},{1,7},{3,1},{5,3},{7,5},{8,14},{10,8},{12,... | collective-permute-start | bytes 983048 | tf_op jit(solution)/shard_map/ppermute | solution.py:585
  46.4 17.7 %collective-permute-start = (bf16[128,1280]{1,0:T(8,128)(2,1)S(1)}, bf16[128,1280]{1,0:T(8,128)(2,1)S(1)}, u32[]{:S(2)}, u32[]{:S(2)}) collective-permute-start(bf16[128,1280]{1,0:T(8,128)(2,1)S(1)} %line_rows.1.t0), channel_id=1, source_target_pairs={{0,2},{2,4},{4,6},{6,0},{1,3},{3,5},{5,7},{7,1},{8,10},{10,12},{12... | collective-permute-start | bytes 983048 | tf_op jit(solution)/shard_map/ppermute | solution.py:585
  46.4 20.3 %all-to-all-start.2 = ((bf16[8,32,1152]{2,1,0:T(8,128)(2,1)}), bf16[8,32,1152]{2,1,0:T(8,128)(2,1)S(1)}, u32[]{:S(2)}, u32[]{:S(2)}) async-start(bf16[8,32,1152]{2,1,0:T(8,128)(2,1)} %get-tuple-element.40), calls=%async_computation.2 | async-start | bytes 1179648 | tf_op jit(solution)/shard_map/all_to_all | solution.py:577
  50.6 15.5 %collective-permute-start.3 = (bf16[128,1280]{1,0:T(8,128)(2,1)S(1)}, bf16[128,1280]{1,0:T(8,128)(2,1)S(1)}, u32[]{:S(2)}, u32[]{:S(2)}) collective-permute-start(bf16[128,1280]{1,0:T(8,128)(2,1)S(1)} %line_rows.1.t0), channel_id=1, source_target_pairs={{0,8},{8,0},{1,9},{9,1},{2,10},{10,2},{3,11},{11,3},{4,12},{12,4},... | collective-permute-start | bytes 983048 | tf_op jit(solution)/shard_map/ppermute | solution.py:581
  54.3 12.5 %collective-permute-start.6 = (bf16[128,1280]{1,0:T(8,128)(2,1)S(1)}, bf16[128,1280]{1,0:T(8,128)(2,1)S(1)}, u32[]{:S(2)}, u32[]{:S(2)}) collective-permute-start(bf16[128,1280]{1,0:T(8,128)(2,1)S(1)} %collective-permute-done.2.t3), channel_id=1, source_target_pairs={{0,8},{8,0},{1,9},{9,1},{2,10},{10,2},{3,11},{11,3},{4,12},{12,4},... | collective-permute-start | bytes 983048 | tf_op jit(solution)/shard_map/ppermute | solution.py:581
  58.9 7.9 %collective-permute-start.5 = (bf16[128,1280]{1,0:T(8,128)(2,1)S(1)}, bf16[128,1280]{1,0:T(8,128)(2,1)}, u32[]{:S(2)}, u32[]{:S(2)}) collective-permute-start(bf16[128,1280]{1,0:T(8,128)(2,1)S(1)} %collective-permute-done.1.t2), channel_id=1, source_target_pairs={{0,8},{8,0},{1,9},{9,1},{2,10},{10,2},{3,11},{11,3},{4,12},{12,4},... | collective-permute-start | bytes 983048 | tf_op jit(solution)/shard_map/ppermute | solution.py:581
  64.1 2.7 %collective-permute-start.4 = (bf16[128,1280]{1,0:T(8,128)(2,1)S(1)}, bf16[128,1280]{1,0:T(8,128)(2,1)}, u32[]{:S(2)}, u32[]{:S(2)}) collective-permute-start(bf16[128,1280]{1,0:T(8,128)(2,1)S(1)} %collective-permute-done.t1), channel_id=1, source_target_pairs={{0,8},{8,0},{1,9},{9,1},{2,10},{10,2},{3,11},{11,3},{4,12},{12,4},... | collective-permute-start | bytes 983048 | tf_op jit(solution)/shard_map/ppermute | solution.py:581
  70.3 1.1 copy-start.1
  71.3 0.6 copy-start.4
  71.9 3.7 %collective-permute-start.7 = (bf16[16,32,640]{2,1,0:T(8,128)(2,1)S(1)}, bf16[16,32,640]{2,1,0:T(8,128)(2,1)S(1)}, u32[]{:S(2)}, u32[]{:S(2)}) collective-permute-start(bf16[16,32,640]{2,1,0:T(8,128)(2,1)S(1)} %get-tuple-element.45), channel_id=1, source_target_pairs={{0,8},{8,0},{1,9},{9,1},{2,10},{10,2},{3,11},{11,3},{4,12},{12,4},... | collective-permute-start | bytes 1966088 | tf_op jit(solution)/shard_map/ppermute | solution.py:581
  75.6 0.8 copy-start.6
  78.9 23.5 %all-to-all-start.3 = ((bf16[16,32,640]{2,1,0:T(8,128)(2,1)}), bf16[16,32,640]{2,1,0:T(8,128)(2,1)S(1)}, u32[]{:S(2)}, u32[]{:S(2)}) async-start(bf16[16,32,640]{2,1,0:T(8,128)(2,1)} %strip_add.1), calls=%async_computation.3 | async-start | bytes 1310720 | tf_op jit(solution)/shard_map/all_to_all | solution.py:577
  85.4 8.9 %collective-permute-start.8 = (f32[4,384]{1,0:T(4,128)S(1)}, f32[4,384]{1,0:T(4,128)S(1)}, u32[]{:S(2)}, u32[]{:S(2)}) collective-permute-start(f32[4,384]{1,0:T(4,128)S(1)} %get-tuple-element.47), channel_id=1, source_target_pairs={{0,1},{1,0},{2,3},{3,2},{4,5},{5,4},{6,7},{7,6},{8,9},{9,8},{10,11... | collective-permute-start | bytes 18440 | tf_op jit(solution)/shard_map/ppermute | solution.py:677
  88.0 8.4 %collective-permute-start.9 = (f32[4,384]{1,0:T(4,128)S(1)}, f32[4,384]{1,0:T(4,128)S(1)}, u32[]{:S(2)}, u32[]{:S(2)}) collective-permute-start(f32[4,384]{1,0:T(4,128)S(1)} %get-tuple-element.48), channel_id=1, source_target_pairs={{0,2},{1,3},{2,4},{3,5},{4,6},{5,7},{6,0},{7,1},{8,10},{9,11},{10,... | collective-permute-start | bytes 18440 | tf_op jit(solution)/shard_map/ppermute | solution.py:677
  88.3 9.4 %collective-permute-start.10 = (f32[4,384]{1,0:T(4,128)S(1)}, f32[4,384]{1,0:T(4,128)S(1)}, u32[]{:S(2)}, u32[]{:S(2)}) collective-permute-start(f32[4,384]{1,0:T(4,128)S(1)} %get-tuple-element.49), channel_id=1, source_target_pairs={{0,3},{1,2},{2,5},{3,4},{4,7},{5,6},{6,1},{7,0},{8,11},{9,10},{10,... | collective-permute-start | bytes 18440 | tf_op jit(solution)/shard_map/ppermute | solution.py:677
  89.1 8.6 %collective-permute-start.11 = (f32[4,384]{1,0:T(4,128)S(1)}, f32[4,384]{1,0:T(4,128)S(1)}, u32[]{:S(2)}, u32[]{:S(2)}) collective-permute-start(f32[4,384]{1,0:T(4,128)S(1)} %get-tuple-element.50), channel_id=1, source_target_pairs={{0,4},{1,5},{2,6},{3,7},{4,0},{5,1},{6,2},{7,3},{8,12},{9,13},{10,... | collective-permute-start | bytes 18440 | tf_op jit(solution)/shard_map/ppermute | solution.py:677
  92.0 6.4 %collective-permute-start.12 = (f32[4,384]{1,0:T(4,128)S(1)}, f32[4,384]{1,0:T(4,128)S(1)}, u32[]{:S(2)}, u32[]{:S(2)}) collective-permute-start(f32[4,384]{1,0:T(4,128)S(1)} %get-tuple-element.51), channel_id=1, source_target_pairs={{0,5},{1,4},{2,7},{3,6},{4,1},{5,0},{6,3},{7,2},{8,13},{9,12},{10,... | collective-permute-start | bytes 18440 | tf_op jit(solution)/shard_map/ppermute | solution.py:677
  94.3 17.2 %copy-start.7 = (f32[4,384]{1,0:T(4,128)}, f32[4,384]{1,0:T(4,128)S(1)}, u32[]{:S(2)}) copy-start(f32[4,384]{1,0:T(4,128)S(1)} %collective-permute-done.8.b1) | copy-start | bytes 18436
  94.3 4.2 %collective-permute-start.13 = (f32[4,384]{1,0:T(4,128)S(1)}, f32[4,384]{1,0:T(4,128)S(1)}, u32[]{:S(2)}, u32[]{:S(2)}) collective-permute-start(f32[4,384]{1,0:T(4,128)S(1)} %get-tuple-element.52), channel_id=1, source_target_pairs={{0,6},{1,7},{2,0},{3,1},{4,2},{5,3},{6,4},{7,5},{8,14},{9,15},{10,... | collective-permute-start | bytes 18440 | tf_op jit(solution)/shard_map/ppermute | solution.py:677
  96.4 15.1 %copy-start.8 = (f32[4,384]{1,0:T(4,128)}, f32[4,384]{1,0:T(4,128)S(1)}, u32[]{:S(2)}) copy-start(f32[4,384]{1,0:T(4,128)S(1)} %collective-permute-done.9.b2) | copy-start | bytes 18436
  96.4 5.2 %collective-permute-start.14 = (f32[4,384]{1,0:T(4,128)S(1)}, f32[4,384]{1,0:T(4,128)S(1)}, u32[]{:S(2)}, u32[]{:S(2)}) collective-permute-start(f32[4,384]{1,0:T(4,128)S(1)} %get-tuple-element.53), channel_id=1, source_target_pairs={{0,7},{1,6},{2,1},{3,0},{4,3},{5,2},{6,5},{7,4},{8,15},{9,14},{10,... | collective-permute-start | bytes 18440 | tf_op jit(solution)/shard_map/ppermute | solution.py:677
  97.7 13.8 %copy-start.9 = (f32[4,384]{1,0:T(4,128)}, f32[4,384]{1,0:T(4,128)S(1)}, u32[]{:S(2)}) copy-start(f32[4,384]{1,0:T(4,128)S(1)} %collective-permute-done.10.b3) | copy-start | bytes 18436
  97.7 13.8 %copy-start.10 = (f32[4,384]{1,0:T(4,128)}, f32[4,384]{1,0:T(4,128)S(1)}, u32[]{:S(2)}) copy-start(f32[4,384]{1,0:T(4,128)S(1)} %collective-permute-done.11.b4) | copy-start | bytes 18436
  98.5 13.0 %copy-start.11 = (f32[4,384]{1,0:T(4,128)}, f32[4,384]{1,0:T(4,128)S(1)}, u32[]{:S(2)}) copy-start(f32[4,384]{1,0:T(4,128)S(1)} %collective-permute-done.12.b5) | copy-start | bytes 18436
  98.5 13.0 %copy-start.12 = (f32[4,384]{1,0:T(4,128)}, f32[4,384]{1,0:T(4,128)S(1)}, u32[]{:S(2)}) copy-start(f32[4,384]{1,0:T(4,128)S(1)} %collective-permute-done.13.b6) | copy-start | bytes 18436
  101.6 9.9 %copy-start.13 = (f32[4,384]{1,0:T(4,128)}, f32[4,384]{1,0:T(4,128)S(1)}, u32[]{:S(2)}) copy-start(f32[4,384]{1,0:T(4,128)S(1)} %collective-permute-done.14.b7) | copy-start | bytes 18436
  102.4 0.8 copy-start.5
  105.2 20.2 %all-to-all-start.4 = ((bf16[16,24,640]{2,1,0:T(8,128)(2,1)}), bf16[16,24,640]{2,1,0:T(8,128)(2,1)S(1)}, u32[]{:S(2)}, u32[]{:S(2)}) async-start(bf16[16,24,640]{2,1,0:T(8,128)(2,1)} %get-tuple-element.55), calls=%async_computation.4 | async-start | bytes 983040 | tf_op jit(solution)/shard_map/all_to_all | solution.py:577
  111.5 17.6 %copy-start.14 = (f32[4,640]{1,0:T(4,128)S(1)}, f32[4,640]{1,0:T(4,128)}, u32[]{:S(2)}) copy-start(f32[4,640]{1,0:T(4,128)} %get-tuple-element.71) | copy-start | bytes 30724
  111.5 19.1 %copy-start.2 = (f32[4,640]{1,0:T(4,128)S(1)}, f32[4,640]{1,0:T(4,128)}, u32[]{:S(2)}) copy-start(f32[4,640]{1,0:T(4,128)} %get-tuple-element.69.after_hbm.mine_ref) | copy-start | bytes 30724
  111.5 19.1 %copy-start.3 = (bf16[4,1152]{1,0:T(4,128)(2,1)S(1)}, bf16[4,1152]{1,0:T(4,128)(2,1)}, u32[]{:S(2)}) copy-start(bf16[4,1152]{1,0:T(4,128)(2,1)} %text_ref.1) | copy-start | bytes 27652
  125.4 6.0 %collective-permute-start.16 = (bf16[384,640]{1,0:T(8,128)(2,1)S(1)}, bf16[384,640]{1,0:T(8,128)(2,1)S(1)}, u32[]{:S(2)}, u32[]{:S(2)}) collective-permute-start(bf16[384,640]{1,0:T(8,128)(2,1)S(1)} %bitcast.5), channel_id=1, source_target_pairs={{0,8},{8,0},{1,9},{9,1},{2,10},{10,2},{3,11},{11,3},{4,12},{12,4},... | collective-permute-start | bytes 1474568 | tf_op jit(solution)/shard_map/ppermute | solution.py:581
  129.1 1.5 %collective-permute-start.15 = (f32[4,640]{1,0:T(4,128)S(1)}, f32[4,640]{1,0:T(4,128)S(1)}, u32[]{:S(2)}, u32[]{:S(2)}) collective-permute-start(f32[4,640]{1,0:T(4,128)S(1)} %copy-done.14), channel_id=1, source_target_pairs={{0,8},{8,0},{1,9},{9,1},{2,10},{10,2},{3,11},{11,3},{4,12},{12,4},... | collective-permute-start | bytes 30728 | tf_op jit(solution)/shard_map/ppermute | solution.py:581

commit v3 on v2

--- a/solution.py
+++ b/solution.py
@@ -1,3 +1,5 @@
+import functools
+
 import jax
 import jax.numpy as jnp
 from jax import lax
@@ -11,7 +13,6 @@
 ALL = AXES
 GROUP = ("x", "y_hi")
 LINE = ("y_lo", "z")
-PLANE = ("y_lo", "z", "y_hi")
 MIB = 1024 * 1024
 BIG = 60
 IDS = 128
@@ -33,7 +34,7 @@
     return jax.ShapeDtypeStruct(dims, dtype)
 
 
-def call(body, outs, operands, name, micros, scratch=(), grant=40):
+def call(body, outs, operands, name, micros, scratch=(), grant=40, aliases=None):
     specs = tuple(spec for _, spec in outs)
     shapes = tuple(shape for shape, _ in outs)
     single = len(outs) == 1
@@ -47,6 +48,7 @@
         cost_estimate=pl.CostEstimate(
             flops=0, bytes_accessed=int(micros * 3e6), transcendentals=0
         ),
+        input_output_aliases=aliases or {},
         name=name,
     )(*[operand for operand, _ in operands])
 
@@ -250,7 +252,7 @@
 
 
 def backward_kernel(
-    b0, b1, b2, b3, b4, b5, b6, b7, normal_hbm, gain_hbm, head_gain_hbm,
+    pair, s0, s1, s2, s3, normal_hbm, gain_hbm, head_gain_hbm,
     filtered_hbm, mean_hbm, inverse_hbm, kernel_hbm, after_hbm,
     out_hbm,
     blocks_ref, normal_ref, gain_ref, head_gain_ref, filtered_ref, mean_ref, inverse_ref, kernel_ref,
@@ -259,8 +261,9 @@
 ):
     del after_hbm
     images, channels = even_ref.shape
-    blocks = (b0, b1, b2, b3, b4, b5, b6, b7)
-    share = channels // len(blocks)
+    blocks = (s0, s1, s2, s3)
+    share = channels // len(PEERS)
+    cells = pl.ds(pair * 2 * CELLS, 2 * CELLS)
     wide = channels // STEPS
 
     def block_at(step):
@@ -268,7 +271,7 @@
 
     def out_copy(step):
         at = block_at(step)
-        return pltpu.make_async_copy(out_ref.at[:, at], out_hbm.at[:, at], out_sems.at[step])
+        return pltpu.make_async_copy(out_ref.at[:, at], out_hbm.at[cells, at], out_sems.at[step])
 
     head_copies = [
         pltpu.make_async_copy(block, blocks_ref.at[index], block_sems.at[index])
@@ -278,12 +281,12 @@
         pltpu.make_async_copy(source, target, small_sems.at[index])
         for index, (source, target) in enumerate((
             (head_gain_hbm, head_gain_ref), (gain_hbm, gain_ref), (normal_hbm, normal_ref),
-            (mean_hbm, mean_ref), (inverse_hbm, inverse_ref),
+            (mean_hbm.at[cells, :], mean_ref), (inverse_hbm.at[cells, :], inverse_ref),
         ))
     ]
     filtered_copies = [
         pltpu.make_async_copy(
-            filtered_hbm.at[:, block_at(step)], filtered_ref.at[:, block_at(step)],
+            filtered_hbm.at[cells, block_at(step)], filtered_ref.at[:, block_at(step)],
             filtered_sems.at[step],
         )
         for step in range(STEPS)
@@ -298,10 +301,10 @@
     for copy in (*head_copies, *small_copies):
         copy.wait()
     x, y_hi = lax.axis_index("x"), lax.axis_index("y_hi")
-    for index, (step_x, step_y) in enumerate(PEERS):
+    for step_x, step_y in PEERS:
         owner = group_peer(x, y_hi, 4 - step_x, step_y)
         at = pl.ds(pl.multiple_of(owner * share, LANES), share)
-        tilt_ref[:, at] = blocks_ref[index] * head_gain_ref[:, at]
+        tilt_ref[:, at] = blocks_ref[step_x, step_y] * head_gain_ref[:, at]
     cotangent = tilt_ref[...]
     normal = normal_ref[:, :channels]
     level = jnp.sum(cotangent, axis=1, keepdims=True) * part
@@ -315,16 +318,16 @@
 
     for step in range(STEPS):
         filtered_copies[step].wait()
-        for image in range(images):
-            cells = pl.ds(image * CELLS, CELLS)
-            average = mean_ref[cells, :]
-
-            def lean_chunk(chunk, total):
+        for image in range(2):
+            spot = pl.ds(image * CELLS, CELLS)
+            average = mean_ref[spot, :]
+
+            def lean_chunk(chunk, total, spot=spot, average=average, image=image):
                 at = pl.ds(pl.multiple_of(chunk * LANES, LANES), LANES)
-                return total + (filtered_ref[cells, at] - average) * pull_ref[pl.ds(image, 1), at]
-
-            total = jnp.zeros((CELLS, LANES), F32) if step == 0 else lean_ref[cells, :]
-            lean_ref[cells, :] = lax.fori_loop(
+                return total + (filtered_ref[spot, at] - average) * pull_ref[pl.ds(2 * pair + image, 1), at]
+
+            total = jnp.zeros((CELLS, LANES), F32) if step == 0 else lean_ref[spot, :]
+            lean_ref[spot, :] = lax.fori_loop(
                 step * per_block, (step + 1) * per_block, lean_chunk, total, unroll=True
             )
     inverse = inverse_ref[...]
@@ -334,27 +337,27 @@
 
     def filter_chunk(chunk, carry):
         at = pl.ds(pl.multiple_of(chunk * LANES, LANES), LANES)
-        for first in range(0, images, 2):
-            fields = []
-            sums = []
-            for image in range(first, first + 2):
-                tilt = jnp.broadcast_to(tilt_ref[pl.ds(image, 1), at], (SIDE, LANES))
-                even = jnp.broadcast_to(even_ref[pl.ds(image, 1), at], (SIDE, LANES))
-                rows = []
-                for row in range(SIDE):
-                    cells = pl.ds(image * CELLS + row * SIDE, SIDE)
-                    rows.append(
-                        inverse_ref[cells, :] * tilt
-                        - lean_ref[cells, :] * (filtered_ref[cells, at] - mean_ref[cells, :])
-                    )
-                fields.append(rows)
-                sums.append([even] * SIDE)
-            filter_rows(fields, sums, kernel_ref, at, True)
-            for offset, total in enumerate(sums):
-                for pair in range(SIDE // 2):
-                    both = jnp.concatenate(total[2 * pair : 2 * pair + 2], axis=0)
-                    cells = pl.ds((first + offset) * CELLS + pair * 2 * SIDE, 2 * SIDE)
-                    out_ref[cells, at] = both.astype(jnp.bfloat16)
+        fields = []
+        sums = []
+        for image in range(2):
+            source = pl.ds(2 * pair + image, 1)
+            tilt = jnp.broadcast_to(tilt_ref[source, at], (SIDE, LANES))
+            even = jnp.broadcast_to(even_ref[source, at], (SIDE, LANES))
+            rows = []
+            for row in range(SIDE):
+                spot = pl.ds(image * CELLS + row * SIDE, SIDE)
+                rows.append(
+                    inverse_ref[spot, :] * tilt
+                    - lean_ref[spot, :] * (filtered_ref[spot, at] - mean_ref[spot, :])
+                )
+            fields.append(rows)
+            sums.append([even] * SIDE)
+        filter_rows(fields, sums, kernel_ref, at, True)
+        for image, total in enumerate(sums):
+            for half in range(SIDE // 2):
+                two = jnp.concatenate(total[2 * half : 2 * half + 2], axis=0)
+                spot = pl.ds(image * CELLS + half * 2 * SIDE, 2 * SIDE)
+                out_ref[spot, at] = two.astype(jnp.bfloat16)
         step = chunk // per_block
 
         @pl.when(chunk == step * per_block + per_block - 1)
@@ -368,34 +371,44 @@
         out_copy(step).wait()
 
 
-def block_backward(blocks, normal, norm_gain, head_gain, filtered, mean, inverse, kernel, after):
+def first_backward(pair, *refs):
+    backward_kernel(pair, *refs)
+
+
+def second_backward(pair, *refs):
+    backward_kernel(pair, *refs[:12], *refs[13:])
+
+
+def block_backward(pair, blocks, normal, norm_gain, head_gain, filtered, mean, inverse, kernel, after, held=None):
     cells, channels = filtered.shape
     images = cells // CELLS
+    some = 2 * CELLS
     dma = pltpu.SemaphoreType.DMA
-    out = call(
-        backward_kernel,
+    operands = [
+        *blocks, normal, norm_gain.reshape(1, channels), head_gain.reshape(1, channels),
+        filtered, mean, inverse, kernel, after,
+    ]
+    body = first_backward if held is None else second_backward
+    if held is not None:
+        operands.append(held)
+    return call(
+        functools.partial(body, pair),
         ((shape_of((cells, channels), BF16), HBM),),
-        tuple(
-            (array, HBM)
-            for array in (
-                *blocks, normal, norm_gain.reshape(1, channels), head_gain.reshape(1, channels),
-                filtered, mean, inverse, kernel, after,
-            )
-        ),
+        tuple((array, HBM) for array in operands),
         "block_backward",
-        14,
+        8,
         scratch=(
             pltpu.VMEM((len(blocks),) + blocks[0].shape, F32),
             pltpu.VMEM(normal.shape, F32),
             pltpu.VMEM((1, channels), F32),
             pltpu.VMEM((1, channels), F32),
-            pltpu.VMEM((cells, channels), F32),
-            pltpu.VMEM((cells, LANES), F32),
-            pltpu.VMEM((cells, LANES), F32),
+            pltpu.VMEM((some, channels), F32),
+            pltpu.VMEM((some, LANES), F32),
+            pltpu.VMEM((some, LANES), F32),
             pltpu.VMEM(kernel.shape, F32),
-            pltpu.VMEM((cells, channels), BF16),
+            pltpu.VMEM((some, channels), BF16),
             pltpu.VMEM((images, channels), F32),
-            pltpu.VMEM((cells, LANES), F32),
+            pltpu.VMEM((some, LANES), F32),
             pltpu.VMEM((images, channels), F32),
             pltpu.VMEM((images, channels), F32),
             dma((len(blocks),)),
@@ -404,8 +417,8 @@
             dma((STEPS,)),
         ),
         grant=BIG,
-    )
-    return out.reshape(images, SIDE, SIDE, channels)
+        aliases={} if held is None else {len(operands) - 1: 0},
+    )
 
 
 def dot(left, right, left_dim, right_dim):
@@ -449,17 +462,19 @@
         out_ref[target, :, width:] = hot
 
 
-def line_kernel(plane_ref, after_ref, out_ref):
+def line_kernel(line_ref, out_ref):
+    line, rows, _ = line_ref.shape
+    for first in range(0, line, 4):
+        four = [line_ref[first + offset].astype(F32) for offset in range(4)]
+        at = slice(first * rows, (first + 4) * rows)
+        out_ref[at, :] = jnp.concatenate(four, axis=0).astype(BF16)
+
+
+def join_texts_kernel(own_ref, next_ref, after_ref, out_ref):
     del after_ref
-    plane, rows, _ = plane_ref.shape
-    line = plane // 2
-    y_hi = lax.axis_index("y_hi")
-    for side in range(2):
-        part = lax.rem(y_hi + side, 2)
-        for first in range(0, line, 4):
-            four = [plane_ref[(first + offset) * 2 + part].astype(F32) for offset in range(4)]
-            at = (side * line + first) * rows
-            out_ref[at : at + 4 * rows, :] = jnp.concatenate(four, axis=0).astype(BF16)
+    texts = own_ref.shape[0]
+    out_ref[:texts, :] = own_ref[...]
+    out_ref[texts:, :] = next_ref[...]
 
 
 def partial_kernel(received_ref, projection_ref, out_ref, columns_ref, hot_ref):
@@ -475,21 +490,21 @@
 
 
 def pair_kernel(
-    partials_ref, columns_ref, hot_ref, projection_ref, t0, t1, t2, t3, t4, t5, t6, t7,
+    partials_ref, hot_ref, projection_ref, t0, t1, t2, t3, t4, t5, t6, t7,
     scale_ref, shift_ref,
-    h0, h1, h2, h3, h4, h5, h6, h7, keep_ref, give_ref,
-    low_ref, embed_ref, rows_ref, near_ref, far_ref, head_ref,
+    stay_ref, send_ref, factors_ref,
+    head_ref,
 ):
     group, images, width = partials_ref.shape
     blocks = (t0, t1, t2, t3, t4, t5, t6, t7)
-    scale, shift, core = scale_ref[0], shift_ref[0], lax.axis_index("core")
+    scale, shift = scale_ref[0], shift_ref[0]
     embedded = partials_ref[0].astype(F32)
     for owner in range(1, group):
         embedded += partials_ref[owner].astype(F32)
     inverse = inverse_length(embedded)
     unit = embedded * inverse
     low = unit.astype(BF16)
-    low_ref[...] = low
+    factors_ref[:, width : 2 * width] = low
     hot = hot_ref[...]
     weights = []
     for block in blocks:
@@ -500,39 +515,51 @@
     for weight, block in zip(weights[1:], blocks[1:]):
         image_grad += dot(weight, block[:, :width], 1, 0)
     embed = length_back(unit, inverse, scale * image_grad).astype(BF16)
-    embed_ref[...] = embed
+    factors_ref[:, :width] = embed
+    factors_ref[:, 2 * width : 2 * width + LANES] = weights[0]
+    factors_ref[:, 2 * width + LANES :] = weights[4]
     head = dot(embed, projection_ref[...], 1, 1)
     rows = images // group
     for owner in range(group):
         head_ref[owner] = head[owner * rows : (owner + 1) * rows]
     x, y_hi = lax.axis_index("x"), lax.axis_index("y_hi")
-    for (step_x, step_y), out_ref in zip(PEERS, (h0, h1, h2, h3, h4, h5, h6, h7)):
-        out_ref[...] = head_ref[group_peer(x, y_hi, step_x, step_y)]
-    columns = columns_ref[...]
-    line = keep_ref.shape[0]
-    own = weights[0][:, : line * rows]
-    other = weights[4][:, : line * rows]
-    strip = columns.shape[1] // line
-    for out_ref, side, first, second in (
-        (give_ref, 1 - core, other, own),
-        (keep_ref, core, own, other),
-    ):
-        at = pl.ds(pl.multiple_of(side * (width - HALF), LANES), HALF)
-        rows_ref[...] = dot(columns, embed_ref[:, at], 0, 0)
-        low_half = low_ref[:, at]
-        near_ref[...] = dot(first, low_half, 0, 0)
-        far_ref[...] = dot(second, low_half, 0, 0)
-        for target in range(line):
-            texts = slice(target * rows, (target + 1) * rows)
-            stacked = jnp.concatenate(
-                [rows_ref[target * strip : (target + 1) * strip], near_ref[texts], far_ref[texts]],
-                axis=0,
-            )
-            out_ref[target] = stacked.astype(out_ref.dtype)
-
-
-def add_kernel(keep_ref, got_ref, out_ref):
-    out_ref[...] = (keep_ref[...] + got_ref[...].astype(F32)).astype(BF16)
+    for step in range(4):
+        stay_ref[step] = head_ref[group_peer(x, y_hi, step, 0)]
+        send_ref[step] = head_ref[group_peer(x, y_hi, step, 1)]
+
+
+def merge_kernel(stay_ref, got_ref, s0, s1, s2, s3):
+    for step, out_ref in enumerate((s0, s1, s2, s3)):
+        out_ref[0] = stay_ref[step]
+        out_ref[1] = got_ref[step]
+
+
+def strip_make_kernel(mine_ref, theirs_ref, columns_ref, far_columns_ref, out_ref, rows_ref, near_ref, far_ref):
+    width = (mine_ref.shape[1] - 2 * LANES) // 2
+    line, strip_rows, half = out_ref.shape
+    strip = columns_ref.shape[1] // line
+    rows = (strip_rows - strip) // 2
+    texts = line * rows
+    start = pl.multiple_of(lax.axis_index("core") * (width - half), LANES)
+
+    def both(at):
+        return jnp.concatenate([mine_ref[:, at], theirs_ref[:, at]], axis=0)
+
+    columns = jnp.concatenate([columns_ref[...], far_columns_ref[...]], axis=0)
+    rows_ref[...] = dot(columns, both(pl.ds(start, half)), 0, 0)
+    low = both(pl.ds(pl.multiple_of(start + width, LANES), half))
+    first = slice(2 * width, 2 * width + texts)
+    second = slice(2 * width + LANES, 2 * width + LANES + texts)
+    own = jnp.concatenate([mine_ref[:, first], theirs_ref[:, second]], axis=0)
+    other = jnp.concatenate([mine_ref[:, second], theirs_ref[:, first]], axis=0)
+    near_ref[...] = dot(own, low, 0, 0)
+    far_ref[...] = dot(other, low, 0, 0)
+    for target in range(line):
+        at = slice(target * rows, (target + 1) * rows)
+        stacked = jnp.concatenate(
+            [rows_ref[target * strip : (target + 1) * strip], near_ref[at], far_ref[at]], axis=0
+        )
+        out_ref[target] = stacked.astype(BF16)
 
 
 def strip_kernel(strips_ref, out_ref, mine_ref, theirs_ref):
@@ -608,7 +635,7 @@
 
     packed = call(
         pack_kernel,
-        ((shape_of((2 * line, rows, width + IDS), BF16), VMEM),),
+        ((shape_of((line, rows, width + IDS), BF16), VMEM),),
         ((text_embed, HBM), (txt_ids, HBM)),
         "text_pack", 1,
         scratch=(
@@ -616,7 +643,7 @@
         ),
         grant=BIG,
     )
-    gathered = exchange(packed, PLANE)
+    gathered = exchange(packed, LINE)
     filtered, mean, inverse, normal, send = block_forward(
         features, kernel, norm_gain, head_gain, img_ids, group
     )
@@ -632,50 +659,59 @@
         ((received, VMEM), (projection, VMEM)),
         "partial_embed", 2,
     )
+    own_line = call(
+        line_kernel, ((shape_of((texts, width + IDS), BF16), VMEM),), ((gathered, VMEM),),
+        "line_rows", 1,
+    )
+    next_line = lax.ppermute(own_line, "y_hi", ((0, 1), (1, 0)))
     near = [
         call(
-            line_kernel,
+            join_texts_kernel,
             ((shape_of((2 * texts, width + IDS), BF16), VMEM),),
-            ((gathered, VMEM), (columns, VMEM)),
-            "line_rows", 1,
+            ((own_line, VMEM), (next_line, VMEM), (columns, VMEM)),
+            "join_texts", 1,
         )
     ]
     near += [along_x(near[0], step) for step in (1, 3, 2)]
     far = [swap_core(block) for block in near]
+    far_columns = swap_core(columns)
     partials = exchange(partials, GROUP)
-    results = call(
+    stay, away, factors = call(
         pair_kernel,
-        ((shape_of((rows, share), F32), VMEM),) * group
-        + (
-            (shape_of((line, strip + 2 * rows, HALF), F32), VMEM),
-            (shape_of((line, strip + 2 * rows, HALF), BF16), VMEM),
-        ),
-        tuple((array, VMEM) for array in (partials, columns, hot, projection, *near, *far))
+        (
+            (shape_of((4, rows, share), F32), VMEM),
+            (shape_of((4, rows, share), F32), VMEM),
+            (shape_of((images, 2 * width + 2 * LANES), BF16), VMEM),
+        ),
+        tuple((array, VMEM) for array in (partials, hot, projection, *near, *far))
         + ((logit_scale, SMEM), (logit_bias, SMEM)),
-        "pairs", 6,
+        "pairs", 4,
+        scratch=(pltpu.VMEM((group, rows, share), F32),),
+    )
+    far_factors = swap_core(factors)
+    got = lax.ppermute(away, "y_hi", ((0, 1), (1, 0)))
+    strips = call(
+        strip_make_kernel,
+        ((shape_of((line, strip + 2 * rows, HALF), BF16), VMEM),),
+        tuple((array, VMEM) for array in (factors, far_factors, columns, far_columns)),
+        "strip_make", 2,
         scratch=(
-            pltpu.VMEM((images, width), BF16),
-            pltpu.VMEM((images, width), BF16),
             pltpu.VMEM((share, HALF), F32),
             pltpu.VMEM((texts, HALF), F32),
             pltpu.VMEM((texts, HALF), F32),
-            pltpu.VMEM((group, rows, share), F32),
-        ),
-    )
-    head_parts, (keep, give) = results[:group], results[group:]
-    strips = call(
-        add_kernel, ((shape_of(keep.shape, BF16), VMEM),), ((keep, VMEM), (swap_core(give), VMEM)),
-        "strip_add", 1,
-        grant=BIG,
+        ),
     )
     strips = exchange(strips, LINE)
-    head_blocks = [head_parts[0]]
-    for (step_x, step_y), part in zip(PEERS[1:], head_parts[1:]):
-        pairs = tuple(
-            (at, (at // 2 + step_x) % 4 * 2 + (at % 2 + step_y) % 2) for at in range(group)
-        )
-        head_blocks.append(lax.ppermute(part, GROUP, pairs))
-    strips, *head_blocks = lax.optimization_barrier((strips, *head_blocks))
+    merged = call(
+        merge_kernel,
+        ((shape_of((2, rows, share), F32), VMEM),) * 4,
+        ((stay, VMEM), (got, VMEM)),
+        "head_merge", 1,
+    )
+    blocks = [merged[0]] + [along_x(merged[step], step) for step in (1, 2, 3)]
+    shared = (normal, norm_gain, head_gain, filtered, mean, inverse, kernel)
+    held = block_backward(0, blocks, *shared, mean)
+    strips, held = lax.optimization_barrier((strips, held))
     sums, mine, theirs = call(
         strip_kernel,
         (
@@ -685,25 +721,25 @@
         ),
         ((strips, VMEM),),
         "strip_sum", 1,
-        grant=BIG,
     )
     near_half = exchange(sums, LINE).reshape(share, HALF)
-    grad_features = block_backward(
-        head_blocks, normal, norm_gain, head_gain, filtered, mean, inverse, kernel, mine
-    )
-    near_half, theirs, grad_features = lax.optimization_barrier((near_half, theirs, grad_features))
     grad_text = call(
         text_kernel,
         ((shape_of((rows, width), F32), VMEM),),
         ((text_embed, VMEM), (mine, VMEM), (swap_core(theirs), VMEM), (logit_scale, SMEM)),
         "text_grad", 1,
     )
+    grad_features = block_backward(1, blocks, *shared, mine, held)
+    near_half, grad_features, grad_text = lax.optimization_barrier(
+        (near_half, grad_features, grad_text)
+    )
     grad_proj = call(
         join_kernel,
         ((shape_of((share, width), F32), VMEM),),
         ((near_half, VMEM), (swap_core(near_half), VMEM)),
         "proj_join", 2,
     )
+    grad_features = grad_features.reshape(features.shape)
     return (grad_features, grad_text, grad_proj)
 
 

time: 133 us -> 127 us (0.955)
  blocking collectives: 13 us -> 10.7 us
  waiting for transfers between devices: 8.74 us -> 7.02 us
  local copies, waits for them, and re-layouts: 3.37 us -> 1.8 us
    ppermute x7 -> x2, starting transfers between devices: 12.3 us -> 5.3 us  [the longest x1 2.71 us: local(): next_line = lax.ppermute(own_line, 'y_hi', ((0, 1), (1, 0)))]
    ppermute x3 -> x6, starting transfers between devices: 2.76 us -> 6.27 us  [along_x(): lax.ppermute(block, 'x', tuple(((i, (i + step) % 4) for i in range(4))))]
    ppermute x7 -> x8, starting transfers between devices: 19.6 us -> 23.1 us  [swap_core(): return lax.ppermute(block, 'core', ((0, 1), (1, 0)))]
    all_to_all x1, blocking collectives: 13 us -> 10.7 us  [exchange(): return lax.all_to_all(blocks, axes, 0, 0, tiled=True)]
    ppermute x7 -> x2, waiting for transfers between devices: 3.85 us -> 1.68 us  [the longest x1 1.68 us: local(): got = lax.ppermute(away, 'y_hi', ((0, 1), (1, 0)))]
    ppermute x3 -> x6, waiting for transfers between devices: 0.3 us -> 2.06 us  [along_x(): lax.ppermute(block, 'x', tuple(((i, (i + step) % 4) for i in range(4))))]
    unnamed x30 -> x16, local copies, waits for them, and re-layouts: 3.37 us -> 1.8 us
    pallas_call x10 -> x13, Pallas kernels: 41.6 us -> 40.3 us  [call(): pl.pallas_call(body, out_shape=shapes[0] if single else shapes, in_specs=...]
  transfers between devices with their start and end apart: 21 -> 20, of which waited for: 7 -> 8; matrix products, arithmetic and copies ran while one was open for 0% -> 0% of each run, Pallas kernels for 22% -> 25%
where the time goes in v3:
time: 127 us
  starting transfers between devices  64.9 us (51%)
  Pallas kernels  40.3 us (32%)
  blocking collectives  10.7 us (8%)
  waiting for transfers between devices  7.02 us (6%)
  between operations  2.09 us (2%)
  local copies, waits for them, and re-layouts  1.8 us (1%)
    pallas_call x13, Pallas kernels, call(): pl.pallas_call(body, out_shape=shapes[0] if single else shapes, in_specs=...  40.3 us
    all_to_all x4, starting transfers between devices, exchange(): return lax.all_to_all(blocks, axes, 0, 0, tiled=True)  30.2 us
    ppermute x8, starting transfers between devices, swap_core(): return lax.ppermute(block, 'core', ((0, 1), (1, 0)))  23.1 us
    all_to_all x1, blocking collectives, exchange(): return lax.all_to_all(blocks, axes, 0, 0, tiled=True)  10.7 us
    ppermute x6, starting transfers between devices, along_x(): lax.ppermute(block, 'x', tuple(((i, (i + step) % 4) for i in range(4))))  6.27 us
    ppermute x1, starting transfers between devices, local(): next_line = lax.ppermute(own_line, 'y_hi', ((0, 1), (1, 0)))  2.71 us
    ppermute x8, waiting for transfers between devices, swap_core(): return lax.ppermute(block, 'core', ((0, 1), (1, 0)))  2.6 us
    ppermute x1, starting transfers between devices, local(): got = lax.ppermute(away, 'y_hi', ((0, 1), (1, 0)))  2.59 us
  transfers between devices with their start and end apart: 20, of which 8 were waited for; matrix products, arithmetic and copies ran while one was open for 0% of the time, Pallas kernels for 25%

profile of v3, /device:TPU:1, one launch (start us, length us, event | category | flops | bytes accessed | tf_op | source)
XLA Modules:
  0.0 126.7 jit_solution(10460488142974088021)
XLA Ops:
  0.6 0.0 copy-start
  0.6 1.6 %text_pack.1 = bf16[16,4,1280]{2,1,0:T(4,128)(2,1)} custom-call(bf16[4,1152]{1,0:T(4,128)(2,1)} %text_ref.1, s32[4]{0:T(128)} %ids_hbm.2), custom_call_target="tpu_custom_call" | custom-call | bytes 3000000 | tf_op jit(solution)/shard_map/text_pack/pallas_call | solution.py:41
  2.2 10.1 %all-to-all-start = ((bf16[16,4,1280]{2,1,0:T(4,128)(2,1)}), bf16[16,4,1280]{2,1,0:T(4,128)(2,1)S(1)}, u32[]{:S(2)}, u32[]{:S(2)}) async-start(bf16[16,4,1280]{2,1,0:T(4,128)(2,1)} %text_pack.1), calls=%async_computation | async-start | bytes 327680 | tf_op jit(solution)/shard_map/all_to_all | solution.py:604
  12.4 14.9 %block_forward.1 = (f32[256,3072]{1,0:T(8,128)}, f32[256,128]{1,0:T(8,128)}, f32[256,128]{1,0:T(8,128)}, f32[4,3200]{1,0:T(4,128)}, bf16[8,4,512]{2,1,0:T(4,128)(2,1)}) custom-call(bf16[256,3072]{1,0:T(8,128)(2,1)} %bitcast.8, f32[7,7,3072]{2,1,0:T(8,128)} %refs_10_.3, f32[1,3072]{1,0:T(1,128)} %bitcast.9, f32[1,3072]{1,0:T(1,128)} %bitcast.12, s32[4]{0:T(128)} %ids_hbm.3), custom_call_target="tpu_custom_call" | custom-call | bytes 42000000 | tf_op jit(solution)/shard_map/block_forward/pallas_call | solution.py:41
  27.3 0.0 all-to-all-done.line_ref
  27.4 2.7 %collective-permute-start = (bf16[64,1280]{1,0:T(8,128)(2,1)S(1)}, bf16[64,1280]{1,0:T(8,128)(2,1)S(1)}, u32[]{:S(2)}, u32[]{:S(2)}) collective-permute-start(bf16[64,1280]{1,0:T(8,128)(2,1)S(1)} %line_rows.1.own_ref), channel_id=1, source_target_pairs={{0,1},{1,0},{2,3},{3,2},{4,5},{5,4},{6,7},{7,6},{8,9},{9,8},{10,11... | collective-permute-start | bytes 491528 | tf_op jit(solution)/shard_map/ppermute | solution.py:666
  30.1 10.7 %all_to_all.25.received_ref = bf16[8,4,512]{2,1,0:T(4,128)(2,1)S(1)} all-to-all(bf16[8,4,512]{2,1,0:T(4,128)(2,1)} %get-tuple-element.29), channel_id=1, replica_groups=mesh['y_lo'=2,'z'=8,'core'=2,'x'=4,'y_hi'=2] {'x','y_hi'}, dimensions={0} | all-to-all | bytes 65536 | tf_op jit(solution)/shard_map/all_to_all | solution.py:604
  40.8 0.0 copy-done
  40.8 1.1 partial_embed.1
  41.9 0.0 collective-permute-done.next_ref
  41.9 1.1 collective-permute-start.3
  43.0 1.7 %collective-permute-start.2 = (bf16[128,1280]{1,0:T(8,128)(2,1)S(1)}, bf16[128,1280]{1,0:T(8,128)(2,1)S(1)}, u32[]{:S(2)}, u32[]{:S(2)}) collective-permute-start(bf16[128,1280]{1,0:T(8,128)(2,1)S(1)} %join_texts.1.t0), channel_id=1, source_target_pairs={{0,6},{2,0},{4,2},{6,4},{1,7},{3,1},{5,3},{7,5},{8,14},{10,8},{12,... | collective-permute-start | bytes 983048 | tf_op jit(solution)/shard_map/ppermute | solution.py:612
  44.6 0.0 collective-permute-start.1
  44.6 4.2 %all-to-all-start.2 = ((bf16[8,32,1152]{2,1,0:T(8,128)(2,1)}), bf16[8,32,1152]{2,1,0:T(8,128)(2,1)S(1)}, u32[]{:S(2)}, u32[]{:S(2)}) async-start(bf16[8,32,1152]{2,1,0:T(8,128)(2,1)} %get-tuple-element.30), calls=%async_computation.2 | async-start | bytes 1179648 | tf_op jit(solution)/shard_map/all_to_all | solution.py:604
  48.8 3.7 %collective-permute-start.4 = (bf16[128,1280]{1,0:T(8,128)(2,1)S(1)}, bf16[128,1280]{1,0:T(8,128)(2,1)S(1)}, u32[]{:S(2)}, u32[]{:S(2)}) collective-permute-start(bf16[128,1280]{1,0:T(8,128)(2,1)S(1)} %join_texts.1.t0), channel_id=1, source_target_pairs={{0,8},{8,0},{1,9},{9,1},{2,10},{10,2},{3,11},{11,3},{4,12},{12,4},... | collective-permute-start | bytes 983048 | tf_op jit(solution)/shard_map/ppermute | solution.py:608
  52.5 0.0 collective-permute-done.3.t3
  52.5 4.3 %collective-permute-start.7 = (bf16[128,1280]{1,0:T(8,128)(2,1)S(1)}, bf16[128,1280]{1,0:T(8,128)(2,1)S(1)}, u32[]{:S(2)}, u32[]{:S(2)}) collective-permute-start(bf16[128,1280]{1,0:T(8,128)(2,1)S(1)} %collective-permute-done.3.t3), channel_id=1, source_target_pairs={{0,8},{8,0},{1,9},{9,1},{2,10},{10,2},{3,11},{11,3},{4,12},{12,4},... | collective-permute-start | bytes 983048 | tf_op jit(solution)/shard_map/ppermute | solution.py:608
  56.8 0.3 collective-permute-done.2.t2
  57.1 5.2 %collective-permute-start.6 = (bf16[128,1280]{1,0:T(8,128)(2,1)S(1)}, bf16[128,1280]{1,0:T(8,128)(2,1)}, u32[]{:S(2)}, u32[]{:S(2)}) collective-permute-start(bf16[128,1280]{1,0:T(8,128)(2,1)S(1)} %collective-permute-done.2.t2), channel_id=1, source_target_pairs={{0,8},{8,0},{1,9},{9,1},{2,10},{10,2},{3,11},{11,3},{4,12},{12,4},... | collective-permute-start | bytes 983048 | tf_op jit(solution)/shard_map/ppermute | solution.py:608
  62.3 0.0 collective-permute-done.1.t1
  62.3 0.7 collective-permute-start.5
  64.3 0.0 collective-permute-done.4.t4
  64.3 0.7 all-to-all-done.2.partials_ref
  65.0 0.0 collective-permute-done.7.t7
  65.0 0.0 collective-permute-done.6.t6
  65.0 0.0 collective-permute-done.5.t5
  65.0 3.0 %pairs.1 = (f32[4,4,384]{2,1,0:T(4,128)S(1)}, f32[4,4,384]{2,1,0:T(4,128)S(1)}, bf16[32,2560]{1,0:T(8,128)(2,1)S(1)}) custom-call(bf16[8,32,1152]{2,1,0:T(8,128)(2,1)S(1)} %all-to-all-done.2.partials_ref, bf16[32,128]{1,0:T(8,128)(2,1)S(1)} %get-tuple-element.31.hot_ref, bf16[384,1152]{1,0:T(8,128)(2,1)S(1)} %copy-done, bf16[128,1280]{1,0:T(8,128)(2,1)S(1)} %join_texts.1.t0, ...), custom_call_target="tpu_custom_call" | custom-call | bytes 12000000 | tf_op jit(solution)/shard_map/pairs/pallas_call | solution.py:41
  68.0 2.0 %collective-permute-start.8 = (bf16[32,2560]{1,0:T(8,128)(2,1)S(1)}, bf16[32,2560]{1,0:T(8,128)(2,1)S(1)}, u32[]{:S(2)}, u32[]{:S(2)}) collective-permute-start(bf16[32,2560]{1,0:T(8,128)(2,1)S(1)} %get-tuple-element.34.mine_ref), channel_id=1, source_target_pairs={{0,8},{8,0},{1,9},{9,1},{2,10},{10,2},{3,11},{11,3},{4,12},{12,4},... | collective-permute-start | bytes 491528 | tf_op jit(solution)/shard_map/ppermute | solution.py:608
  70.0 0.1 collective-permute-start.9
  70.1 1.1 collective-permute-done.9.far_columns_ref
  71.2 0.0 collective-permute-done.8.theirs_ref
  71.2 1.2 strip_make.1
  72.5 7.6 %all-to-all-start.3 = ((bf16[16,32,640]{2,1,0:T(8,128)(2,1)}), bf16[16,32,640]{2,1,0:T(8,128)(2,1)S(1)}, u32[]{:S(2)}, u32[]{:S(2)}) async-start(bf16[16,32,640]{2,1,0:T(8,128)(2,1)} %strip_make.1), calls=%async_computation.3 | async-start | bytes 1310720 | tf_op jit(solution)/shard_map/all_to_all | solution.py:604
  80.0 2.6 %collective-permute-start.10 = (f32[4,4,384]{2,1,0:T(4,128)S(1)}, f32[4,4,384]{2,1,0:T(4,128)S(1)}, u32[]{:S(2)}, u32[]{:S(2)}) collective-permute-start(f32[4,4,384]{2,1,0:T(4,128)S(1)} %get-tuple-element.36), channel_id=1, source_target_pairs={{0,1},{1,0},{2,3},{3,2},{4,5},{5,4},{6,7},{7,6},{8,9},{9,8},{10,11... | collective-permute-start | bytes 73736 | tf_op jit(solution)/shard_map/ppermute | solution.py:692
  82.6 1.7 %collective-permute-done.10.got_ref = f32[4,4,384]{2,1,0:T(4,128)S(1)} collective-permute-done((f32[4,4,384]{2,1,0:T(4,128)S(1)}, f32[4,4,384]{2,1,0:T(4,128)S(1)}, u32[]{:S(2)}, u32[]{:S(2)}) %collective-permute-start.10) | collective-permute-done | bytes 24608 | tf_op jit(solution)/shard_map/ppermute | solution.py:692
  84.3 0.0 copy-start.1
  84.3 0.6 copy-done.1
  84.9 0.4 collective-permute-start.11
  85.3 2.0 %collective-permute-start.12 = (f32[2,4,384]{2,1,0:T(4,128)S(1)}, f32[2,4,384]{2,1,0:T(4,128)S(1)}, u32[]{:S(2)}, u32[]{:S(2)}) collective-permute-start(f32[2,4,384]{2,1,0:T(4,128)S(1)} %get-tuple-element.39), channel_id=1, source_target_pairs={{0,4},{2,6},{4,0},{6,2},{1,5},{3,7},{5,1},{7,3},{8,12},{10,14},{12... | collective-permute-start | bytes 36872 | tf_op jit(solution)/shard_map/ppermute | solution.py:612
  87.3 1.1 collective-permute-start.13
  88.4 0.5 collective-permute-done.11.refs_1_
  88.9 0.0 copy-start.5
  89.0 0.7 collective-permute-done.12.refs_2_
  89.7 0.0 copy-start.6
  89.7 0.5 collective-permute-done.13.refs_3_
  90.2 0.0 copy-start.7
  90.2 0.0 copy-done.5
  90.2 0.1 copy-done.6
  90.3 0.5 copy-done.7
  90.8 7.7 %block_backward.2.refs_12_ = bf16[256,3072]{1,0:T(8,128)(2,1)} custom-call(f32[2,4,384]{2,1,0:T(4,128)} %copy-done.1, f32[2,4,384]{2,1,0:T(4,128)} %copy-done.5, f32[2,4,384]{2,1,0:T(4,128)} %copy-done.6, f32[2,4,384]{2,1,0:T(4,128)} %copy-done.7, f32[4,3200]{1,0:T(4,128)} %get-tuple-element.41.refs_4_, f32[1,3072]{1,0:T(1,128)} %bitcast.10, ...), custom_call_target="tpu_custom_call" | custom-call | bytes 24000000 | tf_op jit(solution)/shard_map/block_backward/pallas_call | solution.py:41
  98.4 0.0 all-to-all-done.3.strips_ref
  98.5 0.9 strip_sum.1
  99.3 0.6 copy-done.2
  99.9 8.3 %all-to-all-start.4 = ((bf16[16,24,640]{2,1,0:T(8,128)(2,1)}), bf16[16,24,640]{2,1,0:T(8,128)(2,1)S(1)}, u32[]{:S(2)}, u32[]{:S(2)}) async-start(bf16[16,24,640]{2,1,0:T(8,128)(2,1)} %get-tuple-element.46), calls=%async_computation.4 | async-start | bytes 983040 | tf_op jit(solution)/shard_map/all_to_all | solution.py:604
  108.3 2.8 %collective-permute-start.14 = (f32[4,640]{1,0:T(4,128)S(1)}, f32[4,640]{1,0:T(4,128)S(1)}, u32[]{:S(2)}, u32[]{:S(2)}) collective-permute-start(f32[4,640]{1,0:T(4,128)S(1)} %get-tuple-element.49), channel_id=1, source_target_pairs={{0,8},{8,0},{1,9},{9,1},{2,10},{10,2},{3,11},{11,3},{4,12},{12,4},... | collective-permute-start | bytes 30728 | tf_op jit(solution)/shard_map/ppermute | solution.py:608
  111.0 7.7 %block_backward.3 = bf16[256,3072]{1,0:T(8,128)(2,1)} custom-call(f32[2,4,384]{2,1,0:T(4,128)} %copy-done.1, f32[2,4,384]{2,1,0:T(4,128)} %copy-done.5, f32[2,4,384]{2,1,0:T(4,128)} %copy-done.6, f32[2,4,384]{2,1,0:T(4,128)} %copy-done.7, f32[4,3200]{1,0:T(4,128)} %get-tuple-element.41.refs_4_, f32[1,3072]{1,0:T(1,128)} %bitcast.11, ...), custom_call_target="tpu_custom_call", output_to_operand_aliasing={{}: (12, {})} | custom-call | bytes 24000000 | tf_op jit(solution)/shard_map/block_backward/pallas_call | solution.py:41
  118.8 0.0 collective-permute-done.14.got_ref
  118.8 0.0 copy-done.3
  118.8 0.0 copy-done.4
  118.8 0.8 text_grad.1
  119.6 0.0 all-to-all-done.4
  119.6 4.3 %collective-permute-start.15 = (bf16[384,640]{1,0:T(8,128)(2,1)S(1)}, bf16[384,640]{1,0:T(8,128)(2,1)S(1)}, u32[]{:S(2)}, u32[]{:S(2)}) collective-permute-start(bf16[384,640]{1,0:T(8,128)(2,1)S(1)} %bitcast.5), channel_id=1, source_target_pairs={{0,8},{8,0},{1,9},{9,1},{2,10},{10,2},{3,11},{11,3},{4,12},{12,4},... | collective-permute-start | bytes 1474568 | tf_op jit(solution)/shard_map/ppermute | solution.py:608
  123.9 1.5 %collective-permute-done.15.far_ref = bf16[384,640]{1,0:T(8,128)(2,1)S(1)} collective-permute-done((bf16[384,640]{1,0:T(8,128)(2,1)S(1)}, bf16[384,640]{1,0:T(8,128)(2,1)S(1)}, u32[]{:S(2)}, u32[]{:S(2)}) %collective-permute-start.15) | collective-permute-done | bytes 491552 | tf_op jit(solution)/shard_map/ppermute | solution.py:608
  125.4 1.3 %proj_join.1 = f32[384,1152]{1,0:T(8,128)} custom-call(bf16[384,640]{1,0:T(8,128)(2,1)S(1)} %bitcast.6, bf16[384,640]{1,0:T(8,128)(2,1)S(1)} %collective-permute-done.15.far_ref), custom_call_target="tpu_custom_call" | custom-call | bytes 6000000 | tf_op jit(solution)/shard_map/proj_join/pallas_call | solution.py:41
  (6 shorter events, 0.1 us)
Async XLA Ops:
  0.6 40.1 %copy-start = (bf16[384,1152]{1,0:T(8,128)(2,1)S(1)}, bf16[384,1152]{1,0:T(8,128)(2,1)}, u32[]{:S(2)}) copy-start(bf16[384,1152]{1,0:T(8,128)(2,1)} %projection_ref.3) | copy-start | bytes 2654212
  2.2 25.1 %all-to-all-start = ((bf16[16,4,1280]{2,1,0:T(4,128)(2,1)}), bf16[16,4,1280]{2,1,0:T(4,128)(2,1)S(1)}, u32[]{:S(2)}, u32[]{:S(2)}) async-start(bf16[16,4,1280]{2,1,0:T(4,128)(2,1)} %text_pack.1), calls=%async_computation | async-start | bytes 327680 | tf_op jit(solution)/shard_map/all_to_all | solution.py:604
  27.4 14.5 %collective-permute-start = (bf16[64,1280]{1,0:T(8,128)(2,1)S(1)}, bf16[64,1280]{1,0:T(8,128)(2,1)S(1)}, u32[]{:S(2)}, u32[]{:S(2)}) collective-permute-start(bf16[64,1280]{1,0:T(8,128)(2,1)S(1)} %line_rows.1.own_ref), channel_id=1, source_target_pairs={{0,1},{1,0},{2,3},{3,2},{4,5},{5,4},{6,7},{7,6},{8,9},{9,8},{10,11... | collective-permute-start | bytes 491528 | tf_op jit(solution)/shard_map/ppermute | solution.py:666
  41.9 10.6 %collective-permute-start.3 = (bf16[128,1280]{1,0:T(8,128)(2,1)S(1)}, bf16[128,1280]{1,0:T(8,128)(2,1)S(1)}, u32[]{:S(2)}, u32[]{:S(2)}) collective-permute-start(bf16[128,1280]{1,0:T(8,128)(2,1)S(1)} %join_texts.1.t0), channel_id=1, source_target_pairs={{0,4},{2,6},{4,0},{6,2},{1,5},{3,7},{5,1},{7,3},{8,12},{10,14},{12... | collective-permute-start | bytes 983048 | tf_op jit(solution)/shard_map/ppermute | solution.py:612
  43.0 14.1 %collective-permute-start.2 = (bf16[128,1280]{1,0:T(8,128)(2,1)S(1)}, bf16[128,1280]{1,0:T(8,128)(2,1)S(1)}, u32[]{:S(2)}, u32[]{:S(2)}) collective-permute-start(bf16[128,1280]{1,0:T(8,128)(2,1)S(1)} %join_texts.1.t0), channel_id=1, source_target_pairs={{0,6},{2,0},{4,2},{6,4},{1,7},{3,1},{5,3},{7,5},{8,14},{10,8},{12,... | collective-permute-start | bytes 983048 | tf_op jit(solution)/shard_map/ppermute | solution.py:612
  44.6 17.7 %collective-permute-start.1 = (bf16[128,1280]{1,0:T(8,128)(2,1)S(1)}, bf16[128,1280]{1,0:T(8,128)(2,1)S(1)}, u32[]{:S(2)}, u32[]{:S(2)}) collective-permute-start(bf16[128,1280]{1,0:T(8,128)(2,1)S(1)} %join_texts.1.t0), channel_id=1, source_target_pairs={{0,2},{2,4},{4,6},{6,0},{1,3},{3,5},{5,7},{7,1},{8,10},{10,12},{12... | collective-permute-start | bytes 983048 | tf_op jit(solution)/shard_map/ppermute | solution.py:612
  44.6 20.3 %all-to-all-start.2 = ((bf16[8,32,1152]{2,1,0:T(8,128)(2,1)}), bf16[8,32,1152]{2,1,0:T(8,128)(2,1)S(1)}, u32[]{:S(2)}, u32[]{:S(2)}) async-start(bf16[8,32,1152]{2,1,0:T(8,128)(2,1)} %get-tuple-element.30), calls=%async_computation.2 | async-start | bytes 1179648 | tf_op jit(solution)/shard_map/all_to_all | solution.py:604
  48.8 15.5 %collective-permute-start.4 = (bf16[128,1280]{1,0:T(8,128)(2,1)S(1)}, bf16[128,1280]{1,0:T(8,128)(2,1)S(1)}, u32[]{:S(2)}, u32[]{:S(2)}) collective-permute-start(bf16[128,1280]{1,0:T(8,128)(2,1)S(1)} %join_texts.1.t0), channel_id=1, source_target_pairs={{0,8},{8,0},{1,9},{9,1},{2,10},{10,2},{3,11},{11,3},{4,12},{12,4},... | collective-permute-start | bytes 983048 | tf_op jit(solution)/shard_map/ppermute | solution.py:608
  52.5 12.5 %collective-permute-start.7 = (bf16[128,1280]{1,0:T(8,128)(2,1)S(1)}, bf16[128,1280]{1,0:T(8,128)(2,1)S(1)}, u32[]{:S(2)}, u32[]{:S(2)}) collective-permute-start(bf16[128,1280]{1,0:T(8,128)(2,1)S(1)} %collective-permute-done.3.t3), channel_id=1, source_target_pairs={{0,8},{8,0},{1,9},{9,1},{2,10},{10,2},{3,11},{11,3},{4,12},{12,4},... | collective-permute-start | bytes 983048 | tf_op jit(solution)/shard_map/ppermute | solution.py:608
  57.1 7.9 %collective-permute-start.6 = (bf16[128,1280]{1,0:T(8,128)(2,1)S(1)}, bf16[128,1280]{1,0:T(8,128)(2,1)}, u32[]{:S(2)}, u32[]{:S(2)}) collective-permute-start(bf16[128,1280]{1,0:T(8,128)(2,1)S(1)} %collective-permute-done.2.t2), channel_id=1, source_target_pairs={{0,8},{8,0},{1,9},{9,1},{2,10},{10,2},{3,11},{11,3},{4,12},{12,4},... | collective-permute-start | bytes 983048 | tf_op jit(solution)/shard_map/ppermute | solution.py:608
  62.3 2.7 %collective-permute-start.5 = (bf16[128,1280]{1,0:T(8,128)(2,1)S(1)}, bf16[128,1280]{1,0:T(8,128)(2,1)}, u32[]{:S(2)}, u32[]{:S(2)}) collective-permute-start(bf16[128,1280]{1,0:T(8,128)(2,1)S(1)} %collective-permute-done.1.t1), channel_id=1, source_target_pairs={{0,8},{8,0},{1,9},{9,1},{2,10},{10,2},{3,11},{11,3},{4,12},{12,4},... | collective-permute-start | bytes 983048 | tf_op jit(solution)/shard_map/ppermute | solution.py:608
  68.0 3.2 %collective-permute-start.8 = (bf16[32,2560]{1,0:T(8,128)(2,1)S(1)}, bf16[32,2560]{1,0:T(8,128)(2,1)S(1)}, u32[]{:S(2)}, u32[]{:S(2)}) collective-permute-start(bf16[32,2560]{1,0:T(8,128)(2,1)S(1)} %get-tuple-element.34.mine_ref), channel_id=1, source_target_pairs={{0,8},{8,0},{1,9},{9,1},{2,10},{10,2},{3,11},{11,3},{4,12},{12,4},... | collective-permute-start | bytes 491528 | tf_op jit(solution)/shard_map/ppermute | solution.py:608
  70.0 1.2 collective-permute-start.9
  72.5 26.0 %all-to-all-start.3 = ((bf16[16,32,640]{2,1,0:T(8,128)(2,1)}), bf16[16,32,640]{2,1,0:T(8,128)(2,1)S(1)}, u32[]{:S(2)}, u32[]{:S(2)}) async-start(bf16[16,32,640]{2,1,0:T(8,128)(2,1)} %strip_make.1), calls=%async_computation.3 | async-start | bytes 1310720 | tf_op jit(solution)/shard_map/all_to_all | solution.py:604
  80.0 4.3 %collective-permute-start.10 = (f32[4,4,384]{2,1,0:T(4,128)S(1)}, f32[4,4,384]{2,1,0:T(4,128)S(1)}, u32[]{:S(2)}, u32[]{:S(2)}) collective-permute-start(f32[4,4,384]{2,1,0:T(4,128)S(1)} %get-tuple-element.36), channel_id=1, source_target_pairs={{0,1},{1,0},{2,3},{3,2},{4,5},{5,4},{6,7},{7,6},{8,9},{9,8},{10,11... | collective-permute-start | bytes 73736 | tf_op jit(solution)/shard_map/ppermute | solution.py:692
  84.3 0.6 copy-start.1
  84.9 4.1 %collective-permute-start.11 = (f32[2,4,384]{2,1,0:T(4,128)S(1)}, f32[2,4,384]{2,1,0:T(4,128)S(1)}, u32[]{:S(2)}, u32[]{:S(2)}) collective-permute-start(f32[2,4,384]{2,1,0:T(4,128)S(1)} %get-tuple-element.38), channel_id=1, source_target_pairs={{0,2},{2,4},{4,6},{6,0},{1,3},{3,5},{5,7},{7,1},{8,10},{10,12},{12... | collective-permute-start | bytes 36872 | tf_op jit(solution)/shard_map/ppermute | solution.py:612
  85.3 4.3 %collective-permute-start.12 = (f32[2,4,384]{2,1,0:T(4,128)S(1)}, f32[2,4,384]{2,1,0:T(4,128)S(1)}, u32[]{:S(2)}, u32[]{:S(2)}) collective-permute-start(f32[2,4,384]{2,1,0:T(4,128)S(1)} %get-tuple-element.39), channel_id=1, source_target_pairs={{0,4},{2,6},{4,0},{6,2},{1,5},{3,7},{5,1},{7,3},{8,12},{10,14},{12... | collective-permute-start | bytes 36872 | tf_op jit(solution)/shard_map/ppermute | solution.py:612
  87.3 2.8 %collective-permute-start.13 = (f32[2,4,384]{2,1,0:T(4,128)S(1)}, f32[2,4,384]{2,1,0:T(4,128)S(1)}, u32[]{:S(2)}, u32[]{:S(2)}) collective-permute-start(f32[2,4,384]{2,1,0:T(4,128)S(1)} %get-tuple-element.40), channel_id=1, source_target_pairs={{0,6},{2,0},{4,2},{6,4},{1,7},{3,1},{5,3},{7,5},{8,14},{10,8},{12,... | collective-permute-start | bytes 36872 | tf_op jit(solution)/shard_map/ppermute | solution.py:612
  88.9 1.2 copy-start.5
  89.7 0.6 copy-start.6
  90.2 0.6 copy-start.7
  99.3 0.6 copy-start.2
  99.9 19.7 %all-to-all-start.4 = ((bf16[16,24,640]{2,1,0:T(8,128)(2,1)}), bf16[16,24,640]{2,1,0:T(8,128)(2,1)S(1)}, u32[]{:S(2)}, u32[]{:S(2)}) async-start(bf16[16,24,640]{2,1,0:T(8,128)(2,1)} %get-tuple-element.46), calls=%async_computation.4 | async-start | bytes 983040 | tf_op jit(solution)/shard_map/all_to_all | solution.py:604
  108.3 10.5 %collective-permute-start.14 = (f32[4,640]{1,0:T(4,128)S(1)}, f32[4,640]{1,0:T(4,128)S(1)}, u32[]{:S(2)}, u32[]{:S(2)}) collective-permute-start(f32[4,640]{1,0:T(4,128)S(1)} %get-tuple-element.49), channel_id=1, source_target_pairs={{0,8},{8,0},{1,9},{9,1},{2,10},{10,2},{3,11},{11,3},{4,12},{12,4},... | collective-permute-start | bytes 30728 | tf_op jit(solution)/shard_map/ppermute | solution.py:608
  111.0 7.7 %copy-start.3 = (f32[4,640]{1,0:T(4,128)S(1)}, f32[4,640]{1,0:T(4,128)}, u32[]{:S(2)}) copy-start(f32[4,640]{1,0:T(4,128)} %copy-done.2) | copy-start | bytes 30724
  111.0 7.7 %copy-start.4 = (bf16[4,1152]{1,0:T(4,128)(2,1)S(1)}, bf16[4,1152]{1,0:T(4,128)(2,1)}, u32[]{:S(2)}) copy-start(bf16[4,1152]{1,0:T(4,128)(2,1)} %text_ref.1) | copy-start | bytes 27652
  119.6 5.8 %collective-permute-start.15 = (bf16[384,640]{1,0:T(8,128)(2,1)S(1)}, bf16[384,640]{1,0:T(8,128)(2,1)S(1)}, u32[]{:S(2)}, u32[]{:S(2)}) collective-permute-start(bf16[384,640]{1,0:T(8,128)(2,1)S(1)} %bitcast.5), channel_id=1, source_target_pairs={{0,8},{8,0},{1,9},{9,1},{2,10},{10,2},{3,11},{11,3},{4,12},{12,4},... | collective-permute-start | bytes 1474568 | tf_op jit(solution)/shard_map/ppermute | solution.py:608

commit v4 on v3

--- a/solution.py
+++ b/solution.py
@@ -490,7 +490,7 @@
 
 
 def pair_kernel(
-    partials_ref, hot_ref, projection_ref, t0, t1, t2, t3, t4, t5, t6, t7,
+    partials_ref, columns_ref, hot_ref, projection_ref, t0, t1, t2, t3, t4, t5, t6, t7,
     scale_ref, shift_ref,
     stay_ref, send_ref, factors_ref,
     head_ref,
@@ -517,7 +517,8 @@
     embed = length_back(unit, inverse, scale * image_grad).astype(BF16)
     factors_ref[:, :width] = embed
     factors_ref[:, 2 * width : 2 * width + LANES] = weights[0]
-    factors_ref[:, 2 * width + LANES :] = weights[4]
+    factors_ref[:, 2 * width + LANES : 2 * width + 2 * LANES] = weights[4]
+    factors_ref[:, 2 * width + 2 * LANES :] = columns_ref[...]
     head = dot(embed, projection_ref[...], 1, 1)
     rows = images // group
     for owner in range(group):
@@ -534,30 +535,44 @@
         out_ref[1] = got_ref[step]
 
 
-def strip_make_kernel(mine_ref, theirs_ref, columns_ref, far_columns_ref, out_ref, rows_ref, near_ref, far_ref):
-    width = (mine_ref.shape[1] - 2 * LANES) // 2
+def strip_make_kernel(mine_ref, core_ref, side_ref, both_ref, out_ref, rows_ref, near_ref, far_ref):
     line, strip_rows, half = out_ref.shape
-    strip = columns_ref.shape[1] // line
+    share = rows_ref.shape[0]
+    strip = share // 2 // line
+    width = (mine_ref.shape[1] - share - 2 * LANES) // 2
     rows = (strip_rows - strip) // 2
-    texts = line * rows
+    texts = 2 * line * rows
     start = pl.multiple_of(lax.axis_index("core") * (width - half), LANES)
-
-    def both(at):
-        return jnp.concatenate([mine_ref[:, at], theirs_ref[:, at]], axis=0)
-
-    columns = jnp.concatenate([columns_ref[...], far_columns_ref[...]], axis=0)
-    rows_ref[...] = dot(columns, both(pl.ds(start, half)), 0, 0)
-    low = both(pl.ds(pl.multiple_of(start + width, LANES), half))
+    y_lo = lax.axis_index("y_lo")
     first = slice(2 * width, 2 * width + texts)
     second = slice(2 * width + LANES, 2 * width + LANES + texts)
-    own = jnp.concatenate([mine_ref[:, first], theirs_ref[:, second]], axis=0)
-    other = jnp.concatenate([mine_ref[:, second], theirs_ref[:, first]], axis=0)
-    near_ref[...] = dot(own, low, 0, 0)
-    far_ref[...] = dot(other, low, 0, 0)
+
+    def stack(near_at, far_at):
+        return jnp.concatenate(
+            [mine_ref[:, near_at], side_ref[:, near_at], core_ref[:, far_at], both_ref[:, far_at]],
+            axis=0,
+        )
+
+    columns = stack(slice(2 * width + 2 * LANES, None), slice(2 * width + 2 * LANES, None))
+    at = pl.ds(start, half)
+    rows_ref[...] = dot(columns, stack(at, at), 0, 0)
+    at = pl.ds(pl.multiple_of(start + width, LANES), half)
+    low = stack(at, at)
+    near = dot(stack(first, second), low, 0, 0)
+    far = dot(stack(second, first), low, 0, 0)
+    for side in range(2):
+        at = slice(side * texts // 2, (side + 1) * texts // 2)
+        near_ref[side] = near[at]
+        far_ref[side] = far[at]
     for target in range(line):
         at = slice(target * rows, (target + 1) * rows)
         stacked = jnp.concatenate(
-            [rows_ref[target * strip : (target + 1) * strip], near_ref[at], far_ref[at]], axis=0
+            [
+                rows_ref[pl.ds(pl.multiple_of(y_lo * (share // 2) + target * strip, 8), strip), :],
+                near_ref[y_lo, at],
+                far_ref[y_lo, at],
+            ],
+            axis=0,
         )
         out_ref[target] = stacked.astype(BF16)
 
@@ -588,16 +603,26 @@
     out_ref[...] = length_back(text * inverse, inverse, scale_ref[0] * grad)
 
 
-def join_kernel(near_ref, far_ref, out_ref):
+def join_kernel(mine_ref, side_ref, core_ref, both_ref, out_ref):
+    width = out_ref.shape[1]
+    rows = mine_ref.shape[0]
     core = lax.axis_index("core")
-    width = out_ref.shape[1]
-
-    def put(left, right):
-        out_ref[:, :HALF] = left[...].astype(F32)
-        out_ref[:, HALF:] = right[:, 2 * HALF - width :].astype(F32)
-
-    pl.when(core == 0)(lambda: put(near_ref, far_ref))
-    pl.when(core != 0)(lambda: put(far_ref, near_ref))
+    y_lo = lax.axis_index("y_lo")
+
+    def put(row, left, right):
+        at = pl.ds(pl.multiple_of(row * rows, 16), rows)
+        out_ref[at, :HALF] = left[...].astype(F32)
+        out_ref[at, HALF:] = right[:, 2 * HALF - width :].astype(F32)
+
+    @pl.when(core == 0)
+    def _():
+        put(y_lo, mine_ref, core_ref)
+        put(1 - y_lo, side_ref, both_ref)
+
+    @pl.when(core != 0)
+    def _():
+        put(y_lo, core_ref, mine_ref)
+        put(1 - y_lo, both_ref, side_ref)
 
 
 def exchange(blocks, axes):
@@ -606,6 +631,14 @@
 
 def swap_core(block):
     return lax.ppermute(block, "core", ((0, 1), (1, 0)))
+
+
+def swap_side(block):
+    return lax.ppermute(block, "y_lo", ((0, 1), (1, 0)))
+
+
+def swap_both(block):
+    return lax.ppermute(block, ("y_lo", "core"), tuple((i, 3 - i) for i in range(4)))
 
 
 def along_x(block, step):
@@ -674,34 +707,35 @@
     ]
     near += [along_x(near[0], step) for step in (1, 3, 2)]
     far = [swap_core(block) for block in near]
-    far_columns = swap_core(columns)
     partials = exchange(partials, GROUP)
     stay, away, factors = call(
         pair_kernel,
         (
             (shape_of((4, rows, share), F32), VMEM),
             (shape_of((4, rows, share), F32), VMEM),
-            (shape_of((images, 2 * width + 2 * LANES), BF16), VMEM),
-        ),
-        tuple((array, VMEM) for array in (partials, hot, projection, *near, *far))
+            (shape_of((images, 2 * width + 2 * LANES + share), BF16), VMEM),
+        ),
+        tuple((array, VMEM) for array in (partials, columns, hot, projection, *near, *far))
         + ((logit_scale, SMEM), (logit_bias, SMEM)),
         "pairs", 4,
         scratch=(pltpu.VMEM((group, rows, share), F32),),
     )
-    far_factors = swap_core(factors)
+    factors = (factors, swap_core(factors), swap_side(factors), swap_both(factors))
     got = lax.ppermute(away, "y_hi", ((0, 1), (1, 0)))
+    ring = lax.axis_size("z")
+    strip = share // 2 // ring
     strips = call(
         strip_make_kernel,
-        ((shape_of((line, strip + 2 * rows, HALF), BF16), VMEM),),
-        tuple((array, VMEM) for array in (factors, far_factors, columns, far_columns)),
+        ((shape_of((ring, strip + 2 * rows, HALF), BF16), VMEM),),
+        tuple((array, VMEM) for array in factors),
         "strip_make", 2,
         scratch=(
             pltpu.VMEM((share, HALF), F32),
-            pltpu.VMEM((texts, HALF), F32),
-            pltpu.VMEM((texts, HALF), F32),
-        ),
-    )
-    strips = exchange(strips, LINE)
+            pltpu.VMEM((2, texts // 2, HALF), F32),
+            pltpu.VMEM((2, texts // 2, HALF), F32),
+        ),
+    )
+    strips = exchange(strips, "z")
     merged = call(
         merge_kernel,
         ((shape_of((2, rows, share), F32), VMEM),) * 4,
@@ -710,33 +744,33 @@
     )
     blocks = [merged[0]] + [along_x(merged[step], step) for step in (1, 2, 3)]
     shared = (normal, norm_gain, head_gain, filtered, mean, inverse, kernel)
-    held = block_backward(0, blocks, *shared, mean)
-    strips, held = lax.optimization_barrier((strips, held))
+    strips, *blocks = lax.optimization_barrier((strips, *blocks))
     sums, mine, theirs = call(
         strip_kernel,
         (
-            (shape_of((line, strip, HALF), BF16), VMEM),
+            (shape_of((ring, strip, HALF), BF16), VMEM),
             (shape_of((rows, HALF), F32), VMEM),
             (shape_of((rows, HALF), F32), VMEM),
         ),
         ((strips, VMEM),),
         "strip_sum", 1,
     )
-    near_half = exchange(sums, LINE).reshape(share, HALF)
+    quarter = exchange(sums, "z").reshape(share // 2, HALF)
+    held = block_backward(0, blocks, *shared, mine)
     grad_text = call(
         text_kernel,
         ((shape_of((rows, width), F32), VMEM),),
         ((text_embed, VMEM), (mine, VMEM), (swap_core(theirs), VMEM), (logit_scale, SMEM)),
         "text_grad", 1,
     )
-    grad_features = block_backward(1, blocks, *shared, mine, held)
-    near_half, grad_features, grad_text = lax.optimization_barrier(
-        (near_half, grad_features, grad_text)
-    )
+    quarter, held = lax.optimization_barrier((quarter, held))
+    side = swap_side(quarter)
+    grad_features = block_backward(1, blocks, *shared, quarter, held)
+    side, grad_features, grad_text = lax.optimization_barrier((side, grad_features, grad_text))
     grad_proj = call(
         join_kernel,
         ((shape_of((share, width), F32), VMEM),),
-        ((near_half, VMEM), (swap_core(near_half), VMEM)),
+        ((quarter, VMEM), (side, VMEM), (swap_core(quarter), VMEM), (swap_core(side), VMEM)),
         "proj_join", 2,
     )
     grad_features = grad_features.reshape(features.shape)

time: 127 us -> 135 us (1.063)
  waiting for transfers between devices: 7.02 us -> 21.4 us
  starting transfers between devices: 64.9 us -> 57.9 us
    ppermute x0 -> x3, waiting for transfers between devices: none -> 8.72 us  [the longest x1 4.79 us: swap_both(): lax.ppermute(block, ('y_lo', 'core'), tuple(((i, 3 - i) for i in range(4))))]
    all_to_all x4, starting transfers between devices: 30.2 us -> 24.4 us  [exchange(): return lax.all_to_all(blocks, axes, 0, 0, tiled=True)]
    all_to_all x4, waiting for transfers between devices: 0.67 us -> 5.81 us  [exchange(): return lax.all_to_all(blocks, axes, 0, 0, tiled=True)]
    ppermute x0 -> x3, starting transfers between devices: none -> 3.98 us  [the longest x1 3.28 us: swap_both(): lax.ppermute(block, ('y_lo', 'core'), tuple(((i, 3 - i) for i in range(4))))]
    ppermute x8, starting transfers between devices: 23.1 us -> 19.4 us  [swap_core(): return lax.ppermute(block, 'core', ((0, 1), (1, 0)))]
  transfers between devices with their start and end apart: 20 -> 23, of which waited for: 8 -> 12; matrix products, arithmetic and copies ran while one was open for 0% -> 0% of each run, Pallas kernels for 25% -> 24%
where the time goes in v4:
time: 135 us; the launch traced here: 134 us
  starting transfers between devices  57.9 us (43%)
  Pallas kernels  40 us (30%)
  waiting for transfers between devices  21.4 us (16%)
  blocking collectives  10.7 us (8%)
  local copies, waits for them, and re-layouts  2.17 us (2%)
  between operations  2.11 us (2%)
    pallas_call x13, Pallas kernels, call(): pl.pallas_call(body, out_shape=shapes[0] if single else shapes, in_specs=...  40 us
    all_to_all x4, starting transfers between devices, exchange(): return lax.all_to_all(blocks, axes, 0, 0, tiled=True)  24.4 us
    ppermute x8, starting transfers between devices, swap_core(): return lax.ppermute(block, 'core', ((0, 1), (1, 0)))  19.4 us
    all_to_all x1, blocking collectives, exchange(): return lax.all_to_all(blocks, axes, 0, 0, tiled=True)  10.7 us
    ppermute x6, starting transfers between devices, along_x(): lax.ppermute(block, 'x', tuple(((i, (i + step) % 4) for i in range(4))))  6.05 us
    all_to_all x4, waiting for transfers between devices, exchange(): return lax.all_to_all(blocks, axes, 0, 0, tiled=True)  5.81 us
    ppermute x1, waiting for transfers between devices, swap_both(): lax.ppermute(block, ('y_lo', 'core'), tuple(((i, 3 - i) for i in range(4))))  4.79 us
    ppermute x2, waiting for transfers between devices, swap_side(): return lax.ppermute(block, 'y_lo', ((0, 1), (1, 0)))  3.93 us
  transfers between devices with their start and end apart: 23, of which 12 were waited for; matrix products, arithmetic and copies ran while one was open for 0% of the time, Pallas kernels for 24%

profile of v4, /device:TPU:1, one launch (start us, length us, event | category | flops | bytes accessed | tf_op | source)
XLA Modules:
  0.0 134.3 jit_solution(11361984517328545913)
XLA Ops:
  0.6 1.6 %text_pack.1 = bf16[16,4,1280]{2,1,0:T(4,128)(2,1)} custom-call(bf16[4,1152]{1,0:T(4,128)(2,1)} %text_ref.1, s32[4]{0:T(128)} %ids_hbm.2), custom_call_target="tpu_custom_call" | custom-call | bytes 3000000 | tf_op jit(solution)/shard_map/text_pack/pallas_call | solution.py:41
  2.2 10.1 %all-to-all-start = ((bf16[16,4,1280]{2,1,0:T(4,128)(2,1)}), bf16[16,4,1280]{2,1,0:T(4,128)(2,1)S(1)}, u32[]{:S(2)}, u32[]{:S(2)}) async-start(bf16[16,4,1280]{2,1,0:T(4,128)(2,1)} %text_pack.1), calls=%async_computation | async-start | bytes 327680 | tf_op jit(solution)/shard_map/all_to_all | solution.py:629
  12.4 14.9 %block_forward.1 = (f32[256,3072]{1,0:T(8,128)}, f32[256,128]{1,0:T(8,128)}, f32[256,128]{1,0:T(8,128)}, f32[4,3200]{1,0:T(4,128)}, bf16[8,4,512]{2,1,0:T(4,128)(2,1)}) custom-call(bf16[256,3072]{1,0:T(8,128)(2,1)} %bitcast.10, f32[7,7,3072]{2,1,0:T(8,128)} %refs_10_.3, f32[1,3072]{1,0:T(1,128)} %bitcast.11, f32[1,3072]{1,0:T(1,128)} %bitcast.14, s32[4]{0:T(128)} %ids_hbm.3), custom_call_target="tpu_custom_call" | custom-call | bytes 42000000 | tf_op jit(solution)/shard_map/block_forward/pallas_call | solution.py:41
  27.3 0.0 all-to-all-done.line_ref
  27.4 2.7 %collective-permute-start = (bf16[64,1280]{1,0:T(8,128)(2,1)S(1)}, bf16[64,1280]{1,0:T(8,128)(2,1)S(1)}, u32[]{:S(2)}, u32[]{:S(2)}) collective-permute-start(bf16[64,1280]{1,0:T(8,128)(2,1)S(1)} %line_rows.1.own_ref), channel_id=1, source_target_pairs={{0,1},{1,0},{2,3},{3,2},{4,5},{5,4},{6,7},{7,6},{8,9},{9,8},{10,11... | collective-permute-start | bytes 491528 | tf_op jit(solution)/shard_map/ppermute | solution.py:699
  30.1 10.7 %all_to_all.25.received_ref = bf16[8,4,512]{2,1,0:T(4,128)(2,1)S(1)} all-to-all(bf16[8,4,512]{2,1,0:T(4,128)(2,1)} %get-tuple-element.34), channel_id=1, replica_groups=mesh['y_lo'=2,'z'=8,'core'=2,'x'=4,'y_hi'=2] {'x','y_hi'}, dimensions={0} | all-to-all | bytes 65536 | tf_op jit(solution)/shard_map/all_to_all | solution.py:629
  40.7 0.0 copy-done
  40.7 1.1 partial_embed.1
  41.8 0.0 collective-permute-done.next_ref
  41.9 1.1 collective-permute-start.3
  42.9 1.7 %collective-permute-start.2 = (bf16[128,1280]{1,0:T(8,128)(2,1)S(1)}, bf16[128,1280]{1,0:T(8,128)(2,1)S(1)}, u32[]{:S(2)}, u32[]{:S(2)}) collective-permute-start(bf16[128,1280]{1,0:T(8,128)(2,1)S(1)} %join_texts.1.t0), channel_id=1, source_target_pairs={{0,6},{2,0},{4,2},{6,4},{1,7},{3,1},{5,3},{7,5},{8,14},{10,8},{12,... | collective-permute-start | bytes 983048 | tf_op jit(solution)/shard_map/ppermute | solution.py:645
  44.6 0.0 collective-permute-start.1
  44.6 4.2 %all-to-all-start.2 = ((bf16[8,32,1152]{2,1,0:T(8,128)(2,1)}), bf16[8,32,1152]{2,1,0:T(8,128)(2,1)S(1)}, u32[]{:S(2)}, u32[]{:S(2)}) async-start(bf16[8,32,1152]{2,1,0:T(8,128)(2,1)} %get-tuple-element.35), calls=%async_computation.2 | async-start | bytes 1179648 | tf_op jit(solution)/shard_map/all_to_all | solution.py:629
  48.8 3.7 %collective-permute-start.4 = (bf16[128,1280]{1,0:T(8,128)(2,1)S(1)}, bf16[128,1280]{1,0:T(8,128)(2,1)S(1)}, u32[]{:S(2)}, u32[]{:S(2)}) collective-permute-start(bf16[128,1280]{1,0:T(8,128)(2,1)S(1)} %join_texts.1.t0), channel_id=1, source_target_pairs={{0,8},{8,0},{1,9},{9,1},{2,10},{10,2},{3,11},{11,3},{4,12},{12,4},... | collective-permute-start | bytes 983048 | tf_op jit(solution)/shard_map/ppermute | solution.py:633
  52.5 0.0 collective-permute-done.3.t3
  52.5 4.3 %collective-permute-start.7 = (bf16[128,1280]{1,0:T(8,128)(2,1)S(1)}, bf16[128,1280]{1,0:T(8,128)(2,1)S(1)}, u32[]{:S(2)}, u32[]{:S(2)}) collective-permute-start(bf16[128,1280]{1,0:T(8,128)(2,1)S(1)} %collective-permute-done.3.t3), channel_id=1, source_target_pairs={{0,8},{8,0},{1,9},{9,1},{2,10},{10,2},{3,11},{11,3},{4,12},{12,4},... | collective-permute-start | bytes 983048 | tf_op jit(solution)/shard_map/ppermute | solution.py:633
  56.8 0.3 collective-permute-done.2.t2
  57.1 5.2 %collective-permute-start.6 = (bf16[128,1280]{1,0:T(8,128)(2,1)S(1)}, bf16[128,1280]{1,0:T(8,128)(2,1)}, u32[]{:S(2)}, u32[]{:S(2)}) collective-permute-start(bf16[128,1280]{1,0:T(8,128)(2,1)S(1)} %collective-permute-done.2.t2), channel_id=1, source_target_pairs={{0,8},{8,0},{1,9},{9,1},{2,10},{10,2},{3,11},{11,3},{4,12},{12,4},... | collective-permute-start | bytes 983048 | tf_op jit(solution)/shard_map/ppermute | solution.py:633
  62.3 0.0 collective-permute-done.1.t1
  62.3 0.7 collective-permute-start.5
  64.3 0.0 collective-permute-done.4.t4
  64.3 0.7 all-to-all-done.2.partials_ref
  65.0 0.0 collective-permute-done.7.t7
  65.0 0.0 collective-permute-done.6.t6
  65.0 0.0 collective-permute-done.5.t5
  65.0 3.0 %pairs.1 = (f32[4,4,384]{2,1,0:T(4,128)S(1)}, f32[4,4,384]{2,1,0:T(4,128)S(1)}, bf16[32,2944]{1,0:T(8,128)(2,1)S(1)}) custom-call(bf16[8,32,1152]{2,1,0:T(8,128)(2,1)S(1)} %all-to-all-done.2.partials_ref, bf16[32,384]{1,0:T(8,128)(2,1)S(1)} %get-tuple-element.36.after_ref.columns_ref, bf16[32,128]{1,0:T(8,128)(2,1)S(1)} %get-tuple-element.37.hot_ref, ...), custom_call_target="tpu_custom_call" | custom-call | bytes 12000000 | tf_op jit(solution)/shard_map/pairs/pallas_call | solution.py:41
  68.0 3.3 %collective-permute-start.10 = (bf16[32,2944]{1,0:T(8,128)(2,1)S(1)}, bf16[32,2944]{1,0:T(8,128)(2,1)S(1)}, u32[]{:S(2)}, u32[]{:S(2)}) collective-permute-start(bf16[32,2944]{1,0:T(8,128)(2,1)S(1)} %get-tuple-element.39.mine_ref), channel_id=1, source_target_pairs={{0,136},{8,128},{128,8},{136,0},{1,137},{9,129},{129,9},{137,1},{2... | collective-permute-start | bytes 565256 | tf_op jit(solution)/shard_map/ppermute | solution.py:641
  71.3 0.1 collective-permute-start.9
  71.4 0.4 collective-permute-start.8
  71.8 4.8 %collective-permute-done.10.both_ref = bf16[32,2944]{1,0:T(8,128)(2,1)S(1)} collective-permute-done((bf16[32,2944]{1,0:T(8,128)(2,1)S(1)}, bf16[32,2944]{1,0:T(8,128)(2,1)S(1)}, u32[]{:S(2)}, u32[]{:S(2)}) %collective-permute-start.10) | collective-permute-done | bytes 188448 | tf_op jit(solution)/shard_map/ppermute | solution.py:641
  76.6 3.9 %collective-permute-done.9.side_ref = bf16[32,2944]{1,0:T(8,128)(2,1)S(1)} collective-permute-done((bf16[32,2944]{1,0:T(8,128)(2,1)S(1)}, bf16[32,2944]{1,0:T(8,128)(2,1)S(1)}, u32[]{:S(2)}, u32[]{:S(2)}) %collective-permute-start.9) | collective-permute-done | bytes 188448 | tf_op jit(solution)/shard_map/ppermute | solution.py:637
  80.5 0.0 collective-permute-done.8.core_ref
  80.5 1.1 strip_make.1
  81.6 6.7 %all-to-all-start.3 = ((bf16[8,32,640]{2,1,0:T(8,128)(2,1)}), bf16[8,32,640]{2,1,0:T(8,128)(2,1)S(1)}, u32[]{:S(2)}, u32[]{:S(2)}) async-start(bf16[8,32,640]{2,1,0:T(8,128)(2,1)} %strip_make.1), calls=%async_computation.3 | async-start | bytes 655360 | tf_op jit(solution)/shard_map/all_to_all | solution.py:629
  88.4 1.3 collective-permute-start.11
  89.7 2.8 %collective-permute-done.11.got_ref = f32[4,4,384]{2,1,0:T(4,128)S(1)} collective-permute-done((f32[4,4,384]{2,1,0:T(4,128)S(1)}, f32[4,4,384]{2,1,0:T(4,128)S(1)}, u32[]{:S(2)}, u32[]{:S(2)}) %collective-permute-start.11) | collective-permute-done | bytes 24608 | tf_op jit(solution)/shard_map/ppermute | solution.py:724
  92.6 0.6 copy-done.3
  93.2 0.3 collective-permute-start.12
  93.4 1.7 %collective-permute-start.13 = (f32[2,4,384]{2,1,0:T(4,128)S(1)}, f32[2,4,384]{2,1,0:T(4,128)S(1)}, u32[]{:S(2)}, u32[]{:S(2)}) collective-permute-start(f32[2,4,384]{2,1,0:T(4,128)S(1)} %get-tuple-element.44), channel_id=1, source_target_pairs={{0,4},{2,6},{4,0},{6,2},{1,5},{3,7},{5,1},{7,3},{8,12},{10,14},{12... | collective-permute-start | bytes 36872 | tf_op jit(solution)/shard_map/ppermute | solution.py:645
  95.1 1.3 collective-permute-start.14
  96.4 0.8 collective-permute-done.12.refs_1_
  97.2 0.6 collective-permute-done.13.refs_2_
  97.8 0.2 collective-permute-done.14.refs_3_
  98.0 3.6 %all-to-all-done.3.strips_ref = bf16[8,32,640]{2,1,0:T(8,128)(2,1)S(1)} async-done(((bf16[8,32,640]{2,1,0:T(8,128)(2,1)}), bf16[8,32,640]{2,1,0:T(8,128)(2,1)S(1)}, u32[]{:S(2)}, u32[]{:S(2)}) %all-to-all-start.3) | async-done | bytes 327712 | tf_op jit(solution)/shard_map/all_to_all | solution.py:629
  101.6 0.7 strip_sum.1
  102.3 0.6 copy-done.4
  102.9 3.4 %all-to-all-start.4 = ((bf16[8,24,640]{2,1,0:T(8,128)(2,1)}), bf16[8,24,640]{2,1,0:T(8,128)(2,1)S(1)}, u32[]{:S(2)}, u32[]{:S(2)}) async-start(bf16[8,24,640]{2,1,0:T(8,128)(2,1)} %get-tuple-element.47), calls=%async_computation.4 | async-start | bytes 491520 | tf_op jit(solution)/shard_map/all_to_all | solution.py:629
  106.4 0.0 copy-start.5
  106.4 0.0 copy-start.6
  106.4 7.7 %block_backward.2.refs_12_ = bf16[256,3072]{1,0:T(8,128)(2,1)} custom-call(f32[2,4,384]{2,1,0:T(4,128)} %copy-done.3, f32[2,4,384]{2,1,0:T(4,128)} %copy-done.7, f32[2,4,384]{2,1,0:T(4,128)} %copy-done.8, f32[2,4,384]{2,1,0:T(4,128)} %copy-done.9, f32[4,3200]{1,0:T(4,128)} %get-tuple-element.52.refs_4_, f32[1,3072]{1,0:T(1,128)} %bitcast.12, ...), custom_call_target="tpu_custom_call" | custom-call | bytes 24000000 | tf_op jit(solution)/shard_map/block_backward/pallas_call | solution.py:41
  114.1 1.5 %all-to-all-done.4 = bf16[8,24,640]{2,1,0:T(8,128)(2,1)S(1)} async-done(((bf16[8,24,640]{2,1,0:T(8,128)(2,1)}), bf16[8,24,640]{2,1,0:T(8,128)(2,1)S(1)}, u32[]{:S(2)}, u32[]{:S(2)}) %all-to-all-start.4) | async-done | bytes 245792 | tf_op jit(solution)/shard_map/all_to_all | solution.py:629
  115.6 0.6 collective-permute-start.15
  116.1 4.6 %collective-permute-start.16 = (f32[4,640]{1,0:T(4,128)S(1)}, f32[4,640]{1,0:T(4,128)S(1)}, u32[]{:S(2)}, u32[]{:S(2)}) collective-permute-start(f32[4,640]{1,0:T(4,128)S(1)} %get-tuple-element.59), channel_id=1, source_target_pairs={{0,8},{8,0},{1,9},{9,1},{2,10},{10,2},{3,11},{11,3},{4,12},{12,4},... | collective-permute-start | bytes 30728 | tf_op jit(solution)/shard_map/ppermute | solution.py:633
  120.7 0.8 collective-permute-done.16.got_ref
  121.6 0.8 text_grad.1
  122.4 0.3 collective-permute-start.17
  122.7 0.0 copy-done.1
  122.7 7.7 %block_backward.3 = bf16[256,3072]{1,0:T(8,128)(2,1)} custom-call(f32[2,4,384]{2,1,0:T(4,128)} %copy-done.3, f32[2,4,384]{2,1,0:T(4,128)} %copy-done.7, f32[2,4,384]{2,1,0:T(4,128)} %copy-done.8, f32[2,4,384]{2,1,0:T(4,128)} %copy-done.9, f32[4,3200]{1,0:T(4,128)} %get-tuple-element.52.refs_4_, f32[1,3072]{1,0:T(1,128)} %bitcast.13, ...), custom_call_target="tpu_custom_call", output_to_operand_aliasing={{}: (12, {})} | custom-call | bytes 24000000 | tf_op jit(solution)/shard_map/block_backward/pallas_call | solution.py:41
  130.4 0.0 collective-permute-done.15.side_ref
  130.4 0.3 collective-permute-start.18
  130.6 0.0 collective-permute-done.17.core_ref
  130.7 1.3 collective-permute-done.18.both_ref
  132.0 0.9 copy-done.2
  132.9 1.3 proj_join.1
  (16 shorter events, 0.1 us)
Async XLA Ops:
  0.6 40.1 %copy-start = (bf16[384,1152]{1,0:T(8,128)(2,1)S(1)}, bf16[384,1152]{1,0:T(8,128)(2,1)}, u32[]{:S(2)}) copy-start(bf16[384,1152]{1,0:T(8,128)(2,1)} %projection_ref.3) | copy-start | bytes 2654212
  2.2 25.1 %all-to-all-start = ((bf16[16,4,1280]{2,1,0:T(4,128)(2,1)}), bf16[16,4,1280]{2,1,0:T(4,128)(2,1)S(1)}, u32[]{:S(2)}, u32[]{:S(2)}) async-start(bf16[16,4,1280]{2,1,0:T(4,128)(2,1)} %text_pack.1), calls=%async_computation | async-start | bytes 327680 | tf_op jit(solution)/shard_map/all_to_all | solution.py:629
  27.4 14.5 %collective-permute-start = (bf16[64,1280]{1,0:T(8,128)(2,1)S(1)}, bf16[64,1280]{1,0:T(8,128)(2,1)S(1)}, u32[]{:S(2)}, u32[]{:S(2)}) collective-permute-start(bf16[64,1280]{1,0:T(8,128)(2,1)S(1)} %line_rows.1.own_ref), channel_id=1, source_target_pairs={{0,1},{1,0},{2,3},{3,2},{4,5},{5,4},{6,7},{7,6},{8,9},{9,8},{10,11... | collective-permute-start | bytes 491528 | tf_op jit(solution)/shard_map/ppermute | solution.py:699
  41.9 10.6 %collective-permute-start.3 = (bf16[128,1280]{1,0:T(8,128)(2,1)S(1)}, bf16[128,1280]{1,0:T(8,128)(2,1)S(1)}, u32[]{:S(2)}, u32[]{:S(2)}) collective-permute-start(bf16[128,1280]{1,0:T(8,128)(2,1)S(1)} %join_texts.1.t0), channel_id=1, source_target_pairs={{0,4},{2,6},{4,0},{6,2},{1,5},{3,7},{5,1},{7,3},{8,12},{10,14},{12... | collective-permute-start | bytes 983048 | tf_op jit(solution)/shard_map/ppermute | solution.py:645
  42.9 14.1 %collective-permute-start.2 = (bf16[128,1280]{1,0:T(8,128)(2,1)S(1)}, bf16[128,1280]{1,0:T(8,128)(2,1)S(1)}, u32[]{:S(2)}, u32[]{:S(2)}) collective-permute-start(bf16[128,1280]{1,0:T(8,128)(2,1)S(1)} %join_texts.1.t0), channel_id=1, source_target_pairs={{0,6},{2,0},{4,2},{6,4},{1,7},{3,1},{5,3},{7,5},{8,14},{10,8},{12,... | collective-permute-start | bytes 983048 | tf_op jit(solution)/shard_map/ppermute | solution.py:645
  44.6 17.7 %collective-permute-start.1 = (bf16[128,1280]{1,0:T(8,128)(2,1)S(1)}, bf16[128,1280]{1,0:T(8,128)(2,1)S(1)}, u32[]{:S(2)}, u32[]{:S(2)}) collective-permute-start(bf16[128,1280]{1,0:T(8,128)(2,1)S(1)} %join_texts.1.t0), channel_id=1, source_target_pairs={{0,2},{2,4},{4,6},{6,0},{1,3},{3,5},{5,7},{7,1},{8,10},{10,12},{12... | collective-permute-start | bytes 983048 | tf_op jit(solution)/shard_map/ppermute | solution.py:645
  44.6 20.3 %all-to-all-start.2 = ((bf16[8,32,1152]{2,1,0:T(8,128)(2,1)}), bf16[8,32,1152]{2,1,0:T(8,128)(2,1)S(1)}, u32[]{:S(2)}, u32[]{:S(2)}) async-start(bf16[8,32,1152]{2,1,0:T(8,128)(2,1)} %get-tuple-element.35), calls=%async_computation.2 | async-start | bytes 1179648 | tf_op jit(solution)/shard_map/all_to_all | solution.py:629
  48.8 15.5 %collective-permute-start.4 = (bf16[128,1280]{1,0:T(8,128)(2,1)S(1)}, bf16[128,1280]{1,0:T(8,128)(2,1)S(1)}, u32[]{:S(2)}, u32[]{:S(2)}) collective-permute-start(bf16[128,1280]{1,0:T(8,128)(2,1)S(1)} %join_texts.1.t0), channel_id=1, source_target_pairs={{0,8},{8,0},{1,9},{9,1},{2,10},{10,2},{3,11},{11,3},{4,12},{12,4},... | collective-permute-start | bytes 983048 | tf_op jit(solution)/shard_map/ppermute | solution.py:633
  52.5 12.5 %collective-permute-start.7 = (bf16[128,1280]{1,0:T(8,128)(2,1)S(1)}, bf16[128,1280]{1,0:T(8,128)(2,1)S(1)}, u32[]{:S(2)}, u32[]{:S(2)}) collective-permute-start(bf16[128,1280]{1,0:T(8,128)(2,1)S(1)} %collective-permute-done.3.t3), channel_id=1, source_target_pairs={{0,8},{8,0},{1,9},{9,1},{2,10},{10,2},{3,11},{11,3},{4,12},{12,4},... | collective-permute-start | bytes 983048 | tf_op jit(solution)/shard_map/ppermute | solution.py:633
  57.1 7.9 %collective-permute-start.6 = (bf16[128,1280]{1,0:T(8,128)(2,1)S(1)}, bf16[128,1280]{1,0:T(8,128)(2,1)}, u32[]{:S(2)}, u32[]{:S(2)}) collective-permute-start(bf16[128,1280]{1,0:T(8,128)(2,1)S(1)} %collective-permute-done.2.t2), channel_id=1, source_target_pairs={{0,8},{8,0},{1,9},{9,1},{2,10},{10,2},{3,11},{11,3},{4,12},{12,4},... | collective-permute-start | bytes 983048 | tf_op jit(solution)/shard_map/ppermute | solution.py:633
  62.3 2.7 %collective-permute-start.5 = (bf16[128,1280]{1,0:T(8,128)(2,1)S(1)}, bf16[128,1280]{1,0:T(8,128)(2,1)}, u32[]{:S(2)}, u32[]{:S(2)}) collective-permute-start(bf16[128,1280]{1,0:T(8,128)(2,1)S(1)} %collective-permute-done.1.t1), channel_id=1, source_target_pairs={{0,8},{8,0},{1,9},{9,1},{2,10},{10,2},{3,11},{11,3},{4,12},{12,4},... | collective-permute-start | bytes 983048 | tf_op jit(solution)/shard_map/ppermute | solution.py:633
  68.0 8.6 %collective-permute-start.10 = (bf16[32,2944]{1,0:T(8,128)(2,1)S(1)}, bf16[32,2944]{1,0:T(8,128)(2,1)S(1)}, u32[]{:S(2)}, u32[]{:S(2)}) collective-permute-start(bf16[32,2944]{1,0:T(8,128)(2,1)S(1)} %get-tuple-element.39.mine_ref), channel_id=1, source_target_pairs={{0,136},{8,128},{128,8},{136,0},{1,137},{9,129},{129,9},{137,1},{2... | collective-permute-start | bytes 565256 | tf_op jit(solution)/shard_map/ppermute | solution.py:641
  71.3 9.2 %collective-permute-start.9 = (bf16[32,2944]{1,0:T(8,128)(2,1)S(1)}, bf16[32,2944]{1,0:T(8,128)(2,1)S(1)}, u32[]{:S(2)}, u32[]{:S(2)}) collective-permute-start(bf16[32,2944]{1,0:T(8,128)(2,1)S(1)} %get-tuple-element.39.mine_ref), channel_id=1, source_target_pairs={{0,128},{128,0},{1,129},{129,1},{2,130},{130,2},{3,131},{131,3},{4... | collective-permute-start | bytes 565256 | tf_op jit(solution)/shard_map/ppermute | solution.py:637
  71.4 9.1 %collective-permute-start.8 = (bf16[32,2944]{1,0:T(8,128)(2,1)S(1)}, bf16[32,2944]{1,0:T(8,128)(2,1)S(1)}, u32[]{:S(2)}, u32[]{:S(2)}) collective-permute-start(bf16[32,2944]{1,0:T(8,128)(2,1)S(1)} %get-tuple-element.39.mine_ref), channel_id=1, source_target_pairs={{0,8},{8,0},{1,9},{9,1},{2,10},{10,2},{3,11},{11,3},{4,12},{12,4},... | collective-permute-start | bytes 565256 | tf_op jit(solution)/shard_map/ppermute | solution.py:633
  81.6 20.0 %all-to-all-start.3 = ((bf16[8,32,640]{2,1,0:T(8,128)(2,1)}), bf16[8,32,640]{2,1,0:T(8,128)(2,1)S(1)}, u32[]{:S(2)}, u32[]{:S(2)}) async-start(bf16[8,32,640]{2,1,0:T(8,128)(2,1)} %strip_make.1), calls=%async_computation.3 | async-start | bytes 655360 | tf_op jit(solution)/shard_map/all_to_all | solution.py:629
  88.4 4.2 %collective-permute-start.11 = (f32[4,4,384]{2,1,0:T(4,128)S(1)}, f32[4,4,384]{2,1,0:T(4,128)S(1)}, u32[]{:S(2)}, u32[]{:S(2)}) collective-permute-start(f32[4,4,384]{2,1,0:T(4,128)S(1)} %get-tuple-element.41), channel_id=1, source_target_pairs={{0,1},{1,0},{2,3},{3,2},{4,5},{5,4},{6,7},{7,6},{8,9},{9,8},{10,11... | collective-permute-start | bytes 73736 | tf_op jit(solution)/shard_map/ppermute | solution.py:724
  92.6 0.6 copy-start.3
  93.2 4.1 %collective-permute-start.12 = (f32[2,4,384]{2,1,0:T(4,128)S(1)}, f32[2,4,384]{2,1,0:T(4,128)S(1)}, u32[]{:S(2)}, u32[]{:S(2)}) collective-permute-start(f32[2,4,384]{2,1,0:T(4,128)S(1)} %get-tuple-element.43), channel_id=1, source_target_pairs={{0,2},{2,4},{4,6},{6,0},{1,3},{3,5},{5,7},{7,1},{8,10},{10,12},{12... | collective-permute-start | bytes 36872 | tf_op jit(solution)/shard_map/ppermute | solution.py:645
  93.4 4.3 %collective-permute-start.13 = (f32[2,4,384]{2,1,0:T(4,128)S(1)}, f32[2,4,384]{2,1,0:T(4,128)S(1)}, u32[]{:S(2)}, u32[]{:S(2)}) collective-permute-start(f32[2,4,384]{2,1,0:T(4,128)S(1)} %get-tuple-element.44), channel_id=1, source_target_pairs={{0,4},{2,6},{4,0},{6,2},{1,5},{3,7},{5,1},{7,3},{8,12},{10,14},{12... | collective-permute-start | bytes 36872 | tf_op jit(solution)/shard_map/ppermute | solution.py:645
  95.1 2.8 %collective-permute-start.14 = (f32[2,4,384]{2,1,0:T(4,128)S(1)}, f32[2,4,384]{2,1,0:T(4,128)S(1)}, u32[]{:S(2)}, u32[]{:S(2)}) collective-permute-start(f32[2,4,384]{2,1,0:T(4,128)S(1)} %get-tuple-element.45), channel_id=1, source_target_pairs={{0,6},{2,0},{4,2},{6,4},{1,7},{3,1},{5,3},{7,5},{8,14},{10,8},{12,... | collective-permute-start | bytes 36872 | tf_op jit(solution)/shard_map/ppermute | solution.py:645
  97.2 9.2 %copy-start.7 = (f32[2,4,384]{2,1,0:T(4,128)}, f32[2,4,384]{2,1,0:T(4,128)S(1)}, u32[]{:S(2)}) copy-start(f32[2,4,384]{2,1,0:T(4,128)S(1)} %collective-permute-done.12.refs_1_) | copy-start | bytes 36868
  97.8 8.6 %copy-start.8 = (f32[2,4,384]{2,1,0:T(4,128)}, f32[2,4,384]{2,1,0:T(4,128)S(1)}, u32[]{:S(2)}) copy-start(f32[2,4,384]{2,1,0:T(4,128)S(1)} %collective-permute-done.13.refs_2_) | copy-start | bytes 36868
  98.0 8.4 %copy-start.9 = (f32[2,4,384]{2,1,0:T(4,128)}, f32[2,4,384]{2,1,0:T(4,128)S(1)}, u32[]{:S(2)}) copy-start(f32[2,4,384]{2,1,0:T(4,128)S(1)} %collective-permute-done.14.refs_3_) | copy-start | bytes 36868
  102.3 0.6 copy-start.4
  102.9 12.6 %all-to-all-start.4 = ((bf16[8,24,640]{2,1,0:T(8,128)(2,1)}), bf16[8,24,640]{2,1,0:T(8,128)(2,1)S(1)}, u32[]{:S(2)}, u32[]{:S(2)}) async-start(bf16[8,24,640]{2,1,0:T(8,128)(2,1)} %get-tuple-element.47), calls=%async_computation.4 | async-start | bytes 491520 | tf_op jit(solution)/shard_map/all_to_all | solution.py:629
  106.4 15.2 %copy-start.5 = (f32[4,640]{1,0:T(4,128)S(1)}, f32[4,640]{1,0:T(4,128)}, u32[]{:S(2)}) copy-start(f32[4,640]{1,0:T(4,128)} %copy-done.4) | copy-start | bytes 30724
  106.4 15.2 %copy-start.6 = (bf16[4,1152]{1,0:T(4,128)(2,1)S(1)}, bf16[4,1152]{1,0:T(4,128)(2,1)}, u32[]{:S(2)}) copy-start(bf16[4,1152]{1,0:T(4,128)(2,1)} %text_ref.1) | copy-start | bytes 27652
  115.6 7.1 %copy-start.1 = (bf16[8,24,640]{2,1,0:T(8,128)(2,1)}, bf16[8,24,640]{2,1,0:T(8,128)(2,1)S(1)}, u32[]{:S(2)}) copy-start(bf16[8,24,640]{2,1,0:T(8,128)(2,1)S(1)} %all-to-all-done.4) | copy-start | bytes 737284
  115.6 14.8 %collective-permute-start.15 = (bf16[192,640]{1,0:T(8,128)(2,1)S(1)}, bf16[192,640]{1,0:T(8,128)(2,1)S(1)}, u32[]{:S(2)}, u32[]{:S(2)}) collective-permute-start(bf16[192,640]{1,0:T(8,128)(2,1)S(1)} %bitcast.5), channel_id=1, source_target_pairs={{0,128},{128,0},{1,129},{129,1},{2,130},{130,2},{3,131},{131,3},{4... | collective-permute-start | bytes 737288 | tf_op jit(solution)/shard_map/ppermute | solution.py:637
  116.1 5.4 %collective-permute-start.16 = (f32[4,640]{1,0:T(4,128)S(1)}, f32[4,640]{1,0:T(4,128)S(1)}, u32[]{:S(2)}, u32[]{:S(2)}) collective-permute-start(f32[4,640]{1,0:T(4,128)S(1)} %get-tuple-element.59), channel_id=1, source_target_pairs={{0,8},{8,0},{1,9},{9,1},{2,10},{10,2},{3,11},{11,3},{4,12},{12,4},... | collective-permute-start | bytes 30728 | tf_op jit(solution)/shard_map/ppermute | solution.py:633
  122.4 8.3 %collective-permute-start.17 = (bf16[192,640]{1,0:T(8,128)(2,1)S(1)}, bf16[192,640]{1,0:T(8,128)(2,1)S(1)}, u32[]{:S(2)}, u32[]{:S(2)}) collective-permute-start(bf16[192,640]{1,0:T(8,128)(2,1)S(1)} %bitcast.6), channel_id=1, source_target_pairs={{0,8},{8,0},{1,9},{9,1},{2,10},{10,2},{3,11},{11,3},{4,12},{12,4},... | collective-permute-start | bytes 737288 | tf_op jit(solution)/shard_map/ppermute | solution.py:633
  130.4 1.6 %collective-permute-start.18 = (bf16[192,640]{1,0:T(8,128)(2,1)S(1)}, bf16[192,640]{1,0:T(8,128)(2,1)S(1)}, u32[]{:S(2)}, u32[]{:S(2)}) collective-permute-start(bf16[192,640]{1,0:T(8,128)(2,1)S(1)} %collective-permute-done.15.side_ref), channel_id=1, source_target_pairs={{0,8},{8,0},{1,9},{9,1},{2,10},{10,2},{3,11},{11,3},{4,12},{12,4},... | collective-permute-start | bytes 737288 | tf_op jit(solution)/shard_map/ppermute | solution.py:633
  132.0 0.9 copy-start.2

commit v5 on v3

--- a/solution.py
+++ b/solution.py
@@ -1,5 +1,3 @@
-import functools
-
 import jax
 import jax.numpy as jnp
 from jax import lax
@@ -34,7 +32,7 @@
     return jax.ShapeDtypeStruct(dims, dtype)
 
 
-def call(body, outs, operands, name, micros, scratch=(), grant=40, aliases=None):
+def call(body, outs, operands, name, micros, scratch=(), grant=40):
     specs = tuple(spec for _, spec in outs)
     shapes = tuple(shape for shape, _ in outs)
     single = len(outs) == 1
@@ -48,7 +46,6 @@
         cost_estimate=pl.CostEstimate(
             flops=0, bytes_accessed=int(micros * 3e6), transcendentals=0
         ),
-        input_output_aliases=aliases or {},
         name=name,
     )(*[operand for operand, _ in operands])
 
@@ -252,7 +249,7 @@
 
 
 def backward_kernel(
-    pair, s0, s1, s2, s3, normal_hbm, gain_hbm, head_gain_hbm,
+    s0, s1, s2, s3, normal_hbm, gain_hbm, head_gain_hbm,
     filtered_hbm, mean_hbm, inverse_hbm, kernel_hbm, after_hbm,
     out_hbm,
     blocks_ref, normal_ref, gain_ref, head_gain_ref, filtered_ref, mean_ref, inverse_ref, kernel_ref,
@@ -263,7 +260,6 @@
     images, channels = even_ref.shape
     blocks = (s0, s1, s2, s3)
     share = channels // len(PEERS)
-    cells = pl.ds(pair * 2 * CELLS, 2 * CELLS)
     wide = channels // STEPS
 
     def block_at(step):
@@ -271,7 +267,7 @@
 
     def out_copy(step):
         at = block_at(step)
-        return pltpu.make_async_copy(out_ref.at[:, at], out_hbm.at[cells, at], out_sems.at[step])
+        return pltpu.make_async_copy(out_ref.at[:, at], out_hbm.at[:, at], out_sems.at[step])
 
     head_copies = [
         pltpu.make_async_copy(block, blocks_ref.at[index], block_sems.at[index])
@@ -281,12 +277,12 @@
         pltpu.make_async_copy(source, target, small_sems.at[index])
         for index, (source, target) in enumerate((
             (head_gain_hbm, head_gain_ref), (gain_hbm, gain_ref), (normal_hbm, normal_ref),
-            (mean_hbm.at[cells, :], mean_ref), (inverse_hbm.at[cells, :], inverse_ref),
+            (mean_hbm, mean_ref), (inverse_hbm, inverse_ref),
         ))
     ]
     filtered_copies = [
         pltpu.make_async_copy(
-            filtered_hbm.at[cells, block_at(step)], filtered_ref.at[:, block_at(step)],
+            filtered_hbm.at[:, block_at(step)], filtered_ref.at[:, block_at(step)],
             filtered_sems.at[step],
         )
         for step in range(STEPS)
@@ -318,13 +314,13 @@
 
     for step in range(STEPS):
         filtered_copies[step].wait()
-        for image in range(2):
+        for image in range(images):
             spot = pl.ds(image * CELLS, CELLS)
             average = mean_ref[spot, :]
 
             def lean_chunk(chunk, total, spot=spot, average=average, image=image):
                 at = pl.ds(pl.multiple_of(chunk * LANES, LANES), LANES)
-                return total + (filtered_ref[spot, at] - average) * pull_ref[pl.ds(2 * pair + image, 1), at]
+                return total + (filtered_ref[spot, at] - average) * pull_ref[pl.ds(image, 1), at]
 
             total = jnp.zeros((CELLS, LANES), F32) if step == 0 else lean_ref[spot, :]
             lean_ref[spot, :] = lax.fori_loop(
@@ -337,27 +333,27 @@
 
     def filter_chunk(chunk, carry):
         at = pl.ds(pl.multiple_of(chunk * LANES, LANES), LANES)
-        fields = []
-        sums = []
-        for image in range(2):
-            source = pl.ds(2 * pair + image, 1)
-            tilt = jnp.broadcast_to(tilt_ref[source, at], (SIDE, LANES))
-            even = jnp.broadcast_to(even_ref[source, at], (SIDE, LANES))
-            rows = []
-            for row in range(SIDE):
-                spot = pl.ds(image * CELLS + row * SIDE, SIDE)
-                rows.append(
-                    inverse_ref[spot, :] * tilt
-                    - lean_ref[spot, :] * (filtered_ref[spot, at] - mean_ref[spot, :])
-                )
-            fields.append(rows)
-            sums.append([even] * SIDE)
-        filter_rows(fields, sums, kernel_ref, at, True)
-        for image, total in enumerate(sums):
-            for half in range(SIDE // 2):
-                two = jnp.concatenate(total[2 * half : 2 * half + 2], axis=0)
-                spot = pl.ds(image * CELLS + half * 2 * SIDE, 2 * SIDE)
-                out_ref[spot, at] = two.astype(jnp.bfloat16)
+        for first in range(0, images, 2):
+            fields = []
+            sums = []
+            for image in range(first, first + 2):
+                tilt = jnp.broadcast_to(tilt_ref[pl.ds(image, 1), at], (SIDE, LANES))
+                even = jnp.broadcast_to(even_ref[pl.ds(image, 1), at], (SIDE, LANES))
+                rows = []
+                for row in range(SIDE):
+                    spot = pl.ds(image * CELLS + row * SIDE, SIDE)
+                    rows.append(
+                        inverse_ref[spot, :] * tilt
+                        - lean_ref[spot, :] * (filtered_ref[spot, at] - mean_ref[spot, :])
+                    )
+                fields.append(rows)
+                sums.append([even] * SIDE)
+            filter_rows(fields, sums, kernel_ref, at, True)
+            for offset, total in enumerate(sums):
+                for half in range(SIDE // 2):
+                    two = jnp.concatenate(total[2 * half : 2 * half + 2], axis=0)
+                    spot = pl.ds((first + offset) * CELLS + half * 2 * SIDE, 2 * SIDE)
+                    out_ref[spot, at] = two.astype(jnp.bfloat16)
         step = chunk // per_block
 
         @pl.when(chunk == step * per_block + per_block - 1)
@@ -371,44 +367,32 @@
         out_copy(step).wait()
 
 
-def first_backward(pair, *refs):
-    backward_kernel(pair, *refs)
-
-
-def second_backward(pair, *refs):
-    backward_kernel(pair, *refs[:12], *refs[13:])
-
-
-def block_backward(pair, blocks, normal, norm_gain, head_gain, filtered, mean, inverse, kernel, after, held=None):
+def block_backward(blocks, normal, norm_gain, head_gain, filtered, mean, inverse, kernel, after):
     cells, channels = filtered.shape
     images = cells // CELLS
-    some = 2 * CELLS
     dma = pltpu.SemaphoreType.DMA
     operands = [
         *blocks, normal, norm_gain.reshape(1, channels), head_gain.reshape(1, channels),
         filtered, mean, inverse, kernel, after,
     ]
-    body = first_backward if held is None else second_backward
-    if held is not None:
-        operands.append(held)
     return call(
-        functools.partial(body, pair),
+        backward_kernel,
         ((shape_of((cells, channels), BF16), HBM),),
         tuple((array, HBM) for array in operands),
         "block_backward",
-        8,
+        14,
         scratch=(
             pltpu.VMEM((len(blocks),) + blocks[0].shape, F32),
             pltpu.VMEM(normal.shape, F32),
             pltpu.VMEM((1, channels), F32),
             pltpu.VMEM((1, channels), F32),
-            pltpu.VMEM((some, channels), F32),
-            pltpu.VMEM((some, LANES), F32),
-            pltpu.VMEM((some, LANES), F32),
+            pltpu.VMEM((cells, channels), F32),
+            pltpu.VMEM((cells, LANES), F32),
+            pltpu.VMEM((cells, LANES), F32),
             pltpu.VMEM(kernel.shape, F32),
-            pltpu.VMEM((some, channels), BF16),
+            pltpu.VMEM((cells, channels), BF16),
             pltpu.VMEM((images, channels), F32),
-            pltpu.VMEM((some, LANES), F32),
+            pltpu.VMEM((cells, LANES), F32),
             pltpu.VMEM((images, channels), F32),
             pltpu.VMEM((images, channels), F32),
             dma((len(blocks),)),
@@ -417,7 +401,6 @@
             dma((STEPS,)),
         ),
         grant=BIG,
-        aliases={} if held is None else {len(operands) - 1: 0},
     )
 
 
@@ -710,8 +693,7 @@
     )
     blocks = [merged[0]] + [along_x(merged[step], step) for step in (1, 2, 3)]
     shared = (normal, norm_gain, head_gain, filtered, mean, inverse, kernel)
-    held = block_backward(0, blocks, *shared, mean)
-    strips, held = lax.optimization_barrier((strips, held))
+    strips, *blocks = lax.optimization_barrier((strips, *blocks))
     sums, mine, theirs = call(
         strip_kernel,
         (
@@ -729,7 +711,7 @@
         ((text_embed, VMEM), (mine, VMEM), (swap_core(theirs), VMEM), (logit_scale, SMEM)),
         "text_grad", 1,
     )
-    grad_features = block_backward(1, blocks, *shared, mine, held)
+    grad_features = block_backward(blocks, *shared, mine)
     near_half, grad_features, grad_text = lax.optimization_barrier(
         (near_half, grad_features, grad_text)
     )

time: 127 us -> 124 us (0.976)
  starting transfers between devices: 64.9 us -> 56.6 us
  waiting for transfers between devices: 7.02 us -> 14 us
  Pallas kernels: 40.3 us -> 38.7 us
    ppermute x8, starting transfers between devices: 23.1 us -> 17.2 us  [swap_core(): return lax.ppermute(block, 'core', ((0, 1), (1, 0)))]
    all_to_all x4, waiting for transfers between devices: 0.67 us -> 5.64 us  [exchange(): return lax.all_to_all(blocks, axes, 0, 0, tiled=True)]
    all_to_all x4, starting transfers between devices: 30.2 us -> 28 us  [exchange(): return lax.all_to_all(blocks, axes, 0, 0, tiled=True)]
    pallas_call x13 -> x12, Pallas kernels: 40.3 us -> 38.7 us  [call(): pl.pallas_call(body, out_shape=shapes[0] if single else shapes, in_specs=...]
  transfers between devices with their start and end apart: 20 -> 20, of which waited for: 8 -> 9; matrix products, arithmetic and copies ran while one was open for 0% -> 0% of each run, Pallas kernels for 25% -> 25%
where the time goes in v5:
time: 124 us; the launch traced here: 123 us
  starting transfers between devices  56.6 us (46%)
  Pallas kernels  38.7 us (31%)
  waiting for transfers between devices  14 us (11%)
  blocking collectives  10.7 us (9%)
  between operations  2.09 us (2%)
    pallas_call x12, Pallas kernels, call(): pl.pallas_call(body, out_shape=shapes[0] if single else shapes, in_specs=...  38.7 us
    all_to_all x4, starting transfers between devices, exchange(): return lax.all_to_all(blocks, axes, 0, 0, tiled=True)  28 us
    ppermute x8, starting transfers between devices, swap_core(): return lax.ppermute(block, 'core', ((0, 1), (1, 0)))  17.2 us
    all_to_all x1, blocking collectives, exchange(): return lax.all_to_all(blocks, axes, 0, 0, tiled=True)  10.7 us
    ppermute x6, starting transfers between devices, along_x(): lax.ppermute(block, 'x', tuple(((i, (i + step) % 4) for i in range(4))))  6.71 us
    all_to_all x4, waiting for transfers between devices, exchange(): return lax.all_to_all(blocks, axes, 0, 0, tiled=True)  5.64 us
    ppermute x8, waiting for transfers between devices, swap_core(): return lax.ppermute(block, 'core', ((0, 1), (1, 0)))  3.17 us
    ppermute x6, waiting for transfers between devices, along_x(): lax.ppermute(block, 'x', tuple(((i, (i + step) % 4) for i in range(4))))  2.84 us
  transfers between devices with their start and end apart: 20, of which 9 were waited for; matrix products, arithmetic and copies ran while one was open for 0% of the time, Pallas kernels for 25%

profile of v5, /device:TPU:1, one launch (start us, length us, event | category | flops | bytes accessed | tf_op | source)
XLA Modules:
  0.0 123.3 jit_solution(16832644057375435771)
XLA Ops:
  0.6 0.0 copy-start
  0.6 1.6 %text_pack.1 = bf16[16,4,1280]{2,1,0:T(4,128)(2,1)} custom-call(bf16[4,1152]{1,0:T(4,128)(2,1)} %text_ref.1, s32[4]{0:T(128)} %ids_hbm.2), custom_call_target="tpu_custom_call" | custom-call | bytes 3000000 | tf_op jit(solution)/shard_map/text_pack/pallas_call | solution.py:39
  2.2 10.1 %all-to-all-start = ((bf16[16,4,1280]{2,1,0:T(4,128)(2,1)}), bf16[16,4,1280]{2,1,0:T(4,128)(2,1)S(1)}, u32[]{:S(2)}, u32[]{:S(2)}) async-start(bf16[16,4,1280]{2,1,0:T(4,128)(2,1)} %text_pack.1), calls=%async_computation | async-start | bytes 327680 | tf_op jit(solution)/shard_map/all_to_all | solution.py:587
  12.4 14.9 %block_forward.1 = (f32[256,3072]{1,0:T(8,128)}, f32[256,128]{1,0:T(8,128)}, f32[256,128]{1,0:T(8,128)}, f32[4,3200]{1,0:T(4,128)}, bf16[8,4,512]{2,1,0:T(4,128)(2,1)}) custom-call(bf16[256,3072]{1,0:T(8,128)(2,1)} %bitcast.7, f32[7,7,3072]{2,1,0:T(8,128)} %kernel_hbm.3, f32[1,3072]{1,0:T(1,128)} %bitcast.9, f32[1,3072]{1,0:T(1,128)} %bitcast.11, s32[4]{0:T(128)} %ids_hbm.3), custom_call_target="tpu_custom_call" | custom-call | bytes 42000000 | tf_op jit(solution)/shard_map/block_forward/pallas_call | solution.py:39
  27.3 0.0 all-to-all-done.line_ref
  27.4 2.7 %collective-permute-start = (bf16[64,1280]{1,0:T(8,128)(2,1)S(1)}, bf16[64,1280]{1,0:T(8,128)(2,1)S(1)}, u32[]{:S(2)}, u32[]{:S(2)}) collective-permute-start(bf16[64,1280]{1,0:T(8,128)(2,1)S(1)} %line_rows.1.own_ref), channel_id=1, source_target_pairs={{0,1},{1,0},{2,3},{3,2},{4,5},{5,4},{6,7},{7,6},{8,9},{9,8},{10,11... | collective-permute-start | bytes 491528 | tf_op jit(solution)/shard_map/ppermute | solution.py:649
  30.1 10.7 %all_to_all.25.received_ref = bf16[8,4,512]{2,1,0:T(4,128)(2,1)S(1)} all-to-all(bf16[8,4,512]{2,1,0:T(4,128)(2,1)} %get-tuple-element.32), channel_id=1, replica_groups=mesh['y_lo'=2,'z'=8,'core'=2,'x'=4,'y_hi'=2] {'x','y_hi'}, dimensions={0} | all-to-all | bytes 65536 | tf_op jit(solution)/shard_map/all_to_all | solution.py:587
  40.8 0.0 copy-done
  40.8 1.1 partial_embed.1
  41.9 0.0 collective-permute-done.next_ref
  41.9 0.4 collective-permute-start.1
  42.2 2.4 %collective-permute-start.2 = (bf16[128,1280]{1,0:T(8,128)(2,1)S(1)}, bf16[128,1280]{1,0:T(8,128)(2,1)S(1)}, u32[]{:S(2)}, u32[]{:S(2)}) collective-permute-start(bf16[128,1280]{1,0:T(8,128)(2,1)S(1)} %join_texts.1.t0), channel_id=1, source_target_pairs={{0,6},{2,0},{4,2},{6,4},{1,7},{3,1},{5,3},{7,5},{8,14},{10,8},{12,... | collective-permute-start | bytes 983048 | tf_op jit(solution)/shard_map/ppermute | solution.py:595
  44.6 0.0 collective-permute-start.3
  44.6 4.4 %all-to-all-start.2 = ((bf16[8,32,1152]{2,1,0:T(8,128)(2,1)}), bf16[8,32,1152]{2,1,0:T(8,128)(2,1)S(1)}, u32[]{:S(2)}, u32[]{:S(2)}) async-start(bf16[8,32,1152]{2,1,0:T(8,128)(2,1)} %get-tuple-element.33), calls=%async_computation.2 | async-start | bytes 1179648 | tf_op jit(solution)/shard_map/all_to_all | solution.py:587
  49.0 3.8 %collective-permute-start.4 = (bf16[128,1280]{1,0:T(8,128)(2,1)S(1)}, bf16[128,1280]{1,0:T(8,128)(2,1)S(1)}, u32[]{:S(2)}, u32[]{:S(2)}) collective-permute-start(bf16[128,1280]{1,0:T(8,128)(2,1)S(1)} %join_texts.1.t0), channel_id=1, source_target_pairs={{0,8},{8,0},{1,9},{9,1},{2,10},{10,2},{3,11},{11,3},{4,12},{12,4},... | collective-permute-start | bytes 983048 | tf_op jit(solution)/shard_map/ppermute | solution.py:591
  52.8 0.0 collective-permute-done.1.t1
  52.8 10.7 %collective-permute-start.5 = (bf16[128,1280]{1,0:T(8,128)(2,1)S(1)}, bf16[128,1280]{1,0:T(8,128)(2,1)S(1)}, u32[]{:S(2)}, u32[]{:S(2)}) collective-permute-start(bf16[128,1280]{1,0:T(8,128)(2,1)S(1)} %collective-permute-done.1.t1), channel_id=1, source_target_pairs={{0,8},{8,0},{1,9},{9,1},{2,10},{10,2},{3,11},{11,3},{4,12},{12,4},... | collective-permute-start | bytes 983048 | tf_op jit(solution)/shard_map/ppermute | solution.py:591
  63.5 0.0 collective-permute-done.2.t2
  63.5 0.0 collective-permute-start.6
  63.5 0.0 collective-permute-done.3.t3
  63.5 0.5 collective-permute-start.7
  65.3 0.0 collective-permute-done.4.t4
  65.3 0.1 all-to-all-done.2.partials_ref
  65.4 0.0 collective-permute-done.5.t5
  65.4 0.0 collective-permute-done.6.t6
  65.4 0.4 collective-permute-done.7.t7
  65.8 3.0 %pairs.1 = (f32[4,4,384]{2,1,0:T(4,128)S(1)}, f32[4,4,384]{2,1,0:T(4,128)S(1)}, bf16[32,2560]{1,0:T(8,128)(2,1)S(1)}) custom-call(bf16[8,32,1152]{2,1,0:T(8,128)(2,1)S(1)} %all-to-all-done.2.partials_ref, bf16[32,128]{1,0:T(8,128)(2,1)S(1)} %get-tuple-element.34.hot_ref, bf16[384,1152]{1,0:T(8,128)(2,1)S(1)} %copy-done, bf16[128,1280]{1,0:T(8,128)(2,1)S(1)} %join_texts.1.t0, ...), custom_call_target="tpu_custom_call" | custom-call | bytes 12000000 | tf_op jit(solution)/shard_map/pairs/pallas_call | solution.py:39
  68.8 1.1 collective-permute-start.8
  69.9 0.1 collective-permute-start.9
  70.0 1.1 collective-permute-done.9.far_columns_ref
  71.1 0.0 collective-permute-done.8.theirs_ref
  71.1 1.2 strip_make.1
  72.3 7.6 %all-to-all-start.3 = ((bf16[16,32,640]{2,1,0:T(8,128)(2,1)}), bf16[16,32,640]{2,1,0:T(8,128)(2,1)S(1)}, u32[]{:S(2)}, u32[]{:S(2)}) async-start(bf16[16,32,640]{2,1,0:T(8,128)(2,1)} %strip_make.1), calls=%async_computation.3 | async-start | bytes 1310720 | tf_op jit(solution)/shard_map/all_to_all | solution.py:587
  79.9 1.9 %collective-permute-start.10 = (f32[4,4,384]{2,1,0:T(4,128)S(1)}, f32[4,4,384]{2,1,0:T(4,128)S(1)}, u32[]{:S(2)}, u32[]{:S(2)}) collective-permute-start(f32[4,4,384]{2,1,0:T(4,128)S(1)} %get-tuple-element.39), channel_id=1, source_target_pairs={{0,1},{1,0},{2,3},{3,2},{4,5},{5,4},{6,7},{7,6},{8,9},{9,8},{10,11... | collective-permute-start | bytes 73736 | tf_op jit(solution)/shard_map/ppermute | solution.py:675
  81.8 2.4 %collective-permute-done.10.got_ref = f32[4,4,384]{2,1,0:T(4,128)S(1)} collective-permute-done((f32[4,4,384]{2,1,0:T(4,128)S(1)}, f32[4,4,384]{2,1,0:T(4,128)S(1)}, u32[]{:S(2)}, u32[]{:S(2)}) %collective-permute-start.10) | collective-permute-done | bytes 24608 | tf_op jit(solution)/shard_map/ppermute | solution.py:675
  84.2 0.0 copy-start.4
  84.2 0.6 copy-done.4
  84.8 0.4 collective-permute-start.11
  85.2 3.5 %collective-permute-start.12 = (f32[2,4,384]{2,1,0:T(4,128)S(1)}, f32[2,4,384]{2,1,0:T(4,128)S(1)}, u32[]{:S(2)}, u32[]{:S(2)}) collective-permute-start(f32[2,4,384]{2,1,0:T(4,128)S(1)} %get-tuple-element.42), channel_id=1, source_target_pairs={{0,4},{2,6},{4,0},{6,2},{1,5},{3,7},{5,1},{7,3},{8,12},{10,14},{12... | collective-permute-start | bytes 36872 | tf_op jit(solution)/shard_map/ppermute | solution.py:595
  88.7 0.0 collective-permute-start.13
  88.7 0.2 collective-permute-done.11.s1
  88.9 0.0 copy-start.5
  88.9 1.3 %collective-permute-done.12.s2 = f32[2,4,384]{2,1,0:T(4,128)S(1)} collective-permute-done((f32[2,4,384]{2,1,0:T(4,128)S(1)}, f32[2,4,384]{2,1,0:T(4,128)S(1)}, u32[]{:S(2)}, u32[]{:S(2)}) %collective-permute-start.12) | collective-permute-done | bytes 12320 | tf_op jit(solution)/shard_map/ppermute | solution.py:595
  90.2 0.0 copy-start.6
  90.2 1.3 %collective-permute-done.13.s3 = f32[2,4,384]{2,1,0:T(4,128)S(1)} collective-permute-done((f32[2,4,384]{2,1,0:T(4,128)S(1)}, f32[2,4,384]{2,1,0:T(4,128)S(1)}, u32[]{:S(2)}, u32[]{:S(2)}) %collective-permute-start.13) | collective-permute-done | bytes 12320 | tf_op jit(solution)/shard_map/ppermute | solution.py:595
  91.6 0.0 copy-start.7
  91.6 5.6 %all-to-all-done.3.strips_ref = bf16[16,32,640]{2,1,0:T(8,128)(2,1)S(1)} async-done(((bf16[16,32,640]{2,1,0:T(8,128)(2,1)}), bf16[16,32,640]{2,1,0:T(8,128)(2,1)S(1)}, u32[]{:S(2)}, u32[]{:S(2)}) %all-to-all-start.3) | async-done | bytes 655392 | tf_op jit(solution)/shard_map/all_to_all | solution.py:587
  97.1 0.9 strip_sum.1
  98.0 0.6 copy-done.1
  98.6 5.9 %all-to-all-start.4 = ((bf16[16,24,640]{2,1,0:T(8,128)(2,1)}), bf16[16,24,640]{2,1,0:T(8,128)(2,1)S(1)}, u32[]{:S(2)}, u32[]{:S(2)}) async-start(bf16[16,24,640]{2,1,0:T(8,128)(2,1)} %get-tuple-element.45), calls=%async_computation.4 | async-start | bytes 983040 | tf_op jit(solution)/shard_map/all_to_all | solution.py:587
  104.5 0.9 collective-permute-start.14
  105.4 0.0 copy-done.5
  105.4 0.0 copy-done.6
  105.4 0.0 copy-done.7
  105.4 0.0 copy-start.3
  105.4 13.8 %block_backward.1 = bf16[256,3072]{1,0:T(8,128)(2,1)} custom-call(f32[2,4,384]{2,1,0:T(4,128)} %copy-done.4, f32[2,4,384]{2,1,0:T(4,128)} %copy-done.5, f32[2,4,384]{2,1,0:T(4,128)} %copy-done.6, f32[2,4,384]{2,1,0:T(4,128)} %copy-done.7, f32[4,3200]{1,0:T(4,128)} %get-tuple-element.50.normal_hbm, f32[1,3072]{1,0:T(1,128)} %bitcast.10, f32[1,3072]{1,0:T(1,128)} %bitcast.12, ...), custom_call_target="tpu_custom_call" | custom-call | bytes 42000000 | tf_op jit(solution)/shard_map/block_backward/pallas_call | solution.py:39
  119.2 0.0 collective-permute-done.14.got_ref
  119.3 0.0 copy-done.2
  119.3 0.0 copy-done.3
  119.3 0.8 text_grad.1
  120.1 0.0 all-to-all-done.4
  120.1 0.2 collective-permute-start.15
  120.3 1.6 %collective-permute-done.15.far_ref = bf16[384,640]{1,0:T(8,128)(2,1)S(1)} collective-permute-done((bf16[384,640]{1,0:T(8,128)(2,1)S(1)}, bf16[384,640]{1,0:T(8,128)(2,1)S(1)}, u32[]{:S(2)}, u32[]{:S(2)}) %collective-permute-start.15) | collective-permute-done | bytes 491552 | tf_op jit(solution)/shard_map/ppermute | solution.py:591
  121.9 1.3 %proj_join.1 = f32[384,1152]{1,0:T(8,128)} custom-call(bf16[384,640]{1,0:T(8,128)(2,1)S(1)} %bitcast.6, bf16[384,640]{1,0:T(8,128)(2,1)S(1)} %collective-permute-done.15.far_ref), custom_call_target="tpu_custom_call" | custom-call | bytes 6000000 | tf_op jit(solution)/shard_map/proj_join/pallas_call | solution.py:39
  (5 shorter events, 0.1 us)
Async XLA Ops:
  0.6 40.1 %copy-start = (bf16[384,1152]{1,0:T(8,128)(2,1)S(1)}, bf16[384,1152]{1,0:T(8,128)(2,1)}, u32[]{:S(2)}) copy-start(bf16[384,1152]{1,0:T(8,128)(2,1)} %projection_ref.3) | copy-start | bytes 2654212
  2.2 25.1 %all-to-all-start = ((bf16[16,4,1280]{2,1,0:T(4,128)(2,1)}), bf16[16,4,1280]{2,1,0:T(4,128)(2,1)S(1)}, u32[]{:S(2)}, u32[]{:S(2)}) async-start(bf16[16,4,1280]{2,1,0:T(4,128)(2,1)} %text_pack.1), calls=%async_computation | async-start | bytes 327680 | tf_op jit(solution)/shard_map/all_to_all | solution.py:587
  27.4 14.5 %collective-permute-start = (bf16[64,1280]{1,0:T(8,128)(2,1)S(1)}, bf16[64,1280]{1,0:T(8,128)(2,1)S(1)}, u32[]{:S(2)}, u32[]{:S(2)}) collective-permute-start(bf16[64,1280]{1,0:T(8,128)(2,1)S(1)} %line_rows.1.own_ref), channel_id=1, source_target_pairs={{0,1},{1,0},{2,3},{3,2},{4,5},{5,4},{6,7},{7,6},{8,9},{9,8},{10,11... | collective-permute-start | bytes 491528 | tf_op jit(solution)/shard_map/ppermute | solution.py:649
  41.9 10.9 %collective-permute-start.1 = (bf16[128,1280]{1,0:T(8,128)(2,1)S(1)}, bf16[128,1280]{1,0:T(8,128)(2,1)S(1)}, u32[]{:S(2)}, u32[]{:S(2)}) collective-permute-start(bf16[128,1280]{1,0:T(8,128)(2,1)S(1)} %join_texts.1.t0), channel_id=1, source_target_pairs={{0,2},{2,4},{4,6},{6,0},{1,3},{3,5},{5,7},{7,1},{8,10},{10,12},{12... | collective-permute-start | bytes 983048 | tf_op jit(solution)/shard_map/ppermute | solution.py:595
  42.2 21.2 %collective-permute-start.2 = (bf16[128,1280]{1,0:T(8,128)(2,1)S(1)}, bf16[128,1280]{1,0:T(8,128)(2,1)S(1)}, u32[]{:S(2)}, u32[]{:S(2)}) collective-permute-start(bf16[128,1280]{1,0:T(8,128)(2,1)S(1)} %join_texts.1.t0), channel_id=1, source_target_pairs={{0,6},{2,0},{4,2},{6,4},{1,7},{3,1},{5,3},{7,5},{8,14},{10,8},{12,... | collective-permute-start | bytes 983048 | tf_op jit(solution)/shard_map/ppermute | solution.py:595
  44.6 18.9 %collective-permute-start.3 = (bf16[128,1280]{1,0:T(8,128)(2,1)S(1)}, bf16[128,1280]{1,0:T(8,128)(2,1)S(1)}, u32[]{:S(2)}, u32[]{:S(2)}) collective-permute-start(bf16[128,1280]{1,0:T(8,128)(2,1)S(1)} %join_texts.1.t0), channel_id=1, source_target_pairs={{0,4},{2,6},{4,0},{6,2},{1,5},{3,7},{5,1},{7,3},{8,12},{10,14},{12... | collective-permute-start | bytes 983048 | tf_op jit(solution)/shard_map/ppermute | solution.py:595
  44.6 20.7 %all-to-all-start.2 = ((bf16[8,32,1152]{2,1,0:T(8,128)(2,1)}), bf16[8,32,1152]{2,1,0:T(8,128)(2,1)S(1)}, u32[]{:S(2)}, u32[]{:S(2)}) async-start(bf16[8,32,1152]{2,1,0:T(8,128)(2,1)} %get-tuple-element.33), calls=%async_computation.2 | async-start | bytes 1179648 | tf_op jit(solution)/shard_map/all_to_all | solution.py:587
  49.0 16.3 %collective-permute-start.4 = (bf16[128,1280]{1,0:T(8,128)(2,1)S(1)}, bf16[128,1280]{1,0:T(8,128)(2,1)S(1)}, u32[]{:S(2)}, u32[]{:S(2)}) collective-permute-start(bf16[128,1280]{1,0:T(8,128)(2,1)S(1)} %join_texts.1.t0), channel_id=1, source_target_pairs={{0,8},{8,0},{1,9},{9,1},{2,10},{10,2},{3,11},{11,3},{4,12},{12,4},... | collective-permute-start | bytes 983048 | tf_op jit(solution)/shard_map/ppermute | solution.py:591
  52.8 12.6 %collective-permute-start.5 = (bf16[128,1280]{1,0:T(8,128)(2,1)S(1)}, bf16[128,1280]{1,0:T(8,128)(2,1)S(1)}, u32[]{:S(2)}, u32[]{:S(2)}) collective-permute-start(bf16[128,1280]{1,0:T(8,128)(2,1)S(1)} %collective-permute-done.1.t1), channel_id=1, source_target_pairs={{0,8},{8,0},{1,9},{9,1},{2,10},{10,2},{3,11},{11,3},{4,12},{12,4},... | collective-permute-start | bytes 983048 | tf_op jit(solution)/shard_map/ppermute | solution.py:591
  63.5 1.9 %collective-permute-start.6 = (bf16[128,1280]{1,0:T(8,128)(2,1)S(1)}, bf16[128,1280]{1,0:T(8,128)(2,1)}, u32[]{:S(2)}, u32[]{:S(2)}) collective-permute-start(bf16[128,1280]{1,0:T(8,128)(2,1)S(1)} %collective-permute-done.2.t2), channel_id=1, source_target_pairs={{0,8},{8,0},{1,9},{9,1},{2,10},{10,2},{3,11},{11,3},{4,12},{12,4},... | collective-permute-start | bytes 983048 | tf_op jit(solution)/shard_map/ppermute | solution.py:591
  63.5 2.3 %collective-permute-start.7 = (bf16[128,1280]{1,0:T(8,128)(2,1)S(1)}, bf16[128,1280]{1,0:T(8,128)(2,1)}, u32[]{:S(2)}, u32[]{:S(2)}) collective-permute-start(bf16[128,1280]{1,0:T(8,128)(2,1)S(1)} %collective-permute-done.3.t3), channel_id=1, source_target_pairs={{0,8},{8,0},{1,9},{9,1},{2,10},{10,2},{3,11},{11,3},{4,12},{12,4},... | collective-permute-start | bytes 983048 | tf_op jit(solution)/shard_map/ppermute | solution.py:591
  68.8 2.3 %collective-permute-start.8 = (bf16[32,2560]{1,0:T(8,128)(2,1)S(1)}, bf16[32,2560]{1,0:T(8,128)(2,1)S(1)}, u32[]{:S(2)}, u32[]{:S(2)}) collective-permute-start(bf16[32,2560]{1,0:T(8,128)(2,1)S(1)} %get-tuple-element.37.mine_ref), channel_id=1, source_target_pairs={{0,8},{8,0},{1,9},{9,1},{2,10},{10,2},{3,11},{11,3},{4,12},{12,4},... | collective-permute-start | bytes 491528 | tf_op jit(solution)/shard_map/ppermute | solution.py:591
  69.9 1.2 collective-permute-start.9
  72.3 24.8 %all-to-all-start.3 = ((bf16[16,32,640]{2,1,0:T(8,128)(2,1)}), bf16[16,32,640]{2,1,0:T(8,128)(2,1)S(1)}, u32[]{:S(2)}, u32[]{:S(2)}) async-start(bf16[16,32,640]{2,1,0:T(8,128)(2,1)} %strip_make.1), calls=%async_computation.3 | async-start | bytes 1310720 | tf_op jit(solution)/shard_map/all_to_all | solution.py:587
  79.9 4.3 %collective-permute-start.10 = (f32[4,4,384]{2,1,0:T(4,128)S(1)}, f32[4,4,384]{2,1,0:T(4,128)S(1)}, u32[]{:S(2)}, u32[]{:S(2)}) collective-permute-start(f32[4,4,384]{2,1,0:T(4,128)S(1)} %get-tuple-element.39), channel_id=1, source_target_pairs={{0,1},{1,0},{2,3},{3,2},{4,5},{5,4},{6,7},{7,6},{8,9},{9,8},{10,11... | collective-permute-start | bytes 73736 | tf_op jit(solution)/shard_map/ppermute | solution.py:675
  84.2 0.6 copy-start.4
  84.8 4.1 %collective-permute-start.11 = (f32[2,4,384]{2,1,0:T(4,128)S(1)}, f32[2,4,384]{2,1,0:T(4,128)S(1)}, u32[]{:S(2)}, u32[]{:S(2)}) collective-permute-start(f32[2,4,384]{2,1,0:T(4,128)S(1)} %get-tuple-element.41), channel_id=1, source_target_pairs={{0,2},{2,4},{4,6},{6,0},{1,3},{3,5},{5,7},{7,1},{8,10},{10,12},{12... | collective-permute-start | bytes 36872 | tf_op jit(solution)/shard_map/ppermute | solution.py:595
  85.2 5.0 %collective-permute-start.12 = (f32[2,4,384]{2,1,0:T(4,128)S(1)}, f32[2,4,384]{2,1,0:T(4,128)S(1)}, u32[]{:S(2)}, u32[]{:S(2)}) collective-permute-start(f32[2,4,384]{2,1,0:T(4,128)S(1)} %get-tuple-element.42), channel_id=1, source_target_pairs={{0,4},{2,6},{4,0},{6,2},{1,5},{3,7},{5,1},{7,3},{8,12},{10,14},{12... | collective-permute-start | bytes 36872 | tf_op jit(solution)/shard_map/ppermute | solution.py:595
  88.7 2.8 %collective-permute-start.13 = (f32[2,4,384]{2,1,0:T(4,128)S(1)}, f32[2,4,384]{2,1,0:T(4,128)S(1)}, u32[]{:S(2)}, u32[]{:S(2)}) collective-permute-start(f32[2,4,384]{2,1,0:T(4,128)S(1)} %get-tuple-element.43), channel_id=1, source_target_pairs={{0,6},{2,0},{4,2},{6,4},{1,7},{3,1},{5,3},{7,5},{8,14},{10,8},{12,... | collective-permute-start | bytes 36872 | tf_op jit(solution)/shard_map/ppermute | solution.py:595
  88.9 16.5 %copy-start.5 = (f32[2,4,384]{2,1,0:T(4,128)}, f32[2,4,384]{2,1,0:T(4,128)S(1)}, u32[]{:S(2)}) copy-start(f32[2,4,384]{2,1,0:T(4,128)S(1)} %collective-permute-done.11.s1) | copy-start | bytes 36868
  90.2 15.2 %copy-start.6 = (f32[2,4,384]{2,1,0:T(4,128)}, f32[2,4,384]{2,1,0:T(4,128)S(1)}, u32[]{:S(2)}) copy-start(f32[2,4,384]{2,1,0:T(4,128)S(1)} %collective-permute-done.12.s2) | copy-start | bytes 36868
  91.6 13.8 %copy-start.7 = (f32[2,4,384]{2,1,0:T(4,128)}, f32[2,4,384]{2,1,0:T(4,128)S(1)}, u32[]{:S(2)}) copy-start(f32[2,4,384]{2,1,0:T(4,128)S(1)} %collective-permute-done.13.s3) | copy-start | bytes 36868
  98.0 0.6 copy-start.1
  98.6 21.5 %all-to-all-start.4 = ((bf16[16,24,640]{2,1,0:T(8,128)(2,1)}), bf16[16,24,640]{2,1,0:T(8,128)(2,1)S(1)}, u32[]{:S(2)}, u32[]{:S(2)}) async-start(bf16[16,24,640]{2,1,0:T(8,128)(2,1)} %get-tuple-element.45), calls=%async_computation.4 | async-start | bytes 983040 | tf_op jit(solution)/shard_map/all_to_all | solution.py:587
  104.5 14.7 %collective-permute-start.14 = (f32[4,640]{1,0:T(4,128)S(1)}, f32[4,640]{1,0:T(4,128)S(1)}, u32[]{:S(2)}, u32[]{:S(2)}) collective-permute-start(f32[4,640]{1,0:T(4,128)S(1)} %get-tuple-element.55), channel_id=1, source_target_pairs={{0,8},{8,0},{1,9},{9,1},{2,10},{10,2},{3,11},{11,3},{4,12},{12,4},... | collective-permute-start | bytes 30728 | tf_op jit(solution)/shard_map/ppermute | solution.py:591
  105.4 13.8 %copy-start.2 = (f32[4,640]{1,0:T(4,128)S(1)}, f32[4,640]{1,0:T(4,128)}, u32[]{:S(2)}) copy-start(f32[4,640]{1,0:T(4,128)} %copy-done.1) | copy-start | bytes 30724
  105.4 13.8 %copy-start.3 = (bf16[4,1152]{1,0:T(4,128)(2,1)S(1)}, bf16[4,1152]{1,0:T(4,128)(2,1)}, u32[]{:S(2)}) copy-start(bf16[4,1152]{1,0:T(4,128)(2,1)} %text_ref.1) | copy-start | bytes 27652
  120.1 1.9 %collective-permute-start.15 = (bf16[384,640]{1,0:T(8,128)(2,1)S(1)}, bf16[384,640]{1,0:T(8,128)(2,1)S(1)}, u32[]{:S(2)}, u32[]{:S(2)}) collective-permute-start(bf16[384,640]{1,0:T(8,128)(2,1)S(1)} %bitcast.5), channel_id=1, source_target_pairs={{0,8},{8,0},{1,9},{9,1},{2,10},{10,2},{3,11},{11,3},{4,12},{12,4},... | collective-permute-start | bytes 1474568 | tf_op jit(solution)/shard_map/ppermute | solution.py:591

commit v6 on v5

--- a/solution.py
+++ b/solution.py
@@ -11,6 +11,8 @@
 ALL = AXES
 GROUP = ("x", "y_hi")
 LINE = ("y_lo", "z")
+PLANE = ("y_lo", "x", "y_hi")
+OWN = 16
 MIB = 1024 * 1024
 BIG = 60
 IDS = 128
@@ -83,9 +85,9 @@
 
 
 def forward_kernel(
-    field_hbm, kernel_hbm, gain_hbm, head_gain_hbm, ids_hbm,
-    filtered_hbm, mean_ref, inverse_ref, normal_ref, send_ref,
-    field_ref, kernel_ref, gain_ref, head_gain_ref, ids_ref, filtered_ref, pooled_ref, total_ref,
+    pair, field_hbm, kernel_hbm, gain_hbm,
+    filtered_hbm, mean_ref, inverse_ref,
+    field_ref, kernel_ref, gain_ref, filtered_ref, pooled_ref, total_ref,
     field_sems, kernel_sems, small_sems, out_sems,
 ):
     images = field_ref.shape[0] // CELLS
@@ -100,7 +102,7 @@
 
     def field_copy(step):
         at = block_at(step)
-        return pltpu.make_async_copy(field_hbm.at[:, at], field_ref.at[:, at], field_sems.at[step])
+        return pltpu.make_async_copy(field_hbm.at[pair * images * CELLS : (pair + 1) * images * CELLS, at], field_ref.at[:, at], field_sems.at[step])
 
     def kernel_copy(step):
         at = block_at(step)
@@ -112,11 +114,7 @@
         at = block_at(step)
         return pltpu.make_async_copy(filtered_ref.at[:, at], filtered_hbm.at[:, at], out_sems.at[step])
 
-    small_copies = [
-        pltpu.make_async_copy(gain_hbm, gain_ref, small_sems.at[0]),
-        pltpu.make_async_copy(head_gain_hbm, head_gain_ref, small_sems.at[1]),
-        pltpu.make_async_copy(ids_hbm, ids_ref, small_sems.at[2]),
-    ]
+    small_copies = [pltpu.make_async_copy(gain_hbm, gain_ref, small_sems.at[0])]
     for step in range(STEPS):
         field_copy(step).start()
         kernel_copy(step).start()
@@ -190,7 +188,43 @@
 
         lax.fori_loop(0, chunks, pool_chunk, 0, unroll=2)
 
-    pooled = pooled_ref[...]
+    for step in range(STEPS):
+        filtered_copy(step).wait()
+
+
+def first_forward(
+    field_hbm, kernel_hbm, gain_hbm, filtered_hbm, mean_ref, inverse_ref, pooled_ref, *scratch
+):
+    forward_kernel(
+        0, field_hbm, kernel_hbm, gain_hbm, filtered_hbm, mean_ref, inverse_ref,
+        *scratch[:4], pooled_ref, *scratch[4:],
+    )
+
+
+def second_forward(
+    field_hbm, kernel_hbm, gain_hbm, pooled_hbm, head_gain_hbm, ids_hbm, after_hbm,
+    filtered_hbm, mean_ref, inverse_ref, normal_ref, send_ref,
+    field_ref, kernel_ref, gain_ref, filtered_ref, total_ref, *rest,
+):
+    del after_hbm
+    sems, (late_ref, both_ref, head_gain_ref, ids_ref, late_sems) = rest[:4], rest[4:]
+    half, channels = late_ref.shape
+    images = 2 * half
+    part = 1.0 / channels
+    copies = [
+        pltpu.make_async_copy(pooled_hbm, both_ref, late_sems.at[0]),
+        pltpu.make_async_copy(head_gain_hbm, head_gain_ref, late_sems.at[1]),
+        pltpu.make_async_copy(ids_hbm, ids_ref, late_sems.at[2]),
+    ]
+    for copy in copies:
+        copy.start()
+    forward_kernel(
+        1, field_hbm, kernel_hbm, gain_hbm, filtered_hbm, mean_ref, inverse_ref,
+        field_ref, kernel_ref, gain_ref, filtered_ref, late_ref, total_ref, *sems,
+    )
+    for copy in copies:
+        copy.wait()
+    pooled = jnp.concatenate([both_ref[...], late_ref[...]], axis=0)
     centred = pooled - jnp.sum(pooled, axis=1, keepdims=True) * part
     spread = jnp.sum(centred * centred, axis=1, keepdims=True) * part
     head_inverse = lax.rsqrt(spread + EPSILON)
@@ -204,45 +238,72 @@
     for owner in range(group):
         send_ref[owner, :, :share] = head_input[:, owner * share : (owner + 1) * share]
         send_ref[owner, :, share:] = hot
-    for step in range(STEPS):
-        filtered_copy(step).wait()
-
-
-def block_forward(features, kernel, norm_gain, head_gain, img_ids, group):
+
+
+def forward_scratch(features, kernel):
+    cells, channels = features.shape[0] * CELLS // 2, features.shape[3]
+    return (
+        pltpu.VMEM((cells, channels), BF16),
+        pltpu.VMEM(kernel.shape, F32),
+        pltpu.VMEM((1, channels), F32),
+        pltpu.VMEM((cells, channels), F32),
+        pltpu.VMEM((cells, LANES), F32),
+        pltpu.SemaphoreType.DMA((STEPS,)),
+        pltpu.SemaphoreType.DMA((STEPS,)),
+        pltpu.SemaphoreType.DMA((1,)),
+        pltpu.SemaphoreType.DMA((STEPS,)),
+    )
+
+
+def forward_outs(features):
+    cells, channels = features.shape[0] * CELLS // 2, features.shape[3]
+    return (
+        (shape_of((cells, channels), F32), HBM),
+        (shape_of((cells, LANES), F32), VMEM),
+        (shape_of((cells, LANES), F32), VMEM),
+    )
+
+
+def forward_operands(features, kernel, norm_gain):
     images, channels = features.shape[0], features.shape[3]
-    cells = images * CELLS
-    dma = pltpu.SemaphoreType.DMA
+    return (
+        (features.reshape(images * CELLS, channels), HBM),
+        (kernel, HBM),
+        (norm_gain.reshape(1, channels), HBM),
+    )
+
+
+def block_forward_first(features, kernel, norm_gain):
+    images, channels = features.shape[0], features.shape[3]
     return call(
-        forward_kernel,
-        (
-            (shape_of((cells, channels), F32), HBM),
-            (shape_of((cells, LANES), F32), VMEM),
-            (shape_of((cells, LANES), F32), VMEM),
+        first_forward,
+        forward_outs(features) + ((shape_of((images // 2, channels), F32), VMEM),),
+        forward_operands(features, kernel, norm_gain),
+        "block_forward_first", 8,
+        scratch=forward_scratch(features, kernel),
+        grant=BIG,
+    )
+
+
+def block_forward_second(features, kernel, norm_gain, pooled, head_gain, img_ids, after, group):
+    images, channels = features.shape[0], features.shape[3]
+    return call(
+        second_forward,
+        forward_outs(features)
+        + (
             (shape_of((images, channels + LANES), F32), VMEM),
             (shape_of((group, images, channels // group + IDS), BF16), VMEM),
         ),
-        (
-            (features.reshape(cells, channels), HBM),
-            (kernel, HBM),
-            (norm_gain.reshape(1, channels), HBM),
-            (head_gain.reshape(1, channels), HBM),
-            (img_ids, HBM),
-        ),
-        "block_forward",
-        14,
-        scratch=(
-            pltpu.VMEM((cells, channels), BF16),
-            pltpu.VMEM(kernel.shape, F32),
-            pltpu.VMEM((1, channels), F32),
+        forward_operands(features, kernel, norm_gain)
+        + ((pooled, HBM), (head_gain.reshape(1, channels), HBM), (img_ids, HBM), (after, HBM)),
+        "block_forward_second", 8,
+        scratch=forward_scratch(features, kernel)
+        + (
+            pltpu.VMEM((images // 2, channels), F32),
+            pltpu.VMEM((images // 2, channels), F32),
             pltpu.VMEM((1, channels), F32),
             pltpu.SMEM(img_ids.shape, jnp.int32),
-            pltpu.VMEM((cells, channels), F32),
-            pltpu.VMEM((images, channels), F32),
-            pltpu.VMEM((cells, LANES), F32),
-            dma((STEPS,)),
-            dma((STEPS,)),
-            dma((3,)),
-            dma((STEPS,)),
+            pltpu.SemaphoreType.DMA((3,)),
         ),
         grant=BIG,
     )
@@ -250,7 +311,7 @@
 
 def backward_kernel(
     s0, s1, s2, s3, normal_hbm, gain_hbm, head_gain_hbm,
-    filtered_hbm, mean_hbm, inverse_hbm, kernel_hbm, after_hbm,
+    f0, f1, m0, m1, i0, i1, kernel_hbm, after_hbm,
     out_hbm,
     blocks_ref, normal_ref, gain_ref, head_gain_ref, filtered_ref, mean_ref, inverse_ref, kernel_ref,
     out_ref, even_ref, lean_ref, pull_ref, tilt_ref,
@@ -261,6 +322,7 @@
     blocks = (s0, s1, s2, s3)
     share = channels // len(PEERS)
     wide = channels // STEPS
+    some = images * CELLS // 2
 
     def block_at(step):
         return pl.ds(pl.multiple_of(step * wide, LANES), wide)
@@ -277,17 +339,20 @@
         pltpu.make_async_copy(source, target, small_sems.at[index])
         for index, (source, target) in enumerate((
             (head_gain_hbm, head_gain_ref), (gain_hbm, gain_ref), (normal_hbm, normal_ref),
-            (mean_hbm, mean_ref), (inverse_hbm, inverse_ref),
+            (m0, mean_ref.at[:some, :]), (m1, mean_ref.at[some:, :]),
+            (i0, inverse_ref.at[:some, :]), (i1, inverse_ref.at[some:, :]),
         ))
     ]
     filtered_copies = [
         pltpu.make_async_copy(
-            filtered_hbm.at[:, block_at(step)], filtered_ref.at[:, block_at(step)],
-            filtered_sems.at[step],
+            source.at[:, block_at(step)],
+            filtered_ref.at[half * some : (half + 1) * some, block_at(step)],
+            filtered_sems.at[2 * step + half],
         )
         for step in range(STEPS)
+        for half, source in enumerate((f0, f1))
     ]
-    kernel_copy = pltpu.make_async_copy(kernel_hbm, kernel_ref, small_sems.at[5])
+    kernel_copy = pltpu.make_async_copy(kernel_hbm, kernel_ref, small_sems.at[7])
     for copy in (*head_copies, *small_copies, *filtered_copies, kernel_copy):
         copy.start()
     chunks = channels // LANES
@@ -313,7 +378,8 @@
     tilt_ref[...] = pull - jnp.sum(pull, axis=1, keepdims=True) * part
 
     for step in range(STEPS):
-        filtered_copies[step].wait()
+        filtered_copies[2 * step].wait()
+        filtered_copies[2 * step + 1].wait()
         for image in range(images):
             spot = pl.ds(image * CELLS, CELLS)
             average = mean_ref[spot, :]
@@ -368,12 +434,12 @@
 
 
 def block_backward(blocks, normal, norm_gain, head_gain, filtered, mean, inverse, kernel, after):
-    cells, channels = filtered.shape
+    cells, channels = 2 * filtered[0].shape[0], filtered[0].shape[1]
     images = cells // CELLS
     dma = pltpu.SemaphoreType.DMA
     operands = [
         *blocks, normal, norm_gain.reshape(1, channels), head_gain.reshape(1, channels),
-        filtered, mean, inverse, kernel, after,
+        *filtered, *mean, *inverse, kernel, after,
     ]
     return call(
         backward_kernel,
@@ -396,8 +462,8 @@
             pltpu.VMEM((images, channels), F32),
             pltpu.VMEM((images, channels), F32),
             dma((len(blocks),)),
-            dma((6,)),
-            dma((STEPS,)),
+            dma((8,)),
+            dma((2 * STEPS,)),
             dma((STEPS,)),
         ),
         grant=BIG,
@@ -445,19 +511,19 @@
         out_ref[target, :, width:] = hot
 
 
-def line_kernel(line_ref, out_ref):
-    line, rows, _ = line_ref.shape
-    for first in range(0, line, 4):
-        four = [line_ref[first + offset].astype(F32) for offset in range(4)]
-        at = slice(first * rows, (first + 4) * rows)
+def line_kernel(plane_ref, after_ref, out_ref):
+    del after_ref
+    blocks, rows, _ = plane_ref.shape
+    group = blocks // 2
+    mine = lax.axis_index("x") * 2 + lax.axis_index("y_hi")
+    for first in range(0, group, 2):
+        four = [
+            plane_ref[side * group + lax.rem(mine + first + offset, group)].astype(F32)
+            for offset in range(2)
+            for side in range(2)
+        ]
+        at = slice(2 * first * rows, 2 * (first + 2) * rows)
         out_ref[at, :] = jnp.concatenate(four, axis=0).astype(BF16)
-
-
-def join_texts_kernel(own_ref, next_ref, after_ref, out_ref):
-    del after_ref
-    texts = own_ref.shape[0]
-    out_ref[:texts, :] = own_ref[...]
-    out_ref[texts:, :] = next_ref[...]
 
 
 def partial_kernel(received_ref, projection_ref, out_ref, columns_ref, hot_ref):
@@ -473,13 +539,12 @@
 
 
 def pair_kernel(
-    partials_ref, hot_ref, projection_ref, t0, t1, t2, t3, t4, t5, t6, t7,
+    partials_ref, hot_ref, projection_ref, near_ref, far_ref,
     scale_ref, shift_ref,
     stay_ref, send_ref, factors_ref,
     head_ref,
 ):
     group, images, width = partials_ref.shape
-    blocks = (t0, t1, t2, t3, t4, t5, t6, t7)
     scale, shift = scale_ref[0], shift_ref[0]
     embedded = partials_ref[0].astype(F32)
     for owner in range(1, group):
@@ -489,18 +554,22 @@
     low = unit.astype(BF16)
     factors_ref[:, width : 2 * width] = low
     hot = hot_ref[...]
-    weights = []
-    for block in blocks:
+
+    def weigh(block):
         logits = scale * dot(low, block[:, :width], 1, 1) + shift
         signs = 2.0 * dot(hot, block[:, width:], 1, 1) - 1.0
-        weights.append((-signs * jax.nn.sigmoid(-signs * logits)).astype(BF16))
-    image_grad = dot(weights[0], t0[:, :width], 1, 0)
-    for weight, block in zip(weights[1:], blocks[1:]):
-        image_grad += dot(weight, block[:, :width], 1, 0)
+        return (-signs * jax.nn.sigmoid(-signs * logits)).astype(BF16)
+
+    image_grad = jnp.zeros((images, width), F32)
+    for side, texts_ref in enumerate((near_ref, far_ref)):
+        ring, rows, wide = texts_ref.shape
+        for first in range(0, ring, 2):
+            block = texts_ref[first : first + 2].reshape(2 * rows, wide)
+            image_grad += dot(weigh(block), block[:, :width], 1, 0)
+        own = jnp.concatenate([texts_ref[at, :OWN, :] for at in range(ring)], axis=0)
+        factors_ref[:, 2 * width + side * LANES : 2 * width + (side + 1) * LANES] = weigh(own)
     embed = length_back(unit, inverse, scale * image_grad).astype(BF16)
     factors_ref[:, :width] = embed
-    factors_ref[:, 2 * width : 2 * width + LANES] = weights[0]
-    factors_ref[:, 2 * width + LANES :] = weights[4]
     head = dot(embed, projection_ref[...], 1, 1)
     rows = images // group
     for owner in range(group):
@@ -522,7 +591,6 @@
     line, strip_rows, half = out_ref.shape
     strip = columns_ref.shape[1] // line
     rows = (strip_rows - strip) // 2
-    texts = line * rows
     start = pl.multiple_of(lax.axis_index("core") * (width - half), LANES)
 
     def both(at):
@@ -531,14 +599,14 @@
     columns = jnp.concatenate([columns_ref[...], far_columns_ref[...]], axis=0)
     rows_ref[...] = dot(columns, both(pl.ds(start, half)), 0, 0)
     low = both(pl.ds(pl.multiple_of(start + width, LANES), half))
-    first = slice(2 * width, 2 * width + texts)
-    second = slice(2 * width + LANES, 2 * width + LANES + texts)
+    first, second = slice(2 * width, 2 * width + LANES), slice(2 * width + LANES, None)
     own = jnp.concatenate([mine_ref[:, first], theirs_ref[:, second]], axis=0)
     other = jnp.concatenate([mine_ref[:, second], theirs_ref[:, first]], axis=0)
     near_ref[...] = dot(own, low, 0, 0)
     far_ref[...] = dot(other, low, 0, 0)
     for target in range(line):
-        at = slice(target * rows, (target + 1) * rows)
+        place = target % (line // 2) * OWN + target // (line // 2) * rows
+        at = slice(place, place + rows)
         stacked = jnp.concatenate(
             [rows_ref[target * strip : (target + 1) * strip], near_ref[at], far_ref[at]], axis=0
         )
@@ -626,11 +694,23 @@
         ),
         grant=BIG,
     )
-    gathered = exchange(packed, LINE)
-    filtered, mean, inverse, normal, send = block_forward(
-        features, kernel, norm_gain, head_gain, img_ids, group
-    )
-    gathered, send = lax.optimization_barrier((gathered, send))
+    gathered = exchange(packed, PLANE)
+    early_filtered, early_mean, early_inverse, pooled = block_forward_first(
+        features, kernel, norm_gain
+    )
+    own_texts = call(
+        line_kernel,
+        ((shape_of((texts, width + IDS), BF16), VMEM),),
+        ((gathered, VMEM), (early_mean, HBM)),
+        "line_rows", 1,
+    )
+    near = lax.all_gather(own_texts, "z", axis=0, tiled=False)
+    late_filtered, late_mean, late_inverse, normal, send = block_forward_second(
+        features, kernel, norm_gain, pooled, head_gain, img_ids, own_texts, group
+    )
+    filtered = (early_filtered, late_filtered)
+    mean = (early_mean, late_mean)
+    inverse = (early_inverse, late_inverse)
     received = exchange(send, GROUP)
     partials, columns, hot = call(
         partial_kernel,
@@ -642,23 +722,10 @@
         ((received, VMEM), (projection, VMEM)),
         "partial_embed", 2,
     )
-    own_line = call(
-        line_kernel, ((shape_of((texts, width + IDS), BF16), VMEM),), ((gathered, VMEM),),
-        "line_rows", 1,
-    )
-    next_line = lax.ppermute(own_line, "y_hi", ((0, 1), (1, 0)))
-    near = [
-        call(
-            join_texts_kernel,
-            ((shape_of((2 * texts, width + IDS), BF16), VMEM),),
-            ((own_line, VMEM), (next_line, VMEM), (columns, VMEM)),
-            "join_texts", 1,
-        )
-    ]
-    near += [along_x(near[0], step) for step in (1, 3, 2)]
-    far = [swap_core(block) for block in near]
     far_columns = swap_core(columns)
     partials = exchange(partials, GROUP)
+    near, partials = lax.optimization_barrier((near, partials))
+    far = swap_core(near)
     stay, away, factors = call(
         pair_kernel,
         (
@@ -666,7 +733,7 @@
             (shape_of((4, rows, share), F32), VMEM),
             (shape_of((images, 2 * width + 2 * LANES), BF16), VMEM),
         ),
-        tuple((array, VMEM) for array in (partials, hot, projection, *near, *far))
+        tuple((array, VMEM) for array in (partials, hot, projection, near, far))
         + ((logit_scale, SMEM), (logit_bias, SMEM)),
         "pairs", 4,
         scratch=(pltpu.VMEM((group, rows, share), F32),),
@@ -680,8 +747,8 @@
         "strip_make", 2,
         scratch=(
             pltpu.VMEM((share, HALF), F32),
-            pltpu.VMEM((texts, HALF), F32),
-            pltpu.VMEM((texts, HALF), F32),
+            pltpu.VMEM((LANES, HALF), F32),
+            pltpu.VMEM((LANES, HALF), F32),
         ),
     )
     strips = exchange(strips, LINE)

time: 124 us -> 136 us (1.097)
  starting transfers between devices: 56.6 us -> 32.3 us
  blocking collectives: 10.7 us -> 25 us
  between operations: 2.09 us -> 15.5 us
  waiting for transfers between devices: 14 us -> 18.8 us
  local copies, waits for them, and re-layouts: 1.21 us -> 3.44 us
  Pallas kernels: 38.7 us -> 40.4 us
    all_to_all x1 -> x2, blocking collectives: 10.7 us -> 25 us  [exchange(): return lax.all_to_all(blocks, axes, 0, 0, tiled=True)]
    ppermute x8 -> x5, starting transfers between devices: 17.2 us -> 6.24 us  [swap_core(): return lax.ppermute(block, 'core', ((0, 1), (1, 0)))]
    all_to_all x4 -> x3, starting transfers between devices: 28 us -> 18.6 us  [exchange(): return lax.all_to_all(blocks, axes, 0, 0, tiled=True)]
    all_gather x0 -> x1, waiting for transfers between devices: none -> 5.09 us  [local(): near = lax.all_gather(own_texts, 'z', axis=0, tiled=False)]
    ppermute x1 -> x0, starting transfers between devices: 2.71 us -> none  [local(): next_line = lax.ppermute(own_line, 'y_hi', ((0, 1), (1, 0)))]
    unnamed x16 -> x20, local copies, waits for them, and re-layouts: 1.21 us -> 3.44 us
    ppermute x6 -> x3, starting transfers between devices: 6.71 us -> 4.77 us  [along_x(): lax.ppermute(block, 'x', tuple(((i, (i + step) % 4) for i in range(4))))]
    pallas_call x12, Pallas kernels: 38.7 us -> 40.4 us  [call(): pl.pallas_call(body, out_shape=shapes[0] if single else shapes, in_specs=...]
  transfers between devices with their start and end apart: 20 -> 13, of which waited for: 9 -> 8; matrix products, arithmetic and copies ran while one was open for 0% -> 0% of each run, Pallas kernels for 25% -> 23%
where the time goes in v6:
time: 136 us; the launch traced here: 135 us
  Pallas kernels  40.4 us (30%)
  starting transfers between devices  32.3 us (24%)
  blocking collectives  25 us (18%)
  waiting for transfers between devices  18.8 us (14%)
  between operations  15.5 us (11%)
  local copies, waits for them, and re-layouts  3.44 us (3%)
    pallas_call x12, Pallas kernels, call(): pl.pallas_call(body, out_shape=shapes[0] if single else shapes, in_specs=...  40.4 us
    all_to_all x2, blocking collectives, exchange(): return lax.all_to_all(blocks, axes, 0, 0, tiled=True)  25 us
    all_to_all x3, starting transfers between devices, exchange(): return lax.all_to_all(blocks, axes, 0, 0, tiled=True)  18.6 us
    ppermute x5, starting transfers between devices, swap_core(): return lax.ppermute(block, 'core', ((0, 1), (1, 0)))  6.24 us
    all_to_all x3, waiting for transfers between devices, exchange(): return lax.all_to_all(blocks, axes, 0, 0, tiled=True)  5.68 us
    all_gather x1, waiting for transfers between devices, local(): near = lax.all_gather(own_texts, 'z', axis=0, tiled=False)  5.09 us
    ppermute x3, starting transfers between devices, along_x(): lax.ppermute(block, 'x', tuple(((i, (i + step) % 4) for i in range(4))))  4.77 us
    ppermute x5, waiting for transfers between devices, swap_core(): return lax.ppermute(block, 'core', ((0, 1), (1, 0)))  4.43 us
  transfers between devices with their start and end apart: 13, of which 8 were waited for; matrix products, arithmetic and copies ran while one was open for 0% of the time, Pallas kernels for 23%

profile of v6, /device:TPU:1, one launch (start us, length us, event | category | flops | bytes accessed | tf_op | source)
XLA Modules:
  0.0 135.4 jit_solution(6719114431403549865)
XLA Ops:
  7.2 1.6 %text_pack.1 = bf16[16,4,1280]{2,1,0:T(4,128)(2,1)} custom-call(bf16[4,1152]{1,0:T(4,128)(2,1)} %text_ref.1, s32[4]{0:T(128)} %ids_hbm.2), custom_call_target="tpu_custom_call" | custom-call | bytes 3000000 | tf_op jit(solution)/shard_map/text_pack/pallas_call | solution.py:41
  8.8 7.6 %all-to-all-start = ((bf16[16,4,1280]{2,1,0:T(4,128)(2,1)}), bf16[16,4,1280]{2,1,0:T(4,128)(2,1)S(1)}, u32[]{:S(2)}, u32[]{:S(2)}) async-start(bf16[16,4,1280]{2,1,0:T(4,128)(2,1)} %text_pack.1), calls=%async_computation | async-start | bytes 327680 | tf_op jit(solution)/shard_map/all_to_all | solution.py:655
  16.4 0.0 all-gather.3.cloned.1.call-start
  16.4 8.2 %block_forward_first.1 = (f32[128,3072]{1,0:T(8,128)}, f32[128,128]{1,0:T(8,128)}, f32[128,128]{1,0:T(8,128)}, f32[2,3072]{1,0:T(2,128)}) custom-call(bf16[256,3072]{1,0:T(8,128)(2,1)} %bitcast.10, f32[7,7,3072]{2,1,0:T(8,128)} %kernel_hbm.5, f32[1,3072]{1,0:T(1,128)} %bitcast.13), custom_call_target="tpu_custom_call" | custom-call | bytes 24000000 | tf_op jit(solution)/shard_map/block_forward_first/pallas_call | solution.py:41
  24.6 0.0 copy-start
  24.7 0.0 all-to-all-done.plane_ref
  24.7 0.0 copy-start.2
  24.7 0.9 copy-done.2
  25.6 0.7 line_rows.1.after_hbm
  26.3 0.0 all-gather.3.cloned.1.call-update
  26.3 8.4 %block_forward_second.1 = (f32[128,3072]{1,0:T(8,128)}, f32[128,128]{1,0:T(8,128)}, f32[128,128]{1,0:T(8,128)}, f32[4,3200]{1,0:T(4,128)}, bf16[8,4,512]{2,1,0:T(4,128)(2,1)}) custom-call(bf16[256,3072]{1,0:T(8,128)(2,1)} %bitcast.11, f32[7,7,3072]{2,1,0:T(8,128)} %kernel_hbm.5, f32[1,3072]{1,0:T(1,128)} %bitcast.14, ...), custom_call_target="tpu_custom_call" | custom-call | bytes 24000000 | tf_op jit(solution)/shard_map/block_forward_second/pallas_call | solution.py:41
  34.7 13.1 %all_to_all.25.received_ref = bf16[8,4,512]{2,1,0:T(4,128)(2,1)S(1)} all-to-all(bf16[8,4,512]{2,1,0:T(4,128)(2,1)} %get-tuple-element.37), channel_id=1, replica_groups=mesh['y_lo'=2,'z'=8,'core'=2,'x'=4,'y_hi'=2] {'x','y_hi'}, dimensions={0} | all-to-all | bytes 65536 | tf_op jit(solution)/shard_map/all_to_all | solution.py:655
  47.9 0.0 copy-done
  47.9 0.3 partial_embed.1
  48.2 11.8 %all_to_all.26.partials_ref = bf16[8,32,1152]{2,1,0:T(8,128)(2,1)S(1)} all-to-all(bf16[8,32,1152]{2,1,0:T(8,128)(2,1)S(1)} %get-tuple-element.38), channel_id=1, replica_groups=mesh['y_lo'=2,'z'=8,'core'=2,'x'=4,'y_hi'=2] {'x','y_hi'}, dimensions={0} | all-to-all | bytes 1179648 | tf_op jit(solution)/shard_map/all_to_all | solution.py:655
  60.0 5.1 %all-gather.3.cloned.1.call-done = bf16[512,1280]{1,0:T(8,128)(2,1)} async-done(((bf16[64,1280]{1,0:T(8,128)(2,1)}), bf16[512,1280]{1,0:T(8,128)(2,1)}) %all-gather.3.cloned.1.call-update) | async-done | bytes 1310736 | tf_op jit(solution)/shard_map/all_gather | solution.py:707
  65.1 4.7 %collective-permute-start = (bf16[8,64,1280]{2,1,0:T(8,128)(2,1)}, bf16[8,64,1280]{2,1,0:T(8,128)(2,1)S(1)}, u32[]{:S(2)}, u32[]{:S(2)}) collective-permute-start(bf16[8,64,1280]{2,1,0:T(8,128)(2,1)} %bitcast.8), channel_id=1, source_target_pairs={{0,8},{8,0},{1,9},{9,1},{2,10},{10,2},{3,11},{11,3},{4,12},{12,4},... | collective-permute-start | bytes 3932168 | tf_op jit(solution)/shard_map/ppermute | solution.py:659
  71.1 1.6 %collective-permute-done.far_ref = bf16[8,64,1280]{2,1,0:T(8,128)(2,1)S(1)} collective-permute-done((bf16[8,64,1280]{2,1,0:T(8,128)(2,1)}, bf16[8,64,1280]{2,1,0:T(8,128)(2,1)S(1)}, u32[]{:S(2)}, u32[]{:S(2)}) %collective-permute-start) | collective-permute-done | bytes 1310752 | tf_op jit(solution)/shard_map/ppermute | solution.py:659
  72.7 0.0 copy-start.1
  72.7 1.3 copy-done.1
  74.0 3.0 %pairs.1 = (f32[4,4,384]{2,1,0:T(4,128)S(1)}, f32[4,4,384]{2,1,0:T(4,128)S(1)}, bf16[32,2560]{1,0:T(8,128)(2,1)S(1)}) custom-call(bf16[8,32,1152]{2,1,0:T(8,128)(2,1)S(1)} %all_to_all.26.partials_ref, bf16[32,128]{1,0:T(8,128)(2,1)S(1)} %get-tuple-element.40.hot_ref, bf16[384,1152]{1,0:T(8,128)(2,1)S(1)} %copy-done, bf16[8,64,1280]{2,1,0:T(8,128)(2,1)S(1)} %bitcast.9, ...), custom_call_target="tpu_custom_call" | custom-call | bytes 12000000 | tf_op jit(solution)/shard_map/pairs/pallas_call | solution.py:41
  77.0 0.5 collective-permute-start.1
  77.5 0.1 collective-permute-start.2
  77.6 1.1 collective-permute-done.2.far_columns_ref
  78.7 0.0 collective-permute-done.1.theirs_ref
  78.7 1.3 strip_make.1
  79.9 5.0 %all-to-all-start.3 = ((bf16[16,32,640]{2,1,0:T(8,128)(2,1)}), bf16[16,32,640]{2,1,0:T(8,128)(2,1)S(1)}, u32[]{:S(2)}, u32[]{:S(2)}) async-start(bf16[16,32,640]{2,1,0:T(8,128)(2,1)} %strip_make.1), calls=%async_computation.3 | async-start | bytes 1310720 | tf_op jit(solution)/shard_map/all_to_all | solution.py:655
  84.9 2.7 %collective-permute-start.3 = (f32[4,4,384]{2,1,0:T(4,128)S(1)}, f32[4,4,384]{2,1,0:T(4,128)S(1)}, u32[]{:S(2)}, u32[]{:S(2)}) collective-permute-start(f32[4,4,384]{2,1,0:T(4,128)S(1)} %get-tuple-element.45), channel_id=1, source_target_pairs={{0,1},{1,0},{2,3},{3,2},{4,5},{5,4},{6,7},{7,6},{8,9},{9,8},{10,11... | collective-permute-start | bytes 73736 | tf_op jit(solution)/shard_map/ppermute | solution.py:742
  87.6 1.7 %collective-permute-done.3.got_ref = f32[4,4,384]{2,1,0:T(4,128)S(1)} collective-permute-done((f32[4,4,384]{2,1,0:T(4,128)S(1)}, f32[4,4,384]{2,1,0:T(4,128)S(1)}, u32[]{:S(2)}, u32[]{:S(2)}) %collective-permute-start.3) | collective-permute-done | bytes 24608 | tf_op jit(solution)/shard_map/ppermute | solution.py:742
  89.3 0.0 copy-start.6
  89.3 0.6 copy-done.6
  89.9 1.2 collective-permute-start.4
  91.2 2.5 %collective-permute-start.5 = (f32[2,4,384]{2,1,0:T(4,128)S(1)}, f32[2,4,384]{2,1,0:T(4,128)S(1)}, u32[]{:S(2)}, u32[]{:S(2)}) collective-permute-start(f32[2,4,384]{2,1,0:T(4,128)S(1)} %get-tuple-element.48), channel_id=1, source_target_pairs={{0,4},{2,6},{4,0},{6,2},{1,5},{3,7},{5,1},{7,3},{8,12},{10,14},{12... | collective-permute-start | bytes 36872 | tf_op jit(solution)/shard_map/ppermute | solution.py:663
  93.7 1.0 collective-permute-start.6
  94.7 0.0 collective-permute-done.4.s1
  94.7 0.0 copy-start.7
  94.7 0.8 collective-permute-done.5.s2
  95.5 0.0 copy-start.8
  95.5 1.0 collective-permute-done.6.s3
  96.5 0.0 copy-start.9
  96.5 5.7 %all-to-all-done.3.strips_ref = bf16[16,32,640]{2,1,0:T(8,128)(2,1)S(1)} async-done(((bf16[16,32,640]{2,1,0:T(8,128)(2,1)}), bf16[16,32,640]{2,1,0:T(8,128)(2,1)S(1)}, u32[]{:S(2)}, u32[]{:S(2)}) %all-to-all-start.3) | async-done | bytes 655392 | tf_op jit(solution)/shard_map/all_to_all | solution.py:655
  102.2 0.9 strip_sum.1
  103.1 0.0 copy-start.3
  103.1 0.6 copy-done.3
  103.7 6.0 %all-to-all-start.4 = ((bf16[16,24,640]{2,1,0:T(8,128)(2,1)}), bf16[16,24,640]{2,1,0:T(8,128)(2,1)S(1)}, u32[]{:S(2)}, u32[]{:S(2)}) async-start(bf16[16,24,640]{2,1,0:T(8,128)(2,1)} %get-tuple-element.51), calls=%async_computation.4 | async-start | bytes 983040 | tf_op jit(solution)/shard_map/all_to_all | solution.py:655
  109.6 0.9 collective-permute-start.7
  110.5 0.0 copy-done.7
  110.5 0.0 copy-done.8
  110.5 0.0 copy-done.9
  110.5 0.0 copy-start.4
  110.5 0.0 copy-start.5
  110.5 14.0 %block_backward.1 = bf16[256,3072]{1,0:T(8,128)(2,1)} custom-call(f32[2,4,384]{2,1,0:T(4,128)} %copy-done.6, f32[2,4,384]{2,1,0:T(4,128)} %copy-done.7, f32[2,4,384]{2,1,0:T(4,128)} %copy-done.8, f32[2,4,384]{2,1,0:T(4,128)} %copy-done.9, f32[4,3200]{1,0:T(4,128)} %get-tuple-element.56.normal_hbm, f32[1,3072]{1,0:T(1,128)} %bitcast.15, f32[1,3072]{1,0:T(1,128)} %bitcast.17, ...), custom_call_target="tpu_custom_call" | custom-call | bytes 42000000 | tf_op jit(solution)/shard_map/block_backward/pallas_call | solution.py:41
  124.5 0.0 collective-permute-done.7.got_ref
  124.5 0.0 copy-done.4
  124.5 0.0 copy-done.5
  124.5 0.8 text_grad.1
  125.3 0.0 all-to-all-done.4
  125.3 0.1 collective-permute-start.8
  125.4 1.8 %collective-permute-done.8.far_ref = bf16[384,640]{1,0:T(8,128)(2,1)S(1)} collective-permute-done((bf16[384,640]{1,0:T(8,128)(2,1)S(1)}, bf16[384,640]{1,0:T(8,128)(2,1)S(1)}, u32[]{:S(2)}, u32[]{:S(2)}) %collective-permute-start.8) | collective-permute-done | bytes 491552 | tf_op jit(solution)/shard_map/ppermute | solution.py:659
  127.2 1.3 proj_join.1
  (1 shorter events, 0.0 us)
Async XLA Ops:
  8.8 15.9 %all-to-all-start = ((bf16[16,4,1280]{2,1,0:T(4,128)(2,1)}), bf16[16,4,1280]{2,1,0:T(4,128)(2,1)S(1)}, u32[]{:S(2)}, u32[]{:S(2)}) async-start(bf16[16,4,1280]{2,1,0:T(4,128)(2,1)} %text_pack.1), calls=%async_computation | async-start | bytes 327680 | tf_op jit(solution)/shard_map/all_to_all | solution.py:655
  16.4 48.7 %all-gather.3.cloned.1.call-start = ((), (), s32[]{:S(2)}) async-start(), calls=%async_computation.5 | async-start | bytes 1474560 | tf_op jit(solution)/shard_map/all_gather | solution.py:707
  24.6 23.2 %copy-start = (bf16[384,1152]{1,0:T(8,128)(2,1)S(1)}, bf16[384,1152]{1,0:T(8,128)(2,1)}, u32[]{:S(2)}) copy-start(bf16[384,1152]{1,0:T(8,128)(2,1)} %projection_ref.3) | copy-start | bytes 2654212
  24.7 0.9 copy-start.2
  65.1 7.6 %collective-permute-start = (bf16[8,64,1280]{2,1,0:T(8,128)(2,1)}, bf16[8,64,1280]{2,1,0:T(8,128)(2,1)S(1)}, u32[]{:S(2)}, u32[]{:S(2)}) collective-permute-start(bf16[8,64,1280]{2,1,0:T(8,128)(2,1)} %bitcast.8), channel_id=1, source_target_pairs={{0,8},{8,0},{1,9},{9,1},{2,10},{10,2},{3,11},{11,3},{4,12},{12,4},... | collective-permute-start | bytes 3932168 | tf_op jit(solution)/shard_map/ppermute | solution.py:659
  72.7 1.3 copy-start.1
  77.0 1.7 %collective-permute-start.1 = (bf16[32,2560]{1,0:T(8,128)(2,1)S(1)}, bf16[32,2560]{1,0:T(8,128)(2,1)S(1)}, u32[]{:S(2)}, u32[]{:S(2)}) collective-permute-start(bf16[32,2560]{1,0:T(8,128)(2,1)S(1)} %get-tuple-element.42.mine_ref), channel_id=1, source_target_pairs={{0,8},{8,0},{1,9},{9,1},{2,10},{10,2},{3,11},{11,3},{4,12},{12,4},... | collective-permute-start | bytes 491528 | tf_op jit(solution)/shard_map/ppermute | solution.py:659
  77.5 1.2 collective-permute-start.2
  79.9 22.3 %all-to-all-start.3 = ((bf16[16,32,640]{2,1,0:T(8,128)(2,1)}), bf16[16,32,640]{2,1,0:T(8,128)(2,1)S(1)}, u32[]{:S(2)}, u32[]{:S(2)}) async-start(bf16[16,32,640]{2,1,0:T(8,128)(2,1)} %strip_make.1), calls=%async_computation.3 | async-start | bytes 1310720 | tf_op jit(solution)/shard_map/all_to_all | solution.py:655
  84.9 4.4 %collective-permute-start.3 = (f32[4,4,384]{2,1,0:T(4,128)S(1)}, f32[4,4,384]{2,1,0:T(4,128)S(1)}, u32[]{:S(2)}, u32[]{:S(2)}) collective-permute-start(f32[4,4,384]{2,1,0:T(4,128)S(1)} %get-tuple-element.45), channel_id=1, source_target_pairs={{0,1},{1,0},{2,3},{3,2},{4,5},{5,4},{6,7},{7,6},{8,9},{9,8},{10,11... | collective-permute-start | bytes 73736 | tf_op jit(solution)/shard_map/ppermute | solution.py:742
  89.3 0.6 copy-start.6
  89.9 4.8 %collective-permute-start.4 = (f32[2,4,384]{2,1,0:T(4,128)S(1)}, f32[2,4,384]{2,1,0:T(4,128)S(1)}, u32[]{:S(2)}, u32[]{:S(2)}) collective-permute-start(f32[2,4,384]{2,1,0:T(4,128)S(1)} %get-tuple-element.47), channel_id=1, source_target_pairs={{0,2},{2,4},{4,6},{6,0},{1,3},{3,5},{5,7},{7,1},{8,10},{10,12},{12... | collective-permute-start | bytes 36872 | tf_op jit(solution)/shard_map/ppermute | solution.py:663
  91.2 4.3 %collective-permute-start.5 = (f32[2,4,384]{2,1,0:T(4,128)S(1)}, f32[2,4,384]{2,1,0:T(4,128)S(1)}, u32[]{:S(2)}, u32[]{:S(2)}) collective-permute-start(f32[2,4,384]{2,1,0:T(4,128)S(1)} %get-tuple-element.48), channel_id=1, source_target_pairs={{0,4},{2,6},{4,0},{6,2},{1,5},{3,7},{5,1},{7,3},{8,12},{10,14},{12... | collective-permute-start | bytes 36872 | tf_op jit(solution)/shard_map/ppermute | solution.py:663
  93.7 2.8 %collective-permute-start.6 = (f32[2,4,384]{2,1,0:T(4,128)S(1)}, f32[2,4,384]{2,1,0:T(4,128)S(1)}, u32[]{:S(2)}, u32[]{:S(2)}) collective-permute-start(f32[2,4,384]{2,1,0:T(4,128)S(1)} %get-tuple-element.49), channel_id=1, source_target_pairs={{0,6},{2,0},{4,2},{6,4},{1,7},{3,1},{5,3},{7,5},{8,14},{10,8},{12,... | collective-permute-start | bytes 36872 | tf_op jit(solution)/shard_map/ppermute | solution.py:663
  94.7 15.8 %copy-start.7 = (f32[2,4,384]{2,1,0:T(4,128)}, f32[2,4,384]{2,1,0:T(4,128)S(1)}, u32[]{:S(2)}) copy-start(f32[2,4,384]{2,1,0:T(4,128)S(1)} %collective-permute-done.4.s1) | copy-start | bytes 36868
  95.5 15.0 %copy-start.8 = (f32[2,4,384]{2,1,0:T(4,128)}, f32[2,4,384]{2,1,0:T(4,128)S(1)}, u32[]{:S(2)}) copy-start(f32[2,4,384]{2,1,0:T(4,128)S(1)} %collective-permute-done.5.s2) | copy-start | bytes 36868
  96.5 14.0 %copy-start.9 = (f32[2,4,384]{2,1,0:T(4,128)}, f32[2,4,384]{2,1,0:T(4,128)S(1)}, u32[]{:S(2)}) copy-start(f32[2,4,384]{2,1,0:T(4,128)S(1)} %collective-permute-done.6.s3) | copy-start | bytes 36868
  103.1 0.6 copy-start.3
  103.7 21.6 %all-to-all-start.4 = ((bf16[16,24,640]{2,1,0:T(8,128)(2,1)}), bf16[16,24,640]{2,1,0:T(8,128)(2,1)S(1)}, u32[]{:S(2)}, u32[]{:S(2)}) async-start(bf16[16,24,640]{2,1,0:T(8,128)(2,1)} %get-tuple-element.51), calls=%async_computation.4 | async-start | bytes 983040 | tf_op jit(solution)/shard_map/all_to_all | solution.py:655
  109.6 14.9 %collective-permute-start.7 = (f32[4,640]{1,0:T(4,128)S(1)}, f32[4,640]{1,0:T(4,128)S(1)}, u32[]{:S(2)}, u32[]{:S(2)}) collective-permute-start(f32[4,640]{1,0:T(4,128)S(1)} %get-tuple-element.63), channel_id=1, source_target_pairs={{0,8},{8,0},{1,9},{9,1},{2,10},{10,2},{3,11},{11,3},{4,12},{12,4},... | collective-permute-start | bytes 30728 | tf_op jit(solution)/shard_map/ppermute | solution.py:659
  110.5 14.0 %copy-start.4 = (f32[4,640]{1,0:T(4,128)S(1)}, f32[4,640]{1,0:T(4,128)}, u32[]{:S(2)}) copy-start(f32[4,640]{1,0:T(4,128)} %copy-done.3) | copy-start | bytes 30724
  110.5 14.0 %copy-start.5 = (bf16[4,1152]{1,0:T(4,128)(2,1)S(1)}, bf16[4,1152]{1,0:T(4,128)(2,1)}, u32[]{:S(2)}) copy-start(bf16[4,1152]{1,0:T(4,128)(2,1)} %text_ref.1) | copy-start | bytes 27652
  125.3 1.9 %collective-permute-start.8 = (bf16[384,640]{1,0:T(8,128)(2,1)S(1)}, bf16[384,640]{1,0:T(8,128)(2,1)S(1)}, u32[]{:S(2)}, u32[]{:S(2)}) collective-permute-start(bf16[384,640]{1,0:T(8,128)(2,1)S(1)} %bitcast.6), channel_id=1, source_target_pairs={{0,8},{8,0},{1,9},{9,1},{2,10},{10,2},{3,11},{11,3},{4,12},{12,4},... | collective-permute-start | bytes 1474568 | tf_op jit(solution)/shard_map/ppermute | solution.py:659
Sparse Core Ops, SparseCore 0:
  26.4 38.6 all-gather.2

commit v7 on v5

--- a/solution.py
+++ b/solution.py
@@ -85,7 +85,7 @@
 def forward_kernel(
     field_hbm, kernel_hbm, gain_hbm, head_gain_hbm, ids_hbm,
     filtered_hbm, mean_ref, inverse_ref, normal_ref, send_ref,
-    field_ref, kernel_ref, gain_ref, head_gain_ref, ids_ref, filtered_ref, pooled_ref, total_ref,
+    field_ref, kernel_ref, gain_ref, head_gain_ref, ids_ref, filtered_ref, pooled_ref, total_ref, mixed_ref,
     field_sems, kernel_sems, small_sems, out_sems,
 ):
     images = field_ref.shape[0] // CELLS
@@ -134,15 +134,19 @@
             kernel_copy(step).wait()
 
         at = pl.ds(pl.multiple_of(chunk * LANES, LANES), LANES)
-        for first in range(0, images, 2):
+        for first in range(0, images, 4):
             fields = []
-            for image in range(first, first + 2):
+            for image in range(first, first + 4):
                 rows = []
                 for pair in range(SIDE // 2):
                     both = field_ref[pl.ds(image * CELLS + pair * 2 * SIDE, 2 * SIDE), at]
                     both = both.astype(jnp.float32)
                     rows += [both[:SIDE], both[SIDE:]]
                 fields.append(rows)
+                level = rows[0]
+                for row in rows[1:]:
+                    level = level + row
+                mixed_ref[pl.ds(image * SIDE, SIDE), at] = level
             sums = [[None] * SIDE for _ in fields]
             filter_rows(fields, sums, kernel_ref, at, False)
             for offset, total in enumerate(sums):
@@ -171,7 +175,7 @@
             return squares + centred * centred
 
         squares = lax.fori_loop(
-            0, chunks, spread_chunk, jnp.zeros((CELLS, LANES), jnp.float32), unroll=4
+            0, chunks, spread_chunk, jnp.zeros((CELLS, LANES), jnp.float32), unroll=8
         )
         spread = jnp.sum(squares, axis=1, keepdims=True) * part
         inverse_ref[cells, :] = jnp.broadcast_to(lax.rsqrt(spread + EPSILON), (CELLS, LANES))
@@ -184,11 +188,15 @@
         def pool_chunk(chunk, carry):
             at = pl.ds(pl.multiple_of(chunk * LANES, LANES), LANES)
             normal = (filtered_ref[cells, at] - average) * inverse
-            mixed = field_ref[cells, at].astype(jnp.float32) + normal * gain_ref[:, at]
-            pooled_ref[pl.ds(image, 1), at] = jnp.sum(mixed, axis=0, keepdims=True) * (1.0 / CELLS)
+            level = jnp.sum(normal.reshape(SIDE, SIDE, LANES), axis=0)
+            spot = pl.ds(image * SIDE, SIDE)
+            mixed_ref[spot, at] = mixed_ref[spot, at] + level * gain_ref[:, at]
             return carry
 
-        lax.fori_loop(0, chunks, pool_chunk, 0, unroll=2)
+        lax.fori_loop(0, chunks, pool_chunk, 0, unroll=8)
+        pooled_ref[pl.ds(image, 1), :] = jnp.sum(
+            mixed_ref[pl.ds(image * SIDE, SIDE), :], axis=0, keepdims=True
+        ) * (1.0 / CELLS)
 
     pooled = pooled_ref[...]
     centred = pooled - jnp.sum(pooled, axis=1, keepdims=True) * part
@@ -239,6 +247,7 @@
             pltpu.VMEM((cells, channels), F32),
             pltpu.VMEM((images, channels), F32),
             pltpu.VMEM((cells, LANES), F32),
+            pltpu.VMEM((images * SIDE, channels), F32),
             dma((STEPS,)),
             dma((STEPS,)),
             dma((3,)),
@@ -248,16 +257,12 @@
     )
 
 
-def backward_kernel(
-    s0, s1, s2, s3, normal_hbm, gain_hbm, head_gain_hbm,
-    filtered_hbm, mean_hbm, inverse_hbm, kernel_hbm, after_hbm,
-    out_hbm,
-    blocks_ref, normal_ref, gain_ref, head_gain_ref, filtered_ref, mean_ref, inverse_ref, kernel_ref,
-    out_ref, even_ref, lean_ref, pull_ref, tilt_ref,
-    block_sems, small_sems, filtered_sems, out_sems,
+def lean_kernel(
+    s0, s1, s2, s3, normal_ref, gain_ref, head_gain_ref, filtered_hbm, mean_ref, inverse_ref,
+    slopes_ref, lean_ref,
+    filtered_ref, pull_ref, tilt_ref, filtered_sems,
 ):
-    del after_hbm
-    images, channels = even_ref.shape
+    images, channels = pull_ref.shape
     blocks = (s0, s1, s2, s3)
     share = channels // len(PEERS)
     wide = channels // STEPS
@@ -265,21 +270,6 @@
     def block_at(step):
         return pl.ds(pl.multiple_of(step * wide, LANES), wide)
 
-    def out_copy(step):
-        at = block_at(step)
-        return pltpu.make_async_copy(out_ref.at[:, at], out_hbm.at[:, at], out_sems.at[step])
-
-    head_copies = [
-        pltpu.make_async_copy(block, blocks_ref.at[index], block_sems.at[index])
-        for index, block in enumerate(blocks)
-    ]
-    small_copies = [
-        pltpu.make_async_copy(source, target, small_sems.at[index])
-        for index, (source, target) in enumerate((
-            (head_gain_hbm, head_gain_ref), (gain_hbm, gain_ref), (normal_hbm, normal_ref),
-            (mean_hbm, mean_ref), (inverse_hbm, inverse_ref),
-        ))
-    ]
     filtered_copies = [
         pltpu.make_async_copy(
             filtered_hbm.at[:, block_at(step)], filtered_ref.at[:, block_at(step)],
@@ -287,30 +277,27 @@
         )
         for step in range(STEPS)
     ]
-    kernel_copy = pltpu.make_async_copy(kernel_hbm, kernel_ref, small_sems.at[5])
-    for copy in (*head_copies, *small_copies, *filtered_copies, kernel_copy):
+    for copy in filtered_copies:
         copy.start()
     chunks = channels // LANES
     per_block = chunks // STEPS
     part = 1.0 / channels
 
-    for copy in (*head_copies, *small_copies):
-        copy.wait()
     x, y_hi = lax.axis_index("x"), lax.axis_index("y_hi")
     for step_x, step_y in PEERS:
         owner = group_peer(x, y_hi, 4 - step_x, step_y)
         at = pl.ds(pl.multiple_of(owner * share, LANES), share)
-        tilt_ref[:, at] = blocks_ref[step_x, step_y] * head_gain_ref[:, at]
+        tilt_ref[:, at] = blocks[step_x][step_y] * head_gain_ref[:, at]
     cotangent = tilt_ref[...]
     normal = normal_ref[:, :channels]
     level = jnp.sum(cotangent, axis=1, keepdims=True) * part
     lean = jnp.sum(cotangent * normal, axis=1, keepdims=True) * part
     pooled_grad = normal_ref[:, channels : channels + 1] * (cotangent - level - normal * lean)
     even = pooled_grad * (1.0 / CELLS)
-    even_ref[...] = even
+    slopes_ref[0] = even
     pull = even * gain_ref[...]
     pull_ref[...] = pull
-    tilt_ref[...] = pull - jnp.sum(pull, axis=1, keepdims=True) * part
+    slopes_ref[1] = pull - jnp.sum(pull, axis=1, keepdims=True) * part
 
     for step in range(STEPS):
         filtered_copies[step].wait()
@@ -329,9 +316,63 @@
     inverse = inverse_ref[...]
     mean_lean = jnp.sum(lean_ref[...], axis=1, keepdims=True) * part
     lean_ref[...] = inverse * (inverse * (inverse * mean_lean))
-    kernel_copy.wait()
+
+
+def backward_kernel(
+    slopes_hbm, lean_hbm, filtered_hbm, mean_hbm, inverse_hbm, kernel_hbm, after_hbm,
+    out_hbm,
+    slopes_ref, lean_ref, filtered_ref, mean_ref, inverse_ref, kernel_ref, out_ref,
+    small_sems, filtered_sems, kernel_sems, out_sems,
+):
+    del after_hbm
+    images, channels = slopes_ref.shape[1:]
+    even_ref, tilt_ref = slopes_ref.at[0], slopes_ref.at[1]
+    wide = channels // STEPS
+    chunks = channels // LANES
+    per_block = chunks // STEPS
+
+    def block_at(step):
+        return pl.ds(pl.multiple_of(step * wide, LANES), wide)
+
+    def out_copy(step):
+        at = block_at(step)
+        return pltpu.make_async_copy(out_ref.at[:, at], out_hbm.at[:, at], out_sems.at[step])
+
+    def filtered_copy(step):
+        at = block_at(step)
+        return pltpu.make_async_copy(
+            filtered_hbm.at[:, at], filtered_ref.at[:, at], filtered_sems.at[step]
+        )
+
+    def kernel_copy(step):
+        at = block_at(step)
+        return pltpu.make_async_copy(
+            kernel_hbm.at[:, :, at], kernel_ref.at[:, :, at], kernel_sems.at[step]
+        )
+
+    small_copies = [
+        pltpu.make_async_copy(source, target, small_sems.at[index])
+        for index, (source, target) in enumerate((
+            (slopes_hbm, slopes_ref), (lean_hbm, lean_ref), (mean_hbm, mean_ref),
+            (inverse_hbm, inverse_ref),
+        ))
+    ]
+    for copy in small_copies:
+        copy.start()
+    for step in range(STEPS):
+        filtered_copy(step).start()
+        kernel_copy(step).start()
+    for copy in small_copies:
+        copy.wait()
 
     def filter_chunk(chunk, carry):
+        step = chunk // per_block
+
+        @pl.when(chunk == step * per_block)
+        def _():
+            filtered_copy(step).wait()
+            kernel_copy(step).wait()
+
         at = pl.ds(pl.multiple_of(chunk * LANES, LANES), LANES)
         for first in range(0, images, 2):
             fields = []
@@ -354,8 +395,6 @@
                     two = jnp.concatenate(total[2 * half : 2 * half + 2], axis=0)
                     spot = pl.ds((first + offset) * CELLS + half * 2 * SIDE, 2 * SIDE)
                     out_ref[spot, at] = two.astype(jnp.bfloat16)
-        step = chunk // per_block
-
         @pl.when(chunk == step * per_block + per_block - 1)
         def _():
             out_copy(step).start()
@@ -367,36 +406,51 @@
         out_copy(step).wait()
 
 
-def block_backward(blocks, normal, norm_gain, head_gain, filtered, mean, inverse, kernel, after):
+def block_lean(blocks, normal, norm_gain, head_gain, filtered, mean, inverse):
     cells, channels = filtered.shape
     images = cells // CELLS
+    return call(
+        lean_kernel,
+        (
+            (shape_of((2, images, channels), F32), VMEM),
+            (shape_of((cells, LANES), F32), VMEM),
+        ),
+        tuple(
+            (array, VMEM)
+            for array in (
+                *blocks, normal, norm_gain.reshape(1, channels), head_gain.reshape(1, channels)
+            )
+        )
+        + ((filtered, HBM), (mean, VMEM), (inverse, VMEM)),
+        "block_lean", 3,
+        scratch=(
+            pltpu.VMEM((cells, channels), F32),
+            pltpu.VMEM((images, channels), F32),
+            pltpu.VMEM((images, channels), F32),
+            pltpu.SemaphoreType.DMA((STEPS,)),
+        ),
+        grant=BIG,
+    )
+
+
+def block_backward(slopes, lean, filtered, mean, inverse, kernel, after):
+    cells, channels = filtered.shape
     dma = pltpu.SemaphoreType.DMA
-    operands = [
-        *blocks, normal, norm_gain.reshape(1, channels), head_gain.reshape(1, channels),
-        filtered, mean, inverse, kernel, after,
-    ]
     return call(
         backward_kernel,
         ((shape_of((cells, channels), BF16), HBM),),
-        tuple((array, HBM) for array in operands),
-        "block_backward",
-        14,
+        tuple((array, HBM) for array in (slopes, lean, filtered, mean, inverse, kernel, after)),
+        "block_backward", 13,
         scratch=(
-            pltpu.VMEM((len(blocks),) + blocks[0].shape, F32),
-            pltpu.VMEM(normal.shape, F32),
-            pltpu.VMEM((1, channels), F32),
-            pltpu.VMEM((1, channels), F32),
+            pltpu.VMEM(slopes.shape, F32),
+            pltpu.VMEM((cells, LANES), F32),
             pltpu.VMEM((cells, channels), F32),
             pltpu.VMEM((cells, LANES), F32),
             pltpu.VMEM((cells, LANES), F32),
             pltpu.VMEM(kernel.shape, F32),
             pltpu.VMEM((cells, channels), BF16),
-            pltpu.VMEM((images, channels), F32),
-            pltpu.VMEM((cells, LANES), F32),
-            pltpu.VMEM((images, channels), F32),
-            pltpu.VMEM((images, channels), F32),
-            dma((len(blocks),)),
-            dma((6,)),
+            dma((4,)),
+            dma((STEPS,)),
             dma((STEPS,)),
             dma((STEPS,)),
         ),
@@ -545,18 +599,26 @@
         out_ref[target] = stacked.astype(BF16)
 
 
-def strip_kernel(strips_ref, out_ref, mine_ref, theirs_ref):
+def strip_kernel(strips_ref, out_ref, mine_hbm, theirs_hbm, texts_ref, sems):
     line, rows, half = strips_ref.shape
-    texts = mine_ref.shape[0]
+    texts = texts_ref.shape[1]
     strip = rows - 2 * texts
     total = strips_ref[0].astype(F32)
     for source in range(1, line):
         total += strips_ref[source].astype(F32)
+    texts_ref[0] = total[strip : strip + texts]
+    texts_ref[1] = total[strip + texts :]
+    copies = [
+        pltpu.make_async_copy(texts_ref.at[side], target, sems.at[side])
+        for side, target in enumerate((mine_hbm, theirs_hbm))
+    ]
+    for copy in copies:
+        copy.start()
     low = total[:strip].astype(BF16)
     for target in range(line):
         out_ref[target] = low
-    mine_ref[...] = total[strip : strip + texts]
-    theirs_ref[...] = total[strip + texts :]
+    for copy in copies:
+        copy.wait()
 
 
 def text_kernel(text_ref, mine_ref, got_ref, scale_ref, out_ref):
@@ -692,17 +754,18 @@
         "head_merge", 1,
     )
     blocks = [merged[0]] + [along_x(merged[step], step) for step in (1, 2, 3)]
-    shared = (normal, norm_gain, head_gain, filtered, mean, inverse, kernel)
-    strips, *blocks = lax.optimization_barrier((strips, *blocks))
+    slopes, lean = block_lean(blocks, normal, norm_gain, head_gain, filtered, mean, inverse)
+    strips, slopes, lean = lax.optimization_barrier((strips, slopes, lean))
     sums, mine, theirs = call(
         strip_kernel,
         (
             (shape_of((line, strip, HALF), BF16), VMEM),
-            (shape_of((rows, HALF), F32), VMEM),
-            (shape_of((rows, HALF), F32), VMEM),
+            (shape_of((rows, HALF), F32), HBM),
+            (shape_of((rows, HALF), F32), HBM),
         ),
         ((strips, VMEM),),
         "strip_sum", 1,
+        scratch=(pltpu.VMEM((2, rows, HALF), F32), dma((2,))),
     )
     near_half = exchange(sums, LINE).reshape(share, HALF)
     grad_text = call(
@@ -711,7 +774,7 @@
         ((text_embed, VMEM), (mine, VMEM), (swap_core(theirs), VMEM), (logit_scale, SMEM)),
         "text_grad", 1,
     )
-    grad_features = block_backward(blocks, *shared, mine)
+    grad_features = block_backward(slopes, lean, filtered, mean, inverse, kernel, mine)
     near_half, grad_features, grad_text = lax.optimization_barrier(
         (near_half, grad_features, grad_text)
     )

time: 124 us -> 126 us (1.016)
  waiting for transfers between devices: 14 us -> 9.78 us
  starting transfers between devices: 56.6 us -> 59.7 us
  Pallas kernels: 38.7 us -> 41.6 us
    all_to_all x4, waiting for transfers between devices: 5.64 us -> 1.2 us  [exchange(): return lax.all_to_all(blocks, axes, 0, 0, tiled=True)]
    pallas_call x12 -> x13, Pallas kernels: 38.7 us -> 41.6 us  [call(): pl.pallas_call(body, out_shape=shapes[0] if single else shapes, in_specs=...]
    ppermute x8, starting transfers between devices: 17.2 us -> 18.9 us  [swap_core(): return lax.ppermute(block, 'core', ((0, 1), (1, 0)))]
    all_to_all x4, starting transfers between devices: 28 us -> 29.3 us  [exchange(): return lax.all_to_all(blocks, axes, 0, 0, tiled=True)]
  transfers between devices with their start and end apart: 20 -> 20, of which waited for: 9 -> 9; matrix products, arithmetic and copies ran while one was open for 0% -> 0% of each run, Pallas kernels for 25% -> 27%
where the time goes in v7:
time: 126 us
  starting transfers between devices  59.7 us (47%)
  Pallas kernels  41.6 us (33%)
  blocking collectives  10.7 us (8%)
  waiting for transfers between devices  9.78 us (8%)
  between operations  2.1 us (2%)
  local copies, waits for them, and re-layouts  1.81 us (1%)
    pallas_call x13, Pallas kernels, call(): pl.pallas_call(body, out_shape=shapes[0] if single else shapes, in_specs=...  41.6 us
    all_to_all x4, starting transfers between devices, exchange(): return lax.all_to_all(blocks, axes, 0, 0, tiled=True)  29.3 us
    ppermute x8, starting transfers between devices, swap_core(): return lax.ppermute(block, 'core', ((0, 1), (1, 0)))  18.9 us
    all_to_all x1, blocking collectives, exchange(): return lax.all_to_all(blocks, axes, 0, 0, tiled=True)  10.7 us
    ppermute x6, starting transfers between devices, along_x(): lax.ppermute(block, 'x', tuple(((i, (i + step) % 4) for i in range(4))))  6.72 us
    ppermute x8, waiting for transfers between devices, swap_core(): return lax.ppermute(block, 'core', ((0, 1), (1, 0)))  3.36 us
    ppermute x6, waiting for transfers between devices, along_x(): lax.ppermute(block, 'x', tuple(((i, (i + step) % 4) for i in range(4))))  2.84 us
    ppermute x1, starting transfers between devices, local(): next_line = lax.ppermute(own_line, 'y_hi', ((0, 1), (1, 0)))  2.71 us
  transfers between devices with their start and end apart: 20, of which 9 were waited for; matrix products, arithmetic and copies ran while one was open for 0% of the time, Pallas kernels for 27%

profile of v7, /device:TPU:1, one launch (start us, length us, event | category | flops | bytes accessed | tf_op | source)
XLA Modules:
  0.0 125.6 jit_solution(2839061398299858409)
XLA Ops:
  0.6 0.0 copy-start
  0.6 1.6 %text_pack.1 = bf16[16,4,1280]{2,1,0:T(4,128)(2,1)} custom-call(bf16[4,1152]{1,0:T(4,128)(2,1)} %text_ref.1, s32[4]{0:T(128)} %ids_hbm.2), custom_call_target="tpu_custom_call" | custom-call | bytes 3000000 | tf_op jit(solution)/shard_map/text_pack/pallas_call | solution.py:39
  2.2 10.1 %all-to-all-start = ((bf16[16,4,1280]{2,1,0:T(4,128)(2,1)}), bf16[16,4,1280]{2,1,0:T(4,128)(2,1)S(1)}, u32[]{:S(2)}, u32[]{:S(2)}) async-start(bf16[16,4,1280]{2,1,0:T(4,128)(2,1)} %text_pack.1), calls=%async_computation | async-start | bytes 327680 | tf_op jit(solution)/shard_map/all_to_all | solution.py:649
  12.4 14.1 %block_forward.1 = (f32[256,3072]{1,0:T(8,128)}, f32[256,128]{1,0:T(8,128)}, f32[256,128]{1,0:T(8,128)}, f32[4,3200]{1,0:T(4,128)}, bf16[8,4,512]{2,1,0:T(4,128)(2,1)}) custom-call(bf16[256,3072]{1,0:T(8,128)(2,1)} %bitcast.7, f32[7,7,3072]{2,1,0:T(8,128)} %kernel_hbm.3, f32[1,3072]{1,0:T(1,128)} %bitcast.9, f32[1,3072]{1,0:T(1,128)} %bitcast.11, s32[4]{0:T(128)} %ids_hbm.3), custom_call_target="tpu_custom_call" | custom-call | bytes 42000000 | tf_op jit(solution)/shard_map/block_forward/pallas_call | solution.py:39
  26.5 0.0 all-to-all-done.line_ref
  26.6 2.7 %collective-permute-start = (bf16[64,1280]{1,0:T(8,128)(2,1)S(1)}, bf16[64,1280]{1,0:T(8,128)(2,1)S(1)}, u32[]{:S(2)}, u32[]{:S(2)}) collective-permute-start(bf16[64,1280]{1,0:T(8,128)(2,1)S(1)} %line_rows.1.own_ref), channel_id=1, source_target_pairs={{0,1},{1,0},{2,3},{3,2},{4,5},{5,4},{6,7},{7,6},{8,9},{9,8},{10,11... | collective-permute-start | bytes 491528 | tf_op jit(solution)/shard_map/ppermute | solution.py:711
  29.3 10.7 %all_to_all.25.received_ref = bf16[8,4,512]{2,1,0:T(4,128)(2,1)S(1)} all-to-all(bf16[8,4,512]{2,1,0:T(4,128)(2,1)} %get-tuple-element.32), channel_id=1, replica_groups=mesh['y_lo'=2,'z'=8,'core'=2,'x'=4,'y_hi'=2] {'x','y_hi'}, dimensions={0} | all-to-all | bytes 65536 | tf_op jit(solution)/shard_map/all_to_all | solution.py:649
  39.9 0.0 copy-done
  39.9 1.1 partial_embed.1
  41.0 0.0 collective-permute-done.next_ref
  41.0 0.4 collective-permute-start.1
  41.4 2.4 %collective-permute-start.2 = (bf16[128,1280]{1,0:T(8,128)(2,1)S(1)}, bf16[128,1280]{1,0:T(8,128)(2,1)S(1)}, u32[]{:S(2)}, u32[]{:S(2)}) collective-permute-start(bf16[128,1280]{1,0:T(8,128)(2,1)S(1)} %join_texts.1.t0), channel_id=1, source_target_pairs={{0,6},{2,0},{4,2},{6,4},{1,7},{3,1},{5,3},{7,5},{8,14},{10,8},{12,... | collective-permute-start | bytes 983048 | tf_op jit(solution)/shard_map/ppermute | solution.py:657
  43.8 0.0 collective-permute-start.3
  43.8 4.4 %all-to-all-start.2 = ((bf16[8,32,1152]{2,1,0:T(8,128)(2,1)}), bf16[8,32,1152]{2,1,0:T(8,128)(2,1)S(1)}, u32[]{:S(2)}, u32[]{:S(2)}) async-start(bf16[8,32,1152]{2,1,0:T(8,128)(2,1)} %get-tuple-element.33), calls=%async_computation.2 | async-start | bytes 1179648 | tf_op jit(solution)/shard_map/all_to_all | solution.py:649
  48.2 3.8 %collective-permute-start.4 = (bf16[128,1280]{1,0:T(8,128)(2,1)S(1)}, bf16[128,1280]{1,0:T(8,128)(2,1)S(1)}, u32[]{:S(2)}, u32[]{:S(2)}) collective-permute-start(bf16[128,1280]{1,0:T(8,128)(2,1)S(1)} %join_texts.1.t0), channel_id=1, source_target_pairs={{0,8},{8,0},{1,9},{9,1},{2,10},{10,2},{3,11},{11,3},{4,12},{12,4},... | collective-permute-start | bytes 983048 | tf_op jit(solution)/shard_map/ppermute | solution.py:653
  52.0 0.0 collective-permute-done.1.t1
  52.0 10.7 %collective-permute-start.5 = (bf16[128,1280]{1,0:T(8,128)(2,1)S(1)}, bf16[128,1280]{1,0:T(8,128)(2,1)S(1)}, u32[]{:S(2)}, u32[]{:S(2)}) collective-permute-start(bf16[128,1280]{1,0:T(8,128)(2,1)S(1)} %collective-permute-done.1.t1), channel_id=1, source_target_pairs={{0,8},{8,0},{1,9},{9,1},{2,10},{10,2},{3,11},{11,3},{4,12},{12,4},... | collective-permute-start | bytes 983048 | tf_op jit(solution)/shard_map/ppermute | solution.py:653
  62.6 0.0 collective-permute-done.2.t2
  62.6 0.0 collective-permute-start.6
  62.7 0.0 collective-permute-done.3.t3
  62.7 0.5 collective-permute-start.7
  64.5 0.0 collective-permute-done.4.t4
  64.5 0.1 all-to-all-done.2.partials_ref
  64.5 0.0 collective-permute-done.5.t5
  64.6 0.0 collective-permute-done.6.t6
  64.6 0.4 collective-permute-done.7.t7
  65.0 3.0 %pairs.1 = (f32[4,4,384]{2,1,0:T(4,128)S(1)}, f32[4,4,384]{2,1,0:T(4,128)S(1)}, bf16[32,2560]{1,0:T(8,128)(2,1)S(1)}) custom-call(bf16[8,32,1152]{2,1,0:T(8,128)(2,1)S(1)} %all-to-all-done.2.partials_ref, bf16[32,128]{1,0:T(8,128)(2,1)S(1)} %get-tuple-element.34.hot_ref, bf16[384,1152]{1,0:T(8,128)(2,1)S(1)} %copy-done, bf16[128,1280]{1,0:T(8,128)(2,1)S(1)} %join_texts.1.t0, ...), custom_call_target="tpu_custom_call" | custom-call | bytes 12000000 | tf_op jit(solution)/shard_map/pairs/pallas_call | solution.py:39
  68.0 1.1 collective-permute-start.8
  69.0 0.1 collective-permute-start.9
  69.1 1.1 collective-permute-done.9.far_columns_ref
  70.2 0.0 collective-permute-done.8.theirs_ref
  70.2 1.2 strip_make.1
  71.5 7.5 %all-to-all-start.3 = ((bf16[16,32,640]{2,1,0:T(8,128)(2,1)}), bf16[16,32,640]{2,1,0:T(8,128)(2,1)S(1)}, u32[]{:S(2)}, u32[]{:S(2)}) async-start(bf16[16,32,640]{2,1,0:T(8,128)(2,1)} %strip_make.1), calls=%async_computation.3 | async-start | bytes 1310720 | tf_op jit(solution)/shard_map/all_to_all | solution.py:649
  79.0 2.0 %collective-permute-start.10 = (f32[4,4,384]{2,1,0:T(4,128)S(1)}, f32[4,4,384]{2,1,0:T(4,128)S(1)}, u32[]{:S(2)}, u32[]{:S(2)}) collective-permute-start(f32[4,4,384]{2,1,0:T(4,128)S(1)} %get-tuple-element.39), channel_id=1, source_target_pairs={{0,1},{1,0},{2,3},{3,2},{4,5},{5,4},{6,7},{7,6},{8,9},{9,8},{10,11... | collective-permute-start | bytes 73736 | tf_op jit(solution)/shard_map/ppermute | solution.py:737
  81.0 2.4 %collective-permute-done.10.got_ref = f32[4,4,384]{2,1,0:T(4,128)S(1)} collective-permute-done((f32[4,4,384]{2,1,0:T(4,128)S(1)}, f32[4,4,384]{2,1,0:T(4,128)S(1)}, u32[]{:S(2)}, u32[]{:S(2)}) %collective-permute-start.10) | collective-permute-done | bytes 24608 | tf_op jit(solution)/shard_map/ppermute | solution.py:737
  83.3 0.0 copy-start.4
  83.3 0.6 copy-done.4
  83.9 0.4 collective-permute-start.11
  84.4 3.5 %collective-permute-start.12 = (f32[2,4,384]{2,1,0:T(4,128)S(1)}, f32[2,4,384]{2,1,0:T(4,128)S(1)}, u32[]{:S(2)}, u32[]{:S(2)}) collective-permute-start(f32[2,4,384]{2,1,0:T(4,128)S(1)} %get-tuple-element.42), channel_id=1, source_target_pairs={{0,4},{2,6},{4,0},{6,2},{1,5},{3,7},{5,1},{7,3},{8,12},{10,14},{12... | collective-permute-start | bytes 36872 | tf_op jit(solution)/shard_map/ppermute | solution.py:657
  87.9 0.0 collective-permute-start.13
  87.9 0.2 collective-permute-done.11.s1
  88.1 0.0 copy-start.5
  88.1 1.3 %collective-permute-done.12.s2 = f32[2,4,384]{2,1,0:T(4,128)S(1)} collective-permute-done((f32[2,4,384]{2,1,0:T(4,128)S(1)}, f32[2,4,384]{2,1,0:T(4,128)S(1)}, u32[]{:S(2)}, u32[]{:S(2)}) %collective-permute-start.12) | collective-permute-done | bytes 12320 | tf_op jit(solution)/shard_map/ppermute | solution.py:657
  89.4 0.0 copy-start.6
  89.4 1.3 %collective-permute-done.13.s3 = f32[2,4,384]{2,1,0:T(4,128)S(1)} collective-permute-done((f32[2,4,384]{2,1,0:T(4,128)S(1)}, f32[2,4,384]{2,1,0:T(4,128)S(1)}, u32[]{:S(2)}, u32[]{:S(2)}) %collective-permute-start.13) | collective-permute-done | bytes 12320 | tf_op jit(solution)/shard_map/ppermute | solution.py:657
  90.7 0.0 copy-done.5
  90.7 0.0 copy-done.6
  90.7 0.6 copy-done.7
  91.3 3.8 %block_lean.1 = (f32[2,4,3072]{2,1,0:T(4,128)}, f32[256,128]{1,0:T(8,128)}) custom-call(f32[2,4,384]{2,1,0:T(4,128)} %copy-done.4, f32[2,4,384]{2,1,0:T(4,128)} %copy-done.5, f32[2,4,384]{2,1,0:T(4,128)} %copy-done.6, f32[2,4,384]{2,1,0:T(4,128)} %copy-done.7, f32[4,3200]{1,0:T(4,128)} %get-tuple-element.44.normal_ref, f32[1,3072]{1,0:T(1,128)} %bitcast.10, ...), custom_call_target="tpu_custom_call" | custom-call | bytes 9000000 | tf_op jit(solution)/shard_map/block_lean/pallas_call | solution.py:39
  95.2 1.1 all-to-all-done.3.strips_ref
  96.3 0.9 strip_sum.1
  97.2 0.0 copy-start.1
  97.2 0.6 copy-done.1
  97.8 7.3 %all-to-all-start.4 = ((bf16[16,24,640]{2,1,0:T(8,128)(2,1)}), bf16[16,24,640]{2,1,0:T(8,128)(2,1)S(1)}, u32[]{:S(2)}, u32[]{:S(2)}) async-start(bf16[16,24,640]{2,1,0:T(8,128)(2,1)} %get-tuple-element.51), calls=%async_computation.4 | async-start | bytes 983040 | tf_op jit(solution)/shard_map/all_to_all | solution.py:649
  105.1 2.8 %collective-permute-start.14 = (f32[4,640]{1,0:T(4,128)S(1)}, f32[4,640]{1,0:T(4,128)S(1)}, u32[]{:S(2)}, u32[]{:S(2)}) collective-permute-start(f32[4,640]{1,0:T(4,128)S(1)} %get-tuple-element.55), channel_id=1, source_target_pairs={{0,8},{8,0},{1,9},{9,1},{2,10},{10,2},{3,11},{11,3},{4,12},{12,4},... | collective-permute-start | bytes 30728 | tf_op jit(solution)/shard_map/ppermute | solution.py:653
  107.9 13.7 %block_backward.1 = bf16[256,3072]{1,0:T(8,128)(2,1)} custom-call(f32[2,4,3072]{2,1,0:T(4,128)} %get-tuple-element.52.slopes_hbm, f32[256,128]{1,0:T(8,128)} %get-tuple-element.53.lean_hbm, f32[256,3072]{1,0:T(8,128)} %get-tuple-element.45.filtered_hbm, f32[256,128]{1,0:T(8,128)} %get-tuple-element.46.mean_ref.mean_hbm, ...), custom_call_target="tpu_custom_call" | custom-call | bytes 39000000 | tf_op jit(solution)/shard_map/block_backward/pallas_call | solution.py:39
  121.6 0.0 collective-permute-done.14.got_ref
  121.6 0.0 copy-done.2
  121.6 0.0 copy-done.3
  121.6 0.8 text_grad.1
  122.4 0.0 all-to-all-done.4
  122.4 0.0 collective-permute-start.15
  122.4 1.8 %collective-permute-done.15.far_ref = bf16[384,640]{1,0:T(8,128)(2,1)S(1)} collective-permute-done((bf16[384,640]{1,0:T(8,128)(2,1)S(1)}, bf16[384,640]{1,0:T(8,128)(2,1)S(1)}, u32[]{:S(2)}, u32[]{:S(2)}) %collective-permute-start.15) | collective-permute-done | bytes 491552 | tf_op jit(solution)/shard_map/ppermute | solution.py:653
  124.3 1.3 %proj_join.1 = f32[384,1152]{1,0:T(8,128)} custom-call(bf16[384,640]{1,0:T(8,128)(2,1)S(1)} %bitcast.6, bf16[384,640]{1,0:T(8,128)(2,1)S(1)} %collective-permute-done.15.far_ref), custom_call_target="tpu_custom_call" | custom-call | bytes 6000000 | tf_op jit(solution)/shard_map/proj_join/pallas_call | solution.py:39
  (6 shorter events, 0.1 us)
Async XLA Ops:
  0.6 39.3 %copy-start = (bf16[384,1152]{1,0:T(8,128)(2,1)S(1)}, bf16[384,1152]{1,0:T(8,128)(2,1)}, u32[]{:S(2)}) copy-start(bf16[384,1152]{1,0:T(8,128)(2,1)} %projection_ref.3) | copy-start | bytes 2654212
  2.2 24.3 %all-to-all-start = ((bf16[16,4,1280]{2,1,0:T(4,128)(2,1)}), bf16[16,4,1280]{2,1,0:T(4,128)(2,1)S(1)}, u32[]{:S(2)}, u32[]{:S(2)}) async-start(bf16[16,4,1280]{2,1,0:T(4,128)(2,1)} %text_pack.1), calls=%async_computation | async-start | bytes 327680 | tf_op jit(solution)/shard_map/all_to_all | solution.py:649
  26.6 14.5 %collective-permute-start = (bf16[64,1280]{1,0:T(8,128)(2,1)S(1)}, bf16[64,1280]{1,0:T(8,128)(2,1)S(1)}, u32[]{:S(2)}, u32[]{:S(2)}) collective-permute-start(bf16[64,1280]{1,0:T(8,128)(2,1)S(1)} %line_rows.1.own_ref), channel_id=1, source_target_pairs={{0,1},{1,0},{2,3},{3,2},{4,5},{5,4},{6,7},{7,6},{8,9},{9,8},{10,11... | collective-permute-start | bytes 491528 | tf_op jit(solution)/shard_map/ppermute | solution.py:711
  41.0 10.9 %collective-permute-start.1 = (bf16[128,1280]{1,0:T(8,128)(2,1)S(1)}, bf16[128,1280]{1,0:T(8,128)(2,1)S(1)}, u32[]{:S(2)}, u32[]{:S(2)}) collective-permute-start(bf16[128,1280]{1,0:T(8,128)(2,1)S(1)} %join_texts.1.t0), channel_id=1, source_target_pairs={{0,2},{2,4},{4,6},{6,0},{1,3},{3,5},{5,7},{7,1},{8,10},{10,12},{12... | collective-permute-start | bytes 983048 | tf_op jit(solution)/shard_map/ppermute | solution.py:657
  41.4 21.2 %collective-permute-start.2 = (bf16[128,1280]{1,0:T(8,128)(2,1)S(1)}, bf16[128,1280]{1,0:T(8,128)(2,1)S(1)}, u32[]{:S(2)}, u32[]{:S(2)}) collective-permute-start(bf16[128,1280]{1,0:T(8,128)(2,1)S(1)} %join_texts.1.t0), channel_id=1, source_target_pairs={{0,6},{2,0},{4,2},{6,4},{1,7},{3,1},{5,3},{7,5},{8,14},{10,8},{12,... | collective-permute-start | bytes 983048 | tf_op jit(solution)/shard_map/ppermute | solution.py:657
  43.8 18.9 %collective-permute-start.3 = (bf16[128,1280]{1,0:T(8,128)(2,1)S(1)}, bf16[128,1280]{1,0:T(8,128)(2,1)S(1)}, u32[]{:S(2)}, u32[]{:S(2)}) collective-permute-start(bf16[128,1280]{1,0:T(8,128)(2,1)S(1)} %join_texts.1.t0), channel_id=1, source_target_pairs={{0,4},{2,6},{4,0},{6,2},{1,5},{3,7},{5,1},{7,3},{8,12},{10,14},{12... | collective-permute-start | bytes 983048 | tf_op jit(solution)/shard_map/ppermute | solution.py:657
  43.8 20.7 %all-to-all-start.2 = ((bf16[8,32,1152]{2,1,0:T(8,128)(2,1)}), bf16[8,32,1152]{2,1,0:T(8,128)(2,1)S(1)}, u32[]{:S(2)}, u32[]{:S(2)}) async-start(bf16[8,32,1152]{2,1,0:T(8,128)(2,1)} %get-tuple-element.33), calls=%async_computation.2 | async-start | bytes 1179648 | tf_op jit(solution)/shard_map/all_to_all | solution.py:649
  48.2 16.3 %collective-permute-start.4 = (bf16[128,1280]{1,0:T(8,128)(2,1)S(1)}, bf16[128,1280]{1,0:T(8,128)(2,1)S(1)}, u32[]{:S(2)}, u32[]{:S(2)}) collective-permute-start(bf16[128,1280]{1,0:T(8,128)(2,1)S(1)} %join_texts.1.t0), channel_id=1, source_target_pairs={{0,8},{8,0},{1,9},{9,1},{2,10},{10,2},{3,11},{11,3},{4,12},{12,4},... | collective-permute-start | bytes 983048 | tf_op jit(solution)/shard_map/ppermute | solution.py:653
  52.0 12.6 %collective-permute-start.5 = (bf16[128,1280]{1,0:T(8,128)(2,1)S(1)}, bf16[128,1280]{1,0:T(8,128)(2,1)S(1)}, u32[]{:S(2)}, u32[]{:S(2)}) collective-permute-start(bf16[128,1280]{1,0:T(8,128)(2,1)S(1)} %collective-permute-done.1.t1), channel_id=1, source_target_pairs={{0,8},{8,0},{1,9},{9,1},{2,10},{10,2},{3,11},{11,3},{4,12},{12,4},... | collective-permute-start | bytes 983048 | tf_op jit(solution)/shard_map/ppermute | solution.py:653
  62.6 1.9 %collective-permute-start.6 = (bf16[128,1280]{1,0:T(8,128)(2,1)S(1)}, bf16[128,1280]{1,0:T(8,128)(2,1)}, u32[]{:S(2)}, u32[]{:S(2)}) collective-permute-start(bf16[128,1280]{1,0:T(8,128)(2,1)S(1)} %collective-permute-done.2.t2), channel_id=1, source_target_pairs={{0,8},{8,0},{1,9},{9,1},{2,10},{10,2},{3,11},{11,3},{4,12},{12,4},... | collective-permute-start | bytes 983048 | tf_op jit(solution)/shard_map/ppermute | solution.py:653
  62.7 2.3 %collective-permute-start.7 = (bf16[128,1280]{1,0:T(8,128)(2,1)S(1)}, bf16[128,1280]{1,0:T(8,128)(2,1)}, u32[]{:S(2)}, u32[]{:S(2)}) collective-permute-start(bf16[128,1280]{1,0:T(8,128)(2,1)S(1)} %collective-permute-done.3.t3), channel_id=1, source_target_pairs={{0,8},{8,0},{1,9},{9,1},{2,10},{10,2},{3,11},{11,3},{4,12},{12,4},... | collective-permute-start | bytes 983048 | tf_op jit(solution)/shard_map/ppermute | solution.py:653
  68.0 2.3 %collective-permute-start.8 = (bf16[32,2560]{1,0:T(8,128)(2,1)S(1)}, bf16[32,2560]{1,0:T(8,128)(2,1)S(1)}, u32[]{:S(2)}, u32[]{:S(2)}) collective-permute-start(bf16[32,2560]{1,0:T(8,128)(2,1)S(1)} %get-tuple-element.37.mine_ref), channel_id=1, source_target_pairs={{0,8},{8,0},{1,9},{9,1},{2,10},{10,2},{3,11},{11,3},{4,12},{12,4},... | collective-permute-start | bytes 491528 | tf_op jit(solution)/shard_map/ppermute | solution.py:653
  69.0 1.2 collective-permute-start.9
  71.5 24.8 %all-to-all-start.3 = ((bf16[16,32,640]{2,1,0:T(8,128)(2,1)}), bf16[16,32,640]{2,1,0:T(8,128)(2,1)S(1)}, u32[]{:S(2)}, u32[]{:S(2)}) async-start(bf16[16,32,640]{2,1,0:T(8,128)(2,1)} %strip_make.1), calls=%async_computation.3 | async-start | bytes 1310720 | tf_op jit(solution)/shard_map/all_to_all | solution.py:649
  79.0 4.3 %collective-permute-start.10 = (f32[4,4,384]{2,1,0:T(4,128)S(1)}, f32[4,4,384]{2,1,0:T(4,128)S(1)}, u32[]{:S(2)}, u32[]{:S(2)}) collective-permute-start(f32[4,4,384]{2,1,0:T(4,128)S(1)} %get-tuple-element.39), channel_id=1, source_target_pairs={{0,1},{1,0},{2,3},{3,2},{4,5},{5,4},{6,7},{7,6},{8,9},{9,8},{10,11... | collective-permute-start | bytes 73736 | tf_op jit(solution)/shard_map/ppermute | solution.py:737
  83.3 0.6 copy-start.4
  83.9 4.2 %collective-permute-start.11 = (f32[2,4,384]{2,1,0:T(4,128)S(1)}, f32[2,4,384]{2,1,0:T(4,128)S(1)}, u32[]{:S(2)}, u32[]{:S(2)}) collective-permute-start(f32[2,4,384]{2,1,0:T(4,128)S(1)} %get-tuple-element.41), channel_id=1, source_target_pairs={{0,2},{2,4},{4,6},{6,0},{1,3},{3,5},{5,7},{7,1},{8,10},{10,12},{12... | collective-permute-start | bytes 36872 | tf_op jit(solution)/shard_map/ppermute | solution.py:657
  84.4 5.0 %collective-permute-start.12 = (f32[2,4,384]{2,1,0:T(4,128)S(1)}, f32[2,4,384]{2,1,0:T(4,128)S(1)}, u32[]{:S(2)}, u32[]{:S(2)}) collective-permute-start(f32[2,4,384]{2,1,0:T(4,128)S(1)} %get-tuple-element.42), channel_id=1, source_target_pairs={{0,4},{2,6},{4,0},{6,2},{1,5},{3,7},{5,1},{7,3},{8,12},{10,14},{12... | collective-permute-start | bytes 36872 | tf_op jit(solution)/shard_map/ppermute | solution.py:657
  87.9 2.8 %collective-permute-start.13 = (f32[2,4,384]{2,1,0:T(4,128)S(1)}, f32[2,4,384]{2,1,0:T(4,128)S(1)}, u32[]{:S(2)}, u32[]{:S(2)}) collective-permute-start(f32[2,4,384]{2,1,0:T(4,128)S(1)} %get-tuple-element.43), channel_id=1, source_target_pairs={{0,6},{2,0},{4,2},{6,4},{1,7},{3,1},{5,3},{7,5},{8,14},{10,8},{12,... | collective-permute-start | bytes 36872 | tf_op jit(solution)/shard_map/ppermute | solution.py:657
  88.1 2.7 %copy-start.5 = (f32[2,4,384]{2,1,0:T(4,128)}, f32[2,4,384]{2,1,0:T(4,128)S(1)}, u32[]{:S(2)}) copy-start(f32[2,4,384]{2,1,0:T(4,128)S(1)} %collective-permute-done.11.s1) | copy-start | bytes 36868
  89.4 1.3 %copy-start.6 = (f32[2,4,384]{2,1,0:T(4,128)}, f32[2,4,384]{2,1,0:T(4,128)S(1)}, u32[]{:S(2)}) copy-start(f32[2,4,384]{2,1,0:T(4,128)S(1)} %collective-permute-done.12.s2) | copy-start | bytes 36868
  90.7 0.6 copy-start.7
  97.2 0.6 copy-start.1
  97.8 24.6 %all-to-all-start.4 = ((bf16[16,24,640]{2,1,0:T(8,128)(2,1)}), bf16[16,24,640]{2,1,0:T(8,128)(2,1)S(1)}, u32[]{:S(2)}, u32[]{:S(2)}) async-start(bf16[16,24,640]{2,1,0:T(8,128)(2,1)} %get-tuple-element.51), calls=%async_computation.4 | async-start | bytes 983040 | tf_op jit(solution)/shard_map/all_to_all | solution.py:649
  105.1 16.5 %collective-permute-start.14 = (f32[4,640]{1,0:T(4,128)S(1)}, f32[4,640]{1,0:T(4,128)S(1)}, u32[]{:S(2)}, u32[]{:S(2)}) collective-permute-start(f32[4,640]{1,0:T(4,128)S(1)} %get-tuple-element.55), channel_id=1, source_target_pairs={{0,8},{8,0},{1,9},{9,1},{2,10},{10,2},{3,11},{11,3},{4,12},{12,4},... | collective-permute-start | bytes 30728 | tf_op jit(solution)/shard_map/ppermute | solution.py:653
  107.9 13.7 %copy-start.2 = (f32[4,640]{1,0:T(4,128)S(1)}, f32[4,640]{1,0:T(4,128)}, u32[]{:S(2)}) copy-start(f32[4,640]{1,0:T(4,128)} %copy-done.1) | copy-start | bytes 30724
  107.9 13.7 %copy-start.3 = (bf16[4,1152]{1,0:T(4,128)(2,1)S(1)}, bf16[4,1152]{1,0:T(4,128)(2,1)}, u32[]{:S(2)}) copy-start(bf16[4,1152]{1,0:T(4,128)(2,1)} %text_ref.1) | copy-start | bytes 27652
  122.4 1.9 %collective-permute-start.15 = (bf16[384,640]{1,0:T(8,128)(2,1)S(1)}, bf16[384,640]{1,0:T(8,128)(2,1)S(1)}, u32[]{:S(2)}, u32[]{:S(2)}) collective-permute-start(bf16[384,640]{1,0:T(8,128)(2,1)S(1)} %bitcast.5), channel_id=1, source_target_pairs={{0,8},{8,0},{1,9},{9,1},{2,10},{10,2},{3,11},{11,3},{4,12},{12,4},... | collective-permute-start | bytes 1474568 | tf_op jit(solution)/shard_map/ppermute | solution.py:653

commit v8 on v5

--- a/solution.py
+++ b/solution.py
@@ -85,7 +85,7 @@
 def forward_kernel(
     field_hbm, kernel_hbm, gain_hbm, head_gain_hbm, ids_hbm,
     filtered_hbm, mean_ref, inverse_ref, normal_ref, send_ref,
-    field_ref, kernel_ref, gain_ref, head_gain_ref, ids_ref, filtered_ref, pooled_ref, total_ref,
+    field_ref, kernel_ref, gain_ref, head_gain_ref, ids_ref, filtered_ref, pooled_ref, total_ref, mixed_ref,
     field_sems, kernel_sems, small_sems, out_sems,
 ):
     images = field_ref.shape[0] // CELLS
@@ -126,23 +126,20 @@
     total_ref[...] = jnp.zeros_like(total_ref)
 
     def filter_chunk(chunk, carry):
-        step = chunk // per_block
-
-        @pl.when(chunk == step * per_block)
-        def _():
-            field_copy(step).wait()
-            kernel_copy(step).wait()
-
         at = pl.ds(pl.multiple_of(chunk * LANES, LANES), LANES)
-        for first in range(0, images, 2):
+        for first in range(0, images, 4):
             fields = []
-            for image in range(first, first + 2):
+            for image in range(first, first + 4):
                 rows = []
                 for pair in range(SIDE // 2):
                     both = field_ref[pl.ds(image * CELLS + pair * 2 * SIDE, 2 * SIDE), at]
                     both = both.astype(jnp.float32)
                     rows += [both[:SIDE], both[SIDE:]]
                 fields.append(rows)
+                level = rows[0]
+                for row in rows[1:]:
+                    level = level + row
+                mixed_ref[pl.ds(image * SIDE, SIDE), at] = level
             sums = [[None] * SIDE for _ in fields]
             filter_rows(fields, sums, kernel_ref, at, False)
             for offset, total in enumerate(sums):
@@ -152,7 +149,15 @@
                     total_ref[cells, :] += total[row]
         return carry
 
-    lax.fori_loop(0, chunks, filter_chunk, 0)
+    def filter_block(step, carry):
+        field_copy(step).wait()
+        kernel_copy(step).wait()
+        first = step * per_block
+        return lax.fori_loop(
+            0, per_block, lambda chunk, held: filter_chunk(first + chunk, held), carry, unroll=2
+        )
+
+    lax.fori_loop(0, STEPS, filter_block, 0)
     for step in range(STEPS):
         filtered_copy(step).start()
     for copy in small_copies:
@@ -171,7 +176,7 @@
             return squares + centred * centred
 
         squares = lax.fori_loop(
-            0, chunks, spread_chunk, jnp.zeros((CELLS, LANES), jnp.float32), unroll=4
+            0, chunks, spread_chunk, jnp.zeros((CELLS, LANES), jnp.float32), unroll=8
         )
         spread = jnp.sum(squares, axis=1, keepdims=True) * part
         inverse_ref[cells, :] = jnp.broadcast_to(lax.rsqrt(spread + EPSILON), (CELLS, LANES))
@@ -184,11 +189,15 @@
         def pool_chunk(chunk, carry):
             at = pl.ds(pl.multiple_of(chunk * LANES, LANES), LANES)
             normal = (filtered_ref[cells, at] - average) * inverse
-            mixed = field_ref[cells, at].astype(jnp.float32) + normal * gain_ref[:, at]
-            pooled_ref[pl.ds(image, 1), at] = jnp.sum(mixed, axis=0, keepdims=True) * (1.0 / CELLS)
+            level = jnp.sum(normal.reshape(SIDE, SIDE, LANES), axis=0)
+            spot = pl.ds(image * SIDE, SIDE)
+            mixed_ref[spot, at] = mixed_ref[spot, at] + level * gain_ref[:, at]
             return carry
 
-        lax.fori_loop(0, chunks, pool_chunk, 0, unroll=2)
+        lax.fori_loop(0, chunks, pool_chunk, 0, unroll=8)
+        pooled_ref[pl.ds(image, 1), :] = jnp.sum(
+            mixed_ref[pl.ds(image * SIDE, SIDE), :], axis=0, keepdims=True
+        ) * (1.0 / CELLS)
 
     pooled = pooled_ref[...]
     centred = pooled - jnp.sum(pooled, axis=1, keepdims=True) * part
@@ -239,6 +248,7 @@
             pltpu.VMEM((cells, channels), F32),
             pltpu.VMEM((images, channels), F32),
             pltpu.VMEM((cells, LANES), F32),
+            pltpu.VMEM((images * SIDE, channels), F32),
             dma((STEPS,)),
             dma((STEPS,)),
             dma((3,)),
@@ -354,15 +364,17 @@
                     two = jnp.concatenate(total[2 * half : 2 * half + 2], axis=0)
                     spot = pl.ds((first + offset) * CELLS + half * 2 * SIDE, 2 * SIDE)
                     out_ref[spot, at] = two.astype(jnp.bfloat16)
-        step = chunk // per_block
-
-        @pl.when(chunk == step * per_block + per_block - 1)
-        def _():
-            out_copy(step).start()
-
         return carry
 
-    lax.fori_loop(0, chunks, filter_chunk, 0)
+    def filter_block(step, carry):
+        first = step * per_block
+        lax.fori_loop(
+            0, per_block, lambda chunk, held: filter_chunk(first + chunk, held), 0, unroll=2
+        )
+        out_copy(step).start()
+        return carry
+
+    lax.fori_loop(0, STEPS, filter_block, 0)
     for step in range(STEPS):
         out_copy(step).wait()
 

time: 124 us -> 122 us (0.984)
  Pallas kernels: 38.7 us -> 36.3 us
    pallas_call x12, Pallas kernels: 38.7 us -> 36.3 us  [call(): pl.pallas_call(body, out_shape=shapes[0] if single else shapes, in_specs=...]
  transfers between devices with their start and end apart: 20 -> 20, of which waited for: 9 -> 9; matrix products, arithmetic and copies ran while one was open for 0% -> 0% of each run, Pallas kernels for 25% -> 23%
where the time goes in v8:
time: 122 us; the launch traced here: 121 us
  starting transfers between devices  57 us (47%)
  Pallas kernels  36.3 us (30%)
  waiting for transfers between devices  13.9 us (11%)
  blocking collectives  10.7 us (9%)
  between operations  2.09 us (2%)
    pallas_call x12, Pallas kernels, call(): pl.pallas_call(body, out_shape=shapes[0] if single else shapes, in_specs=...  36.3 us
    all_to_all x4, starting transfers between devices, exchange(): return lax.all_to_all(blocks, axes, 0, 0, tiled=True)  28 us
    ppermute x8, starting transfers between devices, swap_core(): return lax.ppermute(block, 'core', ((0, 1), (1, 0)))  17.6 us
    all_to_all x1, blocking collectives, exchange(): return lax.all_to_all(blocks, axes, 0, 0, tiled=True)  10.7 us
    ppermute x6, starting transfers between devices, along_x(): lax.ppermute(block, 'x', tuple(((i, (i + step) % 4) for i in range(4))))  6.71 us
    all_to_all x4, waiting for transfers between devices, exchange(): return lax.all_to_all(blocks, axes, 0, 0, tiled=True)  5.64 us
    ppermute x8, waiting for transfers between devices, swap_core(): return lax.ppermute(block, 'core', ((0, 1), (1, 0)))  3.01 us
    ppermute x6, waiting for transfers between devices, along_x(): lax.ppermute(block, 'x', tuple(((i, (i + step) % 4) for i in range(4))))  2.84 us
  transfers between devices with their start and end apart: 20, of which 9 were waited for; matrix products, arithmetic and copies ran while one was open for 0% of the time, Pallas kernels for 23%

profile of v8, /device:TPU:1, one launch (start us, length us, event | category | flops | bytes accessed | tf_op | source)
XLA Modules:
  0.0 121.1 jit_solution(7680998237921983221)
XLA Ops:
  0.6 0.0 copy-start
  0.6 1.6 %text_pack.1 = bf16[16,4,1280]{2,1,0:T(4,128)(2,1)} custom-call(bf16[4,1152]{1,0:T(4,128)(2,1)} %text_ref.1, s32[4]{0:T(128)} %ids_hbm.2), custom_call_target="tpu_custom_call" | custom-call | bytes 3000000 | tf_op jit(solution)/shard_map/text_pack/pallas_call | solution.py:39
  2.2 10.1 %all-to-all-start = ((bf16[16,4,1280]{2,1,0:T(4,128)(2,1)}), bf16[16,4,1280]{2,1,0:T(4,128)(2,1)S(1)}, u32[]{:S(2)}, u32[]{:S(2)}) async-start(bf16[16,4,1280]{2,1,0:T(4,128)(2,1)} %text_pack.1), calls=%async_computation | async-start | bytes 327680 | tf_op jit(solution)/shard_map/all_to_all | solution.py:599
  12.4 12.9 %block_forward.1 = (f32[256,3072]{1,0:T(8,128)}, f32[256,128]{1,0:T(8,128)}, f32[256,128]{1,0:T(8,128)}, f32[4,3200]{1,0:T(4,128)}, bf16[8,4,512]{2,1,0:T(4,128)(2,1)}) custom-call(bf16[256,3072]{1,0:T(8,128)(2,1)} %bitcast.7, f32[7,7,3072]{2,1,0:T(8,128)} %kernel_hbm.3, f32[1,3072]{1,0:T(1,128)} %bitcast.9, f32[1,3072]{1,0:T(1,128)} %bitcast.11, s32[4]{0:T(128)} %ids_hbm.3), custom_call_target="tpu_custom_call" | custom-call | bytes 42000000 | tf_op jit(solution)/shard_map/block_forward/pallas_call | solution.py:39
  25.3 0.0 all-to-all-done.line_ref
  25.4 2.7 %collective-permute-start = (bf16[64,1280]{1,0:T(8,128)(2,1)S(1)}, bf16[64,1280]{1,0:T(8,128)(2,1)S(1)}, u32[]{:S(2)}, u32[]{:S(2)}) collective-permute-start(bf16[64,1280]{1,0:T(8,128)(2,1)S(1)} %line_rows.1.own_ref), channel_id=1, source_target_pairs={{0,1},{1,0},{2,3},{3,2},{4,5},{5,4},{6,7},{7,6},{8,9},{9,8},{10,11... | collective-permute-start | bytes 491528 | tf_op jit(solution)/shard_map/ppermute | solution.py:661
  28.1 10.7 %all_to_all.25.received_ref = bf16[8,4,512]{2,1,0:T(4,128)(2,1)S(1)} all-to-all(bf16[8,4,512]{2,1,0:T(4,128)(2,1)} %get-tuple-element.32), channel_id=1, replica_groups=mesh['y_lo'=2,'z'=8,'core'=2,'x'=4,'y_hi'=2] {'x','y_hi'}, dimensions={0} | all-to-all | bytes 65536 | tf_op jit(solution)/shard_map/all_to_all | solution.py:599
  38.8 0.0 copy-done
  38.8 1.1 partial_embed.1
  39.9 0.0 collective-permute-done.next_ref
  39.9 0.4 collective-permute-start.1
  40.2 2.4 %collective-permute-start.2 = (bf16[128,1280]{1,0:T(8,128)(2,1)S(1)}, bf16[128,1280]{1,0:T(8,128)(2,1)S(1)}, u32[]{:S(2)}, u32[]{:S(2)}) collective-permute-start(bf16[128,1280]{1,0:T(8,128)(2,1)S(1)} %join_texts.1.t0), channel_id=1, source_target_pairs={{0,6},{2,0},{4,2},{6,4},{1,7},{3,1},{5,3},{7,5},{8,14},{10,8},{12,... | collective-permute-start | bytes 983048 | tf_op jit(solution)/shard_map/ppermute | solution.py:607
  42.6 0.0 collective-permute-start.3
  42.6 4.4 %all-to-all-start.2 = ((bf16[8,32,1152]{2,1,0:T(8,128)(2,1)}), bf16[8,32,1152]{2,1,0:T(8,128)(2,1)S(1)}, u32[]{:S(2)}, u32[]{:S(2)}) async-start(bf16[8,32,1152]{2,1,0:T(8,128)(2,1)} %get-tuple-element.33), calls=%async_computation.2 | async-start | bytes 1179648 | tf_op jit(solution)/shard_map/all_to_all | solution.py:599
  47.0 3.8 %collective-permute-start.4 = (bf16[128,1280]{1,0:T(8,128)(2,1)S(1)}, bf16[128,1280]{1,0:T(8,128)(2,1)S(1)}, u32[]{:S(2)}, u32[]{:S(2)}) collective-permute-start(bf16[128,1280]{1,0:T(8,128)(2,1)S(1)} %join_texts.1.t0), channel_id=1, source_target_pairs={{0,8},{8,0},{1,9},{9,1},{2,10},{10,2},{3,11},{11,3},{4,12},{12,4},... | collective-permute-start | bytes 983048 | tf_op jit(solution)/shard_map/ppermute | solution.py:603
  50.8 0.0 collective-permute-done.1.t1
  50.8 10.7 %collective-permute-start.5 = (bf16[128,1280]{1,0:T(8,128)(2,1)S(1)}, bf16[128,1280]{1,0:T(8,128)(2,1)S(1)}, u32[]{:S(2)}, u32[]{:S(2)}) collective-permute-start(bf16[128,1280]{1,0:T(8,128)(2,1)S(1)} %collective-permute-done.1.t1), channel_id=1, source_target_pairs={{0,8},{8,0},{1,9},{9,1},{2,10},{10,2},{3,11},{11,3},{4,12},{12,4},... | collective-permute-start | bytes 983048 | tf_op jit(solution)/shard_map/ppermute | solution.py:603
  61.5 0.0 collective-permute-done.2.t2
  61.5 0.0 collective-permute-start.6
  61.5 0.0 collective-permute-done.3.t3
  61.5 0.5 collective-permute-start.7
  63.3 0.0 collective-permute-done.4.t4
  63.3 0.1 all-to-all-done.2.partials_ref
  63.4 0.0 collective-permute-done.5.t5
  63.4 0.0 collective-permute-done.6.t6
  63.4 0.4 collective-permute-done.7.t7
  63.8 3.0 %pairs.1 = (f32[4,4,384]{2,1,0:T(4,128)S(1)}, f32[4,4,384]{2,1,0:T(4,128)S(1)}, bf16[32,2560]{1,0:T(8,128)(2,1)S(1)}) custom-call(bf16[8,32,1152]{2,1,0:T(8,128)(2,1)S(1)} %all-to-all-done.2.partials_ref, bf16[32,128]{1,0:T(8,128)(2,1)S(1)} %get-tuple-element.34.hot_ref, bf16[384,1152]{1,0:T(8,128)(2,1)S(1)} %copy-done, bf16[128,1280]{1,0:T(8,128)(2,1)S(1)} %join_texts.1.t0, ...), custom_call_target="tpu_custom_call" | custom-call | bytes 12000000 | tf_op jit(solution)/shard_map/pairs/pallas_call | solution.py:39
  66.8 1.1 collective-permute-start.8
  67.9 0.1 collective-permute-start.9
  68.0 1.1 collective-permute-done.9.far_columns_ref
  69.1 0.0 collective-permute-done.8.theirs_ref
  69.1 1.2 %strip_make.1 = bf16[16,32,640]{2,1,0:T(8,128)(2,1)} custom-call(bf16[32,2560]{1,0:T(8,128)(2,1)S(1)} %get-tuple-element.37.mine_ref, bf16[32,2560]{1,0:T(8,128)(2,1)S(1)} %collective-permute-done.8.theirs_ref, bf16[32,384]{1,0:T(8,128)(2,1)S(1)} %get-tuple-element.36.after_ref.columns_ref, bf16[32,384]{1,0:T(8,128)(2,1)S(1)} %collective-permute-done.9.far_columns_ref), custom_call_target="tpu_custom_call" | custom-call | bytes 6000000 | tf_op jit(solution)/shard_map/strip_make/pallas_call | solution.py:39
  70.3 7.6 %all-to-all-start.3 = ((bf16[16,32,640]{2,1,0:T(8,128)(2,1)}), bf16[16,32,640]{2,1,0:T(8,128)(2,1)S(1)}, u32[]{:S(2)}, u32[]{:S(2)}) async-start(bf16[16,32,640]{2,1,0:T(8,128)(2,1)} %strip_make.1), calls=%async_computation.3 | async-start | bytes 1310720 | tf_op jit(solution)/shard_map/all_to_all | solution.py:599
  77.9 1.9 %collective-permute-start.10 = (f32[4,4,384]{2,1,0:T(4,128)S(1)}, f32[4,4,384]{2,1,0:T(4,128)S(1)}, u32[]{:S(2)}, u32[]{:S(2)}) collective-permute-start(f32[4,4,384]{2,1,0:T(4,128)S(1)} %get-tuple-element.39), channel_id=1, source_target_pairs={{0,1},{1,0},{2,3},{3,2},{4,5},{5,4},{6,7},{7,6},{8,9},{9,8},{10,11... | collective-permute-start | bytes 73736 | tf_op jit(solution)/shard_map/ppermute | solution.py:687
  79.8 2.4 %collective-permute-done.10.got_ref = f32[4,4,384]{2,1,0:T(4,128)S(1)} collective-permute-done((f32[4,4,384]{2,1,0:T(4,128)S(1)}, f32[4,4,384]{2,1,0:T(4,128)S(1)}, u32[]{:S(2)}, u32[]{:S(2)}) %collective-permute-start.10) | collective-permute-done | bytes 24608 | tf_op jit(solution)/shard_map/ppermute | solution.py:687
  82.2 0.0 copy-start.4
  82.2 0.6 copy-done.4
  82.8 0.4 collective-permute-start.11
  83.2 3.5 %collective-permute-start.12 = (f32[2,4,384]{2,1,0:T(4,128)S(1)}, f32[2,4,384]{2,1,0:T(4,128)S(1)}, u32[]{:S(2)}, u32[]{:S(2)}) collective-permute-start(f32[2,4,384]{2,1,0:T(4,128)S(1)} %get-tuple-element.42), channel_id=1, source_target_pairs={{0,4},{2,6},{4,0},{6,2},{1,5},{3,7},{5,1},{7,3},{8,12},{10,14},{12... | collective-permute-start | bytes 36872 | tf_op jit(solution)/shard_map/ppermute | solution.py:607
  86.7 0.0 collective-permute-start.13
  86.7 0.2 collective-permute-done.11.s1
  86.9 0.0 copy-start.5
  86.9 1.3 %collective-permute-done.12.s2 = f32[2,4,384]{2,1,0:T(4,128)S(1)} collective-permute-done((f32[2,4,384]{2,1,0:T(4,128)S(1)}, f32[2,4,384]{2,1,0:T(4,128)S(1)}, u32[]{:S(2)}, u32[]{:S(2)}) %collective-permute-start.12) | collective-permute-done | bytes 12320 | tf_op jit(solution)/shard_map/ppermute | solution.py:607
  88.2 0.0 copy-start.6
  88.2 1.3 %collective-permute-done.13.s3 = f32[2,4,384]{2,1,0:T(4,128)S(1)} collective-permute-done((f32[2,4,384]{2,1,0:T(4,128)S(1)}, f32[2,4,384]{2,1,0:T(4,128)S(1)}, u32[]{:S(2)}, u32[]{:S(2)}) %collective-permute-start.13) | collective-permute-done | bytes 12320 | tf_op jit(solution)/shard_map/ppermute | solution.py:607
  89.6 0.0 copy-start.7
  89.6 5.6 %all-to-all-done.3.strips_ref = bf16[16,32,640]{2,1,0:T(8,128)(2,1)S(1)} async-done(((bf16[16,32,640]{2,1,0:T(8,128)(2,1)}), bf16[16,32,640]{2,1,0:T(8,128)(2,1)S(1)}, u32[]{:S(2)}, u32[]{:S(2)}) %all-to-all-start.3) | async-done | bytes 655392 | tf_op jit(solution)/shard_map/all_to_all | solution.py:599
  95.1 0.9 strip_sum.1
  96.0 0.6 copy-done.1
  96.6 5.9 %all-to-all-start.4 = ((bf16[16,24,640]{2,1,0:T(8,128)(2,1)}), bf16[16,24,640]{2,1,0:T(8,128)(2,1)S(1)}, u32[]{:S(2)}, u32[]{:S(2)}) async-start(bf16[16,24,640]{2,1,0:T(8,128)(2,1)} %get-tuple-element.45), calls=%async_computation.4 | async-start | bytes 983040 | tf_op jit(solution)/shard_map/all_to_all | solution.py:599
  102.5 0.9 collective-permute-start.14
  103.4 0.0 copy-done.5
  103.4 0.0 copy-done.6
  103.4 0.0 copy-done.7
  103.4 0.0 copy-start.3
  103.4 13.4 %block_backward.1 = bf16[256,3072]{1,0:T(8,128)(2,1)} custom-call(f32[2,4,384]{2,1,0:T(4,128)} %copy-done.4, f32[2,4,384]{2,1,0:T(4,128)} %copy-done.5, f32[2,4,384]{2,1,0:T(4,128)} %copy-done.6, f32[2,4,384]{2,1,0:T(4,128)} %copy-done.7, f32[4,3200]{1,0:T(4,128)} %get-tuple-element.50.normal_hbm, f32[1,3072]{1,0:T(1,128)} %bitcast.10, f32[1,3072]{1,0:T(1,128)} %bitcast.12, ...), custom_call_target="tpu_custom_call" | custom-call | bytes 42000000 | tf_op jit(solution)/shard_map/block_backward/pallas_call | solution.py:39
  116.8 0.0 collective-permute-done.14.got_ref
  116.8 0.0 copy-done.2
  116.8 0.0 copy-done.3
  116.9 0.8 text_grad.1
  117.7 0.0 all-to-all-done.4
  117.7 0.6 collective-permute-start.15
  118.3 1.5 %collective-permute-done.15.far_ref = bf16[384,640]{1,0:T(8,128)(2,1)S(1)} collective-permute-done((bf16[384,640]{1,0:T(8,128)(2,1)S(1)}, bf16[384,640]{1,0:T(8,128)(2,1)S(1)}, u32[]{:S(2)}, u32[]{:S(2)}) %collective-permute-start.15) | collective-permute-done | bytes 491552 | tf_op jit(solution)/shard_map/ppermute | solution.py:603
  119.8 1.3 %proj_join.1 = f32[384,1152]{1,0:T(8,128)} custom-call(bf16[384,640]{1,0:T(8,128)(2,1)S(1)} %bitcast.6, bf16[384,640]{1,0:T(8,128)(2,1)S(1)} %collective-permute-done.15.far_ref), custom_call_target="tpu_custom_call" | custom-call | bytes 6000000 | tf_op jit(solution)/shard_map/proj_join/pallas_call | solution.py:39
  (5 shorter events, 0.1 us)
Async XLA Ops:
  0.6 38.1 %copy-start = (bf16[384,1152]{1,0:T(8,128)(2,1)S(1)}, bf16[384,1152]{1,0:T(8,128)(2,1)}, u32[]{:S(2)}) copy-start(bf16[384,1152]{1,0:T(8,128)(2,1)} %projection_ref.3) | copy-start | bytes 2654212
  2.2 23.1 %all-to-all-start = ((bf16[16,4,1280]{2,1,0:T(4,128)(2,1)}), bf16[16,4,1280]{2,1,0:T(4,128)(2,1)S(1)}, u32[]{:S(2)}, u32[]{:S(2)}) async-start(bf16[16,4,1280]{2,1,0:T(4,128)(2,1)} %text_pack.1), calls=%async_computation | async-start | bytes 327680 | tf_op jit(solution)/shard_map/all_to_all | solution.py:599
  25.4 14.5 %collective-permute-start = (bf16[64,1280]{1,0:T(8,128)(2,1)S(1)}, bf16[64,1280]{1,0:T(8,128)(2,1)S(1)}, u32[]{:S(2)}, u32[]{:S(2)}) collective-permute-start(bf16[64,1280]{1,0:T(8,128)(2,1)S(1)} %line_rows.1.own_ref), channel_id=1, source_target_pairs={{0,1},{1,0},{2,3},{3,2},{4,5},{5,4},{6,7},{7,6},{8,9},{9,8},{10,11... | collective-permute-start | bytes 491528 | tf_op jit(solution)/shard_map/ppermute | solution.py:661
  39.9 10.9 %collective-permute-start.1 = (bf16[128,1280]{1,0:T(8,128)(2,1)S(1)}, bf16[128,1280]{1,0:T(8,128)(2,1)S(1)}, u32[]{:S(2)}, u32[]{:S(2)}) collective-permute-start(bf16[128,1280]{1,0:T(8,128)(2,1)S(1)} %join_texts.1.t0), channel_id=1, source_target_pairs={{0,2},{2,4},{4,6},{6,0},{1,3},{3,5},{5,7},{7,1},{8,10},{10,12},{12... | collective-permute-start | bytes 983048 | tf_op jit(solution)/shard_map/ppermute | solution.py:607
  40.2 21.2 %collective-permute-start.2 = (bf16[128,1280]{1,0:T(8,128)(2,1)S(1)}, bf16[128,1280]{1,0:T(8,128)(2,1)S(1)}, u32[]{:S(2)}, u32[]{:S(2)}) collective-permute-start(bf16[128,1280]{1,0:T(8,128)(2,1)S(1)} %join_texts.1.t0), channel_id=1, source_target_pairs={{0,6},{2,0},{4,2},{6,4},{1,7},{3,1},{5,3},{7,5},{8,14},{10,8},{12,... | collective-permute-start | bytes 983048 | tf_op jit(solution)/shard_map/ppermute | solution.py:607
  42.6 18.9 %collective-permute-start.3 = (bf16[128,1280]{1,0:T(8,128)(2,1)S(1)}, bf16[128,1280]{1,0:T(8,128)(2,1)S(1)}, u32[]{:S(2)}, u32[]{:S(2)}) collective-permute-start(bf16[128,1280]{1,0:T(8,128)(2,1)S(1)} %join_texts.1.t0), channel_id=1, source_target_pairs={{0,4},{2,6},{4,0},{6,2},{1,5},{3,7},{5,1},{7,3},{8,12},{10,14},{12... | collective-permute-start | bytes 983048 | tf_op jit(solution)/shard_map/ppermute | solution.py:607
  42.6 20.7 %all-to-all-start.2 = ((bf16[8,32,1152]{2,1,0:T(8,128)(2,1)}), bf16[8,32,1152]{2,1,0:T(8,128)(2,1)S(1)}, u32[]{:S(2)}, u32[]{:S(2)}) async-start(bf16[8,32,1152]{2,1,0:T(8,128)(2,1)} %get-tuple-element.33), calls=%async_computation.2 | async-start | bytes 1179648 | tf_op jit(solution)/shard_map/all_to_all | solution.py:599
  47.0 16.3 %collective-permute-start.4 = (bf16[128,1280]{1,0:T(8,128)(2,1)S(1)}, bf16[128,1280]{1,0:T(8,128)(2,1)S(1)}, u32[]{:S(2)}, u32[]{:S(2)}) collective-permute-start(bf16[128,1280]{1,0:T(8,128)(2,1)S(1)} %join_texts.1.t0), channel_id=1, source_target_pairs={{0,8},{8,0},{1,9},{9,1},{2,10},{10,2},{3,11},{11,3},{4,12},{12,4},... | collective-permute-start | bytes 983048 | tf_op jit(solution)/shard_map/ppermute | solution.py:603
  50.8 12.6 %collective-permute-start.5 = (bf16[128,1280]{1,0:T(8,128)(2,1)S(1)}, bf16[128,1280]{1,0:T(8,128)(2,1)S(1)}, u32[]{:S(2)}, u32[]{:S(2)}) collective-permute-start(bf16[128,1280]{1,0:T(8,128)(2,1)S(1)} %collective-permute-done.1.t1), channel_id=1, source_target_pairs={{0,8},{8,0},{1,9},{9,1},{2,10},{10,2},{3,11},{11,3},{4,12},{12,4},... | collective-permute-start | bytes 983048 | tf_op jit(solution)/shard_map/ppermute | solution.py:603
  61.5 1.9 %collective-permute-start.6 = (bf16[128,1280]{1,0:T(8,128)(2,1)S(1)}, bf16[128,1280]{1,0:T(8,128)(2,1)}, u32[]{:S(2)}, u32[]{:S(2)}) collective-permute-start(bf16[128,1280]{1,0:T(8,128)(2,1)S(1)} %collective-permute-done.2.t2), channel_id=1, source_target_pairs={{0,8},{8,0},{1,9},{9,1},{2,10},{10,2},{3,11},{11,3},{4,12},{12,4},... | collective-permute-start | bytes 983048 | tf_op jit(solution)/shard_map/ppermute | solution.py:603
  61.5 2.3 %collective-permute-start.7 = (bf16[128,1280]{1,0:T(8,128)(2,1)S(1)}, bf16[128,1280]{1,0:T(8,128)(2,1)}, u32[]{:S(2)}, u32[]{:S(2)}) collective-permute-start(bf16[128,1280]{1,0:T(8,128)(2,1)S(1)} %collective-permute-done.3.t3), channel_id=1, source_target_pairs={{0,8},{8,0},{1,9},{9,1},{2,10},{10,2},{3,11},{11,3},{4,12},{12,4},... | collective-permute-start | bytes 983048 | tf_op jit(solution)/shard_map/ppermute | solution.py:603
  66.8 2.3 %collective-permute-start.8 = (bf16[32,2560]{1,0:T(8,128)(2,1)S(1)}, bf16[32,2560]{1,0:T(8,128)(2,1)S(1)}, u32[]{:S(2)}, u32[]{:S(2)}) collective-permute-start(bf16[32,2560]{1,0:T(8,128)(2,1)S(1)} %get-tuple-element.37.mine_ref), channel_id=1, source_target_pairs={{0,8},{8,0},{1,9},{9,1},{2,10},{10,2},{3,11},{11,3},{4,12},{12,4},... | collective-permute-start | bytes 491528 | tf_op jit(solution)/shard_map/ppermute | solution.py:603
  67.9 1.2 collective-permute-start.9
  70.3 24.8 %all-to-all-start.3 = ((bf16[16,32,640]{2,1,0:T(8,128)(2,1)}), bf16[16,32,640]{2,1,0:T(8,128)(2,1)S(1)}, u32[]{:S(2)}, u32[]{:S(2)}) async-start(bf16[16,32,640]{2,1,0:T(8,128)(2,1)} %strip_make.1), calls=%async_computation.3 | async-start | bytes 1310720 | tf_op jit(solution)/shard_map/all_to_all | solution.py:599
  77.9 4.3 %collective-permute-start.10 = (f32[4,4,384]{2,1,0:T(4,128)S(1)}, f32[4,4,384]{2,1,0:T(4,128)S(1)}, u32[]{:S(2)}, u32[]{:S(2)}) collective-permute-start(f32[4,4,384]{2,1,0:T(4,128)S(1)} %get-tuple-element.39), channel_id=1, source_target_pairs={{0,1},{1,0},{2,3},{3,2},{4,5},{5,4},{6,7},{7,6},{8,9},{9,8},{10,11... | collective-permute-start | bytes 73736 | tf_op jit(solution)/shard_map/ppermute | solution.py:687
  82.2 0.6 copy-start.4
  82.8 4.1 %collective-permute-start.11 = (f32[2,4,384]{2,1,0:T(4,128)S(1)}, f32[2,4,384]{2,1,0:T(4,128)S(1)}, u32[]{:S(2)}, u32[]{:S(2)}) collective-permute-start(f32[2,4,384]{2,1,0:T(4,128)S(1)} %get-tuple-element.41), channel_id=1, source_target_pairs={{0,2},{2,4},{4,6},{6,0},{1,3},{3,5},{5,7},{7,1},{8,10},{10,12},{12... | collective-permute-start | bytes 36872 | tf_op jit(solution)/shard_map/ppermute | solution.py:607
  83.2 5.0 %collective-permute-start.12 = (f32[2,4,384]{2,1,0:T(4,128)S(1)}, f32[2,4,384]{2,1,0:T(4,128)S(1)}, u32[]{:S(2)}, u32[]{:S(2)}) collective-permute-start(f32[2,4,384]{2,1,0:T(4,128)S(1)} %get-tuple-element.42), channel_id=1, source_target_pairs={{0,4},{2,6},{4,0},{6,2},{1,5},{3,7},{5,1},{7,3},{8,12},{10,14},{12... | collective-permute-start | bytes 36872 | tf_op jit(solution)/shard_map/ppermute | solution.py:607
  86.7 2.8 %collective-permute-start.13 = (f32[2,4,384]{2,1,0:T(4,128)S(1)}, f32[2,4,384]{2,1,0:T(4,128)S(1)}, u32[]{:S(2)}, u32[]{:S(2)}) collective-permute-start(f32[2,4,384]{2,1,0:T(4,128)S(1)} %get-tuple-element.43), channel_id=1, source_target_pairs={{0,6},{2,0},{4,2},{6,4},{1,7},{3,1},{5,3},{7,5},{8,14},{10,8},{12,... | collective-permute-start | bytes 36872 | tf_op jit(solution)/shard_map/ppermute | solution.py:607
  86.9 16.5 %copy-start.5 = (f32[2,4,384]{2,1,0:T(4,128)}, f32[2,4,384]{2,1,0:T(4,128)S(1)}, u32[]{:S(2)}) copy-start(f32[2,4,384]{2,1,0:T(4,128)S(1)} %collective-permute-done.11.s1) | copy-start | bytes 36868
  88.2 15.2 %copy-start.6 = (f32[2,4,384]{2,1,0:T(4,128)}, f32[2,4,384]{2,1,0:T(4,128)S(1)}, u32[]{:S(2)}) copy-start(f32[2,4,384]{2,1,0:T(4,128)S(1)} %collective-permute-done.12.s2) | copy-start | bytes 36868
  89.6 13.8 %copy-start.7 = (f32[2,4,384]{2,1,0:T(4,128)}, f32[2,4,384]{2,1,0:T(4,128)S(1)}, u32[]{:S(2)}) copy-start(f32[2,4,384]{2,1,0:T(4,128)S(1)} %collective-permute-done.13.s3) | copy-start | bytes 36868
  96.0 0.6 copy-start.1
  96.6 21.1 %all-to-all-start.4 = ((bf16[16,24,640]{2,1,0:T(8,128)(2,1)}), bf16[16,24,640]{2,1,0:T(8,128)(2,1)S(1)}, u32[]{:S(2)}, u32[]{:S(2)}) async-start(bf16[16,24,640]{2,1,0:T(8,128)(2,1)} %get-tuple-element.45), calls=%async_computation.4 | async-start | bytes 983040 | tf_op jit(solution)/shard_map/all_to_all | solution.py:599
  102.5 14.3 %collective-permute-start.14 = (f32[4,640]{1,0:T(4,128)S(1)}, f32[4,640]{1,0:T(4,128)S(1)}, u32[]{:S(2)}, u32[]{:S(2)}) collective-permute-start(f32[4,640]{1,0:T(4,128)S(1)} %get-tuple-element.55), channel_id=1, source_target_pairs={{0,8},{8,0},{1,9},{9,1},{2,10},{10,2},{3,11},{11,3},{4,12},{12,4},... | collective-permute-start | bytes 30728 | tf_op jit(solution)/shard_map/ppermute | solution.py:603
  103.4 13.4 %copy-start.2 = (f32[4,640]{1,0:T(4,128)S(1)}, f32[4,640]{1,0:T(4,128)}, u32[]{:S(2)}) copy-start(f32[4,640]{1,0:T(4,128)} %copy-done.1) | copy-start | bytes 30724
  103.4 13.4 %copy-start.3 = (bf16[4,1152]{1,0:T(4,128)(2,1)S(1)}, bf16[4,1152]{1,0:T(4,128)(2,1)}, u32[]{:S(2)}) copy-start(bf16[4,1152]{1,0:T(4,128)(2,1)} %text_ref.1) | copy-start | bytes 27652
  117.7 2.1 %collective-permute-start.15 = (bf16[384,640]{1,0:T(8,128)(2,1)S(1)}, bf16[384,640]{1,0:T(8,128)(2,1)S(1)}, u32[]{:S(2)}, u32[]{:S(2)}) collective-permute-start(bf16[384,640]{1,0:T(8,128)(2,1)S(1)} %bitcast.5), channel_id=1, source_target_pairs={{0,8},{8,0},{1,9},{9,1},{2,10},{10,2},{3,11},{11,3},{4,12},{12,4},... | collective-permute-start | bytes 1474568 | tf_op jit(solution)/shard_map/ppermute | solution.py:603

commit v9 on v8

--- a/solution.py
+++ b/solution.py
@@ -154,7 +154,7 @@
         kernel_copy(step).wait()
         first = step * per_block
         return lax.fori_loop(
-            0, per_block, lambda chunk, held: filter_chunk(first + chunk, held), carry, unroll=2
+            0, per_block, lambda chunk, held: filter_chunk(first + chunk, held), carry, unroll=3
         )
 
     lax.fori_loop(0, STEPS, filter_block, 0)

time: 122 us -> 122 us (level)
  no operation moved by 1% of the time
where the time goes in v9:
time: 122 us; the launch traced here: 121 us
  starting transfers between devices  57 us (47%)
  Pallas kernels  36.2 us (30%)
  waiting for transfers between devices  13.9 us (11%)
  blocking collectives  10.7 us (9%)
  between operations  2.09 us (2%)
    pallas_call x12, Pallas kernels, call(): pl.pallas_call(body, out_shape=shapes[0] if single else shapes, in_specs=...  36.2 us
    all_to_all x4, starting transfers between devices, exchange(): return lax.all_to_all(blocks, axes, 0, 0, tiled=True)  28 us
    ppermute x8, starting transfers between devices, swap_core(): return lax.ppermute(block, 'core', ((0, 1), (1, 0)))  17.6 us
    all_to_all x1, blocking collectives, exchange(): return lax.all_to_all(blocks, axes, 0, 0, tiled=True)  10.7 us
    ppermute x6, starting transfers between devices, along_x(): lax.ppermute(block, 'x', tuple(((i, (i + step) % 4) for i in range(4))))  6.71 us
    all_to_all x4, waiting for transfers between devices, exchange(): return lax.all_to_all(blocks, axes, 0, 0, tiled=True)  5.64 us
    ppermute x8, waiting for transfers between devices, swap_core(): return lax.ppermute(block, 'core', ((0, 1), (1, 0)))  3.01 us
    ppermute x6, waiting for transfers between devices, along_x(): lax.ppermute(block, 'x', tuple(((i, (i + step) % 4) for i in range(4))))  2.84 us
  transfers between devices with their start and end apart: 20, of which 9 were waited for; matrix products, arithmetic and copies ran while one was open for 0% of the time, Pallas kernels for 23%

profile of v9, /device:TPU:1, one launch (start us, length us, event | category | flops | bytes accessed | tf_op | source)
XLA Modules:
  0.0 121.1 jit_solution(14248930561291110909)
XLA Ops:
  0.6 0.0 copy-start
  0.6 1.6 %text_pack.1 = bf16[16,4,1280]{2,1,0:T(4,128)(2,1)} custom-call(bf16[4,1152]{1,0:T(4,128)(2,1)} %text_ref.1, s32[4]{0:T(128)} %ids_hbm.2), custom_call_target="tpu_custom_call" | custom-call | bytes 3000000 | tf_op jit(solution)/shard_map/text_pack/pallas_call | solution.py:39
  2.2 10.1 %all-to-all-start = ((bf16[16,4,1280]{2,1,0:T(4,128)(2,1)}), bf16[16,4,1280]{2,1,0:T(4,128)(2,1)S(1)}, u32[]{:S(2)}, u32[]{:S(2)}) async-start(bf16[16,4,1280]{2,1,0:T(4,128)(2,1)} %text_pack.1), calls=%async_computation | async-start | bytes 327680 | tf_op jit(solution)/shard_map/all_to_all | solution.py:599
  12.4 12.9 %block_forward.1 = (f32[256,3072]{1,0:T(8,128)}, f32[256,128]{1,0:T(8,128)}, f32[256,128]{1,0:T(8,128)}, f32[4,3200]{1,0:T(4,128)}, bf16[8,4,512]{2,1,0:T(4,128)(2,1)}) custom-call(bf16[256,3072]{1,0:T(8,128)(2,1)} %bitcast.7, f32[7,7,3072]{2,1,0:T(8,128)} %kernel_hbm.3, f32[1,3072]{1,0:T(1,128)} %bitcast.9, f32[1,3072]{1,0:T(1,128)} %bitcast.11, s32[4]{0:T(128)} %ids_hbm.3), custom_call_target="tpu_custom_call" | custom-call | bytes 42000000 | tf_op jit(solution)/shard_map/block_forward/pallas_call | solution.py:39
  25.3 0.0 all-to-all-done.line_ref
  25.4 2.7 %collective-permute-start = (bf16[64,1280]{1,0:T(8,128)(2,1)S(1)}, bf16[64,1280]{1,0:T(8,128)(2,1)S(1)}, u32[]{:S(2)}, u32[]{:S(2)}) collective-permute-start(bf16[64,1280]{1,0:T(8,128)(2,1)S(1)} %line_rows.1.own_ref), channel_id=1, source_target_pairs={{0,1},{1,0},{2,3},{3,2},{4,5},{5,4},{6,7},{7,6},{8,9},{9,8},{10,11... | collective-permute-start | bytes 491528 | tf_op jit(solution)/shard_map/ppermute | solution.py:661
  28.1 10.7 %all_to_all.25.received_ref = bf16[8,4,512]{2,1,0:T(4,128)(2,1)S(1)} all-to-all(bf16[8,4,512]{2,1,0:T(4,128)(2,1)} %get-tuple-element.32), channel_id=1, replica_groups=mesh['y_lo'=2,'z'=8,'core'=2,'x'=4,'y_hi'=2] {'x','y_hi'}, dimensions={0} | all-to-all | bytes 65536 | tf_op jit(solution)/shard_map/all_to_all | solution.py:599
  38.7 0.0 copy-done
  38.7 1.1 partial_embed.1
  39.8 0.0 collective-permute-done.next_ref
  39.8 0.4 collective-permute-start.1
  40.2 2.4 %collective-permute-start.2 = (bf16[128,1280]{1,0:T(8,128)(2,1)S(1)}, bf16[128,1280]{1,0:T(8,128)(2,1)S(1)}, u32[]{:S(2)}, u32[]{:S(2)}) collective-permute-start(bf16[128,1280]{1,0:T(8,128)(2,1)S(1)} %join_texts.1.t0), channel_id=1, source_target_pairs={{0,6},{2,0},{4,2},{6,4},{1,7},{3,1},{5,3},{7,5},{8,14},{10,8},{12,... | collective-permute-start | bytes 983048 | tf_op jit(solution)/shard_map/ppermute | solution.py:607
  42.6 0.0 collective-permute-start.3
  42.6 4.4 %all-to-all-start.2 = ((bf16[8,32,1152]{2,1,0:T(8,128)(2,1)}), bf16[8,32,1152]{2,1,0:T(8,128)(2,1)S(1)}, u32[]{:S(2)}, u32[]{:S(2)}) async-start(bf16[8,32,1152]{2,1,0:T(8,128)(2,1)} %get-tuple-element.33), calls=%async_computation.2 | async-start | bytes 1179648 | tf_op jit(solution)/shard_map/all_to_all | solution.py:599
  47.0 3.8 %collective-permute-start.4 = (bf16[128,1280]{1,0:T(8,128)(2,1)S(1)}, bf16[128,1280]{1,0:T(8,128)(2,1)S(1)}, u32[]{:S(2)}, u32[]{:S(2)}) collective-permute-start(bf16[128,1280]{1,0:T(8,128)(2,1)S(1)} %join_texts.1.t0), channel_id=1, source_target_pairs={{0,8},{8,0},{1,9},{9,1},{2,10},{10,2},{3,11},{11,3},{4,12},{12,4},... | collective-permute-start | bytes 983048 | tf_op jit(solution)/shard_map/ppermute | solution.py:603
  50.8 0.0 collective-permute-done.1.t1
  50.8 10.7 %collective-permute-start.5 = (bf16[128,1280]{1,0:T(8,128)(2,1)S(1)}, bf16[128,1280]{1,0:T(8,128)(2,1)S(1)}, u32[]{:S(2)}, u32[]{:S(2)}) collective-permute-start(bf16[128,1280]{1,0:T(8,128)(2,1)S(1)} %collective-permute-done.1.t1), channel_id=1, source_target_pairs={{0,8},{8,0},{1,9},{9,1},{2,10},{10,2},{3,11},{11,3},{4,12},{12,4},... | collective-permute-start | bytes 983048 | tf_op jit(solution)/shard_map/ppermute | solution.py:603
  61.4 0.0 collective-permute-done.2.t2
  61.4 0.0 collective-permute-start.6
  61.4 0.0 collective-permute-done.3.t3
  61.4 0.5 collective-permute-start.7
  63.2 0.0 collective-permute-done.4.t4
  63.3 0.1 all-to-all-done.2.partials_ref
  63.3 0.0 collective-permute-done.5.t5
  63.3 0.0 collective-permute-done.6.t6
  63.3 0.4 collective-permute-done.7.t7
  63.8 3.0 %pairs.1 = (f32[4,4,384]{2,1,0:T(4,128)S(1)}, f32[4,4,384]{2,1,0:T(4,128)S(1)}, bf16[32,2560]{1,0:T(8,128)(2,1)S(1)}) custom-call(bf16[8,32,1152]{2,1,0:T(8,128)(2,1)S(1)} %all-to-all-done.2.partials_ref, bf16[32,128]{1,0:T(8,128)(2,1)S(1)} %get-tuple-element.34.hot_ref, bf16[384,1152]{1,0:T(8,128)(2,1)S(1)} %copy-done, bf16[128,1280]{1,0:T(8,128)(2,1)S(1)} %join_texts.1.t0, ...), custom_call_target="tpu_custom_call" | custom-call | bytes 12000000 | tf_op jit(solution)/shard_map/pairs/pallas_call | solution.py:39
  66.8 1.1 collective-permute-start.8
  67.8 0.1 collective-permute-start.9
  67.9 1.1 collective-permute-done.9.far_columns_ref
  69.0 0.0 collective-permute-done.8.theirs_ref
  69.0 1.2 %strip_make.1 = bf16[16,32,640]{2,1,0:T(8,128)(2,1)} custom-call(bf16[32,2560]{1,0:T(8,128)(2,1)S(1)} %get-tuple-element.37.mine_ref, bf16[32,2560]{1,0:T(8,128)(2,1)S(1)} %collective-permute-done.8.theirs_ref, bf16[32,384]{1,0:T(8,128)(2,1)S(1)} %get-tuple-element.36.after_ref.columns_ref, bf16[32,384]{1,0:T(8,128)(2,1)S(1)} %collective-permute-done.9.far_columns_ref), custom_call_target="tpu_custom_call" | custom-call | bytes 6000000 | tf_op jit(solution)/shard_map/strip_make/pallas_call | solution.py:39
  70.2 7.6 %all-to-all-start.3 = ((bf16[16,32,640]{2,1,0:T(8,128)(2,1)}), bf16[16,32,640]{2,1,0:T(8,128)(2,1)S(1)}, u32[]{:S(2)}, u32[]{:S(2)}) async-start(bf16[16,32,640]{2,1,0:T(8,128)(2,1)} %strip_make.1), calls=%async_computation.3 | async-start | bytes 1310720 | tf_op jit(solution)/shard_map/all_to_all | solution.py:599
  77.8 1.9 %collective-permute-start.10 = (f32[4,4,384]{2,1,0:T(4,128)S(1)}, f32[4,4,384]{2,1,0:T(4,128)S(1)}, u32[]{:S(2)}, u32[]{:S(2)}) collective-permute-start(f32[4,4,384]{2,1,0:T(4,128)S(1)} %get-tuple-element.39), channel_id=1, source_target_pairs={{0,1},{1,0},{2,3},{3,2},{4,5},{5,4},{6,7},{7,6},{8,9},{9,8},{10,11... | collective-permute-start | bytes 73736 | tf_op jit(solution)/shard_map/ppermute | solution.py:687
  79.8 2.4 %collective-permute-done.10.got_ref = f32[4,4,384]{2,1,0:T(4,128)S(1)} collective-permute-done((f32[4,4,384]{2,1,0:T(4,128)S(1)}, f32[4,4,384]{2,1,0:T(4,128)S(1)}, u32[]{:S(2)}, u32[]{:S(2)}) %collective-permute-start.10) | collective-permute-done | bytes 24608 | tf_op jit(solution)/shard_map/ppermute | solution.py:687
  82.1 0.0 copy-start.4
  82.1 0.6 copy-done.4
  82.7 0.4 collective-permute-start.11
  83.1 3.5 %collective-permute-start.12 = (f32[2,4,384]{2,1,0:T(4,128)S(1)}, f32[2,4,384]{2,1,0:T(4,128)S(1)}, u32[]{:S(2)}, u32[]{:S(2)}) collective-permute-start(f32[2,4,384]{2,1,0:T(4,128)S(1)} %get-tuple-element.42), channel_id=1, source_target_pairs={{0,4},{2,6},{4,0},{6,2},{1,5},{3,7},{5,1},{7,3},{8,12},{10,14},{12... | collective-permute-start | bytes 36872 | tf_op jit(solution)/shard_map/ppermute | solution.py:607
  86.7 0.0 collective-permute-start.13
  86.7 0.2 collective-permute-done.11.s1
  86.9 0.0 copy-start.5
  86.9 1.3 %collective-permute-done.12.s2 = f32[2,4,384]{2,1,0:T(4,128)S(1)} collective-permute-done((f32[2,4,384]{2,1,0:T(4,128)S(1)}, f32[2,4,384]{2,1,0:T(4,128)S(1)}, u32[]{:S(2)}, u32[]{:S(2)}) %collective-permute-start.12) | collective-permute-done | bytes 12320 | tf_op jit(solution)/shard_map/ppermute | solution.py:607
  88.2 0.0 copy-start.6
  88.2 1.3 %collective-permute-done.13.s3 = f32[2,4,384]{2,1,0:T(4,128)S(1)} collective-permute-done((f32[2,4,384]{2,1,0:T(4,128)S(1)}, f32[2,4,384]{2,1,0:T(4,128)S(1)}, u32[]{:S(2)}, u32[]{:S(2)}) %collective-permute-start.13) | collective-permute-done | bytes 12320 | tf_op jit(solution)/shard_map/ppermute | solution.py:607
  89.5 0.0 copy-start.7
  89.5 5.6 %all-to-all-done.3.strips_ref = bf16[16,32,640]{2,1,0:T(8,128)(2,1)S(1)} async-done(((bf16[16,32,640]{2,1,0:T(8,128)(2,1)}), bf16[16,32,640]{2,1,0:T(8,128)(2,1)S(1)}, u32[]{:S(2)}, u32[]{:S(2)}) %all-to-all-start.3) | async-done | bytes 655392 | tf_op jit(solution)/shard_map/all_to_all | solution.py:599
  95.1 0.9 strip_sum.1
  95.9 0.6 copy-done.1
  96.5 5.9 %all-to-all-start.4 = ((bf16[16,24,640]{2,1,0:T(8,128)(2,1)}), bf16[16,24,640]{2,1,0:T(8,128)(2,1)S(1)}, u32[]{:S(2)}, u32[]{:S(2)}) async-start(bf16[16,24,640]{2,1,0:T(8,128)(2,1)} %get-tuple-element.45), calls=%async_computation.4 | async-start | bytes 983040 | tf_op jit(solution)/shard_map/all_to_all | solution.py:599
  102.5 0.9 collective-permute-start.14
  103.4 0.0 copy-done.5
  103.4 0.0 copy-done.6
  103.4 0.0 copy-done.7
  103.4 0.0 copy-start.3
  103.4 13.4 %block_backward.1 = bf16[256,3072]{1,0:T(8,128)(2,1)} custom-call(f32[2,4,384]{2,1,0:T(4,128)} %copy-done.4, f32[2,4,384]{2,1,0:T(4,128)} %copy-done.5, f32[2,4,384]{2,1,0:T(4,128)} %copy-done.6, f32[2,4,384]{2,1,0:T(4,128)} %copy-done.7, f32[4,3200]{1,0:T(4,128)} %get-tuple-element.50.normal_hbm, f32[1,3072]{1,0:T(1,128)} %bitcast.10, f32[1,3072]{1,0:T(1,128)} %bitcast.12, ...), custom_call_target="tpu_custom_call" | custom-call | bytes 42000000 | tf_op jit(solution)/shard_map/block_backward/pallas_call | solution.py:39
  116.8 0.0 collective-permute-done.14.got_ref
  116.8 0.0 copy-done.2
  116.8 0.0 copy-done.3
  116.8 0.8 text_grad.1
  117.6 0.0 all-to-all-done.4
  117.6 0.6 collective-permute-start.15
  118.2 1.5 %collective-permute-done.15.far_ref = bf16[384,640]{1,0:T(8,128)(2,1)S(1)} collective-permute-done((bf16[384,640]{1,0:T(8,128)(2,1)S(1)}, bf16[384,640]{1,0:T(8,128)(2,1)S(1)}, u32[]{:S(2)}, u32[]{:S(2)}) %collective-permute-start.15) | collective-permute-done | bytes 491552 | tf_op jit(solution)/shard_map/ppermute | solution.py:603
  119.7 1.3 %proj_join.1 = f32[384,1152]{1,0:T(8,128)} custom-call(bf16[384,640]{1,0:T(8,128)(2,1)S(1)} %bitcast.6, bf16[384,640]{1,0:T(8,128)(2,1)S(1)} %collective-permute-done.15.far_ref), custom_call_target="tpu_custom_call" | custom-call | bytes 6000000 | tf_op jit(solution)/shard_map/proj_join/pallas_call | solution.py:39
  (5 shorter events, 0.1 us)
Async XLA Ops:
  0.6 38.1 %copy-start = (bf16[384,1152]{1,0:T(8,128)(2,1)S(1)}, bf16[384,1152]{1,0:T(8,128)(2,1)}, u32[]{:S(2)}) copy-start(bf16[384,1152]{1,0:T(8,128)(2,1)} %projection_ref.3) | copy-start | bytes 2654212
  2.2 23.1 %all-to-all-start = ((bf16[16,4,1280]{2,1,0:T(4,128)(2,1)}), bf16[16,4,1280]{2,1,0:T(4,128)(2,1)S(1)}, u32[]{:S(2)}, u32[]{:S(2)}) async-start(bf16[16,4,1280]{2,1,0:T(4,128)(2,1)} %text_pack.1), calls=%async_computation | async-start | bytes 327680 | tf_op jit(solution)/shard_map/all_to_all | solution.py:599
  25.4 14.5 %collective-permute-start = (bf16[64,1280]{1,0:T(8,128)(2,1)S(1)}, bf16[64,1280]{1,0:T(8,128)(2,1)S(1)}, u32[]{:S(2)}, u32[]{:S(2)}) collective-permute-start(bf16[64,1280]{1,0:T(8,128)(2,1)S(1)} %line_rows.1.own_ref), channel_id=1, source_target_pairs={{0,1},{1,0},{2,3},{3,2},{4,5},{5,4},{6,7},{7,6},{8,9},{9,8},{10,11... | collective-permute-start | bytes 491528 | tf_op jit(solution)/shard_map/ppermute | solution.py:661
  39.8 10.9 %collective-permute-start.1 = (bf16[128,1280]{1,0:T(8,128)(2,1)S(1)}, bf16[128,1280]{1,0:T(8,128)(2,1)S(1)}, u32[]{:S(2)}, u32[]{:S(2)}) collective-permute-start(bf16[128,1280]{1,0:T(8,128)(2,1)S(1)} %join_texts.1.t0), channel_id=1, source_target_pairs={{0,2},{2,4},{4,6},{6,0},{1,3},{3,5},{5,7},{7,1},{8,10},{10,12},{12... | collective-permute-start | bytes 983048 | tf_op jit(solution)/shard_map/ppermute | solution.py:607
  40.2 21.2 %collective-permute-start.2 = (bf16[128,1280]{1,0:T(8,128)(2,1)S(1)}, bf16[128,1280]{1,0:T(8,128)(2,1)S(1)}, u32[]{:S(2)}, u32[]{:S(2)}) collective-permute-start(bf16[128,1280]{1,0:T(8,128)(2,1)S(1)} %join_texts.1.t0), channel_id=1, source_target_pairs={{0,6},{2,0},{4,2},{6,4},{1,7},{3,1},{5,3},{7,5},{8,14},{10,8},{12,... | collective-permute-start | bytes 983048 | tf_op jit(solution)/shard_map/ppermute | solution.py:607
  42.6 18.9 %collective-permute-start.3 = (bf16[128,1280]{1,0:T(8,128)(2,1)S(1)}, bf16[128,1280]{1,0:T(8,128)(2,1)S(1)}, u32[]{:S(2)}, u32[]{:S(2)}) collective-permute-start(bf16[128,1280]{1,0:T(8,128)(2,1)S(1)} %join_texts.1.t0), channel_id=1, source_target_pairs={{0,4},{2,6},{4,0},{6,2},{1,5},{3,7},{5,1},{7,3},{8,12},{10,14},{12... | collective-permute-start | bytes 983048 | tf_op jit(solution)/shard_map/ppermute | solution.py:607
  42.6 20.7 %all-to-all-start.2 = ((bf16[8,32,1152]{2,1,0:T(8,128)(2,1)}), bf16[8,32,1152]{2,1,0:T(8,128)(2,1)S(1)}, u32[]{:S(2)}, u32[]{:S(2)}) async-start(bf16[8,32,1152]{2,1,0:T(8,128)(2,1)} %get-tuple-element.33), calls=%async_computation.2 | async-start | bytes 1179648 | tf_op jit(solution)/shard_map/all_to_all | solution.py:599
  47.0 16.3 %collective-permute-start.4 = (bf16[128,1280]{1,0:T(8,128)(2,1)S(1)}, bf16[128,1280]{1,0:T(8,128)(2,1)S(1)}, u32[]{:S(2)}, u32[]{:S(2)}) collective-permute-start(bf16[128,1280]{1,0:T(8,128)(2,1)S(1)} %join_texts.1.t0), channel_id=1, source_target_pairs={{0,8},{8,0},{1,9},{9,1},{2,10},{10,2},{3,11},{11,3},{4,12},{12,4},... | collective-permute-start | bytes 983048 | tf_op jit(solution)/shard_map/ppermute | solution.py:603
  50.8 12.6 %collective-permute-start.5 = (bf16[128,1280]{1,0:T(8,128)(2,1)S(1)}, bf16[128,1280]{1,0:T(8,128)(2,1)S(1)}, u32[]{:S(2)}, u32[]{:S(2)}) collective-permute-start(bf16[128,1280]{1,0:T(8,128)(2,1)S(1)} %collective-permute-done.1.t1), channel_id=1, source_target_pairs={{0,8},{8,0},{1,9},{9,1},{2,10},{10,2},{3,11},{11,3},{4,12},{12,4},... | collective-permute-start | bytes 983048 | tf_op jit(solution)/shard_map/ppermute | solution.py:603
  61.4 1.9 %collective-permute-start.6 = (bf16[128,1280]{1,0:T(8,128)(2,1)S(1)}, bf16[128,1280]{1,0:T(8,128)(2,1)}, u32[]{:S(2)}, u32[]{:S(2)}) collective-permute-start(bf16[128,1280]{1,0:T(8,128)(2,1)S(1)} %collective-permute-done.2.t2), channel_id=1, source_target_pairs={{0,8},{8,0},{1,9},{9,1},{2,10},{10,2},{3,11},{11,3},{4,12},{12,4},... | collective-permute-start | bytes 983048 | tf_op jit(solution)/shard_map/ppermute | solution.py:603
  61.4 2.3 %collective-permute-start.7 = (bf16[128,1280]{1,0:T(8,128)(2,1)S(1)}, bf16[128,1280]{1,0:T(8,128)(2,1)}, u32[]{:S(2)}, u32[]{:S(2)}) collective-permute-start(bf16[128,1280]{1,0:T(8,128)(2,1)S(1)} %collective-permute-done.3.t3), channel_id=1, source_target_pairs={{0,8},{8,0},{1,9},{9,1},{2,10},{10,2},{3,11},{11,3},{4,12},{12,4},... | collective-permute-start | bytes 983048 | tf_op jit(solution)/shard_map/ppermute | solution.py:603
  66.8 2.3 %collective-permute-start.8 = (bf16[32,2560]{1,0:T(8,128)(2,1)S(1)}, bf16[32,2560]{1,0:T(8,128)(2,1)S(1)}, u32[]{:S(2)}, u32[]{:S(2)}) collective-permute-start(bf16[32,2560]{1,0:T(8,128)(2,1)S(1)} %get-tuple-element.37.mine_ref), channel_id=1, source_target_pairs={{0,8},{8,0},{1,9},{9,1},{2,10},{10,2},{3,11},{11,3},{4,12},{12,4},... | collective-permute-start | bytes 491528 | tf_op jit(solution)/shard_map/ppermute | solution.py:603
  67.8 1.2 collective-permute-start.9
  70.2 24.8 %all-to-all-start.3 = ((bf16[16,32,640]{2,1,0:T(8,128)(2,1)}), bf16[16,32,640]{2,1,0:T(8,128)(2,1)S(1)}, u32[]{:S(2)}, u32[]{:S(2)}) async-start(bf16[16,32,640]{2,1,0:T(8,128)(2,1)} %strip_make.1), calls=%async_computation.3 | async-start | bytes 1310720 | tf_op jit(solution)/shard_map/all_to_all | solution.py:599
  77.8 4.3 %collective-permute-start.10 = (f32[4,4,384]{2,1,0:T(4,128)S(1)}, f32[4,4,384]{2,1,0:T(4,128)S(1)}, u32[]{:S(2)}, u32[]{:S(2)}) collective-permute-start(f32[4,4,384]{2,1,0:T(4,128)S(1)} %get-tuple-element.39), channel_id=1, source_target_pairs={{0,1},{1,0},{2,3},{3,2},{4,5},{5,4},{6,7},{7,6},{8,9},{9,8},{10,11... | collective-permute-start | bytes 73736 | tf_op jit(solution)/shard_map/ppermute | solution.py:687
  82.1 0.6 copy-start.4
  82.7 4.1 %collective-permute-start.11 = (f32[2,4,384]{2,1,0:T(4,128)S(1)}, f32[2,4,384]{2,1,0:T(4,128)S(1)}, u32[]{:S(2)}, u32[]{:S(2)}) collective-permute-start(f32[2,4,384]{2,1,0:T(4,128)S(1)} %get-tuple-element.41), channel_id=1, source_target_pairs={{0,2},{2,4},{4,6},{6,0},{1,3},{3,5},{5,7},{7,1},{8,10},{10,12},{12... | collective-permute-start | bytes 36872 | tf_op jit(solution)/shard_map/ppermute | solution.py:607
  83.1 5.0 %collective-permute-start.12 = (f32[2,4,384]{2,1,0:T(4,128)S(1)}, f32[2,4,384]{2,1,0:T(4,128)S(1)}, u32[]{:S(2)}, u32[]{:S(2)}) collective-permute-start(f32[2,4,384]{2,1,0:T(4,128)S(1)} %get-tuple-element.42), channel_id=1, source_target_pairs={{0,4},{2,6},{4,0},{6,2},{1,5},{3,7},{5,1},{7,3},{8,12},{10,14},{12... | collective-permute-start | bytes 36872 | tf_op jit(solution)/shard_map/ppermute | solution.py:607
  86.7 2.8 %collective-permute-start.13 = (f32[2,4,384]{2,1,0:T(4,128)S(1)}, f32[2,4,384]{2,1,0:T(4,128)S(1)}, u32[]{:S(2)}, u32[]{:S(2)}) collective-permute-start(f32[2,4,384]{2,1,0:T(4,128)S(1)} %get-tuple-element.43), channel_id=1, source_target_pairs={{0,6},{2,0},{4,2},{6,4},{1,7},{3,1},{5,3},{7,5},{8,14},{10,8},{12,... | collective-permute-start | bytes 36872 | tf_op jit(solution)/shard_map/ppermute | solution.py:607
  86.9 16.5 %copy-start.5 = (f32[2,4,384]{2,1,0:T(4,128)}, f32[2,4,384]{2,1,0:T(4,128)S(1)}, u32[]{:S(2)}) copy-start(f32[2,4,384]{2,1,0:T(4,128)S(1)} %collective-permute-done.11.s1) | copy-start | bytes 36868
  88.2 15.2 %copy-start.6 = (f32[2,4,384]{2,1,0:T(4,128)}, f32[2,4,384]{2,1,0:T(4,128)S(1)}, u32[]{:S(2)}) copy-start(f32[2,4,384]{2,1,0:T(4,128)S(1)} %collective-permute-done.12.s2) | copy-start | bytes 36868
  89.5 13.8 %copy-start.7 = (f32[2,4,384]{2,1,0:T(4,128)}, f32[2,4,384]{2,1,0:T(4,128)S(1)}, u32[]{:S(2)}) copy-start(f32[2,4,384]{2,1,0:T(4,128)S(1)} %collective-permute-done.13.s3) | copy-start | bytes 36868
  95.9 0.6 copy-start.1
  96.5 21.1 %all-to-all-start.4 = ((bf16[16,24,640]{2,1,0:T(8,128)(2,1)}), bf16[16,24,640]{2,1,0:T(8,128)(2,1)S(1)}, u32[]{:S(2)}, u32[]{:S(2)}) async-start(bf16[16,24,640]{2,1,0:T(8,128)(2,1)} %get-tuple-element.45), calls=%async_computation.4 | async-start | bytes 983040 | tf_op jit(solution)/shard_map/all_to_all | solution.py:599
  102.5 14.3 %collective-permute-start.14 = (f32[4,640]{1,0:T(4,128)S(1)}, f32[4,640]{1,0:T(4,128)S(1)}, u32[]{:S(2)}, u32[]{:S(2)}) collective-permute-start(f32[4,640]{1,0:T(4,128)S(1)} %get-tuple-element.55), channel_id=1, source_target_pairs={{0,8},{8,0},{1,9},{9,1},{2,10},{10,2},{3,11},{11,3},{4,12},{12,4},... | collective-permute-start | bytes 30728 | tf_op jit(solution)/shard_map/ppermute | solution.py:603
  103.4 13.4 %copy-start.2 = (f32[4,640]{1,0:T(4,128)S(1)}, f32[4,640]{1,0:T(4,128)}, u32[]{:S(2)}) copy-start(f32[4,640]{1,0:T(4,128)} %copy-done.1) | copy-start | bytes 30724
  103.4 13.4 %copy-start.3 = (bf16[4,1152]{1,0:T(4,128)(2,1)S(1)}, bf16[4,1152]{1,0:T(4,128)(2,1)}, u32[]{:S(2)}) copy-start(bf16[4,1152]{1,0:T(4,128)(2,1)} %text_ref.1) | copy-start | bytes 27652
  117.6 2.1 %collective-permute-start.15 = (bf16[384,640]{1,0:T(8,128)(2,1)S(1)}, bf16[384,640]{1,0:T(8,128)(2,1)S(1)}, u32[]{:S(2)}, u32[]{:S(2)}) collective-permute-start(bf16[384,640]{1,0:T(8,128)(2,1)S(1)} %bitcast.5), channel_id=1, source_target_pairs={{0,8},{8,0},{1,9},{9,1},{2,10},{10,2},{3,11},{11,3},{4,12},{12,4},... | collective-permute-start | bytes 1474568 | tf_op jit(solution)/shard_map/ppermute | solution.py:603

commit v10 on v9

--- a/solution.py
+++ b/solution.py
@@ -667,7 +667,7 @@
             "join_texts", 1,
         )
     ]
-    near += [along_x(near[0], step) for step in (1, 3, 2)]
+    near += [along_x(near[0], step) for step in (2, 1, 3)]
     far = [swap_core(block) for block in near]
     far_columns = swap_core(columns)
     partials = exchange(partials, GROUP)

time: 122 us -> 122 us (level)
  waiting for transfers between devices: 13.9 us -> 19.2 us
  starting transfers between devices: 57 us -> 51.9 us
    ppermute x8, starting transfers between devices: 17.6 us -> 12.3 us  [swap_core(): return lax.ppermute(block, 'core', ((0, 1), (1, 0)))]
    all_to_all x4, waiting for transfers between devices: 5.64 us -> 9.72 us  [exchange(): return lax.all_to_all(blocks, axes, 0, 0, tiled=True)]
    ppermute x6, waiting for transfers between devices: 2.84 us -> 5.2 us  [along_x(): lax.ppermute(block, 'x', tuple(((i, (i + step) % 4) for i in range(4))))]
  transfers between devices with their start and end apart: 20 -> 20, of which waited for: 9 -> 8; matrix products, arithmetic and copies ran while one was open for 0% -> 0% of each run, Pallas kernels for 23% -> 23%
where the time goes in v10:
time: 122 us; the launch traced here: 121 us
  starting transfers between devices  51.9 us (43%)
  Pallas kernels  36.2 us (30%)
  waiting for transfers between devices  19.2 us (16%)
  blocking collectives  10.7 us (9%)
  between operations  2.1 us (2%)
    pallas_call x12, Pallas kernels, call(): pl.pallas_call(body, out_shape=shapes[0] if single else shapes, in_specs=...  36.2 us
    all_to_all x4, starting transfers between devices, exchange(): return lax.all_to_all(blocks, axes, 0, 0, tiled=True)  27.1 us
    ppermute x8, starting transfers between devices, swap_core(): return lax.ppermute(block, 'core', ((0, 1), (1, 0)))  12.3 us
    all_to_all x1, blocking collectives, exchange(): return lax.all_to_all(blocks, axes, 0, 0, tiled=True)  10.7 us
    all_to_all x4, waiting for transfers between devices, exchange(): return lax.all_to_all(blocks, axes, 0, 0, tiled=True)  9.72 us
    ppermute x6, starting transfers between devices, along_x(): lax.ppermute(block, 'x', tuple(((i, (i + step) % 4) for i in range(4))))  7.18 us
    ppermute x6, waiting for transfers between devices, along_x(): lax.ppermute(block, 'x', tuple(((i, (i + step) % 4) for i in range(4))))  5.2 us
    ppermute x1, starting transfers between devices, local(): next_line = lax.ppermute(own_line, 'y_hi', ((0, 1), (1, 0)))  2.71 us
  transfers between devices with their start and end apart: 20, of which 8 were waited for; matrix products, arithmetic and copies ran while one was open for 0% of the time, Pallas kernels for 23%

profile of v10, /device:TPU:1, one launch (start us, length us, event | category | flops | bytes accessed | tf_op | source)
XLA Modules:
  0.0 121.3 jit_solution(8420635099975557189)
XLA Ops:
  0.6 0.0 copy-start
  0.6 1.6 %text_pack.1 = bf16[16,4,1280]{2,1,0:T(4,128)(2,1)} custom-call(bf16[4,1152]{1,0:T(4,128)(2,1)} %text_ref.1, s32[4]{0:T(128)} %ids_hbm.2), custom_call_target="tpu_custom_call" | custom-call | bytes 3000000 | tf_op jit(solution)/shard_map/text_pack/pallas_call | solution.py:39
  2.2 10.1 %all-to-all-start = ((bf16[16,4,1280]{2,1,0:T(4,128)(2,1)}), bf16[16,4,1280]{2,1,0:T(4,128)(2,1)S(1)}, u32[]{:S(2)}, u32[]{:S(2)}) async-start(bf16[16,4,1280]{2,1,0:T(4,128)(2,1)} %text_pack.1), calls=%async_computation | async-start | bytes 327680 | tf_op jit(solution)/shard_map/all_to_all | solution.py:599
  12.4 12.9 %block_forward.1 = (f32[256,3072]{1,0:T(8,128)}, f32[256,128]{1,0:T(8,128)}, f32[256,128]{1,0:T(8,128)}, f32[4,3200]{1,0:T(4,128)}, bf16[8,4,512]{2,1,0:T(4,128)(2,1)}) custom-call(bf16[256,3072]{1,0:T(8,128)(2,1)} %bitcast.7, f32[7,7,3072]{2,1,0:T(8,128)} %kernel_hbm.3, f32[1,3072]{1,0:T(1,128)} %bitcast.9, f32[1,3072]{1,0:T(1,128)} %bitcast.11, s32[4]{0:T(128)} %ids_hbm.3), custom_call_target="tpu_custom_call" | custom-call | bytes 42000000 | tf_op jit(solution)/shard_map/block_forward/pallas_call | solution.py:39
  25.3 0.0 all-to-all-done.line_ref
  25.4 2.7 %collective-permute-start = (bf16[64,1280]{1,0:T(8,128)(2,1)S(1)}, bf16[64,1280]{1,0:T(8,128)(2,1)S(1)}, u32[]{:S(2)}, u32[]{:S(2)}) collective-permute-start(bf16[64,1280]{1,0:T(8,128)(2,1)S(1)} %line_rows.1.own_ref), channel_id=1, source_target_pairs={{0,1},{1,0},{2,3},{3,2},{4,5},{5,4},{6,7},{7,6},{8,9},{9,8},{10,11... | collective-permute-start | bytes 491528 | tf_op jit(solution)/shard_map/ppermute | solution.py:661
  28.1 10.7 %all_to_all.25.received_ref = bf16[8,4,512]{2,1,0:T(4,128)(2,1)S(1)} all-to-all(bf16[8,4,512]{2,1,0:T(4,128)(2,1)} %get-tuple-element.32), channel_id=1, replica_groups=mesh['y_lo'=2,'z'=8,'core'=2,'x'=4,'y_hi'=2] {'x','y_hi'}, dimensions={0} | all-to-all | bytes 65536 | tf_op jit(solution)/shard_map/all_to_all | solution.py:599
  38.7 0.0 copy-done
  38.7 1.1 partial_embed.1
  39.8 0.0 collective-permute-done.next_ref
  39.8 1.1 collective-permute-start.1
  40.9 0.5 collective-permute-start.2
  41.4 2.2 %collective-permute-start.3 = (bf16[128,1280]{1,0:T(8,128)(2,1)S(1)}, bf16[128,1280]{1,0:T(8,128)(2,1)S(1)}, u32[]{:S(2)}, u32[]{:S(2)}) collective-permute-start(bf16[128,1280]{1,0:T(8,128)(2,1)S(1)} %join_texts.1.t0), channel_id=1, source_target_pairs={{0,6},{2,0},{4,2},{6,4},{1,7},{3,1},{5,3},{7,5},{8,14},{10,8},{12,... | collective-permute-start | bytes 983048 | tf_op jit(solution)/shard_map/ppermute | solution.py:607
  43.6 3.5 %all-to-all-start.2 = ((bf16[8,32,1152]{2,1,0:T(8,128)(2,1)}), bf16[8,32,1152]{2,1,0:T(8,128)(2,1)S(1)}, u32[]{:S(2)}, u32[]{:S(2)}) async-start(bf16[8,32,1152]{2,1,0:T(8,128)(2,1)} %get-tuple-element.33), calls=%async_computation.2 | async-start | bytes 1179648 | tf_op jit(solution)/shard_map/all_to_all | solution.py:599
  47.1 3.6 %collective-permute-start.4 = (bf16[128,1280]{1,0:T(8,128)(2,1)S(1)}, bf16[128,1280]{1,0:T(8,128)(2,1)S(1)}, u32[]{:S(2)}, u32[]{:S(2)}) collective-permute-start(bf16[128,1280]{1,0:T(8,128)(2,1)S(1)} %join_texts.1.t0), channel_id=1, source_target_pairs={{0,8},{8,0},{1,9},{9,1},{2,10},{10,2},{3,11},{11,3},{4,12},{12,4},... | collective-permute-start | bytes 983048 | tf_op jit(solution)/shard_map/ppermute | solution.py:603
  50.7 0.0 collective-permute-done.1.t1
  50.7 4.0 %collective-permute-start.5 = (bf16[128,1280]{1,0:T(8,128)(2,1)S(1)}, bf16[128,1280]{1,0:T(8,128)(2,1)S(1)}, u32[]{:S(2)}, u32[]{:S(2)}) collective-permute-start(bf16[128,1280]{1,0:T(8,128)(2,1)S(1)} %collective-permute-done.1.t1), channel_id=1, source_target_pairs={{0,8},{8,0},{1,9},{9,1},{2,10},{10,2},{3,11},{11,3},{4,12},{12,4},... | collective-permute-start | bytes 983048 | tf_op jit(solution)/shard_map/ppermute | solution.py:603
  54.7 3.3 %collective-permute-done.2.t2 = bf16[128,1280]{1,0:T(8,128)(2,1)S(1)} collective-permute-done((bf16[128,1280]{1,0:T(8,128)(2,1)S(1)}, bf16[128,1280]{1,0:T(8,128)(2,1)S(1)}, u32[]{:S(2)}, u32[]{:S(2)}) %collective-permute-start.2) | collective-permute-done | bytes 327712 | tf_op jit(solution)/shard_map/ppermute | solution.py:607
  58.1 1.0 collective-permute-start.6
  59.0 0.0 collective-permute-done.3.t3
  59.0 1.2 collective-permute-start.7
  61.5 0.0 collective-permute-done.4.t4
  61.5 2.7 %all-to-all-done.2.partials_ref = bf16[8,32,1152]{2,1,0:T(8,128)(2,1)S(1)} async-done(((bf16[8,32,1152]{2,1,0:T(8,128)(2,1)}), bf16[8,32,1152]{2,1,0:T(8,128)(2,1)S(1)}, u32[]{:S(2)}, u32[]{:S(2)}) %all-to-all-start.2) | async-done | bytes 589856 | tf_op jit(solution)/shard_map/all_to_all | solution.py:599
  64.2 0.0 collective-permute-done.5.t5
  64.2 0.0 collective-permute-done.6.t6
  64.2 0.0 collective-permute-done.7.t7
  64.3 3.0 %pairs.1 = (f32[4,4,384]{2,1,0:T(4,128)S(1)}, f32[4,4,384]{2,1,0:T(4,128)S(1)}, bf16[32,2560]{1,0:T(8,128)(2,1)S(1)}) custom-call(bf16[8,32,1152]{2,1,0:T(8,128)(2,1)S(1)} %all-to-all-done.2.partials_ref, bf16[32,128]{1,0:T(8,128)(2,1)S(1)} %get-tuple-element.34.hot_ref, bf16[384,1152]{1,0:T(8,128)(2,1)S(1)} %copy-done, bf16[128,1280]{1,0:T(8,128)(2,1)S(1)} %join_texts.1.t0, ...), custom_call_target="tpu_custom_call" | custom-call | bytes 12000000 | tf_op jit(solution)/shard_map/pairs/pallas_call | solution.py:39
  67.3 0.9 collective-permute-start.8
  68.1 0.1 collective-permute-start.9
  68.2 1.1 collective-permute-done.9.far_columns_ref
  69.3 0.0 collective-permute-done.8.theirs_ref
  69.3 1.2 %strip_make.1 = bf16[16,32,640]{2,1,0:T(8,128)(2,1)} custom-call(bf16[32,2560]{1,0:T(8,128)(2,1)S(1)} %get-tuple-element.37.mine_ref, bf16[32,2560]{1,0:T(8,128)(2,1)S(1)} %collective-permute-done.8.theirs_ref, bf16[32,384]{1,0:T(8,128)(2,1)S(1)} %get-tuple-element.36.after_ref.columns_ref, bf16[32,384]{1,0:T(8,128)(2,1)S(1)} %collective-permute-done.9.far_columns_ref), custom_call_target="tpu_custom_call" | custom-call | bytes 6000000 | tf_op jit(solution)/shard_map/strip_make/pallas_call | solution.py:39
  70.5 7.5 %all-to-all-start.3 = ((bf16[16,32,640]{2,1,0:T(8,128)(2,1)}), bf16[16,32,640]{2,1,0:T(8,128)(2,1)S(1)}, u32[]{:S(2)}, u32[]{:S(2)}) async-start(bf16[16,32,640]{2,1,0:T(8,128)(2,1)} %strip_make.1), calls=%async_computation.3 | async-start | bytes 1310720 | tf_op jit(solution)/shard_map/all_to_all | solution.py:599
  78.0 2.6 %collective-permute-start.10 = (f32[4,4,384]{2,1,0:T(4,128)S(1)}, f32[4,4,384]{2,1,0:T(4,128)S(1)}, u32[]{:S(2)}, u32[]{:S(2)}) collective-permute-start(f32[4,4,384]{2,1,0:T(4,128)S(1)} %get-tuple-element.39), channel_id=1, source_target_pairs={{0,1},{1,0},{2,3},{3,2},{4,5},{5,4},{6,7},{7,6},{8,9},{9,8},{10,11... | collective-permute-start | bytes 73736 | tf_op jit(solution)/shard_map/ppermute | solution.py:687
  80.6 1.7 %collective-permute-done.10.got_ref = f32[4,4,384]{2,1,0:T(4,128)S(1)} collective-permute-done((f32[4,4,384]{2,1,0:T(4,128)S(1)}, f32[4,4,384]{2,1,0:T(4,128)S(1)}, u32[]{:S(2)}, u32[]{:S(2)}) %collective-permute-start.10) | collective-permute-done | bytes 24608 | tf_op jit(solution)/shard_map/ppermute | solution.py:687
  82.3 0.0 copy-start.4
  82.3 0.6 copy-done.4
  82.9 1.0 collective-permute-start.11
  83.9 1.0 collective-permute-start.12
  84.9 1.4 %collective-permute-start.13 = (f32[2,4,384]{2,1,0:T(4,128)S(1)}, f32[2,4,384]{2,1,0:T(4,128)S(1)}, u32[]{:S(2)}, u32[]{:S(2)}) collective-permute-start(f32[2,4,384]{2,1,0:T(4,128)S(1)} %get-tuple-element.43), channel_id=1, source_target_pairs={{0,6},{2,0},{4,2},{6,4},{1,7},{3,1},{5,3},{7,5},{8,14},{10,8},{12,... | collective-permute-start | bytes 36872 | tf_op jit(solution)/shard_map/ppermute | solution.py:607
  86.4 0.6 collective-permute-done.11.s1
  87.0 0.0 copy-start.5
  87.0 1.3 %collective-permute-done.12.s2 = f32[2,4,384]{2,1,0:T(4,128)S(1)} collective-permute-done((f32[2,4,384]{2,1,0:T(4,128)S(1)}, f32[2,4,384]{2,1,0:T(4,128)S(1)}, u32[]{:S(2)}, u32[]{:S(2)}) %collective-permute-start.12) | collective-permute-done | bytes 12320 | tf_op jit(solution)/shard_map/ppermute | solution.py:607
  88.2 0.0 copy-start.6
  88.2 0.0 collective-permute-done.13.s3
  88.2 0.0 copy-start.7
  88.2 7.0 %all-to-all-done.3.strips_ref = bf16[16,32,640]{2,1,0:T(8,128)(2,1)S(1)} async-done(((bf16[16,32,640]{2,1,0:T(8,128)(2,1)}), bf16[16,32,640]{2,1,0:T(8,128)(2,1)S(1)}, u32[]{:S(2)}, u32[]{:S(2)}) %all-to-all-start.3) | async-done | bytes 655392 | tf_op jit(solution)/shard_map/all_to_all | solution.py:599
  95.3 0.9 strip_sum.1
  96.1 0.6 copy-done.1
  96.7 6.0 %all-to-all-start.4 = ((bf16[16,24,640]{2,1,0:T(8,128)(2,1)}), bf16[16,24,640]{2,1,0:T(8,128)(2,1)S(1)}, u32[]{:S(2)}, u32[]{:S(2)}) async-start(bf16[16,24,640]{2,1,0:T(8,128)(2,1)} %get-tuple-element.45), calls=%async_computation.4 | async-start | bytes 983040 | tf_op jit(solution)/shard_map/all_to_all | solution.py:599
  102.7 0.9 collective-permute-start.14
  103.6 0.0 copy-done.5
  103.6 0.0 copy-done.6
  103.6 0.0 copy-done.7
  103.6 0.0 copy-start.3
  103.6 13.4 %block_backward.1 = bf16[256,3072]{1,0:T(8,128)(2,1)} custom-call(f32[2,4,384]{2,1,0:T(4,128)} %copy-done.4, f32[2,4,384]{2,1,0:T(4,128)} %copy-done.5, f32[2,4,384]{2,1,0:T(4,128)} %copy-done.6, f32[2,4,384]{2,1,0:T(4,128)} %copy-done.7, f32[4,3200]{1,0:T(4,128)} %get-tuple-element.50.normal_hbm, f32[1,3072]{1,0:T(1,128)} %bitcast.10, f32[1,3072]{1,0:T(1,128)} %bitcast.12, ...), custom_call_target="tpu_custom_call" | custom-call | bytes 42000000 | tf_op jit(solution)/shard_map/block_backward/pallas_call | solution.py:39
  117.0 0.0 collective-permute-done.14.got_ref
  117.0 0.0 copy-done.2
  117.0 0.0 copy-done.3
  117.0 0.8 text_grad.1
  117.8 0.0 all-to-all-done.4
  117.8 0.6 collective-permute-start.15
  118.5 1.5 %collective-permute-done.15.far_ref = bf16[384,640]{1,0:T(8,128)(2,1)S(1)} collective-permute-done((bf16[384,640]{1,0:T(8,128)(2,1)S(1)}, bf16[384,640]{1,0:T(8,128)(2,1)S(1)}, u32[]{:S(2)}, u32[]{:S(2)}) %collective-permute-start.15) | collective-permute-done | bytes 491552 | tf_op jit(solution)/shard_map/ppermute | solution.py:603
  120.0 1.3 %proj_join.1 = f32[384,1152]{1,0:T(8,128)} custom-call(bf16[384,640]{1,0:T(8,128)(2,1)S(1)} %bitcast.6, bf16[384,640]{1,0:T(8,128)(2,1)S(1)} %collective-permute-done.15.far_ref), custom_call_target="tpu_custom_call" | custom-call | bytes 6000000 | tf_op jit(solution)/shard_map/proj_join/pallas_call | solution.py:39
  (5 shorter events, 0.1 us)
Async XLA Ops:
  0.6 38.1 %copy-start = (bf16[384,1152]{1,0:T(8,128)(2,1)S(1)}, bf16[384,1152]{1,0:T(8,128)(2,1)}, u32[]{:S(2)}) copy-start(bf16[384,1152]{1,0:T(8,128)(2,1)} %projection_ref.3) | copy-start | bytes 2654212
  2.2 23.1 %all-to-all-start = ((bf16[16,4,1280]{2,1,0:T(4,128)(2,1)}), bf16[16,4,1280]{2,1,0:T(4,128)(2,1)S(1)}, u32[]{:S(2)}, u32[]{:S(2)}) async-start(bf16[16,4,1280]{2,1,0:T(4,128)(2,1)} %text_pack.1), calls=%async_computation | async-start | bytes 327680 | tf_op jit(solution)/shard_map/all_to_all | solution.py:599
  25.4 14.5 %collective-permute-start = (bf16[64,1280]{1,0:T(8,128)(2,1)S(1)}, bf16[64,1280]{1,0:T(8,128)(2,1)S(1)}, u32[]{:S(2)}, u32[]{:S(2)}) collective-permute-start(bf16[64,1280]{1,0:T(8,128)(2,1)S(1)} %line_rows.1.own_ref), channel_id=1, source_target_pairs={{0,1},{1,0},{2,3},{3,2},{4,5},{5,4},{6,7},{7,6},{8,9},{9,8},{10,11... | collective-permute-start | bytes 491528 | tf_op jit(solution)/shard_map/ppermute | solution.py:661
  39.8 10.9 %collective-permute-start.1 = (bf16[128,1280]{1,0:T(8,128)(2,1)S(1)}, bf16[128,1280]{1,0:T(8,128)(2,1)S(1)}, u32[]{:S(2)}, u32[]{:S(2)}) collective-permute-start(bf16[128,1280]{1,0:T(8,128)(2,1)S(1)} %join_texts.1.t0), channel_id=1, source_target_pairs={{0,4},{2,6},{4,0},{6,2},{1,5},{3,7},{5,1},{7,3},{8,12},{10,14},{12... | collective-permute-start | bytes 983048 | tf_op jit(solution)/shard_map/ppermute | solution.py:607
  40.9 17.2 %collective-permute-start.2 = (bf16[128,1280]{1,0:T(8,128)(2,1)S(1)}, bf16[128,1280]{1,0:T(8,128)(2,1)S(1)}, u32[]{:S(2)}, u32[]{:S(2)}) collective-permute-start(bf16[128,1280]{1,0:T(8,128)(2,1)S(1)} %join_texts.1.t0), channel_id=1, source_target_pairs={{0,2},{2,4},{4,6},{6,0},{1,3},{3,5},{5,7},{7,1},{8,10},{10,12},{12... | collective-permute-start | bytes 983048 | tf_op jit(solution)/shard_map/ppermute | solution.py:607
  41.4 17.6 %collective-permute-start.3 = (bf16[128,1280]{1,0:T(8,128)(2,1)S(1)}, bf16[128,1280]{1,0:T(8,128)(2,1)S(1)}, u32[]{:S(2)}, u32[]{:S(2)}) collective-permute-start(bf16[128,1280]{1,0:T(8,128)(2,1)S(1)} %join_texts.1.t0), channel_id=1, source_target_pairs={{0,6},{2,0},{4,2},{6,4},{1,7},{3,1},{5,3},{7,5},{8,14},{10,8},{12,... | collective-permute-start | bytes 983048 | tf_op jit(solution)/shard_map/ppermute | solution.py:607
  43.6 20.7 %all-to-all-start.2 = ((bf16[8,32,1152]{2,1,0:T(8,128)(2,1)}), bf16[8,32,1152]{2,1,0:T(8,128)(2,1)S(1)}, u32[]{:S(2)}, u32[]{:S(2)}) async-start(bf16[8,32,1152]{2,1,0:T(8,128)(2,1)} %get-tuple-element.33), calls=%async_computation.2 | async-start | bytes 1179648 | tf_op jit(solution)/shard_map/all_to_all | solution.py:599
  47.1 14.4 %collective-permute-start.4 = (bf16[128,1280]{1,0:T(8,128)(2,1)S(1)}, bf16[128,1280]{1,0:T(8,128)(2,1)S(1)}, u32[]{:S(2)}, u32[]{:S(2)}) collective-permute-start(bf16[128,1280]{1,0:T(8,128)(2,1)S(1)} %join_texts.1.t0), channel_id=1, source_target_pairs={{0,8},{8,0},{1,9},{9,1},{2,10},{10,2},{3,11},{11,3},{4,12},{12,4},... | collective-permute-start | bytes 983048 | tf_op jit(solution)/shard_map/ppermute | solution.py:603
  50.7 13.5 %collective-permute-start.5 = (bf16[128,1280]{1,0:T(8,128)(2,1)S(1)}, bf16[128,1280]{1,0:T(8,128)(2,1)S(1)}, u32[]{:S(2)}, u32[]{:S(2)}) collective-permute-start(bf16[128,1280]{1,0:T(8,128)(2,1)S(1)} %collective-permute-done.1.t1), channel_id=1, source_target_pairs={{0,8},{8,0},{1,9},{9,1},{2,10},{10,2},{3,11},{11,3},{4,12},{12,4},... | collective-permute-start | bytes 983048 | tf_op jit(solution)/shard_map/ppermute | solution.py:603
  58.1 6.2 %collective-permute-start.6 = (bf16[128,1280]{1,0:T(8,128)(2,1)S(1)}, bf16[128,1280]{1,0:T(8,128)(2,1)}, u32[]{:S(2)}, u32[]{:S(2)}) collective-permute-start(bf16[128,1280]{1,0:T(8,128)(2,1)S(1)} %collective-permute-done.2.t2), channel_id=1, source_target_pairs={{0,8},{8,0},{1,9},{9,1},{2,10},{10,2},{3,11},{11,3},{4,12},{12,4},... | collective-permute-start | bytes 983048 | tf_op jit(solution)/shard_map/ppermute | solution.py:603
  59.0 5.2 %collective-permute-start.7 = (bf16[128,1280]{1,0:T(8,128)(2,1)S(1)}, bf16[128,1280]{1,0:T(8,128)(2,1)}, u32[]{:S(2)}, u32[]{:S(2)}) collective-permute-start(bf16[128,1280]{1,0:T(8,128)(2,1)S(1)} %collective-permute-done.3.t3), channel_id=1, source_target_pairs={{0,8},{8,0},{1,9},{9,1},{2,10},{10,2},{3,11},{11,3},{4,12},{12,4},... | collective-permute-start | bytes 983048 | tf_op jit(solution)/shard_map/ppermute | solution.py:603
  67.3 2.1 %collective-permute-start.8 = (bf16[32,2560]{1,0:T(8,128)(2,1)S(1)}, bf16[32,2560]{1,0:T(8,128)(2,1)S(1)}, u32[]{:S(2)}, u32[]{:S(2)}) collective-permute-start(bf16[32,2560]{1,0:T(8,128)(2,1)S(1)} %get-tuple-element.37.mine_ref), channel_id=1, source_target_pairs={{0,8},{8,0},{1,9},{9,1},{2,10},{10,2},{3,11},{11,3},{4,12},{12,4},... | collective-permute-start | bytes 491528 | tf_op jit(solution)/shard_map/ppermute | solution.py:603
  68.1 1.2 collective-permute-start.9
  70.5 24.7 %all-to-all-start.3 = ((bf16[16,32,640]{2,1,0:T(8,128)(2,1)}), bf16[16,32,640]{2,1,0:T(8,128)(2,1)S(1)}, u32[]{:S(2)}, u32[]{:S(2)}) async-start(bf16[16,32,640]{2,1,0:T(8,128)(2,1)} %strip_make.1), calls=%async_computation.3 | async-start | bytes 1310720 | tf_op jit(solution)/shard_map/all_to_all | solution.py:599
  78.0 4.3 %collective-permute-start.10 = (f32[4,4,384]{2,1,0:T(4,128)S(1)}, f32[4,4,384]{2,1,0:T(4,128)S(1)}, u32[]{:S(2)}, u32[]{:S(2)}) collective-permute-start(f32[4,4,384]{2,1,0:T(4,128)S(1)} %get-tuple-element.39), channel_id=1, source_target_pairs={{0,1},{1,0},{2,3},{3,2},{4,5},{5,4},{6,7},{7,6},{8,9},{9,8},{10,11... | collective-permute-start | bytes 73736 | tf_op jit(solution)/shard_map/ppermute | solution.py:687
  82.3 0.6 copy-start.4
  82.9 4.1 %collective-permute-start.11 = (f32[2,4,384]{2,1,0:T(4,128)S(1)}, f32[2,4,384]{2,1,0:T(4,128)S(1)}, u32[]{:S(2)}, u32[]{:S(2)}) collective-permute-start(f32[2,4,384]{2,1,0:T(4,128)S(1)} %get-tuple-element.41), channel_id=1, source_target_pairs={{0,2},{2,4},{4,6},{6,0},{1,3},{3,5},{5,7},{7,1},{8,10},{10,12},{12... | collective-permute-start | bytes 36872 | tf_op jit(solution)/shard_map/ppermute | solution.py:607
  83.9 4.3 %collective-permute-start.12 = (f32[2,4,384]{2,1,0:T(4,128)S(1)}, f32[2,4,384]{2,1,0:T(4,128)S(1)}, u32[]{:S(2)}, u32[]{:S(2)}) collective-permute-start(f32[2,4,384]{2,1,0:T(4,128)S(1)} %get-tuple-element.42), channel_id=1, source_target_pairs={{0,4},{2,6},{4,0},{6,2},{1,5},{3,7},{5,1},{7,3},{8,12},{10,14},{12... | collective-permute-start | bytes 36872 | tf_op jit(solution)/shard_map/ppermute | solution.py:607
  84.9 3.3 %collective-permute-start.13 = (f32[2,4,384]{2,1,0:T(4,128)S(1)}, f32[2,4,384]{2,1,0:T(4,128)S(1)}, u32[]{:S(2)}, u32[]{:S(2)}) collective-permute-start(f32[2,4,384]{2,1,0:T(4,128)S(1)} %get-tuple-element.43), channel_id=1, source_target_pairs={{0,6},{2,0},{4,2},{6,4},{1,7},{3,1},{5,3},{7,5},{8,14},{10,8},{12,... | collective-permute-start | bytes 36872 | tf_op jit(solution)/shard_map/ppermute | solution.py:607
  87.0 16.6 %copy-start.5 = (f32[2,4,384]{2,1,0:T(4,128)}, f32[2,4,384]{2,1,0:T(4,128)S(1)}, u32[]{:S(2)}) copy-start(f32[2,4,384]{2,1,0:T(4,128)S(1)} %collective-permute-done.11.s1) | copy-start | bytes 36868
  88.2 15.3 %copy-start.6 = (f32[2,4,384]{2,1,0:T(4,128)}, f32[2,4,384]{2,1,0:T(4,128)S(1)}, u32[]{:S(2)}) copy-start(f32[2,4,384]{2,1,0:T(4,128)S(1)} %collective-permute-done.12.s2) | copy-start | bytes 36868
  88.2 15.3 %copy-start.7 = (f32[2,4,384]{2,1,0:T(4,128)}, f32[2,4,384]{2,1,0:T(4,128)S(1)}, u32[]{:S(2)}) copy-start(f32[2,4,384]{2,1,0:T(4,128)S(1)} %collective-permute-done.13.s3) | copy-start | bytes 36868
  96.1 0.6 copy-start.1
  96.7 21.1 %all-to-all-start.4 = ((bf16[16,24,640]{2,1,0:T(8,128)(2,1)}), bf16[16,24,640]{2,1,0:T(8,128)(2,1)S(1)}, u32[]{:S(2)}, u32[]{:S(2)}) async-start(bf16[16,24,640]{2,1,0:T(8,128)(2,1)} %get-tuple-element.45), calls=%async_computation.4 | async-start | bytes 983040 | tf_op jit(solution)/shard_map/all_to_all | solution.py:599
  102.7 14.3 %collective-permute-start.14 = (f32[4,640]{1,0:T(4,128)S(1)}, f32[4,640]{1,0:T(4,128)S(1)}, u32[]{:S(2)}, u32[]{:S(2)}) collective-permute-start(f32[4,640]{1,0:T(4,128)S(1)} %get-tuple-element.55), channel_id=1, source_target_pairs={{0,8},{8,0},{1,9},{9,1},{2,10},{10,2},{3,11},{11,3},{4,12},{12,4},... | collective-permute-start | bytes 30728 | tf_op jit(solution)/shard_map/ppermute | solution.py:603
  103.6 13.4 %copy-start.2 = (f32[4,640]{1,0:T(4,128)S(1)}, f32[4,640]{1,0:T(4,128)}, u32[]{:S(2)}) copy-start(f32[4,640]{1,0:T(4,128)} %copy-done.1) | copy-start | bytes 30724
  103.6 13.4 %copy-start.3 = (bf16[4,1152]{1,0:T(4,128)(2,1)S(1)}, bf16[4,1152]{1,0:T(4,128)(2,1)}, u32[]{:S(2)}) copy-start(bf16[4,1152]{1,0:T(4,128)(2,1)} %text_ref.1) | copy-start | bytes 27652
  117.8 2.1 %collective-permute-start.15 = (bf16[384,640]{1,0:T(8,128)(2,1)S(1)}, bf16[384,640]{1,0:T(8,128)(2,1)S(1)}, u32[]{:S(2)}, u32[]{:S(2)}) collective-permute-start(bf16[384,640]{1,0:T(8,128)(2,1)S(1)} %bitcast.5), channel_id=1, source_target_pairs={{0,8},{8,0},{1,9},{9,1},{2,10},{10,2},{3,11},{11,3},{4,12},{12,4},... | collective-permute-start | bytes 1474568 | tf_op jit(solution)/shard_map/ppermute | solution.py:603
